TPU v7x, 32 devices: a whole 2x2x4 slice. The times are simulated.
32 devices in a mesh: row: 8 (over y, x, core), src: 4 (over z).
Axes of the slice: x: 2, y: 2, z: 4, core: 2. Of those that a mesh axis runs over, the one named last changes fastest.
Arguments:
- traces: bfloat16 [16384, 128, 512], P('row', 'src'), may hold values from -6 to 6
- row_source: int32 [16384], P('row'), may hold values from 0 to 16383, as said below
- slice_data: bfloat16 [2, 16384, 8, 2048], P(None, 'row', None, 'src'), may hold values from -0.03125 to 0.03125
- wavelet_inverse: float32 [2], replicated, may hold values from 0.3 to 0.8
Outputs:
- multiples: float32 [16384, 2, 128], P(('row', 'src'))
- primaries: float32 [16384, 2, 128], P(('row', 'src'))
Inputs may be any that keep to these rules, and one draw needn't show every extreme that they name: `row_source`: every recording row is named exactly once; entry e * 2048 + p names a recording row whose index modulo 2048 lies in [e * 256, (e + 1) * 256).
All inputs are finite; a program needn't handle non-finite values.
Results may differ from a plain program's by a relative error of at most 0.0056.
Values may be sent and summed in bfloat16 or wider, within the bound.
No kernel may reach another device: no remote copies, remote signals or barrier semaphores. Data moves between devices by JAX's collectives and lax.ppermute only.
A program may use at most 192 MiB of HBM per device.

v0:
```python
import functools

import jax
import jax.numpy as jnp
import ml_dtypes
import numpy as np
from jax import lax
from jax.experimental import pallas as pl
from jax.experimental.pallas import tpu as pltpu
from jax.sharding import PartitionSpec as P

FREQ = 61
ITERS = 3
LANES = 128
BUFFERS = 4
VMEM = pl.BlockSpec(memory_space=pltpu.VMEM)
ANY = pl.BlockSpec(memory_space=pl.ANY)
SMEM = pl.BlockSpec(memory_space=pltpu.SMEM)


def dft_table(samples):
    ticks = np.arange(samples, dtype=np.int32)
    moment = ticks.astype(np.float32)
    ramp_len = samples // 8
    pi = np.float32(np.pi)
    half = np.float32(0.5)
    rising = half - half * np.cos(pi * (moment + half) / np.float32(ramp_len))
    falling = half - half * np.cos(pi * (np.float32(samples) - moment - half) / np.float32(ramp_len))
    taper = np.where(
        ticks < ramp_len, rising, np.where(ticks >= samples - ramp_len, falling, np.ones_like(rising))
    )
    wrapped = ticks * FREQ % samples
    angles = np.float32(2.0 * np.pi / samples) * wrapped.astype(np.float32)
    factor = np.float32(1.0) / np.sqrt(np.float32(samples))
    table = np.stack([taper * np.cos(angles) * factor, -taper * np.sin(angles) * factor], axis=1)
    return table.astype(ml_dtypes.bfloat16)


def params(megabytes):
    return pltpu.CompilerParams(vmem_limit_bytes=megabytes * 2**20)


def cost(flops, moved):
    return pl.CostEstimate(flops=int(flops), bytes_accessed=int(moved), transcendentals=0)


def streamed(steps, source, held, sems, work):
    slots = held.shape[0]

    def copy(step):
        slot = step % slots
        return pltpu.make_async_copy(source(step), held.at[slot], sems.at[slot])

    for step in range(min(slots - 1, steps)):
        copy(step).start()

    @pl.loop(0, steps)
    def _(step):
        @pl.when(step + slots - 1 < steps)
        def _():
            copy(step + slots - 1).start()

        copy(step).wait()
        work(step, held.at[step % slots])


def spectra_kernel(packs, n_row, place_ref, traces_ref, table_ref, *refs):
    out_refs, held, sems = refs[:n_row], refs[n_row], refs[n_row + 1]
    block = held.shape[1]
    steps = traces_ref.shape[0] // n_row // block

    def source(step):
        first = ((place_ref[0] ^ (step // steps)) * steps + step % steps) * block
        return traces_ref.at[pl.ds(pl.multiple_of(first, block), block)]

    def work(step, traces):
        packed = spectra_of(packs, traces, table_ref)
        for turn, out_ref in enumerate(out_refs):

            @pl.when(step // steps == turn)
            def _():
                out_ref[step % steps] = packed

    streamed(n_row * steps, source, held, sems, work)


def spectra_of(packs, traces_ref, table_ref):
    block, shots, samples = traces_ref.shape
    width = 2 * shots
    half = block // 2
    shot = lax.broadcasted_iota(jnp.int32, (1, shots, 2 * LANES), 1)
    lane = lax.broadcasted_iota(jnp.int32, (1, shots, 2 * LANES), 2)
    own = lane % shots == shot
    sides = [traces_ref[side * half : (side + 1) * half].reshape(half * shots, samples) for side in range(2)]
    terms = jnp.dot(jnp.concatenate(sides, axis=1), table_ref[...], preferred_element_type=jnp.float32)
    rows = jnp.sum(jnp.where(own, terms.reshape(half, shots, 2 * LANES), 0.0), axis=1)
    spectra = jnp.concatenate([rows[:, :LANES], rows[:, LANES:]], axis=0)
    short = block // packs
    column = lax.broadcasted_iota(jnp.int32, (short, LANES), 1)
    packed = spectra[:short]
    for part in range(1, packs):
        packed = jnp.where(column // width == part, spectra[part * short : (part + 1) * short], packed)
    return packed.astype(jnp.bfloat16)


def make_spectra(traces, place, n_row, packs, block):
    block_rows, shots, samples = traces.shape
    steps = block_rows // n_row // block
    short = block // packs
    columns = np.tile(np.repeat(dft_table(samples), shots, axis=1), (1, packs))
    table = jnp.asarray(np.block([[columns, 0 * columns], [0 * columns, columns]]))

    outs = pl.pallas_call(
        functools.partial(spectra_kernel, packs, n_row),
        in_specs=[SMEM, ANY, VMEM],
        out_specs=[VMEM] * n_row,
        out_shape=[jax.ShapeDtypeStruct((steps, short, LANES), jnp.bfloat16)] * n_row,
        scratch_shapes=[
            pltpu.VMEM((BUFFERS, block, shots, samples), jnp.bfloat16),
            pltpu.SemaphoreType.DMA((BUFFERS,)),
        ],
        compiler_params=params(48),
        cost_estimate=cost(2 * traces.size * LANES, 2 * traces.size),
        name="spectra",
    )(place, traces, table)
    return [out.reshape(steps * short, LANES) for out in outs]


def order_kernel(packs, n_src, place_ref, code_ref, *refs):
    pieces, out_refs = refs[: -n_src - 1], refs[-n_src:]
    width = LANES // packs
    held = jnp.concatenate([ref[...] for ref in pieces], axis=0)
    rolled = [held] + [
        pltpu.roll(held.astype(jnp.float32), turn * width, 1).astype(jnp.bfloat16) for turn in range(1, packs)
    ]
    table = jnp.concatenate(rolled, axis=1)
    depth = table.shape[0]
    slice_rows = code_ref.shape[0] // n_src
    short = slice_rows // packs
    column = lax.broadcasted_iota(jnp.int32, (short, LANES), 1)
    for turn, out_ref in enumerate(out_refs):
        first = pl.multiple_of((place_ref[1] ^ turn) * slice_rows, slice_rows)
        packed = None
        for part in range(packs):
            code = code_ref[pl.ds(pl.multiple_of(first + part * short, short), short), :]
            position, side = code // packs, code % packs
            hits = []
            for start in range(0, depth, LANES):
                hits.append(jnp.where(position == column + start, 1.0, 0.0).astype(jnp.bfloat16))
            chosen = jnp.concatenate(hits, axis=1)[:, :depth]
            rows = jnp.dot(chosen, table, preferred_element_type=jnp.float32)
            moved = rows[:, :LANES]
            for turned in range(1, packs):
                moved = jnp.where(
                    (part - side + packs) % packs == turned, rows[:, turned * LANES : (turned + 1) * LANES], moved
                )
            packed = moved if packed is None else jnp.where(column // width == part, moved, packed)
        out_ref[...] = packed.astype(jnp.bfloat16)


def make_order(code, pieces, place, n_src, packs, after):
    slice_rows = code.shape[0] // n_src
    return pl.pallas_call(
        functools.partial(order_kernel, packs, n_src),
        in_specs=[SMEM] + [VMEM] * (1 + len(pieces)) + [ANY],
        out_specs=[VMEM] * n_src,
        out_shape=[jax.ShapeDtypeStruct((slice_rows // packs, LANES), jnp.bfloat16)] * n_src,
        compiler_params=params(6),
        cost_estimate=cost(2 * code.shape[0] * len(pieces) * pieces[0].size * packs, 4 * code.size),
        name="order",
    )(place, code, *pieces, after)


def panel_kernel(packs, place_ref, *refs):
    pieces, panel_ref = refs[:-2], refs[-1]
    short = pieces[0].shape[0]
    width = LANES // packs
    shots = width // 2
    columns = panel_ref.shape[1]
    lane = lax.broadcasted_iota(jnp.int32, (LANES, packs * columns), 0)
    target = lax.broadcasted_iota(jnp.int32, (LANES, packs * columns), 1)
    total = None
    for turn, piece in enumerate(pieces):
        shot = (place_ref[1] ^ turn) * shots + lane % shots
        goes = lane // width * columns + lane % width // shots * (columns // 2) + shot
        chosen = jnp.where(target == goes, 1.0, 0.0).astype(jnp.bfloat16)
        term = jnp.dot(piece[...], chosen, preferred_element_type=jnp.float32)
        total = term if total is None else total + term
    for part in range(packs):
        panel_ref[part * short : (part + 1) * short, :] = total[:, part * columns : (part + 1) * columns].astype(
            jnp.bfloat16
        )


def make_panel(pieces, place, packs, after):
    rows = pieces[0].shape[0] * packs
    columns = len(pieces) * (LANES // packs)
    return pl.pallas_call(
        functools.partial(panel_kernel, packs),
        in_specs=[SMEM] + [VMEM] * len(pieces) + [ANY],
        out_specs=VMEM,
        out_shape=jax.ShapeDtypeStruct((rows, columns), jnp.bfloat16),
        compiler_params=params(4),
        cost_estimate=cost(2 * len(pieces) * rows * LANES * columns, 4 * rows * columns),
        name="panel",
    )(place, *pieces, after)


def relay_kernel(part, data_ref, after_ref, out_ref, token_ref, held, sems):
    token_ref[...] = jnp.zeros_like(token_ref)
    step_rows = held.shape[1]

    def source(step):
        return data_ref.at[part, pl.ds(pl.multiple_of(step * step_rows, step_rows), step_rows)]

    def work(step, data):
        rows = pl.ds(pl.multiple_of(step * step_rows, step_rows), step_rows)
        out_ref[:, rows, :] = jnp.swapaxes(data[...], 0, 1)

    streamed(data_ref.shape[1] // step_rows, source, held, sems, work)


def relay(slice_data, part, after):
    _, block_rows, blocks, offsets = slice_data.shape
    step_rows = min(block_rows, 128)
    return pl.pallas_call(
        functools.partial(relay_kernel, part),
        in_specs=[ANY, ANY],
        out_specs=[VMEM] * 2,
        out_shape=[
            jax.ShapeDtypeStruct((blocks, block_rows, offsets), jnp.bfloat16),
            jax.ShapeDtypeStruct((8, LANES), jnp.float32),
        ],
        scratch_shapes=[
            pltpu.VMEM((BUFFERS, step_rows, blocks, offsets), jnp.bfloat16),
            pltpu.SemaphoreType.DMA((BUFFERS,)),
        ],
        compiler_params=params(12),
        cost_estimate=cost(0, 2 * slice_data.size),
        name="relay",
    )(slice_data, after)


def terms_kernel(turns, n_pieces, place_ref, real_ref, imag_ref, *refs):
    pieces, out_refs = refs[:n_pieces], refs[-len(turns) :]
    columns = pieces[0].shape[1]
    kept = columns // 2
    for turn, out_ref in zip(turns, out_refs):
        size = out_ref.shape[0]
        rows = pl.ds(pl.multiple_of((place_ref[1] ^ turn) * size, size), size)
        total = jnp.zeros((2 * size, columns), jnp.float32)
        for number, piece in enumerate(pieces):
            block = place_ref[0] ^ number
            both = jnp.concatenate([real_ref[block, rows, :], imag_ref[block, rows, :]], axis=0)
            total += jnp.dot(both, piece[...], preferred_element_type=jnp.float32)
        by_real, by_imag = total[:size], total[size:]
        out_ref[:, :kept] = (by_real[:, :kept] - by_imag[:, kept:]).astype(out_ref.dtype)
        out_ref[:, kept:] = (by_real[:, kept:] + by_imag[:, :kept]).astype(out_ref.dtype)


def make_terms(real_data, imag_data, pieces, place, turns, slice_rows, after):
    depth = real_data.shape[0] * real_data.shape[2]
    columns = pieces[0].shape[1]
    rows = len(turns) * slice_rows
    return pl.pallas_call(
        functools.partial(terms_kernel, turns, len(pieces)),
        in_specs=[SMEM] + [VMEM] * (2 + len(pieces)) + [ANY] * len(after),
        out_specs=[VMEM] * len(turns),
        out_shape=[
            jax.ShapeDtypeStruct((slice_rows, columns), jnp.bfloat16 if turn else jnp.float32) for turn in turns
        ],
        compiler_params=params(8),
        cost_estimate=cost(4 * rows * depth * columns, 4 * rows * depth),
        name="terms",
    )(place, real_data, imag_data, *pieces, *after)


def update(wave_ref, own_ref, others, panel_ref):
    predicted = own_ref[...]
    for other in others:
        predicted += other[...].astype(jnp.float32)
    kept = predicted.shape[1] // 2
    turned = jnp.concatenate([-predicted[:, kept:], predicted[:, :kept]], axis=1)
    scaled = wave_ref[0] * predicted + wave_ref[1] * turned
    return predicted, panel_ref[...].astype(jnp.float32) - scaled


def estimate_kernel(wave_ref, own_ref, *refs):
    *others, panel_ref, out_ref = refs
    out_ref[...] = update(wave_ref, own_ref, others, panel_ref)[1].astype(jnp.bfloat16)


def last_kernel(wave_ref, own_ref, *refs):
    *others, panel_ref, multiples_ref, primaries_ref = refs
    predicted, primaries = update(wave_ref, own_ref, others, panel_ref)
    kept = predicted.shape[1] // 2
    multiples_ref[:, 0, :] = predicted[:, :kept]
    multiples_ref[:, 1, :] = predicted[:, kept:]
    primaries_ref[:, 0, :] = primaries[:, :kept]
    primaries_ref[:, 1, :] = primaries[:, kept:]


def make_update(wavelet, own, others, panel, last):
    rows, columns = panel.shape
    if last:
        shape = [jax.ShapeDtypeStruct((rows, 2, columns // 2), jnp.float32)] * 2
    else:
        shape = jax.ShapeDtypeStruct((rows, columns), jnp.bfloat16)
    return pl.pallas_call(
        last_kernel if last else estimate_kernel,
        in_specs=[SMEM] + [VMEM] * (2 + len(others)),
        out_specs=[VMEM] * 2 if last else VMEM,
        out_shape=shape,
        compiler_params=params(8),
        cost_estimate=cost(16 * rows * columns, 16 * rows * columns),
        name="update",
    )(wavelet, own, *others, panel)


def swap(array, axis, bits):
    size = lax.axis_size(axis)
    return lax.ppermute(array, axis, [(index, index ^ bits) for index in range(size)])


def spread(array, axis):
    size = lax.axis_size(axis)
    pieces = {0: array}
    for turn in range(2, size, 2):
        pieces[turn] = swap(array, axis, turn)
    for turn in range(0, size, 2):
        pieces[turn + 1] = swap(pieces[turn], axis, 1)
    return [pieces[turn] for turn in range(size)]


def body(traces, row_source, slice_data, wavelet_inverse):
    block_rows, shots, _ = traces.shape
    n_row, n_src = lax.axis_size("row"), lax.axis_size("src")
    row, src = lax.axis_index("row"), lax.axis_index("src")
    place = jnp.stack([row, src]).astype(jnp.int32)
    packs = LANES // (2 * shots)
    group_rows = block_rows // n_row
    slice_rows = block_rows // n_src
    block = min(group_rows, 128)
    short = block // packs

    spectra = make_spectra(traces, place, n_row, packs, block)
    arrived = [spectra[0]] + [swap(spectra[turn], "row", turn) for turn in range(1, n_row)]

    inside = row_source % group_rows
    position = (row_source // block_rows ^ row) * (group_rows // packs) + inside // block * short + inside % short
    code = position * packs + inside % block // short
    code = jnp.broadcast_to(code[:, None], (block_rows, LANES))
    real_data, real_token = relay(slice_data, 0, spectra[0])
    ordered = make_order(code, arrived, place, n_src, packs, real_token)
    located = [ordered[0]] + [swap(ordered[turn], "src", turn) for turn in range(1, n_src)]
    imag_data, imag_token = relay(slice_data, 1, ordered[0])
    panel = make_panel(located, place, packs, imag_token)

    half = n_src // 2
    estimate = panel
    for iteration in range(ITERS):
        pieces = spread(estimate, "row")
        arriving, after = [], []
        for turn in range(n_src - 1, half - 1, -1):
            after = make_terms(real_data, imag_data, pieces, place, (turn,), slice_rows, [])
            arriving.append(swap(after[0], "src", turn))
        near = tuple(range(half - 1, -1, -1))
        terms = make_terms(real_data, imag_data, pieces, place, near, slice_rows, [])
        arriving += [swap(part, "src", turn) for turn, part in zip(near[:-1], terms)]
        estimate = make_update(wavelet_inverse, terms[-1], arriving, panel, iteration == ITERS - 1)
    return tuple(estimate)


def solution(mesh):
    in_specs = (P("row", "src", None), P("row"), P(None, "row", None, "src"), P())
    out_specs = (P(("row", "src"), None, None), P(("row", "src"), None, None))
    return jax.shard_map(body, mesh=mesh, in_specs=in_specs, out_specs=out_specs, check_vma=False)
```

profile of v0, /device:TPU:0, one launch (start us, length us, event | category | flops | bytes accessed | tf_op | source)
XLA Modules:
  0.0 214.0 jit_solution(5828972359935834325)
XLA Ops:
  0.7 1.0 copy-done
  1.8 23.8 %spectra.1 = (bf16[2,64,128]{2,1,0:T(8,128)(2,1)S(1)}, bf16[2,64,128]{2,1,0:T(8,128)(2,1)S(1)}, bf16[2,64,128]{2,1,0:T(8,128)(2,1)S(1)}, bf16[2,64,128]{2,1,0:T(...) custom-call(s32[2]{0:T(128)S(1)} %pad_add_fusion.place_ref, ...), custom_call_target="tpu_custom_call" | custom-call | flops 8589934592 | bytes 67108864 | tf_op jit(solution)/shard_map/spectra/pallas_call | solution.py:113
  26.1 2.6 %collective-permute-start.1 = (bf16[128,128]{1,0:T(8,128)(2,1)S(1)}, bf16[128,128]{1,0:T(8,128)(2,1)S(1)}, u32[]{:S(2)}, u32[]{:S(2)}) collective-permute-start(bf16[128,128]{1,0:T(8,128)(2,1)S(1)} %bitcast.17), channel_id=1, source_target_pairs={{0,8},{4,12},{8,0},{12,4},{16,24},{20,28},{24,16},{28,20},{1,9},{5... | collective-permute-start | bytes 98312 | tf_op jit(solution)/shard_map/ppermute | solution.py:322
  28.7 1.8 collective-permute-start.3
  30.5 2.6 %collective-permute-start.5 = (bf16[128,128]{1,0:T(8,128)(2,1)S(1)}, bf16[128,128]{1,0:T(8,128)(2,1)S(1)}, u32[]{:S(2)}, u32[]{:S(2)}) collective-permute-start(bf16[128,128]{1,0:T(8,128)(2,1)S(1)} %bitcast.13), channel_id=1, source_target_pairs={{0,24},{4,28},{8,16},{12,20},{16,8},{20,12},{24,0},{28,4},{1,25},{... | collective-permute-start | bytes 98312 | tf_op jit(solution)/shard_map/ppermute | solution.py:322
  33.3 7.7 %relay.2 = (bf16[8,2048,512]{2,1,0:T(8,128)(2,1)S(1)}, f32[8,128]{1,0:T(8,128)S(1)}) custom-call(bf16[2,2048,8,512]{3,2,1,0:T(8,128)(2,1)} %data_ref.3, bf16[128,128]{1,0:T(8,128)(2,1)S(1)} %bitcast.10), custom_call_target="tpu_custom_call" | custom-call | bytes 33554432 | tf_op jit(solution)/shard_map/relay/pallas_call | solution.py:226
  41.3 2.8 %order.1 = (bf16[256,128]{1,0:T(8,128)(2,1)S(1)}, bf16[256,128]{1,0:T(8,128)(2,1)S(1)}, bf16[256,128]{1,0:T(8,128)(2,1)S(1)}, bf16[256,128]{1,0:T(8,128)(2,1)S(1)}) custom-call(s32[2]{0:T(128)S(1)} %pad_add_fusion.place_ref, s32[2048,128]{1,0:T(8,128)S(1)} %broadcast_in_dim.2.code_ref, bf16[128,128]{1,0:T(8,128)(2,1)S(1)} %bitcast.11, ...), custom_call_target="tpu_custom_call" | custom-call | flops 1073741824 | bytes 1048576 | tf_op jit(solution)/shard_map/order/pallas_call | solution.py:163
  44.2 1.8 collective-permute-start.7
  45.9 2.6 %collective-permute-start.8 = (bf16[256,128]{1,0:T(8,128)(2,1)S(1)}, bf16[256,128]{1,0:T(8,128)(2,1)S(1)}, u32[]{:S(2)}, u32[]{:S(2)}) collective-permute-start(bf16[256,128]{1,0:T(8,128)(2,1)S(1)} %get-tuple-element.37), channel_id=1, source_target_pairs={{0,2},{1,3},{2,0},{3,1},{4,6},{5,7},{6,4},{7,5},{8,10},{9,11},{10,... | collective-permute-start | bytes 196616 | tf_op jit(solution)/shard_map/ppermute | solution.py:322
  48.6 7.9 %relay.3 = (bf16[8,2048,512]{2,1,0:T(8,128)(2,1)S(1)}, f32[8,128]{1,0:T(8,128)S(1)}) custom-call(bf16[2,2048,8,512]{3,2,1,0:T(8,128)(2,1)} %data_ref.3, bf16[256,128]{1,0:T(8,128)(2,1)S(1)} %get-tuple-element.34.after_ref.refs_0_), custom_call_target="tpu_custom_call" | custom-call | bytes 33554432 | tf_op jit(solution)/shard_map/relay/pallas_call | solution.py:226
  56.5 1.0 panel.1.refs_0_.refs_3_
  57.5 2.6 %collective-permute-start.15 = (bf16[512,256]{1,0:T(8,128)(2,1)S(1)}, bf16[512,256]{1,0:T(8,128)(2,1)S(1)}, u32[]{:S(2)}, u32[]{:S(2)}) collective-permute-start(bf16[512,256]{1,0:T(8,128)(2,1)S(1)} %panel.1.refs_0_.refs_3_), channel_id=1, source_target_pairs={{0,24},{4,28},{8,16},{12,20},{16,8},{20,12},{24,0},{28,4},{1,25},{... | collective-permute-start | bytes 786440 | tf_op jit(solution)/shard_map/ppermute | solution.py:322
  61.0 6.6 %collective-permute-done.15.refs_6_ = bf16[512,256]{1,0:T(8,128)(2,1)S(1)} collective-permute-done((bf16[512,256]{1,0:T(8,128)(2,1)S(1)}, bf16[512,256]{1,0:T(8,128)(2,1)S(1)}, u32[]{:S(2)}, u32[]{:S(2)}) %collective-permute-start.15) | collective-permute-done | bytes 262176 | tf_op jit(solution)/shard_map/ppermute | solution.py:322
  67.7 4.5 %collective-permute-done.13.refs_4_ = bf16[512,256]{1,0:T(8,128)(2,1)S(1)} collective-permute-done((bf16[512,256]{1,0:T(8,128)(2,1)S(1)}, bf16[512,256]{1,0:T(8,128)(2,1)S(1)}, u32[]{:S(2)}, u32[]{:S(2)}) %collective-permute-start.13) | collective-permute-done | bytes 262176 | tf_op jit(solution)/shard_map/ppermute | solution.py:322
  72.7 1.0 collective-permute-done.14.refs_5_
  74.1 5.0 %terms.9 = (bf16[512,256]{1,0:T(8,128)(2,1)S(1)}, f32[512,256]{1,0:T(8,128)S(1)}) custom-call(s32[2]{0:T(128)S(1)} %pad_add_fusion.place_ref, bf16[8,2048,512]{2,1,0:T(8,128)(2,1)S(1)} %get-tuple-element.25.real_ref, bf16[8,2048,512]{2,1,0:T(8,128)(2,1)S(1)} %get-tuple-element.35.imag_ref, bf16[512,256]{1,0:T(8,128)(2,1)S(1)} %panel.1.refs_0_.refs_3_, ...), custom_call_target="tpu_custom_call" | custom-call | flops 4294967296 | bytes 16777216 | tf_op jit(solution)/shard_map/terms/pallas_call | solution.py:265
  79.8 2.9 %terms.10 = bf16[512,256]{1,0:T(8,128)(2,1)S(1)} custom-call(s32[2]{0:T(128)S(1)} %pad_add_fusion.place_ref, bf16[8,2048,512]{2,1,0:T(8,128)(2,1)S(1)} %get-tuple-element.25.real_ref, bf16[8,2048,512]{2,1,0:T(8,128)(2,1)S(1)} %get-tuple-element.35.imag_ref, bf16[512,256]{1,0:T(8,128)(2,1)S(1)} %panel.1.refs_0_.refs_3_, ...), custom_call_target="tpu_custom_call" | custom-call | flops 2147483648 | bytes 8388608 | tf_op jit(solution)/shard_map/terms/pallas_call | solution.py:265
  82.7 3.0 %collective-permute-start.17 = (bf16[512,256]{1,0:T(8,128)(2,1)S(1)}, bf16[512,256]{1,0:T(8,128)(2,1)S(1)}, u32[]{:S(2)}, u32[]{:S(2)}) collective-permute-start(bf16[512,256]{1,0:T(8,128)(2,1)S(1)} %terms.10), channel_id=1, source_target_pairs={{0,3},{1,2},{2,1},{3,0},{4,7},{5,6},{6,5},{7,4},{8,11},{9,10},{10,... | collective-permute-start | bytes 786440 | tf_op jit(solution)/shard_map/ppermute | solution.py:322
  85.7 2.9 %terms.11 = bf16[512,256]{1,0:T(8,128)(2,1)S(1)} custom-call(s32[2]{0:T(128)S(1)} %pad_add_fusion.place_ref, bf16[8,2048,512]{2,1,0:T(8,128)(2,1)S(1)} %get-tuple-element.25.real_ref, bf16[8,2048,512]{2,1,0:T(8,128)(2,1)S(1)} %get-tuple-element.35.imag_ref, bf16[512,256]{1,0:T(8,128)(2,1)S(1)} %panel.1.refs_0_.refs_3_, ...), custom_call_target="tpu_custom_call" | custom-call | flops 2147483648 | bytes 8388608 | tf_op jit(solution)/shard_map/terms/pallas_call | solution.py:265
  89.2 6.4 %collective-permute-done.17.refs_0_ = bf16[512,256]{1,0:T(8,128)(2,1)S(1)} collective-permute-done((bf16[512,256]{1,0:T(8,128)(2,1)S(1)}, bf16[512,256]{1,0:T(8,128)(2,1)S(1)}, u32[]{:S(2)}, u32[]{:S(2)}) %collective-permute-start.17) | collective-permute-done | bytes 262176 | tf_op jit(solution)/shard_map/ppermute | solution.py:322
  95.6 13.9 %collective-permute-done.18.refs_1_ = bf16[512,256]{1,0:T(8,128)(2,1)S(1)} collective-permute-done((bf16[512,256]{1,0:T(8,128)(2,1)S(1)}, bf16[512,256]{1,0:T(8,128)(2,1)S(1)}, u32[]{:S(2)}, u32[]{:S(2)}) %collective-permute-start.18) | collective-permute-done | bytes 262176 | tf_op jit(solution)/shard_map/ppermute | solution.py:322
  110.2 1.8 collective-permute-start.25
  112.0 1.0 collective-permute-start.23
  113.0 0.8 collective-permute-start.21
  113.8 6.7 %collective-permute-done.25.refs_6_ = bf16[512,256]{1,0:T(8,128)(2,1)S(1)} collective-permute-done((bf16[512,256]{1,0:T(8,128)(2,1)S(1)}, bf16[512,256]{1,0:T(8,128)(2,1)S(1)}, u32[]{:S(2)}, u32[]{:S(2)}) %collective-permute-start.25) | collective-permute-done | bytes 262176 | tf_op jit(solution)/shard_map/ppermute | solution.py:322
  120.5 3.8 %collective-permute-done.23.refs_4_ = bf16[512,256]{1,0:T(8,128)(2,1)S(1)} collective-permute-done((bf16[512,256]{1,0:T(8,128)(2,1)S(1)}, bf16[512,256]{1,0:T(8,128)(2,1)S(1)}, u32[]{:S(2)}, u32[]{:S(2)}) %collective-permute-start.23) | collective-permute-done | bytes 262176 | tf_op jit(solution)/shard_map/ppermute | solution.py:322
  124.8 1.0 collective-permute-done.24.refs_5_
  126.2 5.0 %terms.12 = (bf16[512,256]{1,0:T(8,128)(2,1)S(1)}, f32[512,256]{1,0:T(8,128)S(1)}) custom-call(s32[2]{0:T(128)S(1)} %pad_add_fusion.place_ref, bf16[8,2048,512]{2,1,0:T(8,128)(2,1)S(1)} %get-tuple-element.25.real_ref, bf16[8,2048,512]{2,1,0:T(8,128)(2,1)S(1)} %get-tuple-element.35.imag_ref, bf16[512,256]{1,0:T(8,128)(2,1)S(1)} %update.3.refs_0_, ...), custom_call_target="tpu_custom_call" | custom-call | flops 4294967296 | bytes 16777216 | tf_op jit(solution)/shard_map/terms/pallas_call | solution.py:265
  131.3 2.9 %terms.13 = bf16[512,256]{1,0:T(8,128)(2,1)S(1)} custom-call(s32[2]{0:T(128)S(1)} %pad_add_fusion.place_ref, bf16[8,2048,512]{2,1,0:T(8,128)(2,1)S(1)} %get-tuple-element.25.real_ref, bf16[8,2048,512]{2,1,0:T(8,128)(2,1)S(1)} %get-tuple-element.35.imag_ref, bf16[512,256]{1,0:T(8,128)(2,1)S(1)} %update.3.refs_0_, ...), custom_call_target="tpu_custom_call" | custom-call | flops 2147483648 | bytes 8388608 | tf_op jit(solution)/shard_map/terms/pallas_call | solution.py:265
  134.2 2.8 %collective-permute-start.27 = (bf16[512,256]{1,0:T(8,128)(2,1)S(1)}, bf16[512,256]{1,0:T(8,128)(2,1)S(1)}, u32[]{:S(2)}, u32[]{:S(2)}) collective-permute-start(bf16[512,256]{1,0:T(8,128)(2,1)S(1)} %terms.13), channel_id=1, source_target_pairs={{0,3},{1,2},{2,1},{3,0},{4,7},{5,6},{6,5},{7,4},{8,11},{9,10},{10,... | collective-permute-start | bytes 786440 | tf_op jit(solution)/shard_map/ppermute | solution.py:322
  137.0 2.9 %terms.14 = bf16[512,256]{1,0:T(8,128)(2,1)S(1)} custom-call(s32[2]{0:T(128)S(1)} %pad_add_fusion.place_ref, bf16[8,2048,512]{2,1,0:T(8,128)(2,1)S(1)} %get-tuple-element.25.real_ref, bf16[8,2048,512]{2,1,0:T(8,128)(2,1)S(1)} %get-tuple-element.35.imag_ref, bf16[512,256]{1,0:T(8,128)(2,1)S(1)} %update.3.refs_0_, ...), custom_call_target="tpu_custom_call" | custom-call | flops 2147483648 | bytes 8388608 | tf_op jit(solution)/shard_map/terms/pallas_call | solution.py:265
  139.8 0.8 collective-permute-start.28
  140.7 6.2 %collective-permute-done.27.refs_0_ = bf16[512,256]{1,0:T(8,128)(2,1)S(1)} collective-permute-done((bf16[512,256]{1,0:T(8,128)(2,1)S(1)}, bf16[512,256]{1,0:T(8,128)(2,1)S(1)}, u32[]{:S(2)}, u32[]{:S(2)}) %collective-permute-start.27) | collective-permute-done | bytes 262176 | tf_op jit(solution)/shard_map/ppermute | solution.py:322
  146.8 13.9 %collective-permute-done.28.refs_1_ = bf16[512,256]{1,0:T(8,128)(2,1)S(1)} collective-permute-done((bf16[512,256]{1,0:T(8,128)(2,1)S(1)}, bf16[512,256]{1,0:T(8,128)(2,1)S(1)}, u32[]{:S(2)}, u32[]{:S(2)}) %collective-permute-start.28) | collective-permute-done | bytes 262176 | tf_op jit(solution)/shard_map/ppermute | solution.py:322
  161.5 1.8 collective-permute-start.35
  163.3 1.0 collective-permute-start.33
  164.2 0.8 collective-permute-start.31
  165.0 6.7 %collective-permute-done.35.refs_6_ = bf16[512,256]{1,0:T(8,128)(2,1)S(1)} collective-permute-done((bf16[512,256]{1,0:T(8,128)(2,1)S(1)}, bf16[512,256]{1,0:T(8,128)(2,1)S(1)}, u32[]{:S(2)}, u32[]{:S(2)}) %collective-permute-start.35) | collective-permute-done | bytes 262176 | tf_op jit(solution)/shard_map/ppermute | solution.py:322
  171.7 3.6 %collective-permute-done.33.refs_4_ = bf16[512,256]{1,0:T(8,128)(2,1)S(1)} collective-permute-done((bf16[512,256]{1,0:T(8,128)(2,1)S(1)}, bf16[512,256]{1,0:T(8,128)(2,1)S(1)}, u32[]{:S(2)}, u32[]{:S(2)}) %collective-permute-start.33) | collective-permute-done | bytes 262176 | tf_op jit(solution)/shard_map/ppermute | solution.py:322
  175.8 1.0 collective-permute-done.34.refs_5_
  177.2 5.2 %terms.15 = (bf16[512,256]{1,0:T(8,128)(2,1)S(1)}, f32[512,256]{1,0:T(8,128)S(1)}) custom-call(s32[2]{0:T(128)S(1)} %pad_add_fusion.place_ref, bf16[8,2048,512]{2,1,0:T(8,128)(2,1)S(1)} %get-tuple-element.25.real_ref, bf16[8,2048,512]{2,1,0:T(8,128)(2,1)S(1)} %get-tuple-element.35.imag_ref, bf16[512,256]{1,0:T(8,128)(2,1)S(1)} %update.4.refs_0_, ...), custom_call_target="tpu_custom_call" | custom-call | flops 4294967296 | bytes 16777216 | tf_op jit(solution)/shard_map/terms/pallas_call | solution.py:265
  182.5 2.9 %terms.16 = bf16[512,256]{1,0:T(8,128)(2,1)S(1)} custom-call(s32[2]{0:T(128)S(1)} %pad_add_fusion.place_ref, bf16[8,2048,512]{2,1,0:T(8,128)(2,1)S(1)} %get-tuple-element.25.real_ref, bf16[8,2048,512]{2,1,0:T(8,128)(2,1)S(1)} %get-tuple-element.35.imag_ref, bf16[512,256]{1,0:T(8,128)(2,1)S(1)} %update.4.refs_0_, ...), custom_call_target="tpu_custom_call" | custom-call | flops 2147483648 | bytes 8388608 | tf_op jit(solution)/shard_map/terms/pallas_call | solution.py:265
  185.4 2.8 %collective-permute-start.37 = (bf16[512,256]{1,0:T(8,128)(2,1)S(1)}, bf16[512,256]{1,0:T(8,128)(2,1)S(1)}, u32[]{:S(2)}, u32[]{:S(2)}) collective-permute-start(bf16[512,256]{1,0:T(8,128)(2,1)S(1)} %terms.16), channel_id=1, source_target_pairs={{0,3},{1,2},{2,1},{3,0},{4,7},{5,6},{6,5},{7,4},{8,11},{9,10},{10,... | collective-permute-start | bytes 786440 | tf_op jit(solution)/shard_map/ppermute | solution.py:322
  188.2 2.9 %terms.17 = bf16[512,256]{1,0:T(8,128)(2,1)S(1)} custom-call(s32[2]{0:T(128)S(1)} %pad_add_fusion.place_ref, bf16[8,2048,512]{2,1,0:T(8,128)(2,1)S(1)} %get-tuple-element.25.real_ref, bf16[8,2048,512]{2,1,0:T(8,128)(2,1)S(1)} %get-tuple-element.35.imag_ref, bf16[512,256]{1,0:T(8,128)(2,1)S(1)} %update.4.refs_0_, ...), custom_call_target="tpu_custom_call" | custom-call | flops 2147483648 | bytes 8388608 | tf_op jit(solution)/shard_map/terms/pallas_call | solution.py:265
  191.1 0.8 collective-permute-start.38
  191.9 6.2 %collective-permute-done.37.refs_0_ = bf16[512,256]{1,0:T(8,128)(2,1)S(1)} collective-permute-done((bf16[512,256]{1,0:T(8,128)(2,1)S(1)}, bf16[512,256]{1,0:T(8,128)(2,1)S(1)}, u32[]{:S(2)}, u32[]{:S(2)}) %collective-permute-start.37) | collective-permute-done | bytes 262176 | tf_op jit(solution)/shard_map/ppermute | solution.py:322
  198.1 13.9 %collective-permute-done.38.refs_1_ = bf16[512,256]{1,0:T(8,128)(2,1)S(1)} collective-permute-done((bf16[512,256]{1,0:T(8,128)(2,1)S(1)}, bf16[512,256]{1,0:T(8,128)(2,1)S(1)}, u32[]{:S(2)}, u32[]{:S(2)}) %collective-permute-start.38) | collective-permute-done | bytes 262176 | tf_op jit(solution)/shard_map/ppermute | solution.py:322
  212.0 2.1 update.5
  (58 shorter events, 7.8 us)
Async XLA Ops:
  0.7 1.0 copy-start
  1.8 31.5 %copy-start.2 = (s32[2048]{0:T(1024)S(1)}, s32[2048]{0:T(1024)}, u32[]{:S(2)}) copy-start(s32[2048]{0:T(1024)} %param.6) | copy-start | bytes 24580
  25.6 4.9 %collective-permute-start = (bf16[128,128]{1,0:T(8,128)(2,1)S(1)}, bf16[128,128]{1,0:T(8,128)(2,1)S(1)}, u32[]{:S(2)}, u32[]{:S(2)}) collective-permute-start(bf16[128,128]{1,0:T(8,128)(2,1)S(1)} %bitcast.18), channel_id=1, source_target_pairs={{0,4},{4,0},{8,12},{12,8},{16,20},{20,16},{24,28},{28,24},{1,5},{5... | collective-permute-start | bytes 98312 | tf_op jit(solution)/shard_map/ppermute | solution.py:322
  26.1 7.0 %collective-permute-start.1 = (bf16[128,128]{1,0:T(8,128)(2,1)S(1)}, bf16[128,128]{1,0:T(8,128)(2,1)S(1)}, u32[]{:S(2)}, u32[]{:S(2)}) collective-permute-start(bf16[128,128]{1,0:T(8,128)(2,1)S(1)} %bitcast.17), channel_id=1, source_target_pairs={{0,8},{4,12},{8,0},{12,4},{16,24},{20,28},{24,16},{28,20},{1,9},{5... | collective-permute-start | bytes 98312 | tf_op jit(solution)/shard_map/ppermute | solution.py:322
  28.6 12.3 %collective-permute-start.2 = (bf16[128,128]{1,0:T(8,128)(2,1)S(1)}, bf16[128,128]{1,0:T(8,128)(2,1)S(1)}, u32[]{:S(2)}, u32[]{:S(2)}) collective-permute-start(bf16[128,128]{1,0:T(8,128)(2,1)S(1)} %bitcast.16), channel_id=1, source_target_pairs={{0,12},{4,8},{8,4},{12,0},{16,28},{20,24},{24,20},{28,16},{1,13},{... | collective-permute-start | bytes 98312 | tf_op jit(solution)/shard_map/ppermute | solution.py:322
  28.7 12.2 %collective-permute-start.3 = (bf16[128,128]{1,0:T(8,128)(2,1)S(1)}, bf16[128,128]{1,0:T(8,128)(2,1)S(1)}, u32[]{:S(2)}, u32[]{:S(2)}) collective-permute-start(bf16[128,128]{1,0:T(8,128)(2,1)S(1)} %bitcast.15), channel_id=1, source_target_pairs={{0,16},{4,20},{8,24},{12,28},{16,0},{20,4},{24,8},{28,12},{1,17},{... | collective-permute-start | bytes 98312 | tf_op jit(solution)/shard_map/ppermute | solution.py:322
  30.5 10.5 %collective-permute-start.4 = (bf16[128,128]{1,0:T(8,128)(2,1)S(1)}, bf16[128,128]{1,0:T(8,128)(2,1)S(1)}, u32[]{:S(2)}, u32[]{:S(2)}) collective-permute-start(bf16[128,128]{1,0:T(8,128)(2,1)S(1)} %bitcast.14), channel_id=1, source_target_pairs={{0,20},{4,16},{8,28},{12,24},{16,4},{20,0},{24,12},{28,8},{1,21},{... | collective-permute-start | bytes 98312 | tf_op jit(solution)/shard_map/ppermute | solution.py:322
  30.5 10.5 %collective-permute-start.5 = (bf16[128,128]{1,0:T(8,128)(2,1)S(1)}, bf16[128,128]{1,0:T(8,128)(2,1)S(1)}, u32[]{:S(2)}, u32[]{:S(2)}) collective-permute-start(bf16[128,128]{1,0:T(8,128)(2,1)S(1)} %bitcast.13), channel_id=1, source_target_pairs={{0,24},{4,28},{8,16},{12,20},{16,8},{20,12},{24,0},{28,4},{1,25},{... | collective-permute-start | bytes 98312 | tf_op jit(solution)/shard_map/ppermute | solution.py:322
  33.1 7.9 %collective-permute-start.6 = (bf16[128,128]{1,0:T(8,128)(2,1)S(1)}, bf16[128,128]{1,0:T(8,128)(2,1)S(1)}, u32[]{:S(2)}, u32[]{:S(2)}) collective-permute-start(bf16[128,128]{1,0:T(8,128)(2,1)S(1)} %bitcast.12), channel_id=1, source_target_pairs={{0,28},{4,24},{8,20},{12,16},{16,12},{20,8},{24,4},{28,0},{1,29},{... | collective-permute-start | bytes 98312 | tf_op jit(solution)/shard_map/ppermute | solution.py:322
  44.2 12.3 %collective-permute-start.7 = (bf16[256,128]{1,0:T(8,128)(2,1)S(1)}, bf16[256,128]{1,0:T(8,128)(2,1)S(1)}, u32[]{:S(2)}, u32[]{:S(2)}) collective-permute-start(bf16[256,128]{1,0:T(8,128)(2,1)S(1)} %get-tuple-element.36), channel_id=1, source_target_pairs={{0,1},{1,0},{2,3},{3,2},{4,5},{5,4},{6,7},{7,6},{8,9},{9,8},{10,11... | collective-permute-start | bytes 196616 | tf_op jit(solution)/shard_map/ppermute | solution.py:322
  45.9 10.6 %collective-permute-start.8 = (bf16[256,128]{1,0:T(8,128)(2,1)S(1)}, bf16[256,128]{1,0:T(8,128)(2,1)S(1)}, u32[]{:S(2)}, u32[]{:S(2)}) collective-permute-start(bf16[256,128]{1,0:T(8,128)(2,1)S(1)} %get-tuple-element.37), channel_id=1, source_target_pairs={{0,2},{1,3},{2,0},{3,1},{4,6},{5,7},{6,4},{7,5},{8,10},{9,11},{10,... | collective-permute-start | bytes 196616 | tf_op jit(solution)/shard_map/ppermute | solution.py:322
  48.5 8.0 %collective-permute-start.9 = (bf16[256,128]{1,0:T(8,128)(2,1)S(1)}, bf16[256,128]{1,0:T(8,128)(2,1)S(1)}, u32[]{:S(2)}, u32[]{:S(2)}) collective-permute-start(bf16[256,128]{1,0:T(8,128)(2,1)S(1)} %get-tuple-element.38), channel_id=1, source_target_pairs={{0,3},{1,2},{2,1},{3,0},{4,7},{5,6},{6,5},{7,4},{8,11},{9,10},{10,... | collective-permute-start | bytes 196616 | tf_op jit(solution)/shard_map/ppermute | solution.py:322
  57.5 10.2 %collective-permute-start.15 = (bf16[512,256]{1,0:T(8,128)(2,1)S(1)}, bf16[512,256]{1,0:T(8,128)(2,1)S(1)}, u32[]{:S(2)}, u32[]{:S(2)}) collective-permute-start(bf16[512,256]{1,0:T(8,128)(2,1)S(1)} %panel.1.refs_0_.refs_3_), channel_id=1, source_target_pairs={{0,24},{4,28},{8,16},{12,20},{16,8},{20,12},{24,0},{28,4},{1,25},{... | collective-permute-start | bytes 786440 | tf_op jit(solution)/shard_map/ppermute | solution.py:322
  60.1 12.1 %collective-permute-start.13 = (bf16[512,256]{1,0:T(8,128)(2,1)S(1)}, bf16[512,256]{1,0:T(8,128)(2,1)S(1)}, u32[]{:S(2)}, u32[]{:S(2)}) collective-permute-start(bf16[512,256]{1,0:T(8,128)(2,1)S(1)} %panel.1.refs_0_.refs_3_), channel_id=1, source_target_pairs={{0,16},{4,20},{8,24},{12,28},{16,0},{20,4},{24,8},{28,12},{1,17},{... | collective-permute-start | bytes 786440 | tf_op jit(solution)/shard_map/ppermute | solution.py:322
  60.6 11.6 %collective-permute-start.11 = (bf16[512,256]{1,0:T(8,128)(2,1)S(1)}, bf16[512,256]{1,0:T(8,128)(2,1)S(1)}, u32[]{:S(2)}, u32[]{:S(2)}) collective-permute-start(bf16[512,256]{1,0:T(8,128)(2,1)S(1)} %panel.1.refs_0_.refs_3_), channel_id=1, source_target_pairs={{0,8},{4,12},{8,0},{12,4},{16,24},{20,28},{24,16},{28,20},{1,9},{5... | collective-permute-start | bytes 786440 | tf_op jit(solution)/shard_map/ppermute | solution.py:322
  61.0 11.7 %collective-permute-start.10 = (bf16[512,256]{1,0:T(8,128)(2,1)S(1)}, bf16[512,256]{1,0:T(8,128)(2,1)S(1)}, u32[]{:S(2)}, u32[]{:S(2)}) collective-permute-start(bf16[512,256]{1,0:T(8,128)(2,1)S(1)} %panel.1.refs_0_.refs_3_), channel_id=1, source_target_pairs={{0,4},{4,0},{8,12},{12,8},{16,20},{20,16},{24,28},{28,24},{1,5},{5... | collective-permute-start | bytes 786440 | tf_op jit(solution)/shard_map/ppermute | solution.py:322
  67.7 5.1 %collective-permute-start.16 = (bf16[512,256]{1,0:T(8,128)(2,1)S(1)}, bf16[512,256]{1,0:T(8,128)(2,1)S(1)}, u32[]{:S(2)}, u32[]{:S(2)}) collective-permute-start(bf16[512,256]{1,0:T(8,128)(2,1)S(1)} %collective-permute-done.15.refs_6_), channel_id=1, source_target_pairs={{0,4},{4,0},{8,12},{12,8},{16,20},{20,16},{24,28},{28,24},{1,5},{5... | collective-permute-start | bytes 786440 | tf_op jit(solution)/shard_map/ppermute | solution.py:322
  72.2 1.5 collective-permute-start.14
  72.2 1.9 collective-permute-start.12
  79.2 30.3 %copy-start.1 = (f32[2]{0:T(128)S(1)}, f32[2]{0:T(128)}, u32[]{:S(2)}) copy-start(f32[2]{0:T(128)} %wave_ref.5) | copy-start | bytes 28
  79.2 10.1 %collective-permute-start.19 = (bf16[512,256]{1,0:T(8,128)(2,1)S(1)}, bf16[512,256]{1,0:T(8,128)(2,1)S(1)}, u32[]{:S(2)}, u32[]{:S(2)}) collective-permute-start(bf16[512,256]{1,0:T(8,128)(2,1)S(1)} %get-tuple-element.41), channel_id=1, source_target_pairs={{0,1},{1,0},{2,3},{3,2},{4,5},{5,4},{6,7},{7,6},{8,9},{9,8},{10,11... | collective-permute-start | bytes 786440 | tf_op jit(solution)/shard_map/ppermute | solution.py:322
  82.7 12.9 %collective-permute-start.17 = (bf16[512,256]{1,0:T(8,128)(2,1)S(1)}, bf16[512,256]{1,0:T(8,128)(2,1)S(1)}, u32[]{:S(2)}, u32[]{:S(2)}) collective-permute-start(bf16[512,256]{1,0:T(8,128)(2,1)S(1)} %terms.10), channel_id=1, source_target_pairs={{0,3},{1,2},{2,1},{3,0},{4,7},{5,6},{6,5},{7,4},{8,11},{9,10},{10,... | collective-permute-start | bytes 786440 | tf_op jit(solution)/shard_map/ppermute | solution.py:322
  88.6 20.9 %collective-permute-start.18 = (bf16[512,256]{1,0:T(8,128)(2,1)S(1)}, bf16[512,256]{1,0:T(8,128)(2,1)S(1)}, u32[]{:S(2)}, u32[]{:S(2)}) collective-permute-start(bf16[512,256]{1,0:T(8,128)(2,1)S(1)} %terms.11), channel_id=1, source_target_pairs={{0,2},{1,3},{2,0},{3,1},{4,6},{5,7},{6,4},{7,5},{8,10},{9,11},{10,... | collective-permute-start | bytes 786440 | tf_op jit(solution)/shard_map/ppermute | solution.py:322
  110.2 10.3 %collective-permute-start.25 = (bf16[512,256]{1,0:T(8,128)(2,1)S(1)}, bf16[512,256]{1,0:T(8,128)(2,1)S(1)}, u32[]{:S(2)}, u32[]{:S(2)}) collective-permute-start(bf16[512,256]{1,0:T(8,128)(2,1)S(1)} %update.3.refs_0_), channel_id=1, source_target_pairs={{0,24},{4,28},{8,16},{12,20},{16,8},{20,12},{24,0},{28,4},{1,25},{... | collective-permute-start | bytes 786440 | tf_op jit(solution)/shard_map/ppermute | solution.py:322
  112.0 12.3 %collective-permute-start.23 = (bf16[512,256]{1,0:T(8,128)(2,1)S(1)}, bf16[512,256]{1,0:T(8,128)(2,1)S(1)}, u32[]{:S(2)}, u32[]{:S(2)}) collective-permute-start(bf16[512,256]{1,0:T(8,128)(2,1)S(1)} %update.3.refs_0_), channel_id=1, source_target_pairs={{0,16},{4,20},{8,24},{12,28},{16,0},{20,4},{24,8},{28,12},{1,17},{... | collective-permute-start | bytes 786440 | tf_op jit(solution)/shard_map/ppermute | solution.py:322
  113.0 11.3 %collective-permute-start.21 = (bf16[512,256]{1,0:T(8,128)(2,1)S(1)}, bf16[512,256]{1,0:T(8,128)(2,1)S(1)}, u32[]{:S(2)}, u32[]{:S(2)}) collective-permute-start(bf16[512,256]{1,0:T(8,128)(2,1)S(1)} %update.3.refs_0_), channel_id=1, source_target_pairs={{0,8},{4,12},{8,0},{12,4},{16,24},{20,28},{24,16},{28,20},{1,9},{5... | collective-permute-start | bytes 786440 | tf_op jit(solution)/shard_map/ppermute | solution.py:322
  113.8 11.1 %collective-permute-start.20 = (bf16[512,256]{1,0:T(8,128)(2,1)S(1)}, bf16[512,256]{1,0:T(8,128)(2,1)S(1)}, u32[]{:S(2)}, u32[]{:S(2)}) collective-permute-start(bf16[512,256]{1,0:T(8,128)(2,1)S(1)} %update.3.refs_0_), channel_id=1, source_target_pairs={{0,4},{4,0},{8,12},{12,8},{16,20},{20,16},{24,28},{28,24},{1,5},{5... | collective-permute-start | bytes 786440 | tf_op jit(solution)/shard_map/ppermute | solution.py:322
  120.5 4.4 %collective-permute-start.26 = (bf16[512,256]{1,0:T(8,128)(2,1)S(1)}, bf16[512,256]{1,0:T(8,128)(2,1)S(1)}, u32[]{:S(2)}, u32[]{:S(2)}) collective-permute-start(bf16[512,256]{1,0:T(8,128)(2,1)S(1)} %collective-permute-done.25.refs_6_), channel_id=1, source_target_pairs={{0,4},{4,0},{8,12},{12,8},{16,20},{20,16},{24,28},{28,24},{1,5},{5... | collective-permute-start | bytes 786440 | tf_op jit(solution)/shard_map/ppermute | solution.py:322
  124.3 1.5 collective-permute-start.24
  124.3 1.9 collective-permute-start.22
  131.2 9.4 %collective-permute-start.29 = (bf16[512,256]{1,0:T(8,128)(2,1)S(1)}, bf16[512,256]{1,0:T(8,128)(2,1)S(1)}, u32[]{:S(2)}, u32[]{:S(2)}) collective-permute-start(bf16[512,256]{1,0:T(8,128)(2,1)S(1)} %get-tuple-element.43), channel_id=1, source_target_pairs={{0,1},{1,0},{2,3},{3,2},{4,5},{5,4},{6,7},{7,6},{8,9},{9,8},{10,11... | collective-permute-start | bytes 786440 | tf_op jit(solution)/shard_map/ppermute | solution.py:322
  134.2 12.6 %collective-permute-start.27 = (bf16[512,256]{1,0:T(8,128)(2,1)S(1)}, bf16[512,256]{1,0:T(8,128)(2,1)S(1)}, u32[]{:S(2)}, u32[]{:S(2)}) collective-permute-start(bf16[512,256]{1,0:T(8,128)(2,1)S(1)} %terms.13), channel_id=1, source_target_pairs={{0,3},{1,2},{2,1},{3,0},{4,7},{5,6},{6,5},{7,4},{8,11},{9,10},{10,... | collective-permute-start | bytes 786440 | tf_op jit(solution)/shard_map/ppermute | solution.py:322
  139.8 20.9 %collective-permute-start.28 = (bf16[512,256]{1,0:T(8,128)(2,1)S(1)}, bf16[512,256]{1,0:T(8,128)(2,1)S(1)}, u32[]{:S(2)}, u32[]{:S(2)}) collective-permute-start(bf16[512,256]{1,0:T(8,128)(2,1)S(1)} %terms.14), channel_id=1, source_target_pairs={{0,2},{1,3},{2,0},{3,1},{4,6},{5,7},{6,4},{7,5},{8,10},{9,11},{10,... | collective-permute-start | bytes 786440 | tf_op jit(solution)/shard_map/ppermute | solution.py:322
  161.5 10.3 %collective-permute-start.35 = (bf16[512,256]{1,0:T(8,128)(2,1)S(1)}, bf16[512,256]{1,0:T(8,128)(2,1)S(1)}, u32[]{:S(2)}, u32[]{:S(2)}) collective-permute-start(bf16[512,256]{1,0:T(8,128)(2,1)S(1)} %update.4.refs_0_), channel_id=1, source_target_pairs={{0,24},{4,28},{8,16},{12,20},{16,8},{20,12},{24,0},{28,4},{1,25},{... | collective-permute-start | bytes 786440 | tf_op jit(solution)/shard_map/ppermute | solution.py:322
  163.3 12.0 %collective-permute-start.33 = (bf16[512,256]{1,0:T(8,128)(2,1)S(1)}, bf16[512,256]{1,0:T(8,128)(2,1)S(1)}, u32[]{:S(2)}, u32[]{:S(2)}) collective-permute-start(bf16[512,256]{1,0:T(8,128)(2,1)S(1)} %update.4.refs_0_), channel_id=1, source_target_pairs={{0,16},{4,20},{8,24},{12,28},{16,0},{20,4},{24,8},{28,12},{1,17},{... | collective-permute-start | bytes 786440 | tf_op jit(solution)/shard_map/ppermute | solution.py:322
  164.2 11.1 %collective-permute-start.31 = (bf16[512,256]{1,0:T(8,128)(2,1)S(1)}, bf16[512,256]{1,0:T(8,128)(2,1)S(1)}, u32[]{:S(2)}, u32[]{:S(2)}) collective-permute-start(bf16[512,256]{1,0:T(8,128)(2,1)S(1)} %update.4.refs_0_), channel_id=1, source_target_pairs={{0,8},{4,12},{8,0},{12,4},{16,24},{20,28},{24,16},{28,20},{1,9},{5... | collective-permute-start | bytes 786440 | tf_op jit(solution)/shard_map/ppermute | solution.py:322
  165.0 10.8 %collective-permute-start.30 = (bf16[512,256]{1,0:T(8,128)(2,1)S(1)}, bf16[512,256]{1,0:T(8,128)(2,1)S(1)}, u32[]{:S(2)}, u32[]{:S(2)}) collective-permute-start(bf16[512,256]{1,0:T(8,128)(2,1)S(1)} %update.4.refs_0_), channel_id=1, source_target_pairs={{0,4},{4,0},{8,12},{12,8},{16,20},{20,16},{24,28},{28,24},{1,5},{5... | collective-permute-start | bytes 786440 | tf_op jit(solution)/shard_map/ppermute | solution.py:322
  171.7 4.1 %collective-permute-start.36 = (bf16[512,256]{1,0:T(8,128)(2,1)S(1)}, bf16[512,256]{1,0:T(8,128)(2,1)S(1)}, u32[]{:S(2)}, u32[]{:S(2)}) collective-permute-start(bf16[512,256]{1,0:T(8,128)(2,1)S(1)} %collective-permute-done.35.refs_6_), channel_id=1, source_target_pairs={{0,4},{4,0},{8,12},{12,8},{16,20},{20,16},{24,28},{28,24},{1,5},{5... | collective-permute-start | bytes 786440 | tf_op jit(solution)/shard_map/ppermute | solution.py:322
  175.3 1.5 collective-permute-start.34
  175.3 1.9 collective-permute-start.32
  182.5 9.4 %collective-permute-start.39 = (bf16[512,256]{1,0:T(8,128)(2,1)S(1)}, bf16[512,256]{1,0:T(8,128)(2,1)S(1)}, u32[]{:S(2)}, u32[]{:S(2)}) collective-permute-start(bf16[512,256]{1,0:T(8,128)(2,1)S(1)} %get-tuple-element.45), channel_id=1, source_target_pairs={{0,1},{1,0},{2,3},{3,2},{4,5},{5,4},{6,7},{7,6},{8,9},{9,8},{10,11... | collective-permute-start | bytes 786440 | tf_op jit(solution)/shard_map/ppermute | solution.py:322
  185.4 12.7 %collective-permute-start.37 = (bf16[512,256]{1,0:T(8,128)(2,1)S(1)}, bf16[512,256]{1,0:T(8,128)(2,1)S(1)}, u32[]{:S(2)}, u32[]{:S(2)}) collective-permute-start(bf16[512,256]{1,0:T(8,128)(2,1)S(1)} %terms.16), channel_id=1, source_target_pairs={{0,3},{1,2},{2,1},{3,0},{4,7},{5,6},{6,5},{7,4},{8,11},{9,10},{10,... | collective-permute-start | bytes 786440 | tf_op jit(solution)/shard_map/ppermute | solution.py:322
  191.1 20.9 %collective-permute-start.38 = (bf16[512,256]{1,0:T(8,128)(2,1)S(1)}, bf16[512,256]{1,0:T(8,128)(2,1)S(1)}, u32[]{:S(2)}, u32[]{:S(2)}) collective-permute-start(bf16[512,256]{1,0:T(8,128)(2,1)S(1)} %terms.17), channel_id=1, source_target_pairs={{0,2},{1,3},{2,0},{3,1},{4,6},{5,7},{6,4},{7,5},{8,10},{9,11},{10,... | collective-permute-start | bytes 786440 | tf_op jit(solution)/shard_map/ppermute | solution.py:322
where the time goes:
time: 214 us
  waiting for transfers between devices  96.6 us (45%)
  Pallas kernels  79.2 us (37%)
  starting transfers between devices  36 us (17%)
    ppermute x40, waiting for transfers between devices, swap(): lax.ppermute(array, axis, [(index, index ^ bits) for index in range(size)])  96.6 us
    ppermute x40, starting transfers between devices, swap(): lax.ppermute(array, axis, [(index, index ^ bits) for index in range(size)])  36 us
    pallas_call x9, Pallas kernels, make_terms(): pl.pallas_call(functools.partial(terms_kernel, turns, len(pieces)), in_sp...  32.5 us
    pallas_call x1, Pallas kernels, make_spectra(): pl.pallas_call(functools.partial(spectra_kernel, packs, n_row), in_specs=...  23.8 us
    pallas_call x2, Pallas kernels, relay(): pl.pallas_call(functools.partial(relay_kernel, part), in_specs=[ANY, ANY]...  15.5 us
  transfers between devices with their start and end apart: 40, of which 18 were waited for; matrix products, arithmetic and copies ran while one was open for 0% of the time, Pallas kernels for 15%

commit v1 on v0

--- a/solution.py
+++ b/solution.py
@@ -127,7 +127,7 @@
 
 
 def order_kernel(packs, n_src, place_ref, code_ref, *refs):
-    pieces, out_refs = refs[: -n_src - 1], refs[-n_src:]
+    pieces, out_refs = refs[:-n_src], refs[-n_src:]
     width = LANES // packs
     held = jnp.concatenate([ref[...] for ref in pieces], axis=0)
     rolled = [held] + [
@@ -158,17 +158,17 @@
         out_ref[...] = packed.astype(jnp.bfloat16)
 
 
-def make_order(code, pieces, place, n_src, packs, after):
+def make_order(code, pieces, place, n_src, packs):
     slice_rows = code.shape[0] // n_src
     return pl.pallas_call(
         functools.partial(order_kernel, packs, n_src),
-        in_specs=[SMEM] + [VMEM] * (1 + len(pieces)) + [ANY],
+        in_specs=[SMEM] + [VMEM] * (1 + len(pieces)),
         out_specs=[VMEM] * n_src,
         out_shape=[jax.ShapeDtypeStruct((slice_rows // packs, LANES), jnp.bfloat16)] * n_src,
-        compiler_params=params(6),
+        compiler_params=params(8),
         cost_estimate=cost(2 * code.shape[0] * len(pieces) * pieces[0].size * packs, 4 * code.size),
         name="order",
-    )(place, code, *pieces, after)
+    )(place, code, *pieces)
 
 
 def panel_kernel(packs, place_ref, *refs):
@@ -200,7 +200,7 @@
         in_specs=[SMEM] + [VMEM] * len(pieces) + [ANY],
         out_specs=VMEM,
         out_shape=jax.ShapeDtypeStruct((rows, columns), jnp.bfloat16),
-        compiler_params=params(4),
+        compiler_params=params(8),
         cost_estimate=cost(2 * len(pieces) * rows * LANES * columns, 4 * rows * columns),
         name="panel",
     )(place, *pieces, after)
@@ -241,58 +241,100 @@
     )(slice_data, after)
 
 
-def terms_kernel(turns, n_pieces, place_ref, real_ref, imag_ref, *refs):
-    pieces, out_refs = refs[:n_pieces], refs[-len(turns) :]
+def terms_kernel(turn, n_pieces, place_ref, real_ref, imag_ref, *refs):
+    pieces, out_refs = refs[:n_pieces], refs[n_pieces:]
     columns = pieces[0].shape[1]
     kept = columns // 2
-    for turn, out_ref in zip(turns, out_refs):
-        size = out_ref.shape[0]
-        rows = pl.ds(pl.multiple_of((place_ref[1] ^ turn) * size, size), size)
-        total = jnp.zeros((2 * size, columns), jnp.float32)
-        for number, piece in enumerate(pieces):
-            block = place_ref[0] ^ number
-            both = jnp.concatenate([real_ref[block, rows, :], imag_ref[block, rows, :]], axis=0)
-            total += jnp.dot(both, piece[...], preferred_element_type=jnp.float32)
-        by_real, by_imag = total[:size], total[size:]
+    size = out_refs[0].shape[0]
+    rows = pl.ds(pl.multiple_of((place_ref[1] ^ turn) * size, size), size)
+    total = jnp.zeros((2 * size, columns), jnp.float32)
+    for number, piece in enumerate(pieces):
+        block = place_ref[0] ^ number
+        both = jnp.concatenate([real_ref[block, rows, :], imag_ref[block, rows, :]], axis=0)
+        total += jnp.dot(both, piece[...], preferred_element_type=jnp.float32)
+    by_real, by_imag = total[:size], total[size:]
+    for out_ref in out_refs:
         out_ref[:, :kept] = (by_real[:, :kept] - by_imag[:, kept:]).astype(out_ref.dtype)
         out_ref[:, kept:] = (by_real[:, kept:] + by_imag[:, :kept]).astype(out_ref.dtype)
 
 
-def make_terms(real_data, imag_data, pieces, place, turns, slice_rows, after):
+def make_terms(real_data, imag_data, pieces, place, turn, slice_rows, types):
     depth = real_data.shape[0] * real_data.shape[2]
     columns = pieces[0].shape[1]
-    rows = len(turns) * slice_rows
-    return pl.pallas_call(
-        functools.partial(terms_kernel, turns, len(pieces)),
-        in_specs=[SMEM] + [VMEM] * (2 + len(pieces)) + [ANY] * len(after),
-        out_specs=[VMEM] * len(turns),
-        out_shape=[
-            jax.ShapeDtypeStruct((slice_rows, columns), jnp.bfloat16 if turn else jnp.float32) for turn in turns
-        ],
-        compiler_params=params(8),
-        cost_estimate=cost(4 * rows * depth * columns, 4 * rows * depth),
+    return pl.pallas_call(
+        functools.partial(terms_kernel, turn, len(pieces)),
+        in_specs=[SMEM] + [VMEM] * (2 + len(pieces)),
+        out_specs=[VMEM] * len(types),
+        out_shape=[jax.ShapeDtypeStruct((slice_rows, columns), kind) for kind in types],
+        compiler_params=params(8),
+        cost_estimate=cost(4 * slice_rows * depth * columns, 4 * slice_rows * depth),
         name="terms",
-    )(place, real_data, imag_data, *pieces, *after)
-
-
-def update(wave_ref, own_ref, others, panel_ref):
+    )(place, real_data, imag_data, *pieces)
+
+
+def add_kernel(own_ref, other_ref, out_ref):
+    out_ref[...] = (own_ref[...] + other_ref[...].astype(jnp.float32)).astype(out_ref.dtype)
+
+
+def make_sum(own, other):
+    return pl.pallas_call(
+        add_kernel,
+        in_specs=[VMEM] * 2,
+        out_specs=VMEM,
+        out_shape=jax.ShapeDtypeStruct(other.shape, other.dtype),
+        compiler_params=params(8),
+        cost_estimate=cost(other.size, 8 * other.size),
+        name="sum",
+    )(own, other)
+
+
+def pick_kernel(place_ref, even_ref, odd_ref, *refs):
+    out_ref = refs[-1]
+
+    @pl.when(place_ref[0] % 2 == 0)
+    def _():
+        out_ref[...] = even_ref[...]
+
+    @pl.when(place_ref[0] % 2 == 1)
+    def _():
+        out_ref[...] = odd_ref[...]
+
+
+def make_pick(place, even, odd, after):
+    return pl.pallas_call(
+        pick_kernel,
+        in_specs=[SMEM] + [VMEM] * 2 + [ANY] * len(after),
+        out_specs=VMEM,
+        out_shape=jax.ShapeDtypeStruct(even.shape, even.dtype),
+        compiler_params=params(8),
+        cost_estimate=cost(0, 4 * even.size),
+        name="pick",
+    )(place, even, odd, *after)
+
+
+def update(place_ref, wave_ref, own_ref, others, panel_ref, folded):
     predicted = own_ref[...]
-    for other in others:
-        predicted += other[...].astype(jnp.float32)
+    for number, other in enumerate(others):
+        term = other[...].astype(jnp.float32)
+        if folded and number == 0:
+            inner = place_ref[1] % 2 != place_ref[1] // 2 % 2
+            term = jnp.where(inner, 0.0, term)
+        predicted += term
     kept = predicted.shape[1] // 2
     turned = jnp.concatenate([-predicted[:, kept:], predicted[:, :kept]], axis=1)
     scaled = wave_ref[0] * predicted + wave_ref[1] * turned
     return predicted, panel_ref[...].astype(jnp.float32) - scaled
 
 
-def estimate_kernel(wave_ref, own_ref, *refs):
+def estimate_kernel(folded, place_ref, wave_ref, own_ref, *refs):
     *others, panel_ref, out_ref = refs
-    out_ref[...] = update(wave_ref, own_ref, others, panel_ref)[1].astype(jnp.bfloat16)
-
-
-def last_kernel(wave_ref, own_ref, *refs):
+    primaries = update(place_ref, wave_ref, own_ref, others, panel_ref, folded)[1]
+    out_ref[...] = primaries.astype(jnp.bfloat16)
+
+
+def last_kernel(folded, place_ref, wave_ref, own_ref, *refs):
     *others, panel_ref, multiples_ref, primaries_ref = refs
-    predicted, primaries = update(wave_ref, own_ref, others, panel_ref)
+    predicted, primaries = update(place_ref, wave_ref, own_ref, others, panel_ref, folded)
     kept = predicted.shape[1] // 2
     multiples_ref[:, 0, :] = predicted[:, :kept]
     multiples_ref[:, 1, :] = predicted[:, kept:]
@@ -300,21 +342,21 @@
     primaries_ref[:, 1, :] = primaries[:, kept:]
 
 
-def make_update(wavelet, own, others, panel, last):
+def make_update(place, wavelet, own, others, panel, folded, last):
     rows, columns = panel.shape
     if last:
         shape = [jax.ShapeDtypeStruct((rows, 2, columns // 2), jnp.float32)] * 2
     else:
         shape = jax.ShapeDtypeStruct((rows, columns), jnp.bfloat16)
     return pl.pallas_call(
-        last_kernel if last else estimate_kernel,
-        in_specs=[SMEM] + [VMEM] * (2 + len(others)),
+        functools.partial(last_kernel if last else estimate_kernel, folded),
+        in_specs=[SMEM] * 2 + [VMEM] * (2 + len(others)),
         out_specs=[VMEM] * 2 if last else VMEM,
         out_shape=shape,
         compiler_params=params(8),
         cost_estimate=cost(16 * rows * columns, 16 * rows * columns),
         name="update",
-    )(wavelet, own, *others, panel)
+    )(place, wavelet, own, *others, panel)
 
 
 def swap(array, axis, bits):
@@ -322,14 +364,35 @@
     return lax.ppermute(array, axis, [(index, index ^ bits) for index in range(size)])
 
 
-def spread(array, axis):
-    size = lax.axis_size(axis)
+def spread(array, place, after):
+    size = lax.axis_size("row")
     pieces = {0: array}
-    for turn in range(2, size, 2):
-        pieces[turn] = swap(array, axis, turn)
+    turns = sorted(range(2, size, 2), key=lambda turn: (turn.bit_count(), turn))
+    for turn in turns:
+        high, low = 1 << turn.bit_length() - 1, turn & -turn
+        if high == low:
+            pieces[turn] = swap(array, "row", turn)
+            continue
+        chosen = make_pick(place, pieces[turn ^ high], pieces[turn ^ low], after)
+        pairs = [(index, index ^ (low if index % 2 else high)) for index in range(size)]
+        pieces[turn] = lax.ppermute(chosen, "row", pairs)
     for turn in range(0, size, 2):
-        pieces[turn + 1] = swap(pieces[turn], axis, 1)
+        pieces[turn + 1] = swap(pieces[turn], "row", 1)
     return [pieces[turn] for turn in range(size)]
+
+
+def exchange(make, n_src):
+    bf16, f32 = jnp.bfloat16, jnp.float32
+    if n_src != 4:
+        arriving = [swap(make(turn, [bf16])[0], "src", turn) for turn in range(n_src - 1, 0, -1)]
+        return make(0, [f32])[0], arriving, False
+    first = lax.ppermute(make(2, [bf16])[0], "src", [(0, 1), (1, 3), (3, 2), (2, 0)])
+    sent, kept = make(3, [bf16, f32])
+    near = make(1, [bf16])[0]
+    beside = swap(near, "src", 1)
+    outer = lax.ppermute(sent, "src", [(0, 3), (3, 0)])
+    inner = lax.ppermute(make_sum(kept, first), "src", [(1, 2), (2, 1)])
+    return make(0, [f32])[0], [first, beside, outer, inner], True
 
 
 def body(traces, row_source, slice_data, wavelet_inverse):
@@ -351,23 +414,19 @@
     code = position * packs + inside % block // short
     code = jnp.broadcast_to(code[:, None], (block_rows, LANES))
     real_data, real_token = relay(slice_data, 0, spectra[0])
-    ordered = make_order(code, arrived, place, n_src, packs, real_token)
+    ordered = make_order(code, arrived, place, n_src, packs)
     located = [ordered[0]] + [swap(ordered[turn], "src", turn) for turn in range(1, n_src)]
-    imag_data, imag_token = relay(slice_data, 1, ordered[0])
-    panel = make_panel(located, place, packs, imag_token)
-
-    half = n_src // 2
-    estimate = panel
+    imag_data, token = relay(slice_data, 1, ordered[0])
+    panel = make_panel(located, place, packs, token)
+
+    estimate, after = panel, [real_token]
     for iteration in range(ITERS):
-        pieces = spread(estimate, "row")
-        arriving, after = [], []
-        for turn in range(n_src - 1, half - 1, -1):
-            after = make_terms(real_data, imag_data, pieces, place, (turn,), slice_rows, [])
-            arriving.append(swap(after[0], "src", turn))
-        near = tuple(range(half - 1, -1, -1))
-        terms = make_terms(real_data, imag_data, pieces, place, near, slice_rows, [])
-        arriving += [swap(part, "src", turn) for turn, part in zip(near[:-1], terms)]
-        estimate = make_update(wavelet_inverse, terms[-1], arriving, panel, iteration == ITERS - 1)
+        pieces = spread(estimate, place, after)
+        after = []
+        own, arriving, folded = exchange(
+            lambda turn, types: make_terms(real_data, imag_data, pieces, place, turn, slice_rows, types), n_src
+        )
+        estimate = make_update(place, wavelet_inverse, own, arriving, panel, folded, iteration == ITERS - 1)
     return tuple(estimate)
 
 

time: 214 us -> 182 us (0.85)
  waiting for transfers between devices: 96.6 us -> 54.8 us
  starting transfers between devices: 36 us -> 41.6 us
  Pallas kernels: 79.2 us -> 83 us
    ppermute x40 -> x31, waiting for transfers between devices: 96.6 us -> 36.1 us  [swap(): lax.ppermute(array, axis, [(index, index ^ bits) for index in range(size)])]
    ppermute x0 -> x12, starting transfers between devices: none -> 21.4 us  [the longest x3 14.2 us: exchange(): outer = lax.ppermute(sent, 'src', [(0, 3), (3, 0)])]
    ppermute x0 -> x12, waiting for transfers between devices: none -> 18.7 us  [the longest x3 14.2 us: spread(): pieces[turn] = lax.ppermute(chosen, 'row', pairs)]
    ppermute x40 -> x31, starting transfers between devices: 36 us -> 20.2 us  [swap(): lax.ppermute(array, axis, [(index, index ^ bits) for index in range(size)])]
    pallas_call x12 -> x21, Pallas kernels: 36 us -> 40 us  [the longest x12 34.4 us: make_terms(): pl.pallas_call(functools.partial(terms_kernel, turn, len(pieces)), in_spe...]
  transfers between devices with their start and end apart: 40 -> 43, of which waited for: 18 -> 19; matrix products, arithmetic and copies ran while one was open for 0% -> 0% of each run, Pallas kernels for 15% -> 23%
where the time goes in v1:
time: 182 us
  Pallas kernels  83 us (46%)
  waiting for transfers between devices  54.8 us (30%)
  starting transfers between devices  41.6 us (23%)
    ppermute x31, waiting for transfers between devices, swap(): lax.ppermute(array, axis, [(index, index ^ bits) for index in range(size)])  36.1 us
    pallas_call x12, Pallas kernels, make_terms(): pl.pallas_call(functools.partial(terms_kernel, turn, len(pieces)), in_spe...  34.4 us
    pallas_call x1, Pallas kernels, make_spectra(): pl.pallas_call(functools.partial(spectra_kernel, packs, n_row), in_specs=...  23.8 us
    ppermute x31, starting transfers between devices, swap(): lax.ppermute(array, axis, [(index, index ^ bits) for index in range(size)])  20.2 us
    pallas_call x2, Pallas kernels, relay(): pl.pallas_call(functools.partial(relay_kernel, part), in_specs=[ANY, ANY]...  15.4 us
    ppermute x3, starting transfers between devices, exchange(): outer = lax.ppermute(sent, 'src', [(0, 3), (3, 0)])  14.2 us
    ppermute x3, waiting for transfers between devices, spread(): pieces[turn] = lax.ppermute(chosen, 'row', pairs)  14.2 us
    ppermute x3, waiting for transfers between devices, exchange(): outer = lax.ppermute(sent, 'src', [(0, 3), (3, 0)])  4.51 us
  transfers between devices with their start and end apart: 43, of which 19 were waited for; matrix products, arithmetic and copies ran while one was open for 0% of the time, Pallas kernels for 23%

profile of v1, /device:TPU:0, one launch (start us, length us, event | category | flops | bytes accessed | tf_op | source)
XLA Modules:
  0.0 181.9 jit_solution(12399261288148324382)
XLA Ops:
  0.7 1.0 copy-done
  1.8 23.8 %spectra.1 = (bf16[2,64,128]{2,1,0:T(8,128)(2,1)S(1)}, bf16[2,64,128]{2,1,0:T(8,128)(2,1)S(1)}, bf16[2,64,128]{2,1,0:T(8,128)(2,1)S(1)}, bf16[2,64,128]{2,1,0:T(...) custom-call(s32[2]{0:T(128)S(1)} %pad_add_fusion.place_ref, ...), custom_call_target="tpu_custom_call" | custom-call | flops 8589934592 | bytes 67108864 | tf_op jit(solution)/shard_map/spectra/pallas_call | solution.py:113
  26.1 2.6 %collective-permute-start.1 = (bf16[128,128]{1,0:T(8,128)(2,1)S(1)}, bf16[128,128]{1,0:T(8,128)(2,1)S(1)}, u32[]{:S(2)}, u32[]{:S(2)}) collective-permute-start(bf16[128,128]{1,0:T(8,128)(2,1)S(1)} %bitcast.17), channel_id=1, source_target_pairs={{0,8},{4,12},{8,0},{12,4},{16,24},{20,28},{24,16},{28,20},{1,9},{5... | collective-permute-start | bytes 98312 | tf_op jit(solution)/shard_map/ppermute | solution.py:364
  28.7 1.8 collective-permute-start.3
  30.5 2.6 %collective-permute-start.5 = (bf16[128,128]{1,0:T(8,128)(2,1)S(1)}, bf16[128,128]{1,0:T(8,128)(2,1)S(1)}, u32[]{:S(2)}, u32[]{:S(2)}) collective-permute-start(bf16[128,128]{1,0:T(8,128)(2,1)S(1)} %bitcast.13), channel_id=1, source_target_pairs={{0,24},{4,28},{8,16},{12,20},{16,8},{20,12},{24,0},{28,4},{1,25},{... | collective-permute-start | bytes 98312 | tf_op jit(solution)/shard_map/ppermute | solution.py:364
  33.9 1.4 collective-permute-done.5.refs_6_
  35.3 2.0 %collective-permute-done.6.refs_7_ = bf16[128,128]{1,0:T(8,128)(2,1)S(1)} collective-permute-done((bf16[128,128]{1,0:T(8,128)(2,1)S(1)}, bf16[128,128]{1,0:T(8,128)(2,1)S(1)}, u32[]{:S(2)}, u32[]{:S(2)}) %collective-permute-start.6) | collective-permute-done | bytes 32800 | tf_op jit(solution)/shard_map/ppermute | solution.py:364
  37.7 2.8 %order.1 = (bf16[256,128]{1,0:T(8,128)(2,1)S(1)}, bf16[256,128]{1,0:T(8,128)(2,1)S(1)}, bf16[256,128]{1,0:T(8,128)(2,1)S(1)}, bf16[256,128]{1,0:T(8,128)(2,1)S(1)}) custom-call(s32[2]{0:T(128)S(1)} %pad_add_fusion.place_ref, s32[2048,128]{1,0:T(8,128)S(1)} %broadcast_in_dim.2.code_ref, bf16[128,128]{1,0:T(8,128)(2,1)S(1)} %bitcast.10, ...), custom_call_target="tpu_custom_call" | custom-call | flops 1073741824 | bytes 1048576 | tf_op jit(solution)/shard_map/order/pallas_call | solution.py:163
  40.5 1.6 collective-permute-start.7
  42.1 2.6 %collective-permute-start.8 = (bf16[256,128]{1,0:T(8,128)(2,1)S(1)}, bf16[256,128]{1,0:T(8,128)(2,1)S(1)}, u32[]{:S(2)}, u32[]{:S(2)}) collective-permute-start(bf16[256,128]{1,0:T(8,128)(2,1)S(1)} %get-tuple-element.36), channel_id=1, source_target_pairs={{0,2},{1,3},{2,0},{3,1},{4,6},{5,7},{6,4},{7,5},{8,10},{9,11},{10,... | collective-permute-start | bytes 196616 | tf_op jit(solution)/shard_map/ppermute | solution.py:364
  45.0 7.7 %relay.3 = (bf16[8,2048,512]{2,1,0:T(8,128)(2,1)S(1)}, f32[8,128]{1,0:T(8,128)S(1)}) custom-call(bf16[2,2048,8,512]{3,2,1,0:T(8,128)(2,1)} %data_ref.3, bf16[256,128]{1,0:T(8,128)(2,1)S(1)} %get-tuple-element.33.after_ref.refs_0_), custom_call_target="tpu_custom_call" | custom-call | bytes 33554432 | tf_op jit(solution)/shard_map/relay/pallas_call | solution.py:226
  54.3 1.1 collective-permute-start.13
  55.4 7.7 %relay.2 = (bf16[8,2048,512]{2,1,0:T(8,128)(2,1)S(1)}, f32[8,128]{1,0:T(8,128)S(1)}) custom-call(bf16[2,2048,8,512]{3,2,1,0:T(8,128)(2,1)} %data_ref.3, bf16[128,128]{1,0:T(8,128)(2,1)S(1)} %bitcast.11), custom_call_target="tpu_custom_call" | custom-call | bytes 33554432 | tf_op jit(solution)/shard_map/relay/pallas_call | solution.py:226
  63.6 1.0 collective-permute-start.15
  65.2 4.9 %collective-permute-done.15.refs_6_ = bf16[512,256]{1,0:T(8,128)(2,1)S(1)} collective-permute-done((bf16[512,256]{1,0:T(8,128)(2,1)S(1)}, bf16[512,256]{1,0:T(8,128)(2,1)S(1)}, u32[]{:S(2)}, u32[]{:S(2)}) %collective-permute-start.15) | collective-permute-done | bytes 262176 | tf_op jit(solution)/shard_map/ppermute | solution.py:378
  70.1 1.5 collective-permute-done.16.refs_7_
  71.6 2.9 %terms.13 = bf16[512,256]{1,0:T(8,128)(2,1)S(1)} custom-call(s32[2]{0:T(128)S(1)} %pad_add_fusion.place_ref, bf16[8,2048,512]{2,1,0:T(8,128)(2,1)S(1)} %get-tuple-element.25.real_ref, bf16[8,2048,512]{2,1,0:T(8,128)(2,1)S(1)} %get-tuple-element.34.imag_ref, bf16[512,256]{1,0:T(8,128)(2,1)S(1)} %panel.1.refs_0_.refs_4_, ...), custom_call_target="tpu_custom_call" | custom-call | flops 2147483648 | bytes 8388608 | tf_op jit(solution)/shard_map/terms/pallas_call | solution.py:264
  75.2 2.9 %terms.15 = (bf16[512,256]{1,0:T(8,128)(2,1)S(1)}, f32[512,256]{1,0:T(8,128)S(1)}) custom-call(s32[2]{0:T(128)S(1)} %pad_add_fusion.place_ref, bf16[8,2048,512]{2,1,0:T(8,128)(2,1)S(1)} %get-tuple-element.25.real_ref, bf16[8,2048,512]{2,1,0:T(8,128)(2,1)S(1)} %get-tuple-element.34.imag_ref, bf16[512,256]{1,0:T(8,128)(2,1)S(1)} %panel.1.refs_0_.refs_4_, ...), custom_call_target="tpu_custom_call" | custom-call | flops 2147483648 | bytes 8388608 | tf_op jit(solution)/shard_map/terms/pallas_call | solution.py:264
  78.1 4.8 %collective-permute-start.19 = (bf16[512,256]{1,0:T(8,128)(2,1)S(1)}, bf16[512,256]{1,0:T(8,128)(2,1)S(1)}, u32[]{:S(2)}, u32[]{:S(2)}) collective-permute-start(bf16[512,256]{1,0:T(8,128)(2,1)S(1)} %get-tuple-element.40), channel_id=1, source_target_pairs={{0,3},{3,0},{4,7},{7,4},{8,11},{11,8},{12,15},{15,12},{16,19},{19,... | collective-permute-start | bytes 786440 | tf_op jit(solution)/shard_map/ppermute | solution.py:393
  83.0 2.9 %terms.14 = bf16[512,256]{1,0:T(8,128)(2,1)S(1)} custom-call(s32[2]{0:T(128)S(1)} %pad_add_fusion.place_ref, bf16[8,2048,512]{2,1,0:T(8,128)(2,1)S(1)} %get-tuple-element.25.real_ref, bf16[8,2048,512]{2,1,0:T(8,128)(2,1)S(1)} %get-tuple-element.34.imag_ref, bf16[512,256]{1,0:T(8,128)(2,1)S(1)} %panel.1.refs_0_.refs_4_, ...), custom_call_target="tpu_custom_call" | custom-call | flops 2147483648 | bytes 8388608 | tf_op jit(solution)/shard_map/terms/pallas_call | solution.py:264
  86.8 2.9 %terms.12.own_ref = f32[512,256]{1,0:T(8,128)S(1)} custom-call(s32[2]{0:T(128)S(1)} %pad_add_fusion.place_ref, bf16[8,2048,512]{2,1,0:T(8,128)(2,1)S(1)} %get-tuple-element.25.real_ref, bf16[8,2048,512]{2,1,0:T(8,128)(2,1)S(1)} %get-tuple-element.34.imag_ref, bf16[512,256]{1,0:T(8,128)(2,1)S(1)} %panel.1.refs_0_.refs_4_, ...), custom_call_target="tpu_custom_call" | custom-call | flops 2147483648 | bytes 8388608 | tf_op jit(solution)/shard_map/terms/pallas_call | solution.py:264
  89.7 1.3 collective-permute-done.19.refs_2_
  91.0 4.9 %collective-permute-done.18.refs_1_ = bf16[512,256]{1,0:T(8,128)(2,1)S(1)} collective-permute-done((bf16[512,256]{1,0:T(8,128)(2,1)S(1)}, bf16[512,256]{1,0:T(8,128)(2,1)S(1)}, u32[]{:S(2)}, u32[]{:S(2)}) %collective-permute-start.18) | collective-permute-done | bytes 262176 | tf_op jit(solution)/shard_map/ppermute | solution.py:364
  97.8 1.5 collective-permute-start.24
  99.3 5.8 %collective-permute-done.22.even_ref.refs_2_ = bf16[512,256]{1,0:T(8,128)(2,1)S(1)} collective-permute-done((bf16[512,256]{1,0:T(8,128)(2,1)S(1)}, bf16[512,256]{1,0:T(8,128)(2,1)S(1)}, u32[]{:S(2)}, u32[]{:S(2)}) %collective-permute-start.22) | collective-permute-done | bytes 262176 | tf_op jit(solution)/shard_map/ppermute | solution.py:364
  106.3 1.6 collective-permute-start.26
  108.4 4.3 %collective-permute-done.26.refs_6_ = bf16[512,256]{1,0:T(8,128)(2,1)S(1)} collective-permute-done((bf16[512,256]{1,0:T(8,128)(2,1)S(1)}, bf16[512,256]{1,0:T(8,128)(2,1)S(1)}, u32[]{:S(2)}, u32[]{:S(2)}) %collective-permute-start.26) | collective-permute-done | bytes 262176 | tf_op jit(solution)/shard_map/ppermute | solution.py:378
  112.8 1.5 collective-permute-done.27.refs_7_
  114.3 2.9 %terms.17 = bf16[512,256]{1,0:T(8,128)(2,1)S(1)} custom-call(s32[2]{0:T(128)S(1)} %pad_add_fusion.place_ref, bf16[8,2048,512]{2,1,0:T(8,128)(2,1)S(1)} %get-tuple-element.25.real_ref, bf16[8,2048,512]{2,1,0:T(8,128)(2,1)S(1)} %get-tuple-element.34.imag_ref, bf16[512,256]{1,0:T(8,128)(2,1)S(1)} %update.3.refs_0_, ...), custom_call_target="tpu_custom_call" | custom-call | flops 2147483648 | bytes 8388608 | tf_op jit(solution)/shard_map/terms/pallas_call | solution.py:264
  117.5 2.9 %terms.19 = (bf16[512,256]{1,0:T(8,128)(2,1)S(1)}, f32[512,256]{1,0:T(8,128)S(1)}) custom-call(s32[2]{0:T(128)S(1)} %pad_add_fusion.place_ref, bf16[8,2048,512]{2,1,0:T(8,128)(2,1)S(1)} %get-tuple-element.25.real_ref, bf16[8,2048,512]{2,1,0:T(8,128)(2,1)S(1)} %get-tuple-element.34.imag_ref, bf16[512,256]{1,0:T(8,128)(2,1)S(1)} %update.3.refs_0_, ...), custom_call_target="tpu_custom_call" | custom-call | flops 2147483648 | bytes 8388608 | tf_op jit(solution)/shard_map/terms/pallas_call | solution.py:264
  120.4 4.6 %collective-permute-start.30 = (bf16[512,256]{1,0:T(8,128)(2,1)S(1)}, bf16[512,256]{1,0:T(8,128)(2,1)S(1)}, u32[]{:S(2)}, u32[]{:S(2)}) collective-permute-start(bf16[512,256]{1,0:T(8,128)(2,1)S(1)} %get-tuple-element.42), channel_id=1, source_target_pairs={{0,3},{3,0},{4,7},{7,4},{8,11},{11,8},{12,15},{15,12},{16,19},{19,... | collective-permute-start | bytes 786440 | tf_op jit(solution)/shard_map/ppermute | solution.py:393
  125.0 2.9 %terms.18 = bf16[512,256]{1,0:T(8,128)(2,1)S(1)} custom-call(s32[2]{0:T(128)S(1)} %pad_add_fusion.place_ref, bf16[8,2048,512]{2,1,0:T(8,128)(2,1)S(1)} %get-tuple-element.25.real_ref, bf16[8,2048,512]{2,1,0:T(8,128)(2,1)S(1)} %get-tuple-element.34.imag_ref, bf16[512,256]{1,0:T(8,128)(2,1)S(1)} %update.3.refs_0_, ...), custom_call_target="tpu_custom_call" | custom-call | flops 2147483648 | bytes 8388608 | tf_op jit(solution)/shard_map/terms/pallas_call | solution.py:264
  128.7 2.9 %terms.16.own_ref = f32[512,256]{1,0:T(8,128)S(1)} custom-call(s32[2]{0:T(128)S(1)} %pad_add_fusion.place_ref, bf16[8,2048,512]{2,1,0:T(8,128)(2,1)S(1)} %get-tuple-element.25.real_ref, bf16[8,2048,512]{2,1,0:T(8,128)(2,1)S(1)} %get-tuple-element.34.imag_ref, bf16[512,256]{1,0:T(8,128)(2,1)S(1)} %update.3.refs_0_, ...), custom_call_target="tpu_custom_call" | custom-call | flops 2147483648 | bytes 8388608 | tf_op jit(solution)/shard_map/terms/pallas_call | solution.py:264
  131.6 1.7 collective-permute-done.30.refs_2_
  133.3 4.5 %collective-permute-done.29.refs_1_ = bf16[512,256]{1,0:T(8,128)(2,1)S(1)} collective-permute-done((bf16[512,256]{1,0:T(8,128)(2,1)S(1)}, bf16[512,256]{1,0:T(8,128)(2,1)S(1)}, u32[]{:S(2)}, u32[]{:S(2)}) %collective-permute-start.29) | collective-permute-done | bytes 262176 | tf_op jit(solution)/shard_map/ppermute | solution.py:364
  138.6 1.2 collective-permute-start.33
  140.7 6.0 %collective-permute-done.33.even_ref.refs_2_ = bf16[512,256]{1,0:T(8,128)(2,1)S(1)} collective-permute-done((bf16[512,256]{1,0:T(8,128)(2,1)S(1)}, bf16[512,256]{1,0:T(8,128)(2,1)S(1)}, u32[]{:S(2)}, u32[]{:S(2)}) %collective-permute-start.33) | collective-permute-done | bytes 262176 | tf_op jit(solution)/shard_map/ppermute | solution.py:364
  148.2 1.0 collective-permute-start.37
  149.7 4.9 %collective-permute-done.37.refs_6_ = bf16[512,256]{1,0:T(8,128)(2,1)S(1)} collective-permute-done((bf16[512,256]{1,0:T(8,128)(2,1)S(1)}, bf16[512,256]{1,0:T(8,128)(2,1)S(1)}, u32[]{:S(2)}, u32[]{:S(2)}) %collective-permute-start.37) | collective-permute-done | bytes 262176 | tf_op jit(solution)/shard_map/ppermute | solution.py:378
  154.7 1.5 collective-permute-done.38.refs_7_
  156.2 2.9 %terms.21 = bf16[512,256]{1,0:T(8,128)(2,1)S(1)} custom-call(s32[2]{0:T(128)S(1)} %pad_add_fusion.place_ref, bf16[8,2048,512]{2,1,0:T(8,128)(2,1)S(1)} %get-tuple-element.25.real_ref, bf16[8,2048,512]{2,1,0:T(8,128)(2,1)S(1)} %get-tuple-element.34.imag_ref, bf16[512,256]{1,0:T(8,128)(2,1)S(1)} %update.4.refs_0_, ...), custom_call_target="tpu_custom_call" | custom-call | flops 2147483648 | bytes 8388608 | tf_op jit(solution)/shard_map/terms/pallas_call | solution.py:264
  159.3 2.9 %terms.23 = (bf16[512,256]{1,0:T(8,128)(2,1)S(1)}, f32[512,256]{1,0:T(8,128)S(1)}) custom-call(s32[2]{0:T(128)S(1)} %pad_add_fusion.place_ref, bf16[8,2048,512]{2,1,0:T(8,128)(2,1)S(1)} %get-tuple-element.25.real_ref, bf16[8,2048,512]{2,1,0:T(8,128)(2,1)S(1)} %get-tuple-element.34.imag_ref, bf16[512,256]{1,0:T(8,128)(2,1)S(1)} %update.4.refs_0_, ...), custom_call_target="tpu_custom_call" | custom-call | flops 2147483648 | bytes 8388608 | tf_op jit(solution)/shard_map/terms/pallas_call | solution.py:264
  162.2 4.8 %collective-permute-start.41 = (bf16[512,256]{1,0:T(8,128)(2,1)S(1)}, bf16[512,256]{1,0:T(8,128)(2,1)S(1)}, u32[]{:S(2)}, u32[]{:S(2)}) collective-permute-start(bf16[512,256]{1,0:T(8,128)(2,1)S(1)} %get-tuple-element.44), channel_id=1, source_target_pairs={{0,3},{3,0},{4,7},{7,4},{8,11},{11,8},{12,15},{15,12},{16,19},{19,... | collective-permute-start | bytes 786440 | tf_op jit(solution)/shard_map/ppermute | solution.py:393
  167.0 2.9 %terms.22 = bf16[512,256]{1,0:T(8,128)(2,1)S(1)} custom-call(s32[2]{0:T(128)S(1)} %pad_add_fusion.place_ref, bf16[8,2048,512]{2,1,0:T(8,128)(2,1)S(1)} %get-tuple-element.25.real_ref, bf16[8,2048,512]{2,1,0:T(8,128)(2,1)S(1)} %get-tuple-element.34.imag_ref, bf16[512,256]{1,0:T(8,128)(2,1)S(1)} %update.4.refs_0_, ...), custom_call_target="tpu_custom_call" | custom-call | flops 2147483648 | bytes 8388608 | tf_op jit(solution)/shard_map/terms/pallas_call | solution.py:264
  170.7 2.9 %terms.20.own_ref = f32[512,256]{1,0:T(8,128)S(1)} custom-call(s32[2]{0:T(128)S(1)} %pad_add_fusion.place_ref, bf16[8,2048,512]{2,1,0:T(8,128)(2,1)S(1)} %get-tuple-element.25.real_ref, bf16[8,2048,512]{2,1,0:T(8,128)(2,1)S(1)} %get-tuple-element.34.imag_ref, bf16[512,256]{1,0:T(8,128)(2,1)S(1)} %update.4.refs_0_, ...), custom_call_target="tpu_custom_call" | custom-call | flops 2147483648 | bytes 8388608 | tf_op jit(solution)/shard_map/terms/pallas_call | solution.py:264
  173.6 1.5 collective-permute-done.41.refs_2_
  175.1 4.7 %collective-permute-done.40.refs_1_ = bf16[512,256]{1,0:T(8,128)(2,1)S(1)} collective-permute-done((bf16[512,256]{1,0:T(8,128)(2,1)S(1)}, bf16[512,256]{1,0:T(8,128)(2,1)S(1)}, u32[]{:S(2)}, u32[]{:S(2)}) %collective-permute-start.40) | collective-permute-done | bytes 262176 | tf_op jit(solution)/shard_map/ppermute | solution.py:364
  179.8 2.1 %update.5 = (f32[512,2,128]{2,1,0:T(2,128)}, f32[512,2,128]{2,1,0:T(2,128)}) custom-call(s32[2]{0:T(128)S(1)} %pad_add_fusion.place_ref, f32[2]{0:T(128)S(1)} %copy-done.1, f32[512,256]{1,0:T(8,128)S(1)} %terms.20.own_ref, bf16[512,256]{1,0:T(8,128)(2,1)S(1)} %collective-permute-done.39.other_ref.refs_0_, ...), custom_call_target="tpu_custom_call" | custom-call | flops 2097152 | bytes 2097152 | tf_op jit(solution)/shard_map/update/pallas_call | solution.py:351
  (73 shorter events, 15.9 us)
Async XLA Ops:
  0.7 1.0 copy-start
  1.8 31.5 %copy-start.2 = (s32[2048]{0:T(1024)S(1)}, s32[2048]{0:T(1024)}, u32[]{:S(2)}) copy-start(s32[2048]{0:T(1024)} %param.6) | copy-start | bytes 24580
  25.6 4.9 %collective-permute-start = (bf16[128,128]{1,0:T(8,128)(2,1)S(1)}, bf16[128,128]{1,0:T(8,128)(2,1)S(1)}, u32[]{:S(2)}, u32[]{:S(2)}) collective-permute-start(bf16[128,128]{1,0:T(8,128)(2,1)S(1)} %bitcast.18), channel_id=1, source_target_pairs={{0,4},{4,0},{8,12},{12,8},{16,20},{20,16},{24,28},{28,24},{1,5},{5... | collective-permute-start | bytes 98312 | tf_op jit(solution)/shard_map/ppermute | solution.py:364
  26.1 7.0 %collective-permute-start.1 = (bf16[128,128]{1,0:T(8,128)(2,1)S(1)}, bf16[128,128]{1,0:T(8,128)(2,1)S(1)}, u32[]{:S(2)}, u32[]{:S(2)}) collective-permute-start(bf16[128,128]{1,0:T(8,128)(2,1)S(1)} %bitcast.17), channel_id=1, source_target_pairs={{0,8},{4,12},{8,0},{12,4},{16,24},{20,28},{24,16},{28,20},{1,9},{5... | collective-permute-start | bytes 98312 | tf_op jit(solution)/shard_map/ppermute | solution.py:364
  28.6 4.6 %collective-permute-start.2 = (bf16[128,128]{1,0:T(8,128)(2,1)S(1)}, bf16[128,128]{1,0:T(8,128)(2,1)S(1)}, u32[]{:S(2)}, u32[]{:S(2)}) collective-permute-start(bf16[128,128]{1,0:T(8,128)(2,1)S(1)} %bitcast.16), channel_id=1, source_target_pairs={{0,12},{4,8},{8,4},{12,0},{16,28},{20,24},{24,20},{28,16},{1,13},{... | collective-permute-start | bytes 98312 | tf_op jit(solution)/shard_map/ppermute | solution.py:364
  28.7 4.6 %collective-permute-start.3 = (bf16[128,128]{1,0:T(8,128)(2,1)S(1)}, bf16[128,128]{1,0:T(8,128)(2,1)S(1)}, u32[]{:S(2)}, u32[]{:S(2)}) collective-permute-start(bf16[128,128]{1,0:T(8,128)(2,1)S(1)} %bitcast.15), channel_id=1, source_target_pairs={{0,16},{4,20},{8,24},{12,28},{16,0},{20,4},{24,8},{28,12},{1,17},{... | collective-permute-start | bytes 98312 | tf_op jit(solution)/shard_map/ppermute | solution.py:364
  30.5 3.5 %collective-permute-start.4 = (bf16[128,128]{1,0:T(8,128)(2,1)S(1)}, bf16[128,128]{1,0:T(8,128)(2,1)S(1)}, u32[]{:S(2)}, u32[]{:S(2)}) collective-permute-start(bf16[128,128]{1,0:T(8,128)(2,1)S(1)} %bitcast.14), channel_id=1, source_target_pairs={{0,20},{4,16},{8,28},{12,24},{16,4},{20,0},{24,12},{28,8},{1,21},{... | collective-permute-start | bytes 98312 | tf_op jit(solution)/shard_map/ppermute | solution.py:364
  30.5 4.8 %collective-permute-start.5 = (bf16[128,128]{1,0:T(8,128)(2,1)S(1)}, bf16[128,128]{1,0:T(8,128)(2,1)S(1)}, u32[]{:S(2)}, u32[]{:S(2)}) collective-permute-start(bf16[128,128]{1,0:T(8,128)(2,1)S(1)} %bitcast.13), channel_id=1, source_target_pairs={{0,24},{4,28},{8,16},{12,20},{16,8},{20,12},{24,0},{28,4},{1,25},{... | collective-permute-start | bytes 98312 | tf_op jit(solution)/shard_map/ppermute | solution.py:364
  33.1 4.2 %collective-permute-start.6 = (bf16[128,128]{1,0:T(8,128)(2,1)S(1)}, bf16[128,128]{1,0:T(8,128)(2,1)S(1)}, u32[]{:S(2)}, u32[]{:S(2)}) collective-permute-start(bf16[128,128]{1,0:T(8,128)(2,1)S(1)} %bitcast.12), channel_id=1, source_target_pairs={{0,28},{4,24},{8,20},{12,16},{16,12},{20,8},{24,4},{28,0},{1,29},{... | collective-permute-start | bytes 98312 | tf_op jit(solution)/shard_map/ppermute | solution.py:364
  40.5 12.1 %collective-permute-start.7 = (bf16[256,128]{1,0:T(8,128)(2,1)S(1)}, bf16[256,128]{1,0:T(8,128)(2,1)S(1)}, u32[]{:S(2)}, u32[]{:S(2)}) collective-permute-start(bf16[256,128]{1,0:T(8,128)(2,1)S(1)} %get-tuple-element.35), channel_id=1, source_target_pairs={{0,1},{1,0},{2,3},{3,2},{4,5},{5,4},{6,7},{7,6},{8,9},{9,8},{10,11... | collective-permute-start | bytes 196616 | tf_op jit(solution)/shard_map/ppermute | solution.py:364
  42.1 10.5 %collective-permute-start.8 = (bf16[256,128]{1,0:T(8,128)(2,1)S(1)}, bf16[256,128]{1,0:T(8,128)(2,1)S(1)}, u32[]{:S(2)}, u32[]{:S(2)}) collective-permute-start(bf16[256,128]{1,0:T(8,128)(2,1)S(1)} %get-tuple-element.36), channel_id=1, source_target_pairs={{0,2},{1,3},{2,0},{3,1},{4,6},{5,7},{6,4},{7,5},{8,10},{9,11},{10,... | collective-permute-start | bytes 196616 | tf_op jit(solution)/shard_map/ppermute | solution.py:364
  44.7 7.9 %collective-permute-start.9 = (bf16[256,128]{1,0:T(8,128)(2,1)S(1)}, bf16[256,128]{1,0:T(8,128)(2,1)S(1)}, u32[]{:S(2)}, u32[]{:S(2)}) collective-permute-start(bf16[256,128]{1,0:T(8,128)(2,1)S(1)} %get-tuple-element.37), channel_id=1, source_target_pairs={{0,3},{1,2},{2,1},{3,0},{4,7},{5,6},{6,5},{7,4},{8,11},{9,10},{10,... | collective-permute-start | bytes 196616 | tf_op jit(solution)/shard_map/ppermute | solution.py:364
  53.7 9.4 %collective-permute-start.11 = (bf16[512,256]{1,0:T(8,128)(2,1)S(1)}, bf16[512,256]{1,0:T(8,128)(2,1)S(1)}, u32[]{:S(2)}, u32[]{:S(2)}) collective-permute-start(bf16[512,256]{1,0:T(8,128)(2,1)S(1)} %panel.1.refs_0_.refs_4_), channel_id=1, source_target_pairs={{0,8},{4,12},{8,0},{12,4},{16,24},{20,28},{24,16},{28,20},{1,9},{5... | collective-permute-start | bytes 786440 | tf_op jit(solution)/shard_map/ppermute | solution.py:364
  54.3 8.8 %collective-permute-start.13 = (bf16[512,256]{1,0:T(8,128)(2,1)S(1)}, bf16[512,256]{1,0:T(8,128)(2,1)S(1)}, u32[]{:S(2)}, u32[]{:S(2)}) collective-permute-start(bf16[512,256]{1,0:T(8,128)(2,1)S(1)} %panel.1.refs_0_.refs_4_), channel_id=1, source_target_pairs={{0,16},{4,20},{8,24},{12,28},{16,0},{20,4},{24,8},{28,12},{1,17},{... | collective-permute-start | bytes 786440 | tf_op jit(solution)/shard_map/ppermute | solution.py:364
  63.6 6.4 %collective-permute-start.15 = (bf16[512,256]{1,0:T(8,128)(2,1)S(1)}, bf16[512,256]{1,0:T(8,128)(2,1)S(1)}, u32[]{:S(2)}, u32[]{:S(2)}) collective-permute-start(bf16[512,256]{1,0:T(8,128)(2,1)S(1)} %pick.3), channel_id=1, source_target_pairs={{0,16},{4,12},{8,24},{12,4},{16,0},{20,28},{24,8},{28,20},{1,17},{... | collective-permute-start | bytes 786440 | tf_op jit(solution)/shard_map/ppermute | solution.py:378
  64.6 5.5 %collective-permute-start.10 = (bf16[512,256]{1,0:T(8,128)(2,1)S(1)}, bf16[512,256]{1,0:T(8,128)(2,1)S(1)}, u32[]{:S(2)}, u32[]{:S(2)}) collective-permute-start(bf16[512,256]{1,0:T(8,128)(2,1)S(1)} %panel.1.refs_0_.refs_4_), channel_id=1, source_target_pairs={{0,4},{4,0},{8,12},{12,8},{16,20},{20,16},{24,28},{28,24},{1,5},{5... | collective-permute-start | bytes 786440 | tf_op jit(solution)/shard_map/ppermute | solution.py:364
  64.6 5.5 %collective-permute-start.12 = (bf16[512,256]{1,0:T(8,128)(2,1)S(1)}, bf16[512,256]{1,0:T(8,128)(2,1)S(1)}, u32[]{:S(2)}, u32[]{:S(2)}) collective-permute-start(bf16[512,256]{1,0:T(8,128)(2,1)S(1)} %collective-permute-done.11.even_ref.refs_2_), channel_id=1, source_target_pairs={{0,4},{4,0},{8,12},{12,8},{16,20},{20,16},{24,28},{28,24},{1,5},{5... | collective-permute-start | bytes 786440 | tf_op jit(solution)/shard_map/ppermute | solution.py:364
  65.1 4.9 %collective-permute-start.14 = (bf16[512,256]{1,0:T(8,128)(2,1)S(1)}, bf16[512,256]{1,0:T(8,128)(2,1)S(1)}, u32[]{:S(2)}, u32[]{:S(2)}) collective-permute-start(bf16[512,256]{1,0:T(8,128)(2,1)S(1)} %collective-permute-done.13.odd_ref.refs_4_), channel_id=1, source_target_pairs={{0,4},{4,0},{8,12},{12,8},{16,20},{20,16},{24,28},{28,24},{1,5},{5... | collective-permute-start | bytes 786440 | tf_op jit(solution)/shard_map/ppermute | solution.py:364
  70.1 1.5 collective-permute-start.16
  74.5 11.4 %collective-permute-start.17 = (bf16[512,256]{1,0:T(8,128)(2,1)S(1)}, bf16[512,256]{1,0:T(8,128)(2,1)S(1)}, u32[]{:S(2)}, u32[]{:S(2)}) collective-permute-start(bf16[512,256]{1,0:T(8,128)(2,1)S(1)} %terms.13), channel_id=1, source_target_pairs={{0,1},{1,3},{3,2},{2,0},{4,5},{5,7},{7,6},{6,4},{8,9},{9,11},{11,1... | collective-permute-start | bytes 786440 | tf_op jit(solution)/shard_map/ppermute | solution.py:389
  78.1 17.9 %copy-start.1 = (f32[2]{0:T(128)S(1)}, f32[2]{0:T(128)}, u32[]{:S(2)}) copy-start(f32[2]{0:T(128)} %wave_ref.5) | copy-start | bytes 28
  78.1 12.9 %collective-permute-start.19 = (bf16[512,256]{1,0:T(8,128)(2,1)S(1)}, bf16[512,256]{1,0:T(8,128)(2,1)S(1)}, u32[]{:S(2)}, u32[]{:S(2)}) collective-permute-start(bf16[512,256]{1,0:T(8,128)(2,1)S(1)} %get-tuple-element.40), channel_id=1, source_target_pairs={{0,3},{3,0},{4,7},{7,4},{8,11},{11,8},{12,15},{15,12},{16,19},{19,... | collective-permute-start | bytes 786440 | tf_op jit(solution)/shard_map/ppermute | solution.py:393
  85.8 10.2 %collective-permute-start.18 = (bf16[512,256]{1,0:T(8,128)(2,1)S(1)}, bf16[512,256]{1,0:T(8,128)(2,1)S(1)}, u32[]{:S(2)}, u32[]{:S(2)}) collective-permute-start(bf16[512,256]{1,0:T(8,128)(2,1)S(1)} %terms.14), channel_id=1, source_target_pairs={{0,1},{1,0},{2,3},{3,2},{4,5},{5,4},{6,7},{7,6},{8,9},{9,8},{10,11... | collective-permute-start | bytes 786440 | tf_op jit(solution)/shard_map/ppermute | solution.py:364
  86.0 10.0 %collective-permute-start.20 = (bf16[512,256]{1,0:T(8,128)(2,1)S(1)}, bf16[512,256]{1,0:T(8,128)(2,1)S(1)}, u32[]{:S(2)}, u32[]{:S(2)}) collective-permute-start(bf16[512,256]{1,0:T(8,128)(2,1)S(1)} %sum.3), channel_id=1, source_target_pairs={{1,2},{2,1},{5,6},{6,5},{9,10},{10,9},{13,14},{14,13},{17,18},{18,... | collective-permute-start | bytes 786440 | tf_op jit(solution)/shard_map/ppermute | solution.py:394
  96.8 8.3 %collective-permute-start.22 = (bf16[512,256]{1,0:T(8,128)(2,1)S(1)}, bf16[512,256]{1,0:T(8,128)(2,1)S(1)}, u32[]{:S(2)}, u32[]{:S(2)}) collective-permute-start(bf16[512,256]{1,0:T(8,128)(2,1)S(1)} %update.3.refs_0_), channel_id=1, source_target_pairs={{0,8},{4,12},{8,0},{12,4},{16,24},{20,28},{24,16},{28,20},{1,9},{5... | collective-permute-start | bytes 786440 | tf_op jit(solution)/shard_map/ppermute | solution.py:364
  97.8 7.9 %collective-permute-start.24 = (bf16[512,256]{1,0:T(8,128)(2,1)S(1)}, bf16[512,256]{1,0:T(8,128)(2,1)S(1)}, u32[]{:S(2)}, u32[]{:S(2)}) collective-permute-start(bf16[512,256]{1,0:T(8,128)(2,1)S(1)} %update.3.refs_0_), channel_id=1, source_target_pairs={{0,16},{4,20},{8,24},{12,28},{16,0},{20,4},{24,8},{28,12},{1,17},{... | collective-permute-start | bytes 786440 | tf_op jit(solution)/shard_map/ppermute | solution.py:364
  106.3 6.4 %collective-permute-start.26 = (bf16[512,256]{1,0:T(8,128)(2,1)S(1)}, bf16[512,256]{1,0:T(8,128)(2,1)S(1)}, u32[]{:S(2)}, u32[]{:S(2)}) collective-permute-start(bf16[512,256]{1,0:T(8,128)(2,1)S(1)} %pick.4), channel_id=1, source_target_pairs={{0,16},{4,12},{8,24},{12,4},{16,0},{20,28},{24,8},{28,20},{1,17},{... | collective-permute-start | bytes 786440 | tf_op jit(solution)/shard_map/ppermute | solution.py:378
  107.9 4.9 %collective-permute-start.21 = (bf16[512,256]{1,0:T(8,128)(2,1)S(1)}, bf16[512,256]{1,0:T(8,128)(2,1)S(1)}, u32[]{:S(2)}, u32[]{:S(2)}) collective-permute-start(bf16[512,256]{1,0:T(8,128)(2,1)S(1)} %update.3.refs_0_), channel_id=1, source_target_pairs={{0,4},{4,0},{8,12},{12,8},{16,20},{20,16},{24,28},{28,24},{1,5},{5... | collective-permute-start | bytes 786440 | tf_op jit(solution)/shard_map/ppermute | solution.py:364
  107.9 4.9 %collective-permute-start.23 = (bf16[512,256]{1,0:T(8,128)(2,1)S(1)}, bf16[512,256]{1,0:T(8,128)(2,1)S(1)}, u32[]{:S(2)}, u32[]{:S(2)}) collective-permute-start(bf16[512,256]{1,0:T(8,128)(2,1)S(1)} %collective-permute-done.22.even_ref.refs_2_), channel_id=1, source_target_pairs={{0,4},{4,0},{8,12},{12,8},{16,20},{20,16},{24,28},{28,24},{1,5},{5... | collective-permute-start | bytes 786440 | tf_op jit(solution)/shard_map/ppermute | solution.py:364
  108.4 4.4 %collective-permute-start.25 = (bf16[512,256]{1,0:T(8,128)(2,1)S(1)}, bf16[512,256]{1,0:T(8,128)(2,1)S(1)}, u32[]{:S(2)}, u32[]{:S(2)}) collective-permute-start(bf16[512,256]{1,0:T(8,128)(2,1)S(1)} %collective-permute-done.24.odd_ref.refs_4_), channel_id=1, source_target_pairs={{0,4},{4,0},{8,12},{12,8},{16,20},{20,16},{24,28},{28,24},{1,5},{5... | collective-permute-start | bytes 786440 | tf_op jit(solution)/shard_map/ppermute | solution.py:364
  112.8 1.5 collective-permute-start.27
  117.2 10.8 %collective-permute-start.28 = (bf16[512,256]{1,0:T(8,128)(2,1)S(1)}, bf16[512,256]{1,0:T(8,128)(2,1)S(1)}, u32[]{:S(2)}, u32[]{:S(2)}) collective-permute-start(bf16[512,256]{1,0:T(8,128)(2,1)S(1)} %terms.17), channel_id=1, source_target_pairs={{0,1},{1,3},{3,2},{2,0},{4,5},{5,7},{7,6},{6,4},{8,9},{9,11},{11,1... | collective-permute-start | bytes 786440 | tf_op jit(solution)/shard_map/ppermute | solution.py:389
  120.4 12.9 %collective-permute-start.30 = (bf16[512,256]{1,0:T(8,128)(2,1)S(1)}, bf16[512,256]{1,0:T(8,128)(2,1)S(1)}, u32[]{:S(2)}, u32[]{:S(2)}) collective-permute-start(bf16[512,256]{1,0:T(8,128)(2,1)S(1)} %get-tuple-element.42), channel_id=1, source_target_pairs={{0,3},{3,0},{4,7},{7,4},{8,11},{11,8},{12,15},{15,12},{16,19},{19,... | collective-permute-start | bytes 786440 | tf_op jit(solution)/shard_map/ppermute | solution.py:393
  127.9 9.9 %collective-permute-start.29 = (bf16[512,256]{1,0:T(8,128)(2,1)S(1)}, bf16[512,256]{1,0:T(8,128)(2,1)S(1)}, u32[]{:S(2)}, u32[]{:S(2)}) collective-permute-start(bf16[512,256]{1,0:T(8,128)(2,1)S(1)} %terms.18), channel_id=1, source_target_pairs={{0,1},{1,0},{2,3},{3,2},{4,5},{5,4},{6,7},{7,6},{8,9},{9,8},{10,11... | collective-permute-start | bytes 786440 | tf_op jit(solution)/shard_map/ppermute | solution.py:364
  128.0 9.8 %collective-permute-start.31 = (bf16[512,256]{1,0:T(8,128)(2,1)S(1)}, bf16[512,256]{1,0:T(8,128)(2,1)S(1)}, u32[]{:S(2)}, u32[]{:S(2)}) collective-permute-start(bf16[512,256]{1,0:T(8,128)(2,1)S(1)} %sum.4), channel_id=1, source_target_pairs={{1,2},{2,1},{5,6},{6,5},{9,10},{10,9},{13,14},{14,13},{17,18},{18,... | collective-permute-start | bytes 786440 | tf_op jit(solution)/shard_map/ppermute | solution.py:394
  138.6 8.2 %collective-permute-start.33 = (bf16[512,256]{1,0:T(8,128)(2,1)S(1)}, bf16[512,256]{1,0:T(8,128)(2,1)S(1)}, u32[]{:S(2)}, u32[]{:S(2)}) collective-permute-start(bf16[512,256]{1,0:T(8,128)(2,1)S(1)} %update.4.refs_0_), channel_id=1, source_target_pairs={{0,8},{4,12},{8,0},{12,4},{16,24},{20,28},{24,16},{28,20},{1,9},{5... | collective-permute-start | bytes 786440 | tf_op jit(solution)/shard_map/ppermute | solution.py:364
  139.8 7.8 %collective-permute-start.35 = (bf16[512,256]{1,0:T(8,128)(2,1)S(1)}, bf16[512,256]{1,0:T(8,128)(2,1)S(1)}, u32[]{:S(2)}, u32[]{:S(2)}) collective-permute-start(bf16[512,256]{1,0:T(8,128)(2,1)S(1)} %update.4.refs_0_), channel_id=1, source_target_pairs={{0,16},{4,20},{8,24},{12,28},{16,0},{20,4},{24,8},{28,12},{1,17},{... | collective-permute-start | bytes 786440 | tf_op jit(solution)/shard_map/ppermute | solution.py:364
  148.2 6.4 %collective-permute-start.37 = (bf16[512,256]{1,0:T(8,128)(2,1)S(1)}, bf16[512,256]{1,0:T(8,128)(2,1)S(1)}, u32[]{:S(2)}, u32[]{:S(2)}) collective-permute-start(bf16[512,256]{1,0:T(8,128)(2,1)S(1)} %pick.5), channel_id=1, source_target_pairs={{0,16},{4,12},{8,24},{12,4},{16,0},{20,28},{24,8},{28,20},{1,17},{... | collective-permute-start | bytes 786440 | tf_op jit(solution)/shard_map/ppermute | solution.py:378
  149.2 5.4 %collective-permute-start.32 = (bf16[512,256]{1,0:T(8,128)(2,1)S(1)}, bf16[512,256]{1,0:T(8,128)(2,1)S(1)}, u32[]{:S(2)}, u32[]{:S(2)}) collective-permute-start(bf16[512,256]{1,0:T(8,128)(2,1)S(1)} %update.4.refs_0_), channel_id=1, source_target_pairs={{0,4},{4,0},{8,12},{12,8},{16,20},{20,16},{24,28},{28,24},{1,5},{5... | collective-permute-start | bytes 786440 | tf_op jit(solution)/shard_map/ppermute | solution.py:364
  149.2 5.4 %collective-permute-start.34 = (bf16[512,256]{1,0:T(8,128)(2,1)S(1)}, bf16[512,256]{1,0:T(8,128)(2,1)S(1)}, u32[]{:S(2)}, u32[]{:S(2)}) collective-permute-start(bf16[512,256]{1,0:T(8,128)(2,1)S(1)} %collective-permute-done.33.even_ref.refs_2_), channel_id=1, source_target_pairs={{0,4},{4,0},{8,12},{12,8},{16,20},{20,16},{24,28},{28,24},{1,5},{5... | collective-permute-start | bytes 786440 | tf_op jit(solution)/shard_map/ppermute | solution.py:364
  149.7 4.9 %collective-permute-start.36 = (bf16[512,256]{1,0:T(8,128)(2,1)S(1)}, bf16[512,256]{1,0:T(8,128)(2,1)S(1)}, u32[]{:S(2)}, u32[]{:S(2)}) collective-permute-start(bf16[512,256]{1,0:T(8,128)(2,1)S(1)} %collective-permute-done.35.odd_ref.refs_4_), channel_id=1, source_target_pairs={{0,4},{4,0},{8,12},{12,8},{16,20},{20,16},{24,28},{28,24},{1,5},{5... | collective-permute-start | bytes 786440 | tf_op jit(solution)/shard_map/ppermute | solution.py:364
  154.6 1.5 collective-permute-start.38
  159.0 10.9 %collective-permute-start.39 = (bf16[512,256]{1,0:T(8,128)(2,1)S(1)}, bf16[512,256]{1,0:T(8,128)(2,1)S(1)}, u32[]{:S(2)}, u32[]{:S(2)}) collective-permute-start(bf16[512,256]{1,0:T(8,128)(2,1)S(1)} %terms.21), channel_id=1, source_target_pairs={{0,1},{1,3},{3,2},{2,0},{4,5},{5,7},{7,6},{6,4},{8,9},{9,11},{11,1... | collective-permute-start | bytes 786440 | tf_op jit(solution)/shard_map/ppermute | solution.py:389
  162.2 12.9 %collective-permute-start.41 = (bf16[512,256]{1,0:T(8,128)(2,1)S(1)}, bf16[512,256]{1,0:T(8,128)(2,1)S(1)}, u32[]{:S(2)}, u32[]{:S(2)}) collective-permute-start(bf16[512,256]{1,0:T(8,128)(2,1)S(1)} %get-tuple-element.44), channel_id=1, source_target_pairs={{0,3},{3,0},{4,7},{7,4},{8,11},{11,8},{12,15},{15,12},{16,19},{19,... | collective-permute-start | bytes 786440 | tf_op jit(solution)/shard_map/ppermute | solution.py:393
  169.9 9.9 %collective-permute-start.40 = (bf16[512,256]{1,0:T(8,128)(2,1)S(1)}, bf16[512,256]{1,0:T(8,128)(2,1)S(1)}, u32[]{:S(2)}, u32[]{:S(2)}) collective-permute-start(bf16[512,256]{1,0:T(8,128)(2,1)S(1)} %terms.22), channel_id=1, source_target_pairs={{0,1},{1,0},{2,3},{3,2},{4,5},{5,4},{6,7},{7,6},{8,9},{9,8},{10,11... | collective-permute-start | bytes 786440 | tf_op jit(solution)/shard_map/ppermute | solution.py:364
  170.0 9.7 %collective-permute-start.42 = (bf16[512,256]{1,0:T(8,128)(2,1)S(1)}, bf16[512,256]{1,0:T(8,128)(2,1)S(1)}, u32[]{:S(2)}, u32[]{:S(2)}) collective-permute-start(bf16[512,256]{1,0:T(8,128)(2,1)S(1)} %sum.5), channel_id=1, source_target_pairs={{1,2},{2,1},{5,6},{6,5},{9,10},{10,9},{13,14},{14,13},{17,18},{18,... | collective-permute-start | bytes 786440 | tf_op jit(solution)/shard_map/ppermute | solution.py:394

commit v2 on v1

--- a/solution.py
+++ b/solution.py
@@ -44,7 +44,7 @@
     return pl.CostEstimate(flops=int(flops), bytes_accessed=int(moved), transcendentals=0)
 
 
-def streamed(steps, source, held, sems, work):
+def streamed(steps, source, held, sems, work, ready=None):
     slots = held.shape[0]
 
     def copy(step):
@@ -53,6 +53,8 @@
 
     for step in range(min(slots - 1, steps)):
         copy(step).start()
+    if ready is not None:
+        ready()
 
     @pl.loop(0, steps)
     def _(step):
@@ -65,7 +67,8 @@
 
 
 def spectra_kernel(packs, n_row, place_ref, traces_ref, table_ref, *refs):
-    out_refs, held, sems = refs[:n_row], refs[n_row], refs[n_row + 1]
+    out_refs = refs[:n_row]
+    held, sems, table, table_sem = refs[n_row:]
     block = held.shape[1]
     steps = traces_ref.shape[0] // n_row // block
 
@@ -74,14 +77,19 @@
         return traces_ref.at[pl.ds(pl.multiple_of(first, block), block)]
 
     def work(step, traces):
-        packed = spectra_of(packs, traces, table_ref)
+        packed = spectra_of(packs, traces, table)
         for turn, out_ref in enumerate(out_refs):
 
             @pl.when(step // steps == turn)
             def _():
                 out_ref[step % steps] = packed
 
-    streamed(n_row * steps, source, held, sems, work)
+    def ready():
+        copy = pltpu.make_async_copy(table_ref, table, table_sem)
+        copy.start()
+        copy.wait()
+
+    streamed(n_row * steps, source, held, sems, work, ready)
 
 
 def spectra_of(packs, traces_ref, table_ref):
@@ -112,12 +120,14 @@
 
     outs = pl.pallas_call(
         functools.partial(spectra_kernel, packs, n_row),
-        in_specs=[SMEM, ANY, VMEM],
+        in_specs=[SMEM, ANY, ANY],
         out_specs=[VMEM] * n_row,
         out_shape=[jax.ShapeDtypeStruct((steps, short, LANES), jnp.bfloat16)] * n_row,
         scratch_shapes=[
-            pltpu.VMEM((BUFFERS, block, shots, samples), jnp.bfloat16),
-            pltpu.SemaphoreType.DMA((BUFFERS,)),
+            pltpu.VMEM((2 * BUFFERS, block, shots, samples), jnp.bfloat16),
+            pltpu.SemaphoreType.DMA((2 * BUFFERS,)),
+            pltpu.VMEM(table.shape, table.dtype),
+            pltpu.SemaphoreType.DMA,
         ],
         compiler_params=params(48),
         cost_estimate=cost(2 * traces.size * LANES, 2 * traces.size),
@@ -241,35 +251,46 @@
     )(slice_data, after)
 
 
-def terms_kernel(turn, n_pieces, place_ref, real_ref, imag_ref, *refs):
-    pieces, out_refs = refs[:n_pieces], refs[n_pieces:]
+def terms_kernel(turns, numbers, begun, place_ref, real_ref, imag_ref, *refs):
+    pieces = refs[: len(numbers)]
+    partial = refs[len(numbers) : len(numbers) + begun]
+    out_refs = refs[len(numbers) + begun :]
     columns = pieces[0].shape[1]
     kept = columns // 2
     size = out_refs[0].shape[0]
-    rows = pl.ds(pl.multiple_of((place_ref[1] ^ turn) * size, size), size)
-    total = jnp.zeros((2 * size, columns), jnp.float32)
-    for number, piece in enumerate(pieces):
-        block = place_ref[0] ^ number
-        both = jnp.concatenate([real_ref[block, rows, :], imag_ref[block, rows, :]], axis=0)
-        total += jnp.dot(both, piece[...], preferred_element_type=jnp.float32)
-    by_real, by_imag = total[:size], total[size:]
-    for out_ref in out_refs:
-        out_ref[:, :kept] = (by_real[:, :kept] - by_imag[:, kept:]).astype(out_ref.dtype)
-        out_ref[:, kept:] = (by_real[:, kept:] + by_imag[:, :kept]).astype(out_ref.dtype)
-
-
-def make_terms(real_data, imag_data, pieces, place, turn, slice_rows, types):
-    depth = real_data.shape[0] * real_data.shape[2]
-    columns = pieces[0].shape[1]
-    return pl.pallas_call(
-        functools.partial(terms_kernel, turn, len(pieces)),
-        in_specs=[SMEM] + [VMEM] * (2 + len(pieces)),
-        out_specs=[VMEM] * len(types),
-        out_shape=[jax.ShapeDtypeStruct((slice_rows, columns), kind) for kind in types],
+    each = len(out_refs) // len(turns)
+    for index, turn in enumerate(turns):
+        rows = pl.ds(pl.multiple_of((place_ref[1] ^ turn) * size, size), size)
+        total = jnp.zeros((2 * size, columns), jnp.float32)
+        for number, piece in zip(numbers, pieces):
+            block = place_ref[0] ^ number
+            both = jnp.concatenate([real_ref[block, rows, :], imag_ref[block, rows, :]], axis=0)
+            total += jnp.dot(both, piece[...], preferred_element_type=jnp.float32)
+        by_real, by_imag = total[:size], total[size:]
+        real = by_real[:, :kept] - by_imag[:, kept:]
+        imag = by_real[:, kept:] + by_imag[:, :kept]
+        if begun:
+            real += partial[index][:, :kept]
+            imag += partial[index][:, kept:]
+        for out_ref in out_refs[index * each : (index + 1) * each]:
+            out_ref[:, :kept] = real.astype(out_ref.dtype)
+            out_ref[:, kept:] = imag.astype(out_ref.dtype)
+
+
+def make_terms(data, place, pieces, turns, partial, slice_rows, types):
+    real_data, imag_data = data
+    numbers = tuple(pieces)
+    offsets, columns = pieces[numbers[0]].shape
+    size = len(turns) * slice_rows * len(numbers) * offsets
+    return pl.pallas_call(
+        functools.partial(terms_kernel, turns, numbers, len(partial)),
+        in_specs=[SMEM] + [VMEM] * (2 + len(numbers) + len(partial)),
+        out_specs=[VMEM] * len(types) * len(turns),
+        out_shape=[jax.ShapeDtypeStruct((slice_rows, columns), kind) for kind in types] * len(turns),
         compiler_params=params(8),
-        cost_estimate=cost(4 * slice_rows * depth * columns, 4 * slice_rows * depth),
+        cost_estimate=cost(4 * size * columns, 4 * size),
         name="terms",
-    )(place, real_data, imag_data, *pieces)
+    )(place, real_data, imag_data, *pieces.values(), *partial)
 
 
 def add_kernel(own_ref, other_ref, out_ref):
@@ -286,30 +307,6 @@
         cost_estimate=cost(other.size, 8 * other.size),
         name="sum",
     )(own, other)
-
-
-def pick_kernel(place_ref, even_ref, odd_ref, *refs):
-    out_ref = refs[-1]
-
-    @pl.when(place_ref[0] % 2 == 0)
-    def _():
-        out_ref[...] = even_ref[...]
-
-    @pl.when(place_ref[0] % 2 == 1)
-    def _():
-        out_ref[...] = odd_ref[...]
-
-
-def make_pick(place, even, odd, after):
-    return pl.pallas_call(
-        pick_kernel,
-        in_specs=[SMEM] + [VMEM] * 2 + [ANY] * len(after),
-        out_specs=VMEM,
-        out_shape=jax.ShapeDtypeStruct(even.shape, even.dtype),
-        compiler_params=params(8),
-        cost_estimate=cost(0, 4 * even.size),
-        name="pick",
-    )(place, even, odd, *after)
 
 
 def update(place_ref, wave_ref, own_ref, others, panel_ref, folded):
@@ -364,35 +361,47 @@
     return lax.ppermute(array, axis, [(index, index ^ bits) for index in range(size)])
 
 
-def spread(array, place, after):
-    size = lax.axis_size("row")
-    pieces = {0: array}
-    turns = sorted(range(2, size, 2), key=lambda turn: (turn.bit_count(), turn))
-    for turn in turns:
-        high, low = 1 << turn.bit_length() - 1, turn & -turn
-        if high == low:
-            pieces[turn] = swap(array, "row", turn)
-            continue
-        chosen = make_pick(place, pieces[turn ^ high], pieces[turn ^ low], after)
-        pairs = [(index, index ^ (low if index % 2 else high)) for index in range(size)]
-        pieces[turn] = lax.ppermute(chosen, "row", pairs)
-    for turn in range(0, size, 2):
-        pieces[turn + 1] = swap(pieces[turn], "row", 1)
-    return [pieces[turn] for turn in range(size)]
-
-
-def exchange(make, n_src):
+def exchange(n_src, far, near, own):
     bf16, f32 = jnp.bfloat16, jnp.float32
+    half = n_src // 2
     if n_src != 4:
-        arriving = [swap(make(turn, [bf16])[0], "src", turn) for turn in range(n_src - 1, 0, -1)]
-        return make(0, [f32])[0], arriving, False
-    first = lax.ppermute(make(2, [bf16])[0], "src", [(0, 1), (1, 3), (3, 2), (2, 0)])
-    sent, kept = make(3, [bf16, f32])
-    near = make(1, [bf16])[0]
-    beside = swap(near, "src", 1)
+        arriving = [swap(far(turn, [bf16])[0], "src", turn) for turn in range(n_src - 1, half - 1, -1)]
+        arriving += [swap(near(turn, [bf16])[0], "src", turn) for turn in range(half - 1, 0, -1)]
+        return own(0, [f32])[0], arriving, False
+    first = lax.ppermute(far(2, [bf16])[0], "src", [(0, 1), (1, 3), (3, 2), (2, 0)])
+    sent, kept = far(3, [bf16, f32])
+    beside = near(1, [bf16])[0]
+    sent, beside = lax.optimization_barrier((sent, beside))
     outer = lax.ppermute(sent, "src", [(0, 3), (3, 0)])
-    inner = lax.ppermute(make_sum(kept, first), "src", [(1, 2), (2, 1)])
-    return make(0, [f32])[0], [first, beside, outer, inner], True
+    both = make_sum(kept, first)
+    both, beside = lax.optimization_barrier((both, beside))
+    inner = lax.ppermute(both, "src", [(1, 2), (2, 1)])
+    beside = swap(beside, "src", 1)
+    return own(0, [f32])[0], [first, outer, inner, beside], True
+
+
+def iterate(estimate, data, place, n_row, n_src, slice_rows):
+    f32 = jnp.float32
+    half = n_src // 2
+    direct = {turn: swap(estimate, "row", turn) for turn in range(n_row - 2, 0, -2)}
+    first = {0: estimate, 1: swap(estimate, "row", 1)}
+    turns = tuple(range(n_src - 1, -1, -1))
+    begun = make_terms(data, place, first, turns, [], slice_rows, [f32])
+    held = lax.optimization_barrier((*direct.values(), *begun))
+    direct = dict(zip(direct, held))
+    begun = dict(zip(turns, held[len(direct) :]))
+    passed = {turn + 1: swap(piece, "row", 1) for turn, piece in direct.items()}
+    turns = tuple(range(n_src - 1, half - 1, -1))
+    sums = make_terms(data, place, direct, turns, [begun[turn] for turn in turns], slice_rows, [f32])
+    later = dict(zip(turns, sums))
+
+    def far(turn, types):
+        return make_terms(data, place, passed, (turn,), [later[turn]], slice_rows, types)
+
+    def near(turn, types):
+        return make_terms(data, place, {**direct, **passed}, (turn,), [begun[turn]], slice_rows, types)
+
+    return exchange(n_src, far, near, near)
 
 
 def body(traces, row_source, slice_data, wavelet_inverse):
@@ -403,7 +412,7 @@
     packs = LANES // (2 * shots)
     group_rows = block_rows // n_row
     slice_rows = block_rows // n_src
-    block = min(group_rows, 128)
+    block = min(group_rows, 64)
     short = block // packs
 
     spectra = make_spectra(traces, place, n_row, packs, block)
@@ -413,19 +422,15 @@
     position = (row_source // block_rows ^ row) * (group_rows // packs) + inside // block * short + inside % short
     code = position * packs + inside % block // short
     code = jnp.broadcast_to(code[:, None], (block_rows, LANES))
-    real_data, real_token = relay(slice_data, 0, spectra[0])
+    real_data, _ = relay(slice_data, 0, spectra[0])
     ordered = make_order(code, arrived, place, n_src, packs)
     located = [ordered[0]] + [swap(ordered[turn], "src", turn) for turn in range(1, n_src)]
     imag_data, token = relay(slice_data, 1, ordered[0])
     panel = make_panel(located, place, packs, token)
 
-    estimate, after = panel, [real_token]
+    estimate = panel
     for iteration in range(ITERS):
-        pieces = spread(estimate, place, after)
-        after = []
-        own, arriving, folded = exchange(
-            lambda turn, types: make_terms(real_data, imag_data, pieces, place, turn, slice_rows, types), n_src
-        )
+        own, arriving, folded = iterate(estimate, (real_data, imag_data), place, n_row, n_src, slice_rows)
         estimate = make_update(place, wavelet_inverse, own, arriving, panel, folded, iteration == ITERS - 1)
     return tuple(estimate)
 

time: 182 us -> 187 us (1.027)
  waiting for transfers between devices: 54.8 us -> 43 us
  starting transfers between devices: 41.6 us -> 52.2 us
  Pallas kernels: 83 us -> 89.1 us
    ppermute x31 -> x34, starting transfers between devices: 20.2 us -> 33.6 us  [swap(): lax.ppermute(array, axis, [(index, index ^ bits) for index in range(size)])]
    ppermute x9 -> x6, waiting for transfers between devices: 14.2 us -> 1.12 us  [the longest x3 1.11 us: exchange(): lax.ppermute(far(2, [bf16])[0], 'src', [(0, 1), (1, 3), (3, 2), (2, 0)])]
    pallas_call x1, Pallas kernels: 23.8 us -> 26.9 us  [make_spectra(): pl.pallas_call(functools.partial(spectra_kernel, packs, n_row), in_specs=...]
    pallas_call x15 -> x18, Pallas kernels: 36.1 us -> 38.8 us  [make_terms(): pl.pallas_call(functools.partial(terms_kernel, turns, numbers, len(partia...]
    ppermute x9 -> x6, starting transfers between devices: 7.18 us -> 5.27 us  [the longest x3 3.06 us: exchange(): lax.ppermute(far(2, [bf16])[0], 'src', [(0, 1), (1, 3), (3, 2), (2, 0)])]
    ppermute x31 -> x34, waiting for transfers between devices: 36.1 us -> 36.2 us  [swap(): lax.ppermute(array, axis, [(index, index ^ bits) for index in range(size)])]
  transfers between devices with their start and end apart: 43 -> 43, of which waited for: 19 -> 17; matrix products, arithmetic and copies ran while one was open for 0% -> 0% of each run, Pallas kernels for 23% -> 27%
where the time goes in v2:
time: 187 us
  Pallas kernels  89.1 us (48%)
  starting transfers between devices  52.2 us (28%)
  waiting for transfers between devices  43 us (23%)
    pallas_call x18, Pallas kernels, make_terms(): pl.pallas_call(functools.partial(terms_kernel, turns, numbers, len(partia...  38.8 us
    ppermute x34, waiting for transfers between devices, swap(): lax.ppermute(array, axis, [(index, index ^ bits) for index in range(size)])  36.2 us
    ppermute x34, starting transfers between devices, swap(): lax.ppermute(array, axis, [(index, index ^ bits) for index in range(size)])  33.6 us
    pallas_call x1, Pallas kernels, make_spectra(): pl.pallas_call(functools.partial(spectra_kernel, packs, n_row), in_specs=...  26.9 us
    pallas_call x2, Pallas kernels, relay(): pl.pallas_call(functools.partial(relay_kernel, part), in_specs=[ANY, ANY]...  15.7 us
    ppermute x3, starting transfers between devices, exchange(): outer = lax.ppermute(sent, 'src', [(0, 3), (3, 0)])  13.3 us
    ppermute x3, waiting for transfers between devices, exchange(): outer = lax.ppermute(sent, 'src', [(0, 3), (3, 0)])  5.74 us
    pallas_call x3, Pallas kernels, make_update(): pl.pallas_call(functools.partial(last_kernel if last else estimate_kernel...  3.78 us
  transfers between devices with their start and end apart: 43, of which 17 were waited for; matrix products, arithmetic and copies ran while one was open for 0% of the time, Pallas kernels for 27%

profile of v2, /device:TPU:0, one launch (start us, length us, event | category | flops | bytes accessed | tf_op | source)
XLA Modules:
  0.0 186.8 jit_solution(7172268330354301974)
XLA Ops:
  1.8 26.9 %spectra.1 = (bf16[4,32,128]{2,1,0:T(8,128)(2,1)S(1)}, bf16[4,32,128]{2,1,0:T(8,128)(2,1)S(1)}, bf16[4,32,128]{2,1,0:T(8,128)(2,1)S(1)}, bf16[4,32,128]{2,1,0:T(...) custom-call(s32[2]{0:T(128)S(1)} %pad_add_fusion.place_ref, ...), custom_call_target="tpu_custom_call" | custom-call | flops 8589934592 | bytes 67108864 | tf_op jit(solution)/shard_map/spectra/pallas_call | solution.py:121
  29.2 2.6 %collective-permute-start.1 = (bf16[128,128]{1,0:T(8,128)(2,1)S(1)}, bf16[128,128]{1,0:T(8,128)(2,1)S(1)}, u32[]{:S(2)}, u32[]{:S(2)}) collective-permute-start(bf16[128,128]{1,0:T(8,128)(2,1)S(1)} %bitcast.17), channel_id=1, source_target_pairs={{0,8},{4,12},{8,0},{12,4},{16,24},{20,28},{24,16},{28,20},{1,9},{5... | collective-permute-start | bytes 98312 | tf_op jit(solution)/shard_map/ppermute | solution.py:361
  31.8 1.8 collective-permute-start.3
  33.6 2.6 %collective-permute-start.5 = (bf16[128,128]{1,0:T(8,128)(2,1)S(1)}, bf16[128,128]{1,0:T(8,128)(2,1)S(1)}, u32[]{:S(2)}, u32[]{:S(2)}) collective-permute-start(bf16[128,128]{1,0:T(8,128)(2,1)S(1)} %bitcast.13), channel_id=1, source_target_pairs={{0,24},{4,28},{8,16},{12,20},{16,8},{20,12},{24,0},{28,4},{1,25},{... | collective-permute-start | bytes 98312 | tf_op jit(solution)/shard_map/ppermute | solution.py:361
  38.4 2.0 %collective-permute-done.6.refs_7_ = bf16[128,128]{1,0:T(8,128)(2,1)S(1)} collective-permute-done((bf16[128,128]{1,0:T(8,128)(2,1)S(1)}, bf16[128,128]{1,0:T(8,128)(2,1)S(1)}, u32[]{:S(2)}, u32[]{:S(2)}) %collective-permute-start.6) | collective-permute-done | bytes 32800 | tf_op jit(solution)/shard_map/ppermute | solution.py:361
  40.8 2.8 %order.1 = (bf16[256,128]{1,0:T(8,128)(2,1)S(1)}, bf16[256,128]{1,0:T(8,128)(2,1)S(1)}, bf16[256,128]{1,0:T(8,128)(2,1)S(1)}, bf16[256,128]{1,0:T(8,128)(2,1)S(1)}) custom-call(s32[2]{0:T(128)S(1)} %pad_add_fusion.place_ref, s32[2048,128]{1,0:T(8,128)S(1)} %broadcast_in_dim.2.code_ref, bf16[128,128]{1,0:T(8,128)(2,1)S(1)} %bitcast.10, ...), custom_call_target="tpu_custom_call" | custom-call | flops 1073741824 | bytes 1048576 | tf_op jit(solution)/shard_map/order/pallas_call | solution.py:173
  43.6 1.6 collective-permute-start.7
  45.2 2.6 %collective-permute-start.8 = (bf16[256,128]{1,0:T(8,128)(2,1)S(1)}, bf16[256,128]{1,0:T(8,128)(2,1)S(1)}, u32[]{:S(2)}, u32[]{:S(2)}) collective-permute-start(bf16[256,128]{1,0:T(8,128)(2,1)S(1)} %get-tuple-element.86), channel_id=1, source_target_pairs={{0,2},{1,3},{2,0},{3,1},{4,6},{5,7},{6,4},{7,5},{8,10},{9,11},{10,... | collective-permute-start | bytes 196616 | tf_op jit(solution)/shard_map/ppermute | solution.py:361
  48.1 7.7 %relay.3 = (bf16[8,2048,512]{2,1,0:T(8,128)(2,1)S(1)}, f32[8,128]{1,0:T(8,128)S(1)}) custom-call(bf16[2,2048,8,512]{3,2,1,0:T(8,128)(2,1)} %data_ref.3, bf16[256,128]{1,0:T(8,128)(2,1)S(1)} %get-tuple-element.83.after_ref.refs_0_), custom_call_target="tpu_custom_call" | custom-call | bytes 33554432 | tf_op jit(solution)/shard_map/relay/pallas_call | solution.py:236
  58.5 1.9 collective-permute-start.10
  60.4 8.0 %relay.2 = (bf16[8,2048,512]{2,1,0:T(8,128)(2,1)S(1)}, f32[8,128]{1,0:T(8,128)}) custom-call(bf16[2,2048,8,512]{3,2,1,0:T(8,128)(2,1)} %data_ref.3, bf16[128,128]{1,0:T(8,128)(2,1)S(1)} %bitcast.11), custom_call_target="tpu_custom_call" | custom-call | bytes 33554432 | tf_op jit(solution)/shard_map/relay/pallas_call | solution.py:236
  68.4 2.9 %terms.18 = (f32[512,256]{1,0:T(8,128)S(1)}, f32[512,256]{1,0:T(8,128)S(1)}, f32[512,256]{1,0:T(8,128)S(1)}, f32[512,256]{1,0:T(8,128)S(1)}) custom-call(s32[2]{0:T(128)S(1)} %pad_add_fusion.place_ref, bf16[8,2048,512]{2,1,0:T(8,128)(2,1)S(1)} %get-tuple-element.75.real_ref, bf16[8,2048,512]{2,1,0:T(8,128)(2,1)S(1)} %get-tuple-element.84.imag_ref, ...), custom_call_target="tpu_custom_call" | custom-call | flops 2147483648 | bytes 8388608 | tf_op jit(solution)/shard_map/terms/pallas_call | solution.py:285
  72.0 2.3 %terms.20 = (f32[512,256]{1,0:T(8,128)S(1)}, f32[512,256]{1,0:T(8,128)S(1)}) custom-call(s32[2]{0:T(128)S(1)} %pad_add_fusion.place_ref, bf16[8,2048,512]{2,1,0:T(8,128)(2,1)S(1)} %get-tuple-element.75.real_ref, bf16[8,2048,512]{2,1,0:T(8,128)(2,1)S(1)} %get-tuple-element.84.imag_ref, bf16[512,256]{1,0:T(8,128)(2,1)S(1)} %collective-permute-done.10.refs_0_, ...), custom_call_target="tpu_custom_call" | custom-call | flops 1610612736 | bytes 6291456 | tf_op jit(solution)/shard_map/terms/pallas_call | solution.py:285
  74.3 1.5 terms.21
  76.6 1.5 terms.22
  78.2 2.4 %terms.23 = bf16[512,256]{1,0:T(8,128)(2,1)S(1)} custom-call(s32[2]{0:T(128)S(1)} %pad_add_fusion.place_ref, bf16[8,2048,512]{2,1,0:T(8,128)(2,1)S(1)} %get-tuple-element.75.real_ref, bf16[8,2048,512]{2,1,0:T(8,128)(2,1)S(1)} %get-tuple-element.84.imag_ref, bf16[512,256]{1,0:T(8,128)(2,1)S(1)} %collective-permute-done.10.refs_0_, ...), custom_call_target="tpu_custom_call" | custom-call | flops 1610612736 | bytes 6291456 | tf_op jit(solution)/shard_map/terms/pallas_call | solution.py:285
  80.5 4.8 %collective-permute-start.18 = (bf16[512,256]{1,0:T(8,128)(2,1)S(1)}, bf16[512,256]{1,0:T(8,128)(2,1)S(1)}, u32[]{:S(2)}, u32[]{:S(2)}) collective-permute-start(bf16[512,256]{1,0:T(8,128)(2,1)S(1)} %get-tuple-element.103), channel_id=1, source_target_pairs={{0,3},{3,0},{4,7},{7,4},{8,11},{11,8},{12,15},{15,12},{16,19},{19,... | collective-permute-start | bytes 786440 | tf_op jit(solution)/shard_map/ppermute | solution.py:375
  86.4 3.4 %collective-permute-start.20 = (bf16[512,256]{1,0:T(8,128)(2,1)S(1)}, bf16[512,256]{1,0:T(8,128)(2,1)S(1)}, u32[]{:S(2)}, u32[]{:S(2)}) collective-permute-start(bf16[512,256]{1,0:T(8,128)(2,1)S(1)} %terms.23), channel_id=1, source_target_pairs={{0,1},{1,0},{2,3},{3,2},{4,5},{5,4},{6,7},{7,6},{8,9},{9,8},{10,11... | collective-permute-start | bytes 786440 | tf_op jit(solution)/shard_map/ppermute | solution.py:361
  89.8 2.3 %terms.19.own_ref = f32[512,256]{1,0:T(8,128)S(1)} custom-call(s32[2]{0:T(128)S(1)} %pad_add_fusion.place_ref, bf16[8,2048,512]{2,1,0:T(8,128)(2,1)S(1)} %get-tuple-element.75.real_ref, bf16[8,2048,512]{2,1,0:T(8,128)(2,1)S(1)} %get-tuple-element.84.imag_ref, bf16[512,256]{1,0:T(8,128)(2,1)S(1)} %collective-permute-done.10.refs_0_, ...), custom_call_target="tpu_custom_call" | custom-call | flops 1610612736 | bytes 6291456 | tf_op jit(solution)/shard_map/terms/pallas_call | solution.py:285
  93.4 4.9 %collective-permute-done.20.refs_3_ = bf16[512,256]{1,0:T(8,128)(2,1)S(1)} collective-permute-done((bf16[512,256]{1,0:T(8,128)(2,1)S(1)}, bf16[512,256]{1,0:T(8,128)(2,1)S(1)}, u32[]{:S(2)}, u32[]{:S(2)}) %collective-permute-start.20) | collective-permute-done | bytes 262176 | tf_op jit(solution)/shard_map/ppermute | solution.py:361
  99.2 1.6 collective-permute-start.23
  101.2 1.5 collective-permute-start.21
  102.7 2.9 %terms.24 = (f32[512,256]{1,0:T(8,128)S(1)}, f32[512,256]{1,0:T(8,128)S(1)}, f32[512,256]{1,0:T(8,128)S(1)}, f32[512,256]{1,0:T(8,128)S(1)}) custom-call(s32[2]{0:T(128)S(1)} %pad_add_fusion.place_ref, bf16[8,2048,512]{2,1,0:T(8,128)(2,1)S(1)} %get-tuple-element.75.real_ref, bf16[8,2048,512]{2,1,0:T(8,128)(2,1)S(1)} %get-tuple-element.84.imag_ref, ...), custom_call_target="tpu_custom_call" | custom-call | flops 2147483648 | bytes 8388608 | tf_op jit(solution)/shard_map/terms/pallas_call | solution.py:285
  105.6 2.7 %collective-permute-done.23.refs_2_ = bf16[512,256]{1,0:T(8,128)(2,1)S(1)} collective-permute-done((bf16[512,256]{1,0:T(8,128)(2,1)S(1)}, bf16[512,256]{1,0:T(8,128)(2,1)S(1)}, u32[]{:S(2)}, u32[]{:S(2)}) %collective-permute-start.23) | collective-permute-done | bytes 262176 | tf_op jit(solution)/shard_map/ppermute | solution.py:361
  108.3 6.4 %collective-permute-done.22.refs_1_ = bf16[512,256]{1,0:T(8,128)(2,1)S(1)} collective-permute-done((bf16[512,256]{1,0:T(8,128)(2,1)S(1)}, bf16[512,256]{1,0:T(8,128)(2,1)S(1)}, u32[]{:S(2)}, u32[]{:S(2)}) %collective-permute-start.22) | collective-permute-done | bytes 262176 | tf_op jit(solution)/shard_map/ppermute | solution.py:361
  115.2 2.3 %terms.26 = (f32[512,256]{1,0:T(8,128)S(1)}, f32[512,256]{1,0:T(8,128)S(1)}) custom-call(s32[2]{0:T(128)S(1)} %pad_add_fusion.place_ref, bf16[8,2048,512]{2,1,0:T(8,128)(2,1)S(1)} %get-tuple-element.75.real_ref, bf16[8,2048,512]{2,1,0:T(8,128)(2,1)S(1)} %get-tuple-element.84.imag_ref, bf16[512,256]{1,0:T(8,128)(2,1)S(1)} %collective-permute-done.21.refs_0_, ...), custom_call_target="tpu_custom_call" | custom-call | flops 1610612736 | bytes 6291456 | tf_op jit(solution)/shard_map/terms/pallas_call | solution.py:285
  117.6 1.5 terms.27
  120.6 1.5 terms.28
  122.2 2.3 %terms.29 = bf16[512,256]{1,0:T(8,128)(2,1)S(1)} custom-call(s32[2]{0:T(128)S(1)} %pad_add_fusion.place_ref, bf16[8,2048,512]{2,1,0:T(8,128)(2,1)S(1)} %get-tuple-element.75.real_ref, bf16[8,2048,512]{2,1,0:T(8,128)(2,1)S(1)} %get-tuple-element.84.imag_ref, bf16[512,256]{1,0:T(8,128)(2,1)S(1)} %collective-permute-done.21.refs_0_, ...), custom_call_target="tpu_custom_call" | custom-call | flops 1610612736 | bytes 6291456 | tf_op jit(solution)/shard_map/terms/pallas_call | solution.py:285
  124.5 4.2 %collective-permute-start.29 = (bf16[512,256]{1,0:T(8,128)(2,1)S(1)}, bf16[512,256]{1,0:T(8,128)(2,1)S(1)}, u32[]{:S(2)}, u32[]{:S(2)}) collective-permute-start(bf16[512,256]{1,0:T(8,128)(2,1)S(1)} %get-tuple-element.122), channel_id=1, source_target_pairs={{0,3},{3,0},{4,7},{7,4},{8,11},{11,8},{12,15},{15,12},{16,19},{19,... | collective-permute-start | bytes 786440 | tf_op jit(solution)/shard_map/ppermute | solution.py:375
  129.6 3.2 %collective-permute-start.31 = (bf16[512,256]{1,0:T(8,128)(2,1)S(1)}, bf16[512,256]{1,0:T(8,128)(2,1)S(1)}, u32[]{:S(2)}, u32[]{:S(2)}) collective-permute-start(bf16[512,256]{1,0:T(8,128)(2,1)S(1)} %terms.29), channel_id=1, source_target_pairs={{0,1},{1,0},{2,3},{3,2},{4,5},{5,4},{6,7},{7,6},{8,9},{9,8},{10,11... | collective-permute-start | bytes 786440 | tf_op jit(solution)/shard_map/ppermute | solution.py:361
  132.8 2.3 %terms.25.own_ref = f32[512,256]{1,0:T(8,128)S(1)} custom-call(s32[2]{0:T(128)S(1)} %pad_add_fusion.place_ref, bf16[8,2048,512]{2,1,0:T(8,128)(2,1)S(1)} %get-tuple-element.75.real_ref, bf16[8,2048,512]{2,1,0:T(8,128)(2,1)S(1)} %get-tuple-element.84.imag_ref, bf16[512,256]{1,0:T(8,128)(2,1)S(1)} %collective-permute-done.21.refs_0_, ...), custom_call_target="tpu_custom_call" | custom-call | flops 1610612736 | bytes 6291456 | tf_op jit(solution)/shard_map/terms/pallas_call | solution.py:285
  135.1 2.3 %collective-permute-done.29.refs_1_ = bf16[512,256]{1,0:T(8,128)(2,1)S(1)} collective-permute-done((bf16[512,256]{1,0:T(8,128)(2,1)S(1)}, bf16[512,256]{1,0:T(8,128)(2,1)S(1)}, u32[]{:S(2)}, u32[]{:S(2)}) %collective-permute-start.29) | collective-permute-done | bytes 262176 | tf_op jit(solution)/shard_map/ppermute | solution.py:375
  137.4 4.9 %collective-permute-done.31.refs_3_ = bf16[512,256]{1,0:T(8,128)(2,1)S(1)} collective-permute-done((bf16[512,256]{1,0:T(8,128)(2,1)S(1)}, bf16[512,256]{1,0:T(8,128)(2,1)S(1)}, u32[]{:S(2)}, u32[]{:S(2)}) %collective-permute-start.31) | collective-permute-done | bytes 262176 | tf_op jit(solution)/shard_map/ppermute | solution.py:361
  145.0 1.7 collective-permute-start.32
  146.7 2.9 %terms.30 = (f32[512,256]{1,0:T(8,128)S(1)}, f32[512,256]{1,0:T(8,128)S(1)}, f32[512,256]{1,0:T(8,128)S(1)}, f32[512,256]{1,0:T(8,128)S(1)}) custom-call(s32[2]{0:T(128)S(1)} %pad_add_fusion.place_ref, bf16[8,2048,512]{2,1,0:T(8,128)(2,1)S(1)} %get-tuple-element.75.real_ref, bf16[8,2048,512]{2,1,0:T(8,128)(2,1)S(1)} %get-tuple-element.84.imag_ref, ...), custom_call_target="tpu_custom_call" | custom-call | flops 2147483648 | bytes 8388608 | tf_op jit(solution)/shard_map/terms/pallas_call | solution.py:285
  149.6 2.7 %collective-permute-done.34.refs_2_ = bf16[512,256]{1,0:T(8,128)(2,1)S(1)} collective-permute-done((bf16[512,256]{1,0:T(8,128)(2,1)S(1)}, bf16[512,256]{1,0:T(8,128)(2,1)S(1)}, u32[]{:S(2)}, u32[]{:S(2)}) %collective-permute-start.34) | collective-permute-done | bytes 262176 | tf_op jit(solution)/shard_map/ppermute | solution.py:361
  152.3 5.4 %collective-permute-done.33.refs_1_ = bf16[512,256]{1,0:T(8,128)(2,1)S(1)} collective-permute-done((bf16[512,256]{1,0:T(8,128)(2,1)S(1)}, bf16[512,256]{1,0:T(8,128)(2,1)S(1)}, u32[]{:S(2)}, u32[]{:S(2)}) %collective-permute-start.33) | collective-permute-done | bytes 262176 | tf_op jit(solution)/shard_map/ppermute | solution.py:361
  158.3 2.3 %terms.32 = (f32[512,256]{1,0:T(8,128)S(1)}, f32[512,256]{1,0:T(8,128)S(1)}) custom-call(s32[2]{0:T(128)S(1)} %pad_add_fusion.place_ref, bf16[8,2048,512]{2,1,0:T(8,128)(2,1)S(1)} %get-tuple-element.75.real_ref, bf16[8,2048,512]{2,1,0:T(8,128)(2,1)S(1)} %get-tuple-element.84.imag_ref, bf16[512,256]{1,0:T(8,128)(2,1)S(1)} %collective-permute-done.32.refs_0_, ...), custom_call_target="tpu_custom_call" | custom-call | flops 1610612736 | bytes 6291456 | tf_op jit(solution)/shard_map/terms/pallas_call | solution.py:285
  160.7 1.5 terms.33
  163.0 1.5 terms.34
  164.6 2.3 %terms.35 = bf16[512,256]{1,0:T(8,128)(2,1)S(1)} custom-call(s32[2]{0:T(128)S(1)} %pad_add_fusion.place_ref, bf16[8,2048,512]{2,1,0:T(8,128)(2,1)S(1)} %get-tuple-element.75.real_ref, bf16[8,2048,512]{2,1,0:T(8,128)(2,1)S(1)} %get-tuple-element.84.imag_ref, bf16[512,256]{1,0:T(8,128)(2,1)S(1)} %collective-permute-done.32.refs_0_, ...), custom_call_target="tpu_custom_call" | custom-call | flops 1610612736 | bytes 6291456 | tf_op jit(solution)/shard_map/terms/pallas_call | solution.py:285
  166.9 4.2 %collective-permute-start.40 = (bf16[512,256]{1,0:T(8,128)(2,1)S(1)}, bf16[512,256]{1,0:T(8,128)(2,1)S(1)}, u32[]{:S(2)}, u32[]{:S(2)}) collective-permute-start(bf16[512,256]{1,0:T(8,128)(2,1)S(1)} %get-tuple-element.141), channel_id=1, source_target_pairs={{0,3},{3,0},{4,7},{7,4},{8,11},{11,8},{12,15},{15,12},{16,19},{19,... | collective-permute-start | bytes 786440 | tf_op jit(solution)/shard_map/ppermute | solution.py:375
  172.8 2.4 %collective-permute-start.42 = (bf16[512,256]{1,0:T(8,128)(2,1)S(1)}, bf16[512,256]{1,0:T(8,128)(2,1)S(1)}, u32[]{:S(2)}, u32[]{:S(2)}) collective-permute-start(bf16[512,256]{1,0:T(8,128)(2,1)S(1)} %terms.35), channel_id=1, source_target_pairs={{0,1},{1,0},{2,3},{3,2},{4,5},{5,4},{6,7},{7,6},{8,9},{9,8},{10,11... | collective-permute-start | bytes 786440 | tf_op jit(solution)/shard_map/ppermute | solution.py:361
  175.2 2.3 %terms.31.own_ref = f32[512,256]{1,0:T(8,128)S(1)} custom-call(s32[2]{0:T(128)S(1)} %pad_add_fusion.place_ref, bf16[8,2048,512]{2,1,0:T(8,128)(2,1)S(1)} %get-tuple-element.75.real_ref, bf16[8,2048,512]{2,1,0:T(8,128)(2,1)S(1)} %get-tuple-element.84.imag_ref, bf16[512,256]{1,0:T(8,128)(2,1)S(1)} %collective-permute-done.32.refs_0_, ...), custom_call_target="tpu_custom_call" | custom-call | flops 1610612736 | bytes 6291456 | tf_op jit(solution)/shard_map/terms/pallas_call | solution.py:285
  177.6 2.3 %collective-permute-done.40.refs_1_ = bf16[512,256]{1,0:T(8,128)(2,1)S(1)} collective-permute-done((bf16[512,256]{1,0:T(8,128)(2,1)S(1)}, bf16[512,256]{1,0:T(8,128)(2,1)S(1)}, u32[]{:S(2)}, u32[]{:S(2)}) %collective-permute-start.40) | collective-permute-done | bytes 262176 | tf_op jit(solution)/shard_map/ppermute | solution.py:375
  179.8 4.9 %collective-permute-done.42.refs_3_ = bf16[512,256]{1,0:T(8,128)(2,1)S(1)} collective-permute-done((bf16[512,256]{1,0:T(8,128)(2,1)S(1)}, bf16[512,256]{1,0:T(8,128)(2,1)S(1)}, u32[]{:S(2)}, u32[]{:S(2)}) %collective-permute-start.42) | collective-permute-done | bytes 262176 | tf_op jit(solution)/shard_map/ppermute | solution.py:361
  184.7 2.1 %update.5 = (f32[512,2,128]{2,1,0:T(2,128)}, f32[512,2,128]{2,1,0:T(2,128)}) custom-call(s32[2]{0:T(128)S(1)} %pad_add_fusion.place_ref, f32[2]{0:T(128)S(1)} %copy-done.1, f32[512,256]{1,0:T(8,128)S(1)} %terms.31.own_ref, bf16[512,256]{1,0:T(8,128)(2,1)S(1)} %collective-permute-done.39.other_ref.refs_0_, ...), custom_call_target="tpu_custom_call" | custom-call | flops 2097152 | bytes 2097152 | tf_op jit(solution)/shard_map/update/pallas_call | solution.py:348
  (76 shorter events, 20.8 us)
Async XLA Ops:
  0.7 1.0 copy-start
  1.8 34.6 %copy-start.2 = (s32[2048]{0:T(1024)S(1)}, s32[2048]{0:T(1024)}, u32[]{:S(2)}) copy-start(s32[2048]{0:T(1024)} %param.6) | copy-start | bytes 24580
  28.7 4.9 %collective-permute-start = (bf16[128,128]{1,0:T(8,128)(2,1)S(1)}, bf16[128,128]{1,0:T(8,128)(2,1)S(1)}, u32[]{:S(2)}, u32[]{:S(2)}) collective-permute-start(bf16[128,128]{1,0:T(8,128)(2,1)S(1)} %bitcast.18), channel_id=1, source_target_pairs={{0,4},{4,0},{8,12},{12,8},{16,20},{20,16},{24,28},{28,24},{1,5},{5... | collective-permute-start | bytes 98312 | tf_op jit(solution)/shard_map/ppermute | solution.py:361
  29.2 7.0 %collective-permute-start.1 = (bf16[128,128]{1,0:T(8,128)(2,1)S(1)}, bf16[128,128]{1,0:T(8,128)(2,1)S(1)}, u32[]{:S(2)}, u32[]{:S(2)}) collective-permute-start(bf16[128,128]{1,0:T(8,128)(2,1)S(1)} %bitcast.17), channel_id=1, source_target_pairs={{0,8},{4,12},{8,0},{12,4},{16,24},{20,28},{24,16},{28,20},{1,9},{5... | collective-permute-start | bytes 98312 | tf_op jit(solution)/shard_map/ppermute | solution.py:361
  31.8 4.6 %collective-permute-start.2 = (bf16[128,128]{1,0:T(8,128)(2,1)S(1)}, bf16[128,128]{1,0:T(8,128)(2,1)S(1)}, u32[]{:S(2)}, u32[]{:S(2)}) collective-permute-start(bf16[128,128]{1,0:T(8,128)(2,1)S(1)} %bitcast.16), channel_id=1, source_target_pairs={{0,12},{4,8},{8,4},{12,0},{16,28},{20,24},{24,20},{28,16},{1,13},{... | collective-permute-start | bytes 98312 | tf_op jit(solution)/shard_map/ppermute | solution.py:361
  31.8 4.6 %collective-permute-start.3 = (bf16[128,128]{1,0:T(8,128)(2,1)S(1)}, bf16[128,128]{1,0:T(8,128)(2,1)S(1)}, u32[]{:S(2)}, u32[]{:S(2)}) collective-permute-start(bf16[128,128]{1,0:T(8,128)(2,1)S(1)} %bitcast.15), channel_id=1, source_target_pairs={{0,16},{4,20},{8,24},{12,28},{16,0},{20,4},{24,8},{28,12},{1,17},{... | collective-permute-start | bytes 98312 | tf_op jit(solution)/shard_map/ppermute | solution.py:361
  33.6 3.5 %collective-permute-start.4 = (bf16[128,128]{1,0:T(8,128)(2,1)S(1)}, bf16[128,128]{1,0:T(8,128)(2,1)S(1)}, u32[]{:S(2)}, u32[]{:S(2)}) collective-permute-start(bf16[128,128]{1,0:T(8,128)(2,1)S(1)} %bitcast.14), channel_id=1, source_target_pairs={{0,20},{4,16},{8,28},{12,24},{16,4},{20,0},{24,12},{28,8},{1,21},{... | collective-permute-start | bytes 98312 | tf_op jit(solution)/shard_map/ppermute | solution.py:361
  33.6 4.8 %collective-permute-start.5 = (bf16[128,128]{1,0:T(8,128)(2,1)S(1)}, bf16[128,128]{1,0:T(8,128)(2,1)S(1)}, u32[]{:S(2)}, u32[]{:S(2)}) collective-permute-start(bf16[128,128]{1,0:T(8,128)(2,1)S(1)} %bitcast.13), channel_id=1, source_target_pairs={{0,24},{4,28},{8,16},{12,20},{16,8},{20,12},{24,0},{28,4},{1,25},{... | collective-permute-start | bytes 98312 | tf_op jit(solution)/shard_map/ppermute | solution.py:361
  36.2 4.2 %collective-permute-start.6 = (bf16[128,128]{1,0:T(8,128)(2,1)S(1)}, bf16[128,128]{1,0:T(8,128)(2,1)S(1)}, u32[]{:S(2)}, u32[]{:S(2)}) collective-permute-start(bf16[128,128]{1,0:T(8,128)(2,1)S(1)} %bitcast.12), channel_id=1, source_target_pairs={{0,28},{4,24},{8,20},{12,16},{16,12},{20,8},{24,4},{28,0},{1,29},{... | collective-permute-start | bytes 98312 | tf_op jit(solution)/shard_map/ppermute | solution.py:361
  43.6 12.1 %collective-permute-start.7 = (bf16[256,128]{1,0:T(8,128)(2,1)S(1)}, bf16[256,128]{1,0:T(8,128)(2,1)S(1)}, u32[]{:S(2)}, u32[]{:S(2)}) collective-permute-start(bf16[256,128]{1,0:T(8,128)(2,1)S(1)} %get-tuple-element.85), channel_id=1, source_target_pairs={{0,1},{1,0},{2,3},{3,2},{4,5},{5,4},{6,7},{7,6},{8,9},{9,8},{10,11... | collective-permute-start | bytes 196616 | tf_op jit(solution)/shard_map/ppermute | solution.py:361
  45.2 10.5 %collective-permute-start.8 = (bf16[256,128]{1,0:T(8,128)(2,1)S(1)}, bf16[256,128]{1,0:T(8,128)(2,1)S(1)}, u32[]{:S(2)}, u32[]{:S(2)}) collective-permute-start(bf16[256,128]{1,0:T(8,128)(2,1)S(1)} %get-tuple-element.86), channel_id=1, source_target_pairs={{0,2},{1,3},{2,0},{3,1},{4,6},{5,7},{6,4},{7,5},{8,10},{9,11},{10,... | collective-permute-start | bytes 196616 | tf_op jit(solution)/shard_map/ppermute | solution.py:361
  47.8 7.9 %collective-permute-start.9 = (bf16[256,128]{1,0:T(8,128)(2,1)S(1)}, bf16[256,128]{1,0:T(8,128)(2,1)S(1)}, u32[]{:S(2)}, u32[]{:S(2)}) collective-permute-start(bf16[256,128]{1,0:T(8,128)(2,1)S(1)} %get-tuple-element.87), channel_id=1, source_target_pairs={{0,3},{1,2},{2,1},{3,0},{4,7},{5,6},{6,5},{7,4},{8,11},{9,10},{10,... | collective-permute-start | bytes 196616 | tf_op jit(solution)/shard_map/ppermute | solution.py:361
  56.8 11.6 %collective-permute-start.13 = (bf16[512,256]{1,0:T(8,128)(2,1)S(1)}, bf16[512,256]{1,0:T(8,128)(2,1)S(1)}, u32[]{:S(2)}, u32[]{:S(2)}) collective-permute-start(bf16[512,256]{1,0:T(8,128)(2,1)S(1)} %panel.1.refs_0_.refs_4_), channel_id=1, source_target_pairs={{0,4},{4,0},{8,12},{12,8},{16,20},{20,16},{24,28},{28,24},{1,5},{5... | collective-permute-start | bytes 786440 | tf_op jit(solution)/shard_map/ppermute | solution.py:361
  56.8 14.4 %collective-permute-start.12 = (bf16[512,256]{1,0:T(8,128)(2,1)S(1)}, bf16[512,256]{1,0:T(8,128)(2,1)S(1)}, u32[]{:S(2)}, u32[]{:S(2)}) collective-permute-start(bf16[512,256]{1,0:T(8,128)(2,1)S(1)} %panel.1.refs_0_.refs_4_), channel_id=1, source_target_pairs={{0,8},{4,12},{8,0},{12,4},{16,24},{20,28},{24,16},{28,20},{1,9},{5... | collective-permute-start | bytes 786440 | tf_op jit(solution)/shard_map/ppermute | solution.py:361
  57.4 14.0 %collective-permute-start.11 = (bf16[512,256]{1,0:T(8,128)(2,1)S(1)}, bf16[512,256]{1,0:T(8,128)(2,1)S(1)}, u32[]{:S(2)}, u32[]{:S(2)}) collective-permute-start(bf16[512,256]{1,0:T(8,128)(2,1)S(1)} %panel.1.refs_0_.refs_4_), channel_id=1, source_target_pairs={{0,16},{4,20},{8,24},{12,28},{16,0},{20,4},{24,8},{28,12},{1,17},{... | collective-permute-start | bytes 786440 | tf_op jit(solution)/shard_map/ppermute | solution.py:361
  58.5 12.9 %collective-permute-start.10 = (bf16[512,256]{1,0:T(8,128)(2,1)S(1)}, bf16[512,256]{1,0:T(8,128)(2,1)S(1)}, u32[]{:S(2)}, u32[]{:S(2)}) collective-permute-start(bf16[512,256]{1,0:T(8,128)(2,1)S(1)} %panel.1.refs_0_.refs_4_), channel_id=1, source_target_pairs={{0,24},{4,28},{8,16},{12,20},{16,8},{20,12},{24,0},{28,4},{1,25},{... | collective-permute-start | bytes 786440 | tf_op jit(solution)/shard_map/ppermute | solution.py:361
  71.4 2.9 %collective-permute-start.14 = (bf16[512,256]{1,0:T(8,128)(2,1)S(1)}, bf16[512,256]{1,0:T(8,128)(2,1)S(1)}, u32[]{:S(2)}, u32[]{:S(2)}) collective-permute-start(bf16[512,256]{1,0:T(8,128)(2,1)S(1)} %collective-permute-done.10.refs_0_), channel_id=1, source_target_pairs={{0,4},{4,0},{8,12},{12,8},{16,20},{20,16},{24,28},{28,24},{1,5},{5... | collective-permute-start | bytes 786440 | tf_op jit(solution)/shard_map/ppermute | solution.py:361
  71.4 2.9 %collective-permute-start.15 = (bf16[512,256]{1,0:T(8,128)(2,1)S(1)}, bf16[512,256]{1,0:T(8,128)(2,1)S(1)}, u32[]{:S(2)}, u32[]{:S(2)}) collective-permute-start(bf16[512,256]{1,0:T(8,128)(2,1)S(1)} %collective-permute-done.11.refs_1_), channel_id=1, source_target_pairs={{0,4},{4,0},{8,12},{12,8},{16,20},{20,16},{24,28},{28,24},{1,5},{5... | collective-permute-start | bytes 786440 | tf_op jit(solution)/shard_map/ppermute | solution.py:361
  71.9 2.4 %collective-permute-start.16 = (bf16[512,256]{1,0:T(8,128)(2,1)S(1)}, bf16[512,256]{1,0:T(8,128)(2,1)S(1)}, u32[]{:S(2)}, u32[]{:S(2)}) collective-permute-start(bf16[512,256]{1,0:T(8,128)(2,1)S(1)} %collective-permute-done.12.refs_2_), channel_id=1, source_target_pairs={{0,4},{4,0},{8,12},{12,8},{16,20},{20,16},{24,28},{28,24},{1,5},{5... | collective-permute-start | bytes 786440 | tf_op jit(solution)/shard_map/ppermute | solution.py:361
  75.9 9.6 %collective-permute-start.17 = (bf16[512,256]{1,0:T(8,128)(2,1)S(1)}, bf16[512,256]{1,0:T(8,128)(2,1)S(1)}, u32[]{:S(2)}, u32[]{:S(2)}) collective-permute-start(bf16[512,256]{1,0:T(8,128)(2,1)S(1)} %terms.21), channel_id=1, source_target_pairs={{0,1},{1,3},{3,2},{2,0},{4,5},{5,7},{7,6},{6,4},{8,9},{9,11},{11,1... | collective-permute-start | bytes 786440 | tf_op jit(solution)/shard_map/ppermute | solution.py:371
  78.1 20.1 %copy-start.1 = (f32[2]{0:T(128)S(1)}, f32[2]{0:T(128)}, u32[]{:S(2)}) copy-start(f32[2]{0:T(128)} %wave_ref.5) | copy-start | bytes 28
  80.5 12.9 %collective-permute-start.18 = (bf16[512,256]{1,0:T(8,128)(2,1)S(1)}, bf16[512,256]{1,0:T(8,128)(2,1)S(1)}, u32[]{:S(2)}, u32[]{:S(2)}) collective-permute-start(bf16[512,256]{1,0:T(8,128)(2,1)S(1)} %get-tuple-element.103), channel_id=1, source_target_pairs={{0,3},{3,0},{4,7},{7,4},{8,11},{11,8},{12,15},{15,12},{16,19},{19,... | collective-permute-start | bytes 786440 | tf_op jit(solution)/shard_map/ppermute | solution.py:375
  85.6 7.8 %collective-permute-start.19 = (bf16[512,256]{1,0:T(8,128)(2,1)S(1)}, bf16[512,256]{1,0:T(8,128)(2,1)S(1)}, u32[]{:S(2)}, u32[]{:S(2)}) collective-permute-start(bf16[512,256]{1,0:T(8,128)(2,1)S(1)} %sum.3), channel_id=1, source_target_pairs={{1,2},{2,1},{5,6},{6,5},{9,10},{10,9},{13,14},{14,13},{17,18},{18,... | collective-permute-start | bytes 786440 | tf_op jit(solution)/shard_map/ppermute | solution.py:378
  86.4 11.8 %collective-permute-start.20 = (bf16[512,256]{1,0:T(8,128)(2,1)S(1)}, bf16[512,256]{1,0:T(8,128)(2,1)S(1)}, u32[]{:S(2)}, u32[]{:S(2)}) collective-permute-start(bf16[512,256]{1,0:T(8,128)(2,1)S(1)} %terms.23), channel_id=1, source_target_pairs={{0,1},{1,0},{2,3},{3,2},{4,5},{5,4},{6,7},{7,6},{8,9},{9,8},{10,11... | collective-permute-start | bytes 786440 | tf_op jit(solution)/shard_map/ppermute | solution.py:361
  99.1 3.6 %collective-permute-start.24 = (bf16[512,256]{1,0:T(8,128)(2,1)S(1)}, bf16[512,256]{1,0:T(8,128)(2,1)S(1)}, u32[]{:S(2)}, u32[]{:S(2)}) collective-permute-start(bf16[512,256]{1,0:T(8,128)(2,1)S(1)} %update.3.refs_0_), channel_id=1, source_target_pairs={{0,4},{4,0},{8,12},{12,8},{16,20},{20,16},{24,28},{28,24},{1,5},{5... | collective-permute-start | bytes 786440 | tf_op jit(solution)/shard_map/ppermute | solution.py:361
  99.2 9.2 %collective-permute-start.23 = (bf16[512,256]{1,0:T(8,128)(2,1)S(1)}, bf16[512,256]{1,0:T(8,128)(2,1)S(1)}, u32[]{:S(2)}, u32[]{:S(2)}) collective-permute-start(bf16[512,256]{1,0:T(8,128)(2,1)S(1)} %update.3.refs_0_), channel_id=1, source_target_pairs={{0,8},{4,12},{8,0},{12,4},{16,24},{20,28},{24,16},{28,20},{1,9},{5... | collective-permute-start | bytes 786440 | tf_op jit(solution)/shard_map/ppermute | solution.py:361
  100.7 14.0 %collective-permute-start.22 = (bf16[512,256]{1,0:T(8,128)(2,1)S(1)}, bf16[512,256]{1,0:T(8,128)(2,1)S(1)}, u32[]{:S(2)}, u32[]{:S(2)}) collective-permute-start(bf16[512,256]{1,0:T(8,128)(2,1)S(1)} %update.3.refs_0_), channel_id=1, source_target_pairs={{0,16},{4,20},{8,24},{12,28},{16,0},{20,4},{24,8},{28,12},{1,17},{... | collective-permute-start | bytes 786440 | tf_op jit(solution)/shard_map/ppermute | solution.py:361
  101.2 13.5 %collective-permute-start.21 = (bf16[512,256]{1,0:T(8,128)(2,1)S(1)}, bf16[512,256]{1,0:T(8,128)(2,1)S(1)}, u32[]{:S(2)}, u32[]{:S(2)}) collective-permute-start(bf16[512,256]{1,0:T(8,128)(2,1)S(1)} %update.3.refs_0_), channel_id=1, source_target_pairs={{0,24},{4,28},{8,16},{12,20},{16,8},{20,12},{24,0},{28,4},{1,25},{... | collective-permute-start | bytes 786440 | tf_op jit(solution)/shard_map/ppermute | solution.py:361
  114.7 2.8 %collective-permute-start.25 = (bf16[512,256]{1,0:T(8,128)(2,1)S(1)}, bf16[512,256]{1,0:T(8,128)(2,1)S(1)}, u32[]{:S(2)}, u32[]{:S(2)}) collective-permute-start(bf16[512,256]{1,0:T(8,128)(2,1)S(1)} %collective-permute-done.21.refs_0_), channel_id=1, source_target_pairs={{0,4},{4,0},{8,12},{12,8},{16,20},{20,16},{24,28},{28,24},{1,5},{5... | collective-permute-start | bytes 786440 | tf_op jit(solution)/shard_map/ppermute | solution.py:361
  114.7 2.9 %collective-permute-start.26 = (bf16[512,256]{1,0:T(8,128)(2,1)S(1)}, bf16[512,256]{1,0:T(8,128)(2,1)S(1)}, u32[]{:S(2)}, u32[]{:S(2)}) collective-permute-start(bf16[512,256]{1,0:T(8,128)(2,1)S(1)} %collective-permute-done.22.refs_1_), channel_id=1, source_target_pairs={{0,4},{4,0},{8,12},{12,8},{16,20},{20,16},{24,28},{28,24},{1,5},{5... | collective-permute-start | bytes 786440 | tf_op jit(solution)/shard_map/ppermute | solution.py:361
  115.2 2.4 %collective-permute-start.27 = (bf16[512,256]{1,0:T(8,128)(2,1)S(1)}, bf16[512,256]{1,0:T(8,128)(2,1)S(1)}, u32[]{:S(2)}, u32[]{:S(2)}) collective-permute-start(bf16[512,256]{1,0:T(8,128)(2,1)S(1)} %collective-permute-done.23.refs_2_), channel_id=1, source_target_pairs={{0,4},{4,0},{8,12},{12,8},{16,20},{20,16},{24,28},{28,24},{1,5},{5... | collective-permute-start | bytes 786440 | tf_op jit(solution)/shard_map/ppermute | solution.py:361
  119.1 9.7 %collective-permute-start.28 = (bf16[512,256]{1,0:T(8,128)(2,1)S(1)}, bf16[512,256]{1,0:T(8,128)(2,1)S(1)}, u32[]{:S(2)}, u32[]{:S(2)}) collective-permute-start(bf16[512,256]{1,0:T(8,128)(2,1)S(1)} %terms.27), channel_id=1, source_target_pairs={{0,1},{1,3},{3,2},{2,0},{4,5},{5,7},{7,6},{6,4},{8,9},{9,11},{11,1... | collective-permute-start | bytes 786440 | tf_op jit(solution)/shard_map/ppermute | solution.py:371
  124.5 12.9 %collective-permute-start.29 = (bf16[512,256]{1,0:T(8,128)(2,1)S(1)}, bf16[512,256]{1,0:T(8,128)(2,1)S(1)}, u32[]{:S(2)}, u32[]{:S(2)}) collective-permute-start(bf16[512,256]{1,0:T(8,128)(2,1)S(1)} %get-tuple-element.122), channel_id=1, source_target_pairs={{0,3},{3,0},{4,7},{7,4},{8,11},{11,8},{12,15},{15,12},{16,19},{19,... | collective-permute-start | bytes 786440 | tf_op jit(solution)/shard_map/ppermute | solution.py:375
  128.9 8.5 %collective-permute-start.30 = (bf16[512,256]{1,0:T(8,128)(2,1)S(1)}, bf16[512,256]{1,0:T(8,128)(2,1)S(1)}, u32[]{:S(2)}, u32[]{:S(2)}) collective-permute-start(bf16[512,256]{1,0:T(8,128)(2,1)S(1)} %sum.4), channel_id=1, source_target_pairs={{1,2},{2,1},{5,6},{6,5},{9,10},{10,9},{13,14},{14,13},{17,18},{18,... | collective-permute-start | bytes 786440 | tf_op jit(solution)/shard_map/ppermute | solution.py:378
  129.6 12.7 %collective-permute-start.31 = (bf16[512,256]{1,0:T(8,128)(2,1)S(1)}, bf16[512,256]{1,0:T(8,128)(2,1)S(1)}, u32[]{:S(2)}, u32[]{:S(2)}) collective-permute-start(bf16[512,256]{1,0:T(8,128)(2,1)S(1)} %terms.29), channel_id=1, source_target_pairs={{0,1},{1,0},{2,3},{3,2},{4,5},{5,4},{6,7},{7,6},{8,9},{9,8},{10,11... | collective-permute-start | bytes 786440 | tf_op jit(solution)/shard_map/ppermute | solution.py:361
  143.1 3.6 %collective-permute-start.35 = (bf16[512,256]{1,0:T(8,128)(2,1)S(1)}, bf16[512,256]{1,0:T(8,128)(2,1)S(1)}, u32[]{:S(2)}, u32[]{:S(2)}) collective-permute-start(bf16[512,256]{1,0:T(8,128)(2,1)S(1)} %update.4.refs_0_), channel_id=1, source_target_pairs={{0,4},{4,0},{8,12},{12,8},{16,20},{20,16},{24,28},{28,24},{1,5},{5... | collective-permute-start | bytes 786440 | tf_op jit(solution)/shard_map/ppermute | solution.py:361
  143.2 9.2 %collective-permute-start.34 = (bf16[512,256]{1,0:T(8,128)(2,1)S(1)}, bf16[512,256]{1,0:T(8,128)(2,1)S(1)}, u32[]{:S(2)}, u32[]{:S(2)}) collective-permute-start(bf16[512,256]{1,0:T(8,128)(2,1)S(1)} %update.4.refs_0_), channel_id=1, source_target_pairs={{0,8},{4,12},{8,0},{12,4},{16,24},{20,28},{24,16},{28,20},{1,9},{5... | collective-permute-start | bytes 786440 | tf_op jit(solution)/shard_map/ppermute | solution.py:361
  143.8 14.0 %collective-permute-start.33 = (bf16[512,256]{1,0:T(8,128)(2,1)S(1)}, bf16[512,256]{1,0:T(8,128)(2,1)S(1)}, u32[]{:S(2)}, u32[]{:S(2)}) collective-permute-start(bf16[512,256]{1,0:T(8,128)(2,1)S(1)} %update.4.refs_0_), channel_id=1, source_target_pairs={{0,16},{4,20},{8,24},{12,28},{16,0},{20,4},{24,8},{28,12},{1,17},{... | collective-permute-start | bytes 786440 | tf_op jit(solution)/shard_map/ppermute | solution.py:361
  145.0 12.8 %collective-permute-start.32 = (bf16[512,256]{1,0:T(8,128)(2,1)S(1)}, bf16[512,256]{1,0:T(8,128)(2,1)S(1)}, u32[]{:S(2)}, u32[]{:S(2)}) collective-permute-start(bf16[512,256]{1,0:T(8,128)(2,1)S(1)} %update.4.refs_0_), channel_id=1, source_target_pairs={{0,24},{4,28},{8,16},{12,20},{16,8},{20,12},{24,0},{28,4},{1,25},{... | collective-permute-start | bytes 786440 | tf_op jit(solution)/shard_map/ppermute | solution.py:361
  157.8 2.8 %collective-permute-start.36 = (bf16[512,256]{1,0:T(8,128)(2,1)S(1)}, bf16[512,256]{1,0:T(8,128)(2,1)S(1)}, u32[]{:S(2)}, u32[]{:S(2)}) collective-permute-start(bf16[512,256]{1,0:T(8,128)(2,1)S(1)} %collective-permute-done.32.refs_0_), channel_id=1, source_target_pairs={{0,4},{4,0},{8,12},{12,8},{16,20},{20,16},{24,28},{28,24},{1,5},{5... | collective-permute-start | bytes 786440 | tf_op jit(solution)/shard_map/ppermute | solution.py:361
  157.8 2.9 %collective-permute-start.37 = (bf16[512,256]{1,0:T(8,128)(2,1)S(1)}, bf16[512,256]{1,0:T(8,128)(2,1)S(1)}, u32[]{:S(2)}, u32[]{:S(2)}) collective-permute-start(bf16[512,256]{1,0:T(8,128)(2,1)S(1)} %collective-permute-done.33.refs_1_), channel_id=1, source_target_pairs={{0,4},{4,0},{8,12},{12,8},{16,20},{20,16},{24,28},{28,24},{1,5},{5... | collective-permute-start | bytes 786440 | tf_op jit(solution)/shard_map/ppermute | solution.py:361
  158.3 2.4 %collective-permute-start.38 = (bf16[512,256]{1,0:T(8,128)(2,1)S(1)}, bf16[512,256]{1,0:T(8,128)(2,1)S(1)}, u32[]{:S(2)}, u32[]{:S(2)}) collective-permute-start(bf16[512,256]{1,0:T(8,128)(2,1)S(1)} %collective-permute-done.34.refs_2_), channel_id=1, source_target_pairs={{0,4},{4,0},{8,12},{12,8},{16,20},{20,16},{24,28},{28,24},{1,5},{5... | collective-permute-start | bytes 786440 | tf_op jit(solution)/shard_map/ppermute | solution.py:361
  162.2 9.9 %collective-permute-start.39 = (bf16[512,256]{1,0:T(8,128)(2,1)S(1)}, bf16[512,256]{1,0:T(8,128)(2,1)S(1)}, u32[]{:S(2)}, u32[]{:S(2)}) collective-permute-start(bf16[512,256]{1,0:T(8,128)(2,1)S(1)} %terms.33), channel_id=1, source_target_pairs={{0,1},{1,3},{3,2},{2,0},{4,5},{5,7},{7,6},{6,4},{8,9},{9,11},{11,1... | collective-permute-start | bytes 786440 | tf_op jit(solution)/shard_map/ppermute | solution.py:371
  166.9 12.9 %collective-permute-start.40 = (bf16[512,256]{1,0:T(8,128)(2,1)S(1)}, bf16[512,256]{1,0:T(8,128)(2,1)S(1)}, u32[]{:S(2)}, u32[]{:S(2)}) collective-permute-start(bf16[512,256]{1,0:T(8,128)(2,1)S(1)} %get-tuple-element.141), channel_id=1, source_target_pairs={{0,3},{3,0},{4,7},{7,4},{8,11},{11,8},{12,15},{15,12},{16,19},{19,... | collective-permute-start | bytes 786440 | tf_op jit(solution)/shard_map/ppermute | solution.py:375
  172.1 7.7 %collective-permute-start.41 = (bf16[512,256]{1,0:T(8,128)(2,1)S(1)}, bf16[512,256]{1,0:T(8,128)(2,1)S(1)}, u32[]{:S(2)}, u32[]{:S(2)}) collective-permute-start(bf16[512,256]{1,0:T(8,128)(2,1)S(1)} %sum.5), channel_id=1, source_target_pairs={{1,2},{2,1},{5,6},{6,5},{9,10},{10,9},{13,14},{14,13},{17,18},{18,... | collective-permute-start | bytes 786440 | tf_op jit(solution)/shard_map/ppermute | solution.py:378
  172.8 11.9 %collective-permute-start.42 = (bf16[512,256]{1,0:T(8,128)(2,1)S(1)}, bf16[512,256]{1,0:T(8,128)(2,1)S(1)}, u32[]{:S(2)}, u32[]{:S(2)}) collective-permute-start(bf16[512,256]{1,0:T(8,128)(2,1)S(1)} %terms.35), channel_id=1, source_target_pairs={{0,1},{1,0},{2,3},{3,2},{4,5},{5,4},{6,7},{7,6},{8,9},{9,8},{10,11... | collective-permute-start | bytes 786440 | tf_op jit(solution)/shard_map/ppermute | solution.py:361

commit v3 on v2

--- a/solution.py
+++ b/solution.py
@@ -120,12 +120,12 @@
 
     outs = pl.pallas_call(
         functools.partial(spectra_kernel, packs, n_row),
-        in_specs=[SMEM, ANY, ANY],
+        in_specs=[SMEM, ANY, pl.BlockSpec(memory_space=pltpu.HBM)],
         out_specs=[VMEM] * n_row,
         out_shape=[jax.ShapeDtypeStruct((steps, short, LANES), jnp.bfloat16)] * n_row,
         scratch_shapes=[
-            pltpu.VMEM((2 * BUFFERS, block, shots, samples), jnp.bfloat16),
-            pltpu.SemaphoreType.DMA((2 * BUFFERS,)),
+            pltpu.VMEM((BUFFERS, block, shots, samples), jnp.bfloat16),
+            pltpu.SemaphoreType.DMA((BUFFERS,)),
             pltpu.VMEM(table.shape, table.dtype),
             pltpu.SemaphoreType.DMA,
         ],
@@ -361,47 +361,34 @@
     return lax.ppermute(array, axis, [(index, index ^ bits) for index in range(size)])
 
 
-def exchange(n_src, far, near, own):
+def exchange(n_src, make):
     bf16, f32 = jnp.bfloat16, jnp.float32
-    half = n_src // 2
     if n_src != 4:
-        arriving = [swap(far(turn, [bf16])[0], "src", turn) for turn in range(n_src - 1, half - 1, -1)]
-        arriving += [swap(near(turn, [bf16])[0], "src", turn) for turn in range(half - 1, 0, -1)]
-        return own(0, [f32])[0], arriving, False
-    first = lax.ppermute(far(2, [bf16])[0], "src", [(0, 1), (1, 3), (3, 2), (2, 0)])
-    sent, kept = far(3, [bf16, f32])
-    beside = near(1, [bf16])[0]
-    sent, beside = lax.optimization_barrier((sent, beside))
+        arriving = [swap(make(turn, [bf16])[0], "src", turn) for turn in range(n_src - 1, 0, -1)]
+        return make(0, [f32])[0], arriving, False
+    first = lax.ppermute(make(2, [bf16])[0], "src", [(0, 1), (1, 3), (3, 2), (2, 0)])
+    sent, kept = make(3, [bf16, f32])
+    near = make(1, [bf16])[0]
+    both, near = lax.optimization_barrier((make_sum(kept, first), near))
+    beside = swap(near, "src", 1)
     outer = lax.ppermute(sent, "src", [(0, 3), (3, 0)])
-    both = make_sum(kept, first)
-    both, beside = lax.optimization_barrier((both, beside))
     inner = lax.ppermute(both, "src", [(1, 2), (2, 1)])
-    beside = swap(beside, "src", 1)
-    return own(0, [f32])[0], [first, outer, inner, beside], True
+    return make(0, [f32])[0], [first, beside, outer, inner], True
 
 
 def iterate(estimate, data, place, n_row, n_src, slice_rows):
-    f32 = jnp.float32
-    half = n_src // 2
-    direct = {turn: swap(estimate, "row", turn) for turn in range(n_row - 2, 0, -2)}
+    direct = {turn: swap(estimate, "row", turn) for turn in range(2, n_row, 2)}
     first = {0: estimate, 1: swap(estimate, "row", 1)}
-    turns = tuple(range(n_src - 1, -1, -1))
-    begun = make_terms(data, place, first, turns, [], slice_rows, [f32])
+    turns = tuple(range(n_src))
+    begun = make_terms(data, place, first, turns, [], slice_rows, [jnp.float32])
     held = lax.optimization_barrier((*direct.values(), *begun))
-    direct = dict(zip(direct, held))
-    begun = dict(zip(turns, held[len(direct) :]))
+    direct, begun = dict(zip(direct, held)), held[len(direct) :]
     passed = {turn + 1: swap(piece, "row", 1) for turn, piece in direct.items()}
-    turns = tuple(range(n_src - 1, half - 1, -1))
-    sums = make_terms(data, place, direct, turns, [begun[turn] for turn in turns], slice_rows, [f32])
-    later = dict(zip(turns, sums))
-
-    def far(turn, types):
-        return make_terms(data, place, passed, (turn,), [later[turn]], slice_rows, types)
-
-    def near(turn, types):
+
+    def make(turn, types):
         return make_terms(data, place, {**direct, **passed}, (turn,), [begun[turn]], slice_rows, types)
 
-    return exchange(n_src, far, near, near)
+    return exchange(n_src, make)
 
 
 def body(traces, row_source, slice_data, wavelet_inverse):
@@ -412,7 +399,7 @@
     packs = LANES // (2 * shots)
     group_rows = block_rows // n_row
     slice_rows = block_rows // n_src
-    block = min(group_rows, 64)
+    block = min(group_rows, 128)
     short = block // packs
 
     spectra = make_spectra(traces, place, n_row, packs, block)

time: 187 us -> 185 us (0.989)
  Pallas kernels: 89.1 us -> 83.9 us
  waiting for transfers between devices: 43 us -> 46.2 us
    ppermute x34, waiting for transfers between devices: 36.2 us -> 40 us  [swap(): lax.ppermute(array, axis, [(index, index ^ bits) for index in range(size)])]
    ppermute x34, starting transfers between devices: 33.6 us -> 29.7 us  [swap(): lax.ppermute(array, axis, [(index, index ^ bits) for index in range(size)])]
    pallas_call x1, Pallas kernels: 26.9 us -> 23.8 us  [make_spectra(): pl.pallas_call(functools.partial(spectra_kernel, packs, n_row), in_specs=...]
    ppermute x3, starting transfers between devices: 3.06 us -> 6.07 us  [exchange(): lax.ppermute(make(2, [bf16])[0], 'src', [(0, 1), (1, 3), (3, 2), (2, 0)])]
    pallas_call x18 -> x15, Pallas kernels: 38.8 us -> 36.7 us  [make_terms(): pl.pallas_call(functools.partial(terms_kernel, turns, numbers, len(partia...]
  transfers between devices with their start and end apart: 43 -> 43, of which waited for: 17 -> 22; matrix products, arithmetic and copies ran while one was open for 0% -> 0% of each run, Pallas kernels for 27% -> 25%
where the time goes in v3:
time: 185 us; the launch traced here: 184 us
  Pallas kernels  83.9 us (45%)
  starting transfers between devices  51.7 us (28%)
  waiting for transfers between devices  46.2 us (25%)
    ppermute x34, waiting for transfers between devices, swap(): lax.ppermute(array, axis, [(index, index ^ bits) for index in range(size)])  40 us
    pallas_call x15, Pallas kernels, make_terms(): pl.pallas_call(functools.partial(terms_kernel, turns, numbers, len(partia...  36.7 us
    ppermute x34, starting transfers between devices, swap(): lax.ppermute(array, axis, [(index, index ^ bits) for index in range(size)])  29.7 us
    pallas_call x1, Pallas kernels, make_spectra(): pl.pallas_call(functools.partial(spectra_kernel, packs, n_row), in_specs=...  23.8 us
    pallas_call x2, Pallas kernels, relay(): pl.pallas_call(functools.partial(relay_kernel, part), in_specs=[ANY, ANY]...  15.7 us
    ppermute x3, starting transfers between devices, exchange(): outer = lax.ppermute(sent, 'src', [(0, 3), (3, 0)])  13.7 us
    ppermute x3, waiting for transfers between devices, exchange(): outer = lax.ppermute(sent, 'src', [(0, 3), (3, 0)])  6.16 us
    ppermute x3, starting transfers between devices, exchange(): lax.ppermute(make(2, [bf16])[0], 'src', [(0, 1), (1, 3), (3, 2), (2, 0)])  6.07 us
  transfers between devices with their start and end apart: 43, of which 22 were waited for; matrix products, arithmetic and copies ran while one was open for 0% of the time, Pallas kernels for 25%

profile of v3, /device:TPU:0, one launch (start us, length us, event | category | flops | bytes accessed | tf_op | source)
XLA Modules:
  0.0 184.3 jit_solution(1848588636410796290)
XLA Ops:
  0.7 1.0 copy-done
  1.8 23.8 %spectra.1 = (bf16[2,64,128]{2,1,0:T(8,128)(2,1)S(1)}, bf16[2,64,128]{2,1,0:T(8,128)(2,1)S(1)}, bf16[2,64,128]{2,1,0:T(8,128)(2,1)S(1)}, bf16[2,64,128]{2,1,0:T(...) custom-call(s32[2]{0:T(128)S(1)} %pad_add_fusion.place_ref, ...), custom_call_target="tpu_custom_call" | custom-call | flops 8589934592 | bytes 67108864 | tf_op jit(solution)/shard_map/spectra/pallas_call | solution.py:121
  26.1 2.6 %collective-permute-start.1 = (bf16[128,128]{1,0:T(8,128)(2,1)S(1)}, bf16[128,128]{1,0:T(8,128)(2,1)S(1)}, u32[]{:S(2)}, u32[]{:S(2)}) collective-permute-start(bf16[128,128]{1,0:T(8,128)(2,1)S(1)} %bitcast.17), channel_id=1, source_target_pairs={{0,8},{4,12},{8,0},{12,4},{16,24},{20,28},{24,16},{28,20},{1,9},{5... | collective-permute-start | bytes 98312 | tf_op jit(solution)/shard_map/ppermute | solution.py:361
  28.7 1.8 collective-permute-start.3
  30.5 2.6 %collective-permute-start.5 = (bf16[128,128]{1,0:T(8,128)(2,1)S(1)}, bf16[128,128]{1,0:T(8,128)(2,1)S(1)}, u32[]{:S(2)}, u32[]{:S(2)}) collective-permute-start(bf16[128,128]{1,0:T(8,128)(2,1)S(1)} %bitcast.13), channel_id=1, source_target_pairs={{0,24},{4,28},{8,16},{12,20},{16,8},{20,12},{24,0},{28,4},{1,25},{... | collective-permute-start | bytes 98312 | tf_op jit(solution)/shard_map/ppermute | solution.py:361
  34.0 1.4 collective-permute-done.5.refs_6_
  35.3 2.0 %collective-permute-done.6.refs_7_ = bf16[128,128]{1,0:T(8,128)(2,1)S(1)} collective-permute-done((bf16[128,128]{1,0:T(8,128)(2,1)S(1)}, bf16[128,128]{1,0:T(8,128)(2,1)S(1)}, u32[]{:S(2)}, u32[]{:S(2)}) %collective-permute-start.6) | collective-permute-done | bytes 32800 | tf_op jit(solution)/shard_map/ppermute | solution.py:361
  37.7 2.8 %order.1 = (bf16[256,128]{1,0:T(8,128)(2,1)S(1)}, bf16[256,128]{1,0:T(8,128)(2,1)S(1)}, bf16[256,128]{1,0:T(8,128)(2,1)S(1)}, bf16[256,128]{1,0:T(8,128)(2,1)S(1)}) custom-call(s32[2]{0:T(128)S(1)} %pad_add_fusion.place_ref, s32[2048,128]{1,0:T(8,128)S(1)} %broadcast_in_dim.2.code_ref, bf16[128,128]{1,0:T(8,128)(2,1)S(1)} %bitcast.10, ...), custom_call_target="tpu_custom_call" | custom-call | flops 1073741824 | bytes 1048576 | tf_op jit(solution)/shard_map/order/pallas_call | solution.py:173
  40.5 1.6 collective-permute-start.7
  42.2 2.6 %collective-permute-start.8 = (bf16[256,128]{1,0:T(8,128)(2,1)S(1)}, bf16[256,128]{1,0:T(8,128)(2,1)S(1)}, u32[]{:S(2)}, u32[]{:S(2)}) collective-permute-start(bf16[256,128]{1,0:T(8,128)(2,1)S(1)} %get-tuple-element.74), channel_id=1, source_target_pairs={{0,2},{1,3},{2,0},{3,1},{4,6},{5,7},{6,4},{7,5},{8,10},{9,11},{10,... | collective-permute-start | bytes 196616 | tf_op jit(solution)/shard_map/ppermute | solution.py:361
  45.0 7.7 %relay.3 = (bf16[8,2048,512]{2,1,0:T(8,128)(2,1)S(1)}, f32[8,128]{1,0:T(8,128)S(1)}) custom-call(bf16[2,2048,8,512]{3,2,1,0:T(8,128)(2,1)} %data_ref.3, bf16[256,128]{1,0:T(8,128)(2,1)S(1)} %get-tuple-element.71.after_ref.refs_0_), custom_call_target="tpu_custom_call" | custom-call | bytes 33554432 | tf_op jit(solution)/shard_map/relay/pallas_call | solution.py:236
  53.7 1.1 collective-permute-start.12
  55.8 1.5 collective-permute-start.10
  57.3 8.0 %relay.2 = (bf16[8,2048,512]{2,1,0:T(8,128)(2,1)S(1)}, f32[8,128]{1,0:T(8,128)}) custom-call(bf16[2,2048,8,512]{3,2,1,0:T(8,128)(2,1)} %data_ref.3, bf16[128,128]{1,0:T(8,128)(2,1)S(1)} %bitcast.11), custom_call_target="tpu_custom_call" | custom-call | bytes 33554432 | tf_op jit(solution)/shard_map/relay/pallas_call | solution.py:236
  65.3 2.9 %terms.15 = (f32[512,256]{1,0:T(8,128)S(1)}, f32[512,256]{1,0:T(8,128)S(1)}, f32[512,256]{1,0:T(8,128)S(1)}, f32[512,256]{1,0:T(8,128)S(1)}) custom-call(s32[2]{0:T(128)S(1)} %pad_add_fusion.place_ref, bf16[8,2048,512]{2,1,0:T(8,128)(2,1)S(1)} %get-tuple-element.63.real_ref, bf16[8,2048,512]{2,1,0:T(8,128)(2,1)S(1)} %get-tuple-element.72.imag_ref, ...), custom_call_target="tpu_custom_call" | custom-call | flops 2147483648 | bytes 8388608 | tf_op jit(solution)/shard_map/terms/pallas_call | solution.py:285
  71.2 2.3 %terms.17 = bf16[512,256]{1,0:T(8,128)(2,1)S(1)} custom-call(s32[2]{0:T(128)S(1)} %pad_add_fusion.place_ref, bf16[8,2048,512]{2,1,0:T(8,128)(2,1)S(1)} %get-tuple-element.63.real_ref, bf16[8,2048,512]{2,1,0:T(8,128)(2,1)S(1)} %get-tuple-element.72.imag_ref, bf16[512,256]{1,0:T(8,128)(2,1)S(1)} %collective-permute-done.10.refs_0_, ...), custom_call_target="tpu_custom_call" | custom-call | flops 1610612736 | bytes 6291456 | tf_op jit(solution)/shard_map/terms/pallas_call | solution.py:285
  74.2 2.3 %terms.18 = (bf16[512,256]{1,0:T(8,128)(2,1)S(1)}, f32[512,256]{1,0:T(8,128)S(1)}) custom-call(s32[2]{0:T(128)S(1)} %pad_add_fusion.place_ref, bf16[8,2048,512]{2,1,0:T(8,128)(2,1)S(1)} %get-tuple-element.63.real_ref, bf16[8,2048,512]{2,1,0:T(8,128)(2,1)S(1)} %get-tuple-element.72.imag_ref, bf16[512,256]{1,0:T(8,128)(2,1)S(1)} %collective-permute-done.10.refs_0_, ...), custom_call_target="tpu_custom_call" | custom-call | flops 1610612736 | bytes 6291456 | tf_op jit(solution)/shard_map/terms/pallas_call | solution.py:285
  76.6 4.8 %collective-permute-start.19 = (bf16[512,256]{1,0:T(8,128)(2,1)S(1)}, bf16[512,256]{1,0:T(8,128)(2,1)S(1)}, u32[]{:S(2)}, u32[]{:S(2)}) collective-permute-start(bf16[512,256]{1,0:T(8,128)(2,1)S(1)} %get-tuple-element.90), channel_id=1, source_target_pairs={{0,3},{3,0},{4,7},{7,4},{8,11},{11,8},{12,15},{15,12},{16,19},{19,... | collective-permute-start | bytes 786440 | tf_op jit(solution)/shard_map/ppermute | solution.py:374
  81.4 2.3 %terms.19 = bf16[512,256]{1,0:T(8,128)(2,1)S(1)} custom-call(s32[2]{0:T(128)S(1)} %pad_add_fusion.place_ref, bf16[8,2048,512]{2,1,0:T(8,128)(2,1)S(1)} %get-tuple-element.63.real_ref, bf16[8,2048,512]{2,1,0:T(8,128)(2,1)S(1)} %get-tuple-element.72.imag_ref, bf16[512,256]{1,0:T(8,128)(2,1)S(1)} %collective-permute-done.10.refs_0_, ...), custom_call_target="tpu_custom_call" | custom-call | flops 1610612736 | bytes 6291456 | tf_op jit(solution)/shard_map/terms/pallas_call | solution.py:285
  83.9 5.0 %collective-permute-start.18 = (bf16[512,256]{1,0:T(8,128)(2,1)S(1)}, bf16[512,256]{1,0:T(8,128)(2,1)S(1)}, u32[]{:S(2)}, u32[]{:S(2)}) collective-permute-start(bf16[512,256]{1,0:T(8,128)(2,1)S(1)} %terms.19), channel_id=1, source_target_pairs={{0,1},{1,0},{2,3},{3,2},{4,5},{5,4},{6,7},{7,6},{8,9},{9,8},{10,11... | collective-permute-start | bytes 786440 | tf_op jit(solution)/shard_map/ppermute | solution.py:361
  89.7 2.3 %terms.16.own_ref = f32[512,256]{1,0:T(8,128)S(1)} custom-call(s32[2]{0:T(128)S(1)} %pad_add_fusion.place_ref, bf16[8,2048,512]{2,1,0:T(8,128)(2,1)S(1)} %get-tuple-element.63.real_ref, bf16[8,2048,512]{2,1,0:T(8,128)(2,1)S(1)} %get-tuple-element.72.imag_ref, bf16[512,256]{1,0:T(8,128)(2,1)S(1)} %collective-permute-done.10.refs_0_, ...), custom_call_target="tpu_custom_call" | custom-call | flops 1610612736 | bytes 6291456 | tf_op jit(solution)/shard_map/terms/pallas_call | solution.py:285
  92.1 2.9 %collective-permute-done.18.refs_1_ = bf16[512,256]{1,0:T(8,128)(2,1)S(1)} collective-permute-done((bf16[512,256]{1,0:T(8,128)(2,1)S(1)}, bf16[512,256]{1,0:T(8,128)(2,1)S(1)}, u32[]{:S(2)}, u32[]{:S(2)}) %collective-permute-start.18) | collective-permute-done | bytes 262176 | tf_op jit(solution)/shard_map/ppermute | solution.py:361
  95.9 1.2 collective-permute-start.23
  98.1 1.4 collective-permute-start.21
  99.5 2.9 %terms.20 = (f32[512,256]{1,0:T(8,128)S(1)}, f32[512,256]{1,0:T(8,128)S(1)}, f32[512,256]{1,0:T(8,128)S(1)}, f32[512,256]{1,0:T(8,128)S(1)}) custom-call(s32[2]{0:T(128)S(1)} %pad_add_fusion.place_ref, bf16[8,2048,512]{2,1,0:T(8,128)(2,1)S(1)} %get-tuple-element.63.real_ref, bf16[8,2048,512]{2,1,0:T(8,128)(2,1)S(1)} %get-tuple-element.72.imag_ref, ...), custom_call_target="tpu_custom_call" | custom-call | flops 2147483648 | bytes 8388608 | tf_op jit(solution)/shard_map/terms/pallas_call | solution.py:285
  102.3 3.7 %collective-permute-done.23.refs_2_ = bf16[512,256]{1,0:T(8,128)(2,1)S(1)} collective-permute-done((bf16[512,256]{1,0:T(8,128)(2,1)S(1)}, bf16[512,256]{1,0:T(8,128)(2,1)S(1)}, u32[]{:S(2)}, u32[]{:S(2)}) %collective-permute-start.23) | collective-permute-done | bytes 262176 | tf_op jit(solution)/shard_map/ppermute | solution.py:361
  106.0 5.1 %collective-permute-done.22.refs_1_ = bf16[512,256]{1,0:T(8,128)(2,1)S(1)} collective-permute-done((bf16[512,256]{1,0:T(8,128)(2,1)S(1)}, bf16[512,256]{1,0:T(8,128)(2,1)S(1)}, u32[]{:S(2)}, u32[]{:S(2)}) %collective-permute-start.22) | collective-permute-done | bytes 262176 | tf_op jit(solution)/shard_map/ppermute | solution.py:361
  113.4 2.3 %terms.22 = bf16[512,256]{1,0:T(8,128)(2,1)S(1)} custom-call(s32[2]{0:T(128)S(1)} %pad_add_fusion.place_ref, bf16[8,2048,512]{2,1,0:T(8,128)(2,1)S(1)} %get-tuple-element.63.real_ref, bf16[8,2048,512]{2,1,0:T(8,128)(2,1)S(1)} %get-tuple-element.72.imag_ref, bf16[512,256]{1,0:T(8,128)(2,1)S(1)} %collective-permute-done.21.refs_0_, ...), custom_call_target="tpu_custom_call" | custom-call | flops 1610612736 | bytes 6291456 | tf_op jit(solution)/shard_map/terms/pallas_call | solution.py:285
  115.8 4.4 %collective-permute-start.28 = (bf16[512,256]{1,0:T(8,128)(2,1)S(1)}, bf16[512,256]{1,0:T(8,128)(2,1)S(1)}, u32[]{:S(2)}, u32[]{:S(2)}) collective-permute-start(bf16[512,256]{1,0:T(8,128)(2,1)S(1)} %terms.22), channel_id=1, source_target_pairs={{0,1},{1,3},{3,2},{2,0},{4,5},{5,7},{7,6},{6,4},{8,9},{9,11},{11,1... | collective-permute-start | bytes 786440 | tf_op jit(solution)/shard_map/ppermute | solution.py:369
  120.2 2.3 %terms.23 = (bf16[512,256]{1,0:T(8,128)(2,1)S(1)}, f32[512,256]{1,0:T(8,128)S(1)}) custom-call(s32[2]{0:T(128)S(1)} %pad_add_fusion.place_ref, bf16[8,2048,512]{2,1,0:T(8,128)(2,1)S(1)} %get-tuple-element.63.real_ref, bf16[8,2048,512]{2,1,0:T(8,128)(2,1)S(1)} %get-tuple-element.72.imag_ref, bf16[512,256]{1,0:T(8,128)(2,1)S(1)} %collective-permute-done.21.refs_0_, ...), custom_call_target="tpu_custom_call" | custom-call | flops 1610612736 | bytes 6291456 | tf_op jit(solution)/shard_map/terms/pallas_call | solution.py:285
  122.5 4.8 %collective-permute-start.30 = (bf16[512,256]{1,0:T(8,128)(2,1)S(1)}, bf16[512,256]{1,0:T(8,128)(2,1)S(1)}, u32[]{:S(2)}, u32[]{:S(2)}) collective-permute-start(bf16[512,256]{1,0:T(8,128)(2,1)S(1)} %get-tuple-element.105), channel_id=1, source_target_pairs={{0,3},{3,0},{4,7},{7,4},{8,11},{11,8},{12,15},{15,12},{16,19},{19,... | collective-permute-start | bytes 786440 | tf_op jit(solution)/shard_map/ppermute | solution.py:374
  127.3 2.4 %terms.24 = bf16[512,256]{1,0:T(8,128)(2,1)S(1)} custom-call(s32[2]{0:T(128)S(1)} %pad_add_fusion.place_ref, bf16[8,2048,512]{2,1,0:T(8,128)(2,1)S(1)} %get-tuple-element.63.real_ref, bf16[8,2048,512]{2,1,0:T(8,128)(2,1)S(1)} %get-tuple-element.72.imag_ref, bf16[512,256]{1,0:T(8,128)(2,1)S(1)} %collective-permute-done.21.refs_0_, ...), custom_call_target="tpu_custom_call" | custom-call | flops 1610612736 | bytes 6291456 | tf_op jit(solution)/shard_map/terms/pallas_call | solution.py:285
  130.5 2.3 %terms.21.own_ref = f32[512,256]{1,0:T(8,128)S(1)} custom-call(s32[2]{0:T(128)S(1)} %pad_add_fusion.place_ref, bf16[8,2048,512]{2,1,0:T(8,128)(2,1)S(1)} %get-tuple-element.63.real_ref, bf16[8,2048,512]{2,1,0:T(8,128)(2,1)S(1)} %get-tuple-element.72.imag_ref, bf16[512,256]{1,0:T(8,128)(2,1)S(1)} %collective-permute-done.21.refs_0_, ...), custom_call_target="tpu_custom_call" | custom-call | flops 1610612736 | bytes 6291456 | tf_op jit(solution)/shard_map/terms/pallas_call | solution.py:285
  132.9 2.8 %collective-permute-done.30.refs_2_ = bf16[512,256]{1,0:T(8,128)(2,1)S(1)} collective-permute-done((bf16[512,256]{1,0:T(8,128)(2,1)S(1)}, bf16[512,256]{1,0:T(8,128)(2,1)S(1)}, u32[]{:S(2)}, u32[]{:S(2)}) %collective-permute-start.30) | collective-permute-done | bytes 262176 | tf_op jit(solution)/shard_map/ppermute | solution.py:374
  135.7 4.9 %collective-permute-done.29.refs_1_ = bf16[512,256]{1,0:T(8,128)(2,1)S(1)} collective-permute-done((bf16[512,256]{1,0:T(8,128)(2,1)S(1)}, bf16[512,256]{1,0:T(8,128)(2,1)S(1)}, u32[]{:S(2)}, u32[]{:S(2)}) %collective-permute-start.29) | collective-permute-done | bytes 262176 | tf_op jit(solution)/shard_map/ppermute | solution.py:361
  141.5 1.2 collective-permute-start.34
  143.7 1.4 collective-permute-start.32
  145.1 2.9 %terms.25 = (f32[512,256]{1,0:T(8,128)S(1)}, f32[512,256]{1,0:T(8,128)S(1)}, f32[512,256]{1,0:T(8,128)S(1)}, f32[512,256]{1,0:T(8,128)S(1)}) custom-call(s32[2]{0:T(128)S(1)} %pad_add_fusion.place_ref, bf16[8,2048,512]{2,1,0:T(8,128)(2,1)S(1)} %get-tuple-element.63.real_ref, bf16[8,2048,512]{2,1,0:T(8,128)(2,1)S(1)} %get-tuple-element.72.imag_ref, ...), custom_call_target="tpu_custom_call" | custom-call | flops 2147483648 | bytes 8388608 | tf_op jit(solution)/shard_map/terms/pallas_call | solution.py:285
  148.0 3.7 %collective-permute-done.34.refs_2_ = bf16[512,256]{1,0:T(8,128)(2,1)S(1)} collective-permute-done((bf16[512,256]{1,0:T(8,128)(2,1)S(1)}, bf16[512,256]{1,0:T(8,128)(2,1)S(1)}, u32[]{:S(2)}, u32[]{:S(2)}) %collective-permute-start.34) | collective-permute-done | bytes 262176 | tf_op jit(solution)/shard_map/ppermute | solution.py:361
  151.7 5.1 %collective-permute-done.33.refs_1_ = bf16[512,256]{1,0:T(8,128)(2,1)S(1)} collective-permute-done((bf16[512,256]{1,0:T(8,128)(2,1)S(1)}, bf16[512,256]{1,0:T(8,128)(2,1)S(1)}, u32[]{:S(2)}, u32[]{:S(2)}) %collective-permute-start.33) | collective-permute-done | bytes 262176 | tf_op jit(solution)/shard_map/ppermute | solution.py:361
  159.1 2.3 %terms.27 = bf16[512,256]{1,0:T(8,128)(2,1)S(1)} custom-call(s32[2]{0:T(128)S(1)} %pad_add_fusion.place_ref, bf16[8,2048,512]{2,1,0:T(8,128)(2,1)S(1)} %get-tuple-element.63.real_ref, bf16[8,2048,512]{2,1,0:T(8,128)(2,1)S(1)} %get-tuple-element.72.imag_ref, bf16[512,256]{1,0:T(8,128)(2,1)S(1)} %collective-permute-done.32.refs_0_, ...), custom_call_target="tpu_custom_call" | custom-call | flops 1610612736 | bytes 6291456 | tf_op jit(solution)/shard_map/terms/pallas_call | solution.py:285
  162.4 2.3 %terms.28 = (bf16[512,256]{1,0:T(8,128)(2,1)S(1)}, f32[512,256]{1,0:T(8,128)S(1)}) custom-call(s32[2]{0:T(128)S(1)} %pad_add_fusion.place_ref, bf16[8,2048,512]{2,1,0:T(8,128)(2,1)S(1)} %get-tuple-element.63.real_ref, bf16[8,2048,512]{2,1,0:T(8,128)(2,1)S(1)} %get-tuple-element.72.imag_ref, bf16[512,256]{1,0:T(8,128)(2,1)S(1)} %collective-permute-done.32.refs_0_, ...), custom_call_target="tpu_custom_call" | custom-call | flops 1610612736 | bytes 6291456 | tf_op jit(solution)/shard_map/terms/pallas_call | solution.py:285
  164.7 4.0 %collective-permute-start.41 = (bf16[512,256]{1,0:T(8,128)(2,1)S(1)}, bf16[512,256]{1,0:T(8,128)(2,1)S(1)}, u32[]{:S(2)}, u32[]{:S(2)}) collective-permute-start(bf16[512,256]{1,0:T(8,128)(2,1)S(1)} %get-tuple-element.120), channel_id=1, source_target_pairs={{0,3},{3,0},{4,7},{7,4},{8,11},{11,8},{12,15},{15,12},{16,19},{19,... | collective-permute-start | bytes 786440 | tf_op jit(solution)/shard_map/ppermute | solution.py:374
  168.8 2.4 %terms.29 = bf16[512,256]{1,0:T(8,128)(2,1)S(1)} custom-call(s32[2]{0:T(128)S(1)} %pad_add_fusion.place_ref, bf16[8,2048,512]{2,1,0:T(8,128)(2,1)S(1)} %get-tuple-element.63.real_ref, bf16[8,2048,512]{2,1,0:T(8,128)(2,1)S(1)} %get-tuple-element.72.imag_ref, bf16[512,256]{1,0:T(8,128)(2,1)S(1)} %collective-permute-done.32.refs_0_, ...), custom_call_target="tpu_custom_call" | custom-call | flops 1610612736 | bytes 6291456 | tf_op jit(solution)/shard_map/terms/pallas_call | solution.py:285
  172.0 2.3 %terms.26.own_ref = f32[512,256]{1,0:T(8,128)S(1)} custom-call(s32[2]{0:T(128)S(1)} %pad_add_fusion.place_ref, bf16[8,2048,512]{2,1,0:T(8,128)(2,1)S(1)} %get-tuple-element.63.real_ref, bf16[8,2048,512]{2,1,0:T(8,128)(2,1)S(1)} %get-tuple-element.72.imag_ref, bf16[512,256]{1,0:T(8,128)(2,1)S(1)} %collective-permute-done.32.refs_0_, ...), custom_call_target="tpu_custom_call" | custom-call | flops 1610612736 | bytes 6291456 | tf_op jit(solution)/shard_map/terms/pallas_call | solution.py:285
  174.3 3.3 %collective-permute-done.41.refs_2_ = bf16[512,256]{1,0:T(8,128)(2,1)S(1)} collective-permute-done((bf16[512,256]{1,0:T(8,128)(2,1)S(1)}, bf16[512,256]{1,0:T(8,128)(2,1)S(1)}, u32[]{:S(2)}, u32[]{:S(2)}) %collective-permute-start.41) | collective-permute-done | bytes 262176 | tf_op jit(solution)/shard_map/ppermute | solution.py:374
  177.6 4.5 %collective-permute-done.40.refs_1_ = bf16[512,256]{1,0:T(8,128)(2,1)S(1)} collective-permute-done((bf16[512,256]{1,0:T(8,128)(2,1)S(1)}, bf16[512,256]{1,0:T(8,128)(2,1)S(1)}, u32[]{:S(2)}, u32[]{:S(2)}) %collective-permute-start.40) | collective-permute-done | bytes 262176 | tf_op jit(solution)/shard_map/ppermute | solution.py:361
  182.1 2.1 %update.5 = (f32[512,2,128]{2,1,0:T(2,128)}, f32[512,2,128]{2,1,0:T(2,128)}) custom-call(s32[2]{0:T(128)S(1)} %pad_add_fusion.place_ref, f32[2]{0:T(128)S(1)} %copy-done.1, f32[512,256]{1,0:T(8,128)S(1)} %terms.26.own_ref, bf16[512,256]{1,0:T(8,128)(2,1)S(1)} %collective-permute-done.39.other_ref.refs_0_, ...), custom_call_target="tpu_custom_call" | custom-call | flops 2097152 | bytes 2097152 | tf_op jit(solution)/shard_map/update/pallas_call | solution.py:348
  (73 shorter events, 19.5 us)
Async XLA Ops:
  0.7 1.0 copy-start
  1.8 31.5 %copy-start.2 = (s32[2048]{0:T(1024)S(1)}, s32[2048]{0:T(1024)}, u32[]{:S(2)}) copy-start(s32[2048]{0:T(1024)} %param.6) | copy-start | bytes 24580
  25.6 4.9 %collective-permute-start = (bf16[128,128]{1,0:T(8,128)(2,1)S(1)}, bf16[128,128]{1,0:T(8,128)(2,1)S(1)}, u32[]{:S(2)}, u32[]{:S(2)}) collective-permute-start(bf16[128,128]{1,0:T(8,128)(2,1)S(1)} %bitcast.18), channel_id=1, source_target_pairs={{0,4},{4,0},{8,12},{12,8},{16,20},{20,16},{24,28},{28,24},{1,5},{5... | collective-permute-start | bytes 98312 | tf_op jit(solution)/shard_map/ppermute | solution.py:361
  26.1 7.0 %collective-permute-start.1 = (bf16[128,128]{1,0:T(8,128)(2,1)S(1)}, bf16[128,128]{1,0:T(8,128)(2,1)S(1)}, u32[]{:S(2)}, u32[]{:S(2)}) collective-permute-start(bf16[128,128]{1,0:T(8,128)(2,1)S(1)} %bitcast.17), channel_id=1, source_target_pairs={{0,8},{4,12},{8,0},{12,4},{16,24},{20,28},{24,16},{28,20},{1,9},{5... | collective-permute-start | bytes 98312 | tf_op jit(solution)/shard_map/ppermute | solution.py:361
  28.7 4.6 %collective-permute-start.2 = (bf16[128,128]{1,0:T(8,128)(2,1)S(1)}, bf16[128,128]{1,0:T(8,128)(2,1)S(1)}, u32[]{:S(2)}, u32[]{:S(2)}) collective-permute-start(bf16[128,128]{1,0:T(8,128)(2,1)S(1)} %bitcast.16), channel_id=1, source_target_pairs={{0,12},{4,8},{8,4},{12,0},{16,28},{20,24},{24,20},{28,16},{1,13},{... | collective-permute-start | bytes 98312 | tf_op jit(solution)/shard_map/ppermute | solution.py:361
  28.7 4.6 %collective-permute-start.3 = (bf16[128,128]{1,0:T(8,128)(2,1)S(1)}, bf16[128,128]{1,0:T(8,128)(2,1)S(1)}, u32[]{:S(2)}, u32[]{:S(2)}) collective-permute-start(bf16[128,128]{1,0:T(8,128)(2,1)S(1)} %bitcast.15), channel_id=1, source_target_pairs={{0,16},{4,20},{8,24},{12,28},{16,0},{20,4},{24,8},{28,12},{1,17},{... | collective-permute-start | bytes 98312 | tf_op jit(solution)/shard_map/ppermute | solution.py:361
  30.5 3.5 %collective-permute-start.4 = (bf16[128,128]{1,0:T(8,128)(2,1)S(1)}, bf16[128,128]{1,0:T(8,128)(2,1)S(1)}, u32[]{:S(2)}, u32[]{:S(2)}) collective-permute-start(bf16[128,128]{1,0:T(8,128)(2,1)S(1)} %bitcast.14), channel_id=1, source_target_pairs={{0,20},{4,16},{8,28},{12,24},{16,4},{20,0},{24,12},{28,8},{1,21},{... | collective-permute-start | bytes 98312 | tf_op jit(solution)/shard_map/ppermute | solution.py:361
  30.5 4.8 %collective-permute-start.5 = (bf16[128,128]{1,0:T(8,128)(2,1)S(1)}, bf16[128,128]{1,0:T(8,128)(2,1)S(1)}, u32[]{:S(2)}, u32[]{:S(2)}) collective-permute-start(bf16[128,128]{1,0:T(8,128)(2,1)S(1)} %bitcast.13), channel_id=1, source_target_pairs={{0,24},{4,28},{8,16},{12,20},{16,8},{20,12},{24,0},{28,4},{1,25},{... | collective-permute-start | bytes 98312 | tf_op jit(solution)/shard_map/ppermute | solution.py:361
  33.1 4.2 %collective-permute-start.6 = (bf16[128,128]{1,0:T(8,128)(2,1)S(1)}, bf16[128,128]{1,0:T(8,128)(2,1)S(1)}, u32[]{:S(2)}, u32[]{:S(2)}) collective-permute-start(bf16[128,128]{1,0:T(8,128)(2,1)S(1)} %bitcast.12), channel_id=1, source_target_pairs={{0,28},{4,24},{8,20},{12,16},{16,12},{20,8},{24,4},{28,0},{1,29},{... | collective-permute-start | bytes 98312 | tf_op jit(solution)/shard_map/ppermute | solution.py:361
  40.5 12.1 %collective-permute-start.7 = (bf16[256,128]{1,0:T(8,128)(2,1)S(1)}, bf16[256,128]{1,0:T(8,128)(2,1)S(1)}, u32[]{:S(2)}, u32[]{:S(2)}) collective-permute-start(bf16[256,128]{1,0:T(8,128)(2,1)S(1)} %get-tuple-element.73), channel_id=1, source_target_pairs={{0,1},{1,0},{2,3},{3,2},{4,5},{5,4},{6,7},{7,6},{8,9},{9,8},{10,11... | collective-permute-start | bytes 196616 | tf_op jit(solution)/shard_map/ppermute | solution.py:361
  42.2 10.5 %collective-permute-start.8 = (bf16[256,128]{1,0:T(8,128)(2,1)S(1)}, bf16[256,128]{1,0:T(8,128)(2,1)S(1)}, u32[]{:S(2)}, u32[]{:S(2)}) collective-permute-start(bf16[256,128]{1,0:T(8,128)(2,1)S(1)} %get-tuple-element.74), channel_id=1, source_target_pairs={{0,2},{1,3},{2,0},{3,1},{4,6},{5,7},{6,4},{7,5},{8,10},{9,11},{10,... | collective-permute-start | bytes 196616 | tf_op jit(solution)/shard_map/ppermute | solution.py:361
  44.7 7.9 %collective-permute-start.9 = (bf16[256,128]{1,0:T(8,128)(2,1)S(1)}, bf16[256,128]{1,0:T(8,128)(2,1)S(1)}, u32[]{:S(2)}, u32[]{:S(2)}) collective-permute-start(bf16[256,128]{1,0:T(8,128)(2,1)S(1)} %get-tuple-element.75), channel_id=1, source_target_pairs={{0,3},{1,2},{2,1},{3,0},{4,7},{5,6},{6,5},{7,4},{8,11},{9,10},{10,... | collective-permute-start | bytes 196616 | tf_op jit(solution)/shard_map/ppermute | solution.py:361
  53.7 11.6 %collective-permute-start.13 = (bf16[512,256]{1,0:T(8,128)(2,1)S(1)}, bf16[512,256]{1,0:T(8,128)(2,1)S(1)}, u32[]{:S(2)}, u32[]{:S(2)}) collective-permute-start(bf16[512,256]{1,0:T(8,128)(2,1)S(1)} %panel.1.refs_0_.refs_4_), channel_id=1, source_target_pairs={{0,4},{4,0},{8,12},{12,8},{16,20},{20,16},{24,28},{28,24},{1,5},{5... | collective-permute-start | bytes 786440 | tf_op jit(solution)/shard_map/ppermute | solution.py:361
  53.7 14.4 %collective-permute-start.12 = (bf16[512,256]{1,0:T(8,128)(2,1)S(1)}, bf16[512,256]{1,0:T(8,128)(2,1)S(1)}, u32[]{:S(2)}, u32[]{:S(2)}) collective-permute-start(bf16[512,256]{1,0:T(8,128)(2,1)S(1)} %panel.1.refs_0_.refs_4_), channel_id=1, source_target_pairs={{0,24},{4,28},{8,16},{12,20},{16,8},{20,12},{24,0},{28,4},{1,25},{... | collective-permute-start | bytes 786440 | tf_op jit(solution)/shard_map/ppermute | solution.py:361
  54.9 14.0 %collective-permute-start.11 = (bf16[512,256]{1,0:T(8,128)(2,1)S(1)}, bf16[512,256]{1,0:T(8,128)(2,1)S(1)}, u32[]{:S(2)}, u32[]{:S(2)}) collective-permute-start(bf16[512,256]{1,0:T(8,128)(2,1)S(1)} %panel.1.refs_0_.refs_4_), channel_id=1, source_target_pairs={{0,16},{4,20},{8,24},{12,28},{16,0},{20,4},{24,8},{28,12},{1,17},{... | collective-permute-start | bytes 786440 | tf_op jit(solution)/shard_map/ppermute | solution.py:361
  55.8 13.1 %collective-permute-start.10 = (bf16[512,256]{1,0:T(8,128)(2,1)S(1)}, bf16[512,256]{1,0:T(8,128)(2,1)S(1)}, u32[]{:S(2)}, u32[]{:S(2)}) collective-permute-start(bf16[512,256]{1,0:T(8,128)(2,1)S(1)} %panel.1.refs_0_.refs_4_), channel_id=1, source_target_pairs={{0,8},{4,12},{8,0},{12,4},{16,24},{20,28},{24,16},{28,20},{1,9},{5... | collective-permute-start | bytes 786440 | tf_op jit(solution)/shard_map/ppermute | solution.py:361
  68.9 1.5 collective-permute-start.14
  68.9 1.9 %collective-permute-start.15 = (bf16[512,256]{1,0:T(8,128)(2,1)S(1)}, bf16[512,256]{1,0:T(8,128)(2,1)S(1)}, u32[]{:S(2)}, u32[]{:S(2)}) collective-permute-start(bf16[512,256]{1,0:T(8,128)(2,1)S(1)} %collective-permute-done.11.refs_1_), channel_id=1, source_target_pairs={{0,4},{4,0},{8,12},{12,8},{16,20},{20,16},{24,28},{28,24},{1,5},{5... | collective-permute-start | bytes 786440 | tf_op jit(solution)/shard_map/ppermute | solution.py:361
  69.4 1.8 collective-permute-start.16
  73.5 10.3 %collective-permute-start.17 = (bf16[512,256]{1,0:T(8,128)(2,1)S(1)}, bf16[512,256]{1,0:T(8,128)(2,1)S(1)}, u32[]{:S(2)}, u32[]{:S(2)}) collective-permute-start(bf16[512,256]{1,0:T(8,128)(2,1)S(1)} %terms.17), channel_id=1, source_target_pairs={{0,1},{1,3},{3,2},{2,0},{4,5},{5,7},{7,6},{6,4},{8,9},{9,11},{11,1... | collective-permute-start | bytes 786440 | tf_op jit(solution)/shard_map/ppermute | solution.py:369
  76.6 18.4 %copy-start.1 = (f32[2]{0:T(128)S(1)}, f32[2]{0:T(128)}, u32[]{:S(2)}) copy-start(f32[2]{0:T(128)} %wave_ref.5) | copy-start | bytes 28
  76.6 15.5 %collective-permute-start.19 = (bf16[512,256]{1,0:T(8,128)(2,1)S(1)}, bf16[512,256]{1,0:T(8,128)(2,1)S(1)}, u32[]{:S(2)}, u32[]{:S(2)}) collective-permute-start(bf16[512,256]{1,0:T(8,128)(2,1)S(1)} %get-tuple-element.90), channel_id=1, source_target_pairs={{0,3},{3,0},{4,7},{7,4},{8,11},{11,8},{12,15},{15,12},{16,19},{19,... | collective-permute-start | bytes 786440 | tf_op jit(solution)/shard_map/ppermute | solution.py:374
  83.9 11.1 %collective-permute-start.18 = (bf16[512,256]{1,0:T(8,128)(2,1)S(1)}, bf16[512,256]{1,0:T(8,128)(2,1)S(1)}, u32[]{:S(2)}, u32[]{:S(2)}) collective-permute-start(bf16[512,256]{1,0:T(8,128)(2,1)S(1)} %terms.19), channel_id=1, source_target_pairs={{0,1},{1,0},{2,3},{3,2},{4,5},{5,4},{6,7},{7,6},{8,9},{9,8},{10,11... | collective-permute-start | bytes 786440 | tf_op jit(solution)/shard_map/ppermute | solution.py:361
  88.9 6.1 %collective-permute-start.20 = (bf16[512,256]{1,0:T(8,128)(2,1)S(1)}, bf16[512,256]{1,0:T(8,128)(2,1)S(1)}, u32[]{:S(2)}, u32[]{:S(2)}) collective-permute-start(bf16[512,256]{1,0:T(8,128)(2,1)S(1)} %sum.3), channel_id=1, source_target_pairs={{1,2},{2,1},{5,6},{6,5},{9,10},{10,9},{13,14},{14,13},{17,18},{18,... | collective-permute-start | bytes 786440 | tf_op jit(solution)/shard_map/ppermute | solution.py:375
  95.8 3.6 %collective-permute-start.24 = (bf16[512,256]{1,0:T(8,128)(2,1)S(1)}, bf16[512,256]{1,0:T(8,128)(2,1)S(1)}, u32[]{:S(2)}, u32[]{:S(2)}) collective-permute-start(bf16[512,256]{1,0:T(8,128)(2,1)S(1)} %update.3.refs_0_), channel_id=1, source_target_pairs={{0,4},{4,0},{8,12},{12,8},{16,20},{20,16},{24,28},{28,24},{1,5},{5... | collective-permute-start | bytes 786440 | tf_op jit(solution)/shard_map/ppermute | solution.py:361
  95.9 10.1 %collective-permute-start.23 = (bf16[512,256]{1,0:T(8,128)(2,1)S(1)}, bf16[512,256]{1,0:T(8,128)(2,1)S(1)}, u32[]{:S(2)}, u32[]{:S(2)}) collective-permute-start(bf16[512,256]{1,0:T(8,128)(2,1)S(1)} %update.3.refs_0_), channel_id=1, source_target_pairs={{0,24},{4,28},{8,16},{12,20},{16,8},{20,12},{24,0},{28,4},{1,25},{... | collective-permute-start | bytes 786440 | tf_op jit(solution)/shard_map/ppermute | solution.py:361
  97.2 14.0 %collective-permute-start.22 = (bf16[512,256]{1,0:T(8,128)(2,1)S(1)}, bf16[512,256]{1,0:T(8,128)(2,1)S(1)}, u32[]{:S(2)}, u32[]{:S(2)}) collective-permute-start(bf16[512,256]{1,0:T(8,128)(2,1)S(1)} %update.3.refs_0_), channel_id=1, source_target_pairs={{0,16},{4,20},{8,24},{12,28},{16,0},{20,4},{24,8},{28,12},{1,17},{... | collective-permute-start | bytes 786440 | tf_op jit(solution)/shard_map/ppermute | solution.py:361
  98.1 13.1 %collective-permute-start.21 = (bf16[512,256]{1,0:T(8,128)(2,1)S(1)}, bf16[512,256]{1,0:T(8,128)(2,1)S(1)}, u32[]{:S(2)}, u32[]{:S(2)}) collective-permute-start(bf16[512,256]{1,0:T(8,128)(2,1)S(1)} %update.3.refs_0_), channel_id=1, source_target_pairs={{0,8},{4,12},{8,0},{12,4},{16,24},{20,28},{24,16},{28,20},{1,9},{5... | collective-permute-start | bytes 786440 | tf_op jit(solution)/shard_map/ppermute | solution.py:361
  111.2 1.5 collective-permute-start.25
  111.2 1.9 %collective-permute-start.26 = (bf16[512,256]{1,0:T(8,128)(2,1)S(1)}, bf16[512,256]{1,0:T(8,128)(2,1)S(1)}, u32[]{:S(2)}, u32[]{:S(2)}) collective-permute-start(bf16[512,256]{1,0:T(8,128)(2,1)S(1)} %collective-permute-done.22.refs_1_), channel_id=1, source_target_pairs={{0,4},{4,0},{8,12},{12,8},{16,20},{20,16},{24,28},{28,24},{1,5},{5... | collective-permute-start | bytes 786440 | tf_op jit(solution)/shard_map/ppermute | solution.py:361
  111.7 1.8 collective-permute-start.27
  115.8 13.9 %collective-permute-start.28 = (bf16[512,256]{1,0:T(8,128)(2,1)S(1)}, bf16[512,256]{1,0:T(8,128)(2,1)S(1)}, u32[]{:S(2)}, u32[]{:S(2)}) collective-permute-start(bf16[512,256]{1,0:T(8,128)(2,1)S(1)} %terms.22), channel_id=1, source_target_pairs={{0,1},{1,3},{3,2},{2,0},{4,5},{5,7},{7,6},{6,4},{8,9},{9,11},{11,1... | collective-permute-start | bytes 786440 | tf_op jit(solution)/shard_map/ppermute | solution.py:369
  122.5 13.2 %collective-permute-start.30 = (bf16[512,256]{1,0:T(8,128)(2,1)S(1)}, bf16[512,256]{1,0:T(8,128)(2,1)S(1)}, u32[]{:S(2)}, u32[]{:S(2)}) collective-permute-start(bf16[512,256]{1,0:T(8,128)(2,1)S(1)} %get-tuple-element.105), channel_id=1, source_target_pairs={{0,3},{3,0},{4,7},{7,4},{8,11},{11,8},{12,15},{15,12},{16,19},{19,... | collective-permute-start | bytes 786440 | tf_op jit(solution)/shard_map/ppermute | solution.py:374
  129.8 10.9 %collective-permute-start.29 = (bf16[512,256]{1,0:T(8,128)(2,1)S(1)}, bf16[512,256]{1,0:T(8,128)(2,1)S(1)}, u32[]{:S(2)}, u32[]{:S(2)}) collective-permute-start(bf16[512,256]{1,0:T(8,128)(2,1)S(1)} %terms.24), channel_id=1, source_target_pairs={{0,1},{1,0},{2,3},{3,2},{4,5},{5,4},{6,7},{7,6},{8,9},{9,8},{10,11... | collective-permute-start | bytes 786440 | tf_op jit(solution)/shard_map/ppermute | solution.py:361
  129.8 10.8 %collective-permute-start.31 = (bf16[512,256]{1,0:T(8,128)(2,1)S(1)}, bf16[512,256]{1,0:T(8,128)(2,1)S(1)}, u32[]{:S(2)}, u32[]{:S(2)}) collective-permute-start(bf16[512,256]{1,0:T(8,128)(2,1)S(1)} %sum.4), channel_id=1, source_target_pairs={{1,2},{2,1},{5,6},{6,5},{9,10},{10,9},{13,14},{14,13},{17,18},{18,... | collective-permute-start | bytes 786440 | tf_op jit(solution)/shard_map/ppermute | solution.py:375
  141.5 3.6 %collective-permute-start.35 = (bf16[512,256]{1,0:T(8,128)(2,1)S(1)}, bf16[512,256]{1,0:T(8,128)(2,1)S(1)}, u32[]{:S(2)}, u32[]{:S(2)}) collective-permute-start(bf16[512,256]{1,0:T(8,128)(2,1)S(1)} %update.4.refs_0_), channel_id=1, source_target_pairs={{0,4},{4,0},{8,12},{12,8},{16,20},{20,16},{24,28},{28,24},{1,5},{5... | collective-permute-start | bytes 786440 | tf_op jit(solution)/shard_map/ppermute | solution.py:361
  141.5 10.1 %collective-permute-start.34 = (bf16[512,256]{1,0:T(8,128)(2,1)S(1)}, bf16[512,256]{1,0:T(8,128)(2,1)S(1)}, u32[]{:S(2)}, u32[]{:S(2)}) collective-permute-start(bf16[512,256]{1,0:T(8,128)(2,1)S(1)} %update.4.refs_0_), channel_id=1, source_target_pairs={{0,24},{4,28},{8,16},{12,20},{16,8},{20,12},{24,0},{28,4},{1,25},{... | collective-permute-start | bytes 786440 | tf_op jit(solution)/shard_map/ppermute | solution.py:361
  142.8 14.0 %collective-permute-start.33 = (bf16[512,256]{1,0:T(8,128)(2,1)S(1)}, bf16[512,256]{1,0:T(8,128)(2,1)S(1)}, u32[]{:S(2)}, u32[]{:S(2)}) collective-permute-start(bf16[512,256]{1,0:T(8,128)(2,1)S(1)} %update.4.refs_0_), channel_id=1, source_target_pairs={{0,16},{4,20},{8,24},{12,28},{16,0},{20,4},{24,8},{28,12},{1,17},{... | collective-permute-start | bytes 786440 | tf_op jit(solution)/shard_map/ppermute | solution.py:361
  143.7 13.1 %collective-permute-start.32 = (bf16[512,256]{1,0:T(8,128)(2,1)S(1)}, bf16[512,256]{1,0:T(8,128)(2,1)S(1)}, u32[]{:S(2)}, u32[]{:S(2)}) collective-permute-start(bf16[512,256]{1,0:T(8,128)(2,1)S(1)} %update.4.refs_0_), channel_id=1, source_target_pairs={{0,8},{4,12},{8,0},{12,4},{16,24},{20,28},{24,16},{28,20},{1,9},{5... | collective-permute-start | bytes 786440 | tf_op jit(solution)/shard_map/ppermute | solution.py:361
  156.8 1.5 collective-permute-start.36
  156.8 1.9 %collective-permute-start.37 = (bf16[512,256]{1,0:T(8,128)(2,1)S(1)}, bf16[512,256]{1,0:T(8,128)(2,1)S(1)}, u32[]{:S(2)}, u32[]{:S(2)}) collective-permute-start(bf16[512,256]{1,0:T(8,128)(2,1)S(1)} %collective-permute-done.33.refs_1_), channel_id=1, source_target_pairs={{0,4},{4,0},{8,12},{12,8},{16,20},{20,16},{24,28},{28,24},{1,5},{5... | collective-permute-start | bytes 786440 | tf_op jit(solution)/shard_map/ppermute | solution.py:361
  157.3 1.8 collective-permute-start.38
  161.4 9.7 %collective-permute-start.39 = (bf16[512,256]{1,0:T(8,128)(2,1)S(1)}, bf16[512,256]{1,0:T(8,128)(2,1)S(1)}, u32[]{:S(2)}, u32[]{:S(2)}) collective-permute-start(bf16[512,256]{1,0:T(8,128)(2,1)S(1)} %terms.27), channel_id=1, source_target_pairs={{0,1},{1,3},{3,2},{2,0},{4,5},{5,7},{7,6},{6,4},{8,9},{9,11},{11,1... | collective-permute-start | bytes 786440 | tf_op jit(solution)/shard_map/ppermute | solution.py:369
  164.7 12.9 %collective-permute-start.41 = (bf16[512,256]{1,0:T(8,128)(2,1)S(1)}, bf16[512,256]{1,0:T(8,128)(2,1)S(1)}, u32[]{:S(2)}, u32[]{:S(2)}) collective-permute-start(bf16[512,256]{1,0:T(8,128)(2,1)S(1)} %get-tuple-element.120), channel_id=1, source_target_pairs={{0,3},{3,0},{4,7},{7,4},{8,11},{11,8},{12,15},{15,12},{16,19},{19,... | collective-permute-start | bytes 786440 | tf_op jit(solution)/shard_map/ppermute | solution.py:374
  171.2 10.9 %collective-permute-start.40 = (bf16[512,256]{1,0:T(8,128)(2,1)S(1)}, bf16[512,256]{1,0:T(8,128)(2,1)S(1)}, u32[]{:S(2)}, u32[]{:S(2)}) collective-permute-start(bf16[512,256]{1,0:T(8,128)(2,1)S(1)} %terms.29), channel_id=1, source_target_pairs={{0,1},{1,0},{2,3},{3,2},{4,5},{5,4},{6,7},{7,6},{8,9},{9,8},{10,11... | collective-permute-start | bytes 786440 | tf_op jit(solution)/shard_map/ppermute | solution.py:361
  171.3 10.8 %collective-permute-start.42 = (bf16[512,256]{1,0:T(8,128)(2,1)S(1)}, bf16[512,256]{1,0:T(8,128)(2,1)S(1)}, u32[]{:S(2)}, u32[]{:S(2)}) collective-permute-start(bf16[512,256]{1,0:T(8,128)(2,1)S(1)} %sum.5), channel_id=1, source_target_pairs={{1,2},{2,1},{5,6},{6,5},{9,10},{10,9},{13,14},{14,13},{17,18},{18,... | collective-permute-start | bytes 786440 | tf_op jit(solution)/shard_map/ppermute | solution.py:375

commit v4 on v3

--- a/solution.py
+++ b/solution.py
@@ -368,27 +368,29 @@
         return make(0, [f32])[0], arriving, False
     first = lax.ppermute(make(2, [bf16])[0], "src", [(0, 1), (1, 3), (3, 2), (2, 0)])
     sent, kept = make(3, [bf16, f32])
-    near = make(1, [bf16])[0]
-    both, near = lax.optimization_barrier((make_sum(kept, first), near))
-    beside = swap(near, "src", 1)
+    beside = swap(make(1, [bf16])[0], "src", 1)
     outer = lax.ppermute(sent, "src", [(0, 3), (3, 0)])
-    inner = lax.ppermute(both, "src", [(1, 2), (2, 1)])
+    inner = lax.ppermute(make_sum(kept, first), "src", [(1, 2), (2, 1)])
     return make(0, [f32])[0], [first, beside, outer, inner], True
 
 
-def iterate(estimate, data, place, n_row, n_src, slice_rows):
-    direct = {turn: swap(estimate, "row", turn) for turn in range(2, n_row, 2)}
-    first = {0: estimate, 1: swap(estimate, "row", 1)}
-    turns = tuple(range(n_src))
-    begun = make_terms(data, place, first, turns, [], slice_rows, [jnp.float32])
-    held = lax.optimization_barrier((*direct.values(), *begun))
-    direct, begun = dict(zip(direct, held)), held[len(direct) :]
-    passed = {turn + 1: swap(piece, "row", 1) for turn, piece in direct.items()}
+def iterate(estimate, data, place, n_row, n_src, slice_rows, fresh):
+    turns = range(2, n_row, 2)
+    direct = {turn: swap(estimate, "row", turn) for turn in (reversed(turns) if fresh else turns)}
+    if fresh:
+        real_data, *held = lax.optimization_barrier((data[0], *direct.values()))
+        data, direct = (real_data, data[1]), dict(zip(direct, held))
+    passed = {turn + 1: swap(piece, "row", 1) for turn, piece in {0: estimate, **direct}.items()}
+    early = {0: estimate, 1: passed[1], **direct}
+    late = {turn: passed[turn] for turn in range(n_row - 1, 1, -2)}
+    begun = make_terms(data, place, early, (n_src // 2,), [], slice_rows, [jnp.float32])
 
     def make(turn, types):
-        return make_terms(data, place, {**direct, **passed}, (turn,), [begun[turn]], slice_rows, types)
-
-    return exchange(n_src, make)
+        if turn == n_src // 2:
+            return make_terms(data, place, late, (turn,), begun, slice_rows, types)
+        return make_terms(data, place, {**early, **late}, (turn,), [], slice_rows, types)
+
+    return *exchange(n_src, make), data
 
 
 def body(traces, row_source, slice_data, wavelet_inverse):
@@ -416,8 +418,9 @@
     panel = make_panel(located, place, packs, token)
 
     estimate = panel
+    data = real_data, imag_data
     for iteration in range(ITERS):
-        own, arriving, folded = iterate(estimate, (real_data, imag_data), place, n_row, n_src, slice_rows)
+        own, arriving, folded, data = iterate(estimate, data, place, n_row, n_src, slice_rows, iteration == 0)
         estimate = make_update(place, wavelet_inverse, own, arriving, panel, folded, iteration == ITERS - 1)
     return tuple(estimate)
 

time: 185 us -> 177 us (0.957)
  starting transfers between devices: 51.7 us -> 41.9 us
  waiting for transfers between devices: 46.2 us -> 48.4 us
    ppermute x34, starting transfers between devices: 29.7 us -> 24.5 us  [swap(): lax.ppermute(array, axis, [(index, index ^ bits) for index in range(size)])]
    ppermute x3, starting transfers between devices: 6.07 us -> 1.66 us  [exchange(): lax.ppermute(make(2, [bf16])[0], 'src', [(0, 1), (1, 3), (3, 2), (2, 0)])]
    ppermute x34, waiting for transfers between devices: 40 us -> 43.2 us  [swap(): lax.ppermute(array, axis, [(index, index ^ bits) for index in range(size)])]
  transfers between devices with their start and end apart: 43 -> 43, of which waited for: 22 -> 14; matrix products, arithmetic and copies ran while one was open for 0% -> 0% of each run, Pallas kernels for 25% -> 27%
where the time goes in v4:
time: 177 us
  Pallas kernels  83.8 us (47%)
  waiting for transfers between devices  48.4 us (27%)
  starting transfers between devices  41.9 us (24%)
    ppermute x34, waiting for transfers between devices, swap(): lax.ppermute(array, axis, [(index, index ^ bits) for index in range(size)])  43.2 us
    pallas_call x15, Pallas kernels, make_terms(): pl.pallas_call(functools.partial(terms_kernel, turns, numbers, len(partia...  36.6 us
    ppermute x34, starting transfers between devices, swap(): lax.ppermute(array, axis, [(index, index ^ bits) for index in range(size)])  24.5 us
    pallas_call x1, Pallas kernels, make_spectra(): pl.pallas_call(functools.partial(spectra_kernel, packs, n_row), in_specs=...  23.8 us
    pallas_call x2, Pallas kernels, relay(): pl.pallas_call(functools.partial(relay_kernel, part), in_specs=[ANY, ANY]...  15.7 us
    ppermute x3, starting transfers between devices, exchange(): outer = lax.ppermute(sent, 'src', [(0, 3), (3, 0)])  13.5 us
    ppermute x3, waiting for transfers between devices, exchange(): outer = lax.ppermute(sent, 'src', [(0, 3), (3, 0)])  5.18 us
    pallas_call x3, Pallas kernels, make_update(): pl.pallas_call(functools.partial(last_kernel if last else estimate_kernel...  3.77 us
  transfers between devices with their start and end apart: 43, of which 14 were waited for; matrix products, arithmetic and copies ran while one was open for 0% of the time, Pallas kernels for 27%

profile of v4, /device:TPU:0, one launch (start us, length us, event | category | flops | bytes accessed | tf_op | source)
XLA Modules:
  0.0 176.7 jit_solution(6856931638760561277)
XLA Ops:
  0.7 1.0 copy-done
  1.8 23.8 %spectra.1 = (bf16[2,64,128]{2,1,0:T(8,128)(2,1)S(1)}, bf16[2,64,128]{2,1,0:T(8,128)(2,1)S(1)}, bf16[2,64,128]{2,1,0:T(8,128)(2,1)S(1)}, bf16[2,64,128]{2,1,0:T(...) custom-call(s32[2]{0:T(128)S(1)} %pad_add_fusion.place_ref, ...), custom_call_target="tpu_custom_call" | custom-call | flops 8589934592 | bytes 67108864 | tf_op jit(solution)/shard_map/spectra/pallas_call | solution.py:121
  26.1 2.6 %collective-permute-start.1 = (bf16[128,128]{1,0:T(8,128)(2,1)S(1)}, bf16[128,128]{1,0:T(8,128)(2,1)S(1)}, u32[]{:S(2)}, u32[]{:S(2)}) collective-permute-start(bf16[128,128]{1,0:T(8,128)(2,1)S(1)} %bitcast.17), channel_id=1, source_target_pairs={{0,8},{4,12},{8,0},{12,4},{16,24},{20,28},{24,16},{28,20},{1,9},{5... | collective-permute-start | bytes 98312 | tf_op jit(solution)/shard_map/ppermute | solution.py:361
  28.7 1.8 %collective-permute-start.3 = (bf16[128,128]{1,0:T(8,128)(2,1)S(1)}, bf16[128,128]{1,0:T(8,128)(2,1)S(1)}, u32[]{:S(2)}, u32[]{:S(2)}) collective-permute-start(bf16[128,128]{1,0:T(8,128)(2,1)S(1)} %bitcast.15), channel_id=1, source_target_pairs={{0,16},{4,20},{8,24},{12,28},{16,0},{20,4},{24,8},{28,12},{1,17},{... | collective-permute-start | bytes 98312 | tf_op jit(solution)/shard_map/ppermute | solution.py:361
  30.5 2.6 %collective-permute-start.5 = (bf16[128,128]{1,0:T(8,128)(2,1)S(1)}, bf16[128,128]{1,0:T(8,128)(2,1)S(1)}, u32[]{:S(2)}, u32[]{:S(2)}) collective-permute-start(bf16[128,128]{1,0:T(8,128)(2,1)S(1)} %bitcast.13), channel_id=1, source_target_pairs={{0,24},{4,28},{8,16},{12,20},{16,8},{20,12},{24,0},{28,4},{1,25},{... | collective-permute-start | bytes 98312 | tf_op jit(solution)/shard_map/ppermute | solution.py:361
  34.0 1.4 collective-permute-done.5.refs_6_
  35.3 2.0 %collective-permute-done.6.refs_7_ = bf16[128,128]{1,0:T(8,128)(2,1)S(1)} collective-permute-done((bf16[128,128]{1,0:T(8,128)(2,1)S(1)}, bf16[128,128]{1,0:T(8,128)(2,1)S(1)}, u32[]{:S(2)}, u32[]{:S(2)}) %collective-permute-start.6) | collective-permute-done | bytes 32800 | tf_op jit(solution)/shard_map/ppermute | solution.py:361
  37.7 2.8 %order.1 = (bf16[256,128]{1,0:T(8,128)(2,1)S(1)}, bf16[256,128]{1,0:T(8,128)(2,1)S(1)}, bf16[256,128]{1,0:T(8,128)(2,1)S(1)}, bf16[256,128]{1,0:T(8,128)(2,1)S(1)}) custom-call(s32[2]{0:T(128)S(1)} %pad_add_fusion.place_ref, s32[2048,128]{1,0:T(8,128)S(1)} %broadcast_in_dim.2.code_ref, bf16[128,128]{1,0:T(8,128)(2,1)S(1)} %bitcast.10, ...), custom_call_target="tpu_custom_call" | custom-call | flops 1073741824 | bytes 1048576 | tf_op jit(solution)/shard_map/order/pallas_call | solution.py:173
  40.5 1.6 collective-permute-start.7
  42.2 2.6 %collective-permute-start.8 = (bf16[256,128]{1,0:T(8,128)(2,1)S(1)}, bf16[256,128]{1,0:T(8,128)(2,1)S(1)}, u32[]{:S(2)}, u32[]{:S(2)}) collective-permute-start(bf16[256,128]{1,0:T(8,128)(2,1)S(1)} %get-tuple-element.38), channel_id=1, source_target_pairs={{0,2},{1,3},{2,0},{3,1},{4,6},{5,7},{6,4},{7,5},{8,10},{9,11},{10,... | collective-permute-start | bytes 196616 | tf_op jit(solution)/shard_map/ppermute | solution.py:361
  45.0 7.7 %relay.3 = (bf16[8,2048,512]{2,1,0:T(8,128)(2,1)S(1)}, f32[8,128]{1,0:T(8,128)S(1)}) custom-call(bf16[2,2048,8,512]{3,2,1,0:T(8,128)(2,1)} %data_ref.3, bf16[256,128]{1,0:T(8,128)(2,1)S(1)} %get-tuple-element.36.after_ref.refs_0_), custom_call_target="tpu_custom_call" | custom-call | bytes 33554432 | tf_op jit(solution)/shard_map/relay/pallas_call | solution.py:236
  53.7 1.1 collective-permute-start.10
  55.7 1.5 collective-permute-start.12
  57.2 8.0 %relay.2 = (bf16[8,2048,512]{2,1,0:T(8,128)(2,1)S(1)}, f32[8,128]{1,0:T(8,128)}) custom-call(bf16[2,2048,8,512]{3,2,1,0:T(8,128)(2,1)} %data_ref.3, bf16[128,128]{1,0:T(8,128)(2,1)S(1)} %bitcast.11), custom_call_target="tpu_custom_call" | custom-call | bytes 33554432 | tf_op jit(solution)/shard_map/relay/pallas_call | solution.py:236
  65.2 2.5 %collective-permute-done.11.refs_3_ = bf16[512,256]{1,0:T(8,128)(2,1)S(1)} collective-permute-done((bf16[512,256]{1,0:T(8,128)(2,1)S(1)}, bf16[512,256]{1,0:T(8,128)(2,1)S(1)}, u32[]{:S(2)}, u32[]{:S(2)}) %collective-permute-start.11) | collective-permute-done | bytes 262176 | tf_op jit(solution)/shard_map/ppermute | solution.py:361
  68.2 2.1 %terms.16.refs_3_ = f32[512,256]{1,0:T(8,128)S(1)} custom-call(s32[2]{0:T(128)S(1)} %pad_add_fusion.place_ref, bf16[8,2048,512]{2,1,0:T(8,128)(2,1)S(1)} %get-tuple-element.41.real_ref, bf16[8,2048,512]{2,1,0:T(8,128)(2,1)S(1)} %get-tuple-element.42.imag_ref, bf16[512,256]{1,0:T(8,128)(2,1)S(1)} %panel.1.refs_0_.refs_4_, ...), custom_call_target="tpu_custom_call" | custom-call | flops 1342177280 | bytes 5242880 | tf_op jit(solution)/shard_map/terms/pallas_call | solution.py:285
  70.3 1.5 terms.17
  72.5 2.9 %terms.19 = (bf16[512,256]{1,0:T(8,128)(2,1)S(1)}, f32[512,256]{1,0:T(8,128)S(1)}) custom-call(s32[2]{0:T(128)S(1)} %pad_add_fusion.place_ref, bf16[8,2048,512]{2,1,0:T(8,128)(2,1)S(1)} %get-tuple-element.41.real_ref, bf16[8,2048,512]{2,1,0:T(8,128)(2,1)S(1)} %get-tuple-element.42.imag_ref, bf16[512,256]{1,0:T(8,128)(2,1)S(1)} %panel.1.refs_0_.refs_4_, ...), custom_call_target="tpu_custom_call" | custom-call | flops 2147483648 | bytes 8388608 | tf_op jit(solution)/shard_map/terms/pallas_call | solution.py:285
  75.4 4.8 %collective-permute-start.19 = (bf16[512,256]{1,0:T(8,128)(2,1)S(1)}, bf16[512,256]{1,0:T(8,128)(2,1)S(1)}, u32[]{:S(2)}, u32[]{:S(2)}) collective-permute-start(bf16[512,256]{1,0:T(8,128)(2,1)S(1)} %get-tuple-element.46), channel_id=1, source_target_pairs={{0,3},{3,0},{4,7},{7,4},{8,11},{11,8},{12,15},{15,12},{16,19},{19,... | collective-permute-start | bytes 786440 | tf_op jit(solution)/shard_map/ppermute | solution.py:372
  80.3 2.9 %terms.18 = bf16[512,256]{1,0:T(8,128)(2,1)S(1)} custom-call(s32[2]{0:T(128)S(1)} %pad_add_fusion.place_ref, bf16[8,2048,512]{2,1,0:T(8,128)(2,1)S(1)} %get-tuple-element.41.real_ref, bf16[8,2048,512]{2,1,0:T(8,128)(2,1)S(1)} %get-tuple-element.42.imag_ref, bf16[512,256]{1,0:T(8,128)(2,1)S(1)} %panel.1.refs_0_.refs_4_, ...), custom_call_target="tpu_custom_call" | custom-call | flops 2147483648 | bytes 8388608 | tf_op jit(solution)/shard_map/terms/pallas_call | solution.py:285
  84.2 2.9 %terms.15.own_ref = f32[512,256]{1,0:T(8,128)S(1)} custom-call(s32[2]{0:T(128)S(1)} %pad_add_fusion.place_ref, bf16[8,2048,512]{2,1,0:T(8,128)(2,1)S(1)} %get-tuple-element.41.real_ref, bf16[8,2048,512]{2,1,0:T(8,128)(2,1)S(1)} %get-tuple-element.42.imag_ref, bf16[512,256]{1,0:T(8,128)(2,1)S(1)} %panel.1.refs_0_.refs_4_, ...), custom_call_target="tpu_custom_call" | custom-call | flops 2147483648 | bytes 8388608 | tf_op jit(solution)/shard_map/terms/pallas_call | solution.py:285
  87.0 1.3 collective-permute-done.19.refs_2_
  88.3 5.3 %collective-permute-done.18.refs_1_ = bf16[512,256]{1,0:T(8,128)(2,1)S(1)} collective-permute-done((bf16[512,256]{1,0:T(8,128)(2,1)S(1)}, bf16[512,256]{1,0:T(8,128)(2,1)S(1)}, u32[]{:S(2)}, u32[]{:S(2)}) %collective-permute-start.18) | collective-permute-done | bytes 262176 | tf_op jit(solution)/shard_map/ppermute | solution.py:361
  94.5 1.2 collective-permute-start.24
  96.7 1.3 collective-permute-start.22
  98.0 6.6 %collective-permute-done.24.refs_4_ = bf16[512,256]{1,0:T(8,128)(2,1)S(1)} collective-permute-done((bf16[512,256]{1,0:T(8,128)(2,1)S(1)}, bf16[512,256]{1,0:T(8,128)(2,1)S(1)}, u32[]{:S(2)}, u32[]{:S(2)}) %collective-permute-start.24) | collective-permute-done | bytes 262176 | tf_op jit(solution)/shard_map/ppermute | solution.py:361
  104.7 4.7 %collective-permute-done.23.refs_3_ = bf16[512,256]{1,0:T(8,128)(2,1)S(1)} collective-permute-done((bf16[512,256]{1,0:T(8,128)(2,1)S(1)}, bf16[512,256]{1,0:T(8,128)(2,1)S(1)}, u32[]{:S(2)}, u32[]{:S(2)}) %collective-permute-start.23) | collective-permute-done | bytes 262176 | tf_op jit(solution)/shard_map/ppermute | solution.py:361
  109.8 2.1 %terms.21.refs_3_ = f32[512,256]{1,0:T(8,128)S(1)} custom-call(s32[2]{0:T(128)S(1)} %pad_add_fusion.place_ref, bf16[8,2048,512]{2,1,0:T(8,128)(2,1)S(1)} %get-tuple-element.41.real_ref, bf16[8,2048,512]{2,1,0:T(8,128)(2,1)S(1)} %get-tuple-element.42.imag_ref, bf16[512,256]{1,0:T(8,128)(2,1)S(1)} %update.3.refs_0_, ...), custom_call_target="tpu_custom_call" | custom-call | flops 1342177280 | bytes 5242880 | tf_op jit(solution)/shard_map/terms/pallas_call | solution.py:285
  111.9 1.5 terms.22
  114.3 2.9 %terms.24 = (bf16[512,256]{1,0:T(8,128)(2,1)S(1)}, f32[512,256]{1,0:T(8,128)S(1)}) custom-call(s32[2]{0:T(128)S(1)} %pad_add_fusion.place_ref, bf16[8,2048,512]{2,1,0:T(8,128)(2,1)S(1)} %get-tuple-element.41.real_ref, bf16[8,2048,512]{2,1,0:T(8,128)(2,1)S(1)} %get-tuple-element.42.imag_ref, bf16[512,256]{1,0:T(8,128)(2,1)S(1)} %update.3.refs_0_, ...), custom_call_target="tpu_custom_call" | custom-call | flops 2147483648 | bytes 8388608 | tf_op jit(solution)/shard_map/terms/pallas_call | solution.py:285
  117.1 4.2 %collective-permute-start.30 = (bf16[512,256]{1,0:T(8,128)(2,1)S(1)}, bf16[512,256]{1,0:T(8,128)(2,1)S(1)}, u32[]{:S(2)}, u32[]{:S(2)}) collective-permute-start(bf16[512,256]{1,0:T(8,128)(2,1)S(1)} %get-tuple-element.48), channel_id=1, source_target_pairs={{0,3},{3,0},{4,7},{7,4},{8,11},{11,8},{12,15},{15,12},{16,19},{19,... | collective-permute-start | bytes 786440 | tf_op jit(solution)/shard_map/ppermute | solution.py:372
  121.4 2.9 %terms.23 = bf16[512,256]{1,0:T(8,128)(2,1)S(1)} custom-call(s32[2]{0:T(128)S(1)} %pad_add_fusion.place_ref, bf16[8,2048,512]{2,1,0:T(8,128)(2,1)S(1)} %get-tuple-element.41.real_ref, bf16[8,2048,512]{2,1,0:T(8,128)(2,1)S(1)} %get-tuple-element.42.imag_ref, bf16[512,256]{1,0:T(8,128)(2,1)S(1)} %update.3.refs_0_, ...), custom_call_target="tpu_custom_call" | custom-call | flops 2147483648 | bytes 8388608 | tf_op jit(solution)/shard_map/terms/pallas_call | solution.py:285
  125.1 2.9 %terms.20.own_ref = f32[512,256]{1,0:T(8,128)S(1)} custom-call(s32[2]{0:T(128)S(1)} %pad_add_fusion.place_ref, bf16[8,2048,512]{2,1,0:T(8,128)(2,1)S(1)} %get-tuple-element.41.real_ref, bf16[8,2048,512]{2,1,0:T(8,128)(2,1)S(1)} %get-tuple-element.42.imag_ref, bf16[512,256]{1,0:T(8,128)(2,1)S(1)} %update.3.refs_0_, ...), custom_call_target="tpu_custom_call" | custom-call | flops 2147483648 | bytes 8388608 | tf_op jit(solution)/shard_map/terms/pallas_call | solution.py:285
  128.0 2.1 %collective-permute-done.30.refs_2_ = bf16[512,256]{1,0:T(8,128)(2,1)S(1)} collective-permute-done((bf16[512,256]{1,0:T(8,128)(2,1)S(1)}, bf16[512,256]{1,0:T(8,128)(2,1)S(1)}, u32[]{:S(2)}, u32[]{:S(2)}) %collective-permute-start.30) | collective-permute-done | bytes 262176 | tf_op jit(solution)/shard_map/ppermute | solution.py:372
  130.0 4.3 %collective-permute-done.29.refs_1_ = bf16[512,256]{1,0:T(8,128)(2,1)S(1)} collective-permute-done((bf16[512,256]{1,0:T(8,128)(2,1)S(1)}, bf16[512,256]{1,0:T(8,128)(2,1)S(1)}, u32[]{:S(2)}, u32[]{:S(2)}) %collective-permute-start.29) | collective-permute-done | bytes 262176 | tf_op jit(solution)/shard_map/ppermute | solution.py:361
  135.2 1.3 collective-permute-start.35
  137.4 1.3 collective-permute-start.33
  138.8 6.6 %collective-permute-done.35.refs_4_ = bf16[512,256]{1,0:T(8,128)(2,1)S(1)} collective-permute-done((bf16[512,256]{1,0:T(8,128)(2,1)S(1)}, bf16[512,256]{1,0:T(8,128)(2,1)S(1)}, u32[]{:S(2)}, u32[]{:S(2)}) %collective-permute-start.35) | collective-permute-done | bytes 262176 | tf_op jit(solution)/shard_map/ppermute | solution.py:361
  145.4 4.5 %collective-permute-done.34.refs_3_ = bf16[512,256]{1,0:T(8,128)(2,1)S(1)} collective-permute-done((bf16[512,256]{1,0:T(8,128)(2,1)S(1)}, bf16[512,256]{1,0:T(8,128)(2,1)S(1)}, u32[]{:S(2)}, u32[]{:S(2)}) %collective-permute-start.34) | collective-permute-done | bytes 262176 | tf_op jit(solution)/shard_map/ppermute | solution.py:361
  150.4 2.1 %terms.26.refs_3_ = f32[512,256]{1,0:T(8,128)S(1)} custom-call(s32[2]{0:T(128)S(1)} %pad_add_fusion.place_ref, bf16[8,2048,512]{2,1,0:T(8,128)(2,1)S(1)} %get-tuple-element.41.real_ref, bf16[8,2048,512]{2,1,0:T(8,128)(2,1)S(1)} %get-tuple-element.42.imag_ref, bf16[512,256]{1,0:T(8,128)(2,1)S(1)} %update.4.refs_0_, ...), custom_call_target="tpu_custom_call" | custom-call | flops 1342177280 | bytes 5242880 | tf_op jit(solution)/shard_map/terms/pallas_call | solution.py:285
  152.5 1.5 terms.27
  154.3 2.9 %terms.29 = (bf16[512,256]{1,0:T(8,128)(2,1)S(1)}, f32[512,256]{1,0:T(8,128)S(1)}) custom-call(s32[2]{0:T(128)S(1)} %pad_add_fusion.place_ref, bf16[8,2048,512]{2,1,0:T(8,128)(2,1)S(1)} %get-tuple-element.41.real_ref, bf16[8,2048,512]{2,1,0:T(8,128)(2,1)S(1)} %get-tuple-element.42.imag_ref, bf16[512,256]{1,0:T(8,128)(2,1)S(1)} %update.4.refs_0_, ...), custom_call_target="tpu_custom_call" | custom-call | flops 2147483648 | bytes 8388608 | tf_op jit(solution)/shard_map/terms/pallas_call | solution.py:285
  157.2 4.5 %collective-permute-start.41 = (bf16[512,256]{1,0:T(8,128)(2,1)S(1)}, bf16[512,256]{1,0:T(8,128)(2,1)S(1)}, u32[]{:S(2)}, u32[]{:S(2)}) collective-permute-start(bf16[512,256]{1,0:T(8,128)(2,1)S(1)} %get-tuple-element.50), channel_id=1, source_target_pairs={{0,3},{3,0},{4,7},{7,4},{8,11},{11,8},{12,15},{15,12},{16,19},{19,... | collective-permute-start | bytes 786440 | tf_op jit(solution)/shard_map/ppermute | solution.py:372
  161.6 2.9 %terms.28 = bf16[512,256]{1,0:T(8,128)(2,1)S(1)} custom-call(s32[2]{0:T(128)S(1)} %pad_add_fusion.place_ref, bf16[8,2048,512]{2,1,0:T(8,128)(2,1)S(1)} %get-tuple-element.41.real_ref, bf16[8,2048,512]{2,1,0:T(8,128)(2,1)S(1)} %get-tuple-element.42.imag_ref, bf16[512,256]{1,0:T(8,128)(2,1)S(1)} %update.4.refs_0_, ...), custom_call_target="tpu_custom_call" | custom-call | flops 2147483648 | bytes 8388608 | tf_op jit(solution)/shard_map/terms/pallas_call | solution.py:285
  165.4 2.9 %terms.25.own_ref = f32[512,256]{1,0:T(8,128)S(1)} custom-call(s32[2]{0:T(128)S(1)} %pad_add_fusion.place_ref, bf16[8,2048,512]{2,1,0:T(8,128)(2,1)S(1)} %get-tuple-element.41.real_ref, bf16[8,2048,512]{2,1,0:T(8,128)(2,1)S(1)} %get-tuple-element.42.imag_ref, bf16[512,256]{1,0:T(8,128)(2,1)S(1)} %update.4.refs_0_, ...), custom_call_target="tpu_custom_call" | custom-call | flops 2147483648 | bytes 8388608 | tf_op jit(solution)/shard_map/terms/pallas_call | solution.py:285
  168.2 1.8 %collective-permute-done.41.refs_2_ = bf16[512,256]{1,0:T(8,128)(2,1)S(1)} collective-permute-done((bf16[512,256]{1,0:T(8,128)(2,1)S(1)}, bf16[512,256]{1,0:T(8,128)(2,1)S(1)}, u32[]{:S(2)}, u32[]{:S(2)}) %collective-permute-start.41) | collective-permute-done | bytes 262176 | tf_op jit(solution)/shard_map/ppermute | solution.py:372
  170.1 4.5 %collective-permute-done.40.refs_1_ = bf16[512,256]{1,0:T(8,128)(2,1)S(1)} collective-permute-done((bf16[512,256]{1,0:T(8,128)(2,1)S(1)}, bf16[512,256]{1,0:T(8,128)(2,1)S(1)}, u32[]{:S(2)}, u32[]{:S(2)}) %collective-permute-start.40) | collective-permute-done | bytes 262176 | tf_op jit(solution)/shard_map/ppermute | solution.py:361
  174.6 2.1 %update.5 = (f32[512,2,128]{2,1,0:T(2,128)}, f32[512,2,128]{2,1,0:T(2,128)}) custom-call(s32[2]{0:T(128)S(1)} %pad_add_fusion.place_ref, f32[2]{0:T(128)S(1)} %copy-done.1, f32[512,256]{1,0:T(8,128)S(1)} %terms.25.own_ref, bf16[512,256]{1,0:T(8,128)(2,1)S(1)} %collective-permute-done.39.other_ref.refs_0_, ...), custom_call_target="tpu_custom_call" | custom-call | flops 2097152 | bytes 2097152 | tf_op jit(solution)/shard_map/update/pallas_call | solution.py:348
  (73 shorter events, 13.4 us)
Async XLA Ops:
  0.7 1.0 copy-start
  1.8 31.5 %copy-start.2 = (s32[2048]{0:T(1024)S(1)}, s32[2048]{0:T(1024)}, u32[]{:S(2)}) copy-start(s32[2048]{0:T(1024)} %param.6) | copy-start | bytes 24580
  25.6 4.9 %collective-permute-start = (bf16[128,128]{1,0:T(8,128)(2,1)S(1)}, bf16[128,128]{1,0:T(8,128)(2,1)S(1)}, u32[]{:S(2)}, u32[]{:S(2)}) collective-permute-start(bf16[128,128]{1,0:T(8,128)(2,1)S(1)} %bitcast.18), channel_id=1, source_target_pairs={{0,4},{4,0},{8,12},{12,8},{16,20},{20,16},{24,28},{28,24},{1,5},{5... | collective-permute-start | bytes 98312 | tf_op jit(solution)/shard_map/ppermute | solution.py:361
  26.1 7.0 %collective-permute-start.1 = (bf16[128,128]{1,0:T(8,128)(2,1)S(1)}, bf16[128,128]{1,0:T(8,128)(2,1)S(1)}, u32[]{:S(2)}, u32[]{:S(2)}) collective-permute-start(bf16[128,128]{1,0:T(8,128)(2,1)S(1)} %bitcast.17), channel_id=1, source_target_pairs={{0,8},{4,12},{8,0},{12,4},{16,24},{20,28},{24,16},{28,20},{1,9},{5... | collective-permute-start | bytes 98312 | tf_op jit(solution)/shard_map/ppermute | solution.py:361
  28.7 4.6 %collective-permute-start.2 = (bf16[128,128]{1,0:T(8,128)(2,1)S(1)}, bf16[128,128]{1,0:T(8,128)(2,1)S(1)}, u32[]{:S(2)}, u32[]{:S(2)}) collective-permute-start(bf16[128,128]{1,0:T(8,128)(2,1)S(1)} %bitcast.16), channel_id=1, source_target_pairs={{0,12},{4,8},{8,4},{12,0},{16,28},{20,24},{24,20},{28,16},{1,13},{... | collective-permute-start | bytes 98312 | tf_op jit(solution)/shard_map/ppermute | solution.py:361
  28.7 4.6 %collective-permute-start.3 = (bf16[128,128]{1,0:T(8,128)(2,1)S(1)}, bf16[128,128]{1,0:T(8,128)(2,1)S(1)}, u32[]{:S(2)}, u32[]{:S(2)}) collective-permute-start(bf16[128,128]{1,0:T(8,128)(2,1)S(1)} %bitcast.15), channel_id=1, source_target_pairs={{0,16},{4,20},{8,24},{12,28},{16,0},{20,4},{24,8},{28,12},{1,17},{... | collective-permute-start | bytes 98312 | tf_op jit(solution)/shard_map/ppermute | solution.py:361
  30.5 3.5 %collective-permute-start.4 = (bf16[128,128]{1,0:T(8,128)(2,1)S(1)}, bf16[128,128]{1,0:T(8,128)(2,1)S(1)}, u32[]{:S(2)}, u32[]{:S(2)}) collective-permute-start(bf16[128,128]{1,0:T(8,128)(2,1)S(1)} %bitcast.14), channel_id=1, source_target_pairs={{0,20},{4,16},{8,28},{12,24},{16,4},{20,0},{24,12},{28,8},{1,21},{... | collective-permute-start | bytes 98312 | tf_op jit(solution)/shard_map/ppermute | solution.py:361
  30.5 4.8 %collective-permute-start.5 = (bf16[128,128]{1,0:T(8,128)(2,1)S(1)}, bf16[128,128]{1,0:T(8,128)(2,1)S(1)}, u32[]{:S(2)}, u32[]{:S(2)}) collective-permute-start(bf16[128,128]{1,0:T(8,128)(2,1)S(1)} %bitcast.13), channel_id=1, source_target_pairs={{0,24},{4,28},{8,16},{12,20},{16,8},{20,12},{24,0},{28,4},{1,25},{... | collective-permute-start | bytes 98312 | tf_op jit(solution)/shard_map/ppermute | solution.py:361
  33.1 4.2 %collective-permute-start.6 = (bf16[128,128]{1,0:T(8,128)(2,1)S(1)}, bf16[128,128]{1,0:T(8,128)(2,1)S(1)}, u32[]{:S(2)}, u32[]{:S(2)}) collective-permute-start(bf16[128,128]{1,0:T(8,128)(2,1)S(1)} %bitcast.12), channel_id=1, source_target_pairs={{0,28},{4,24},{8,20},{12,16},{16,12},{20,8},{24,4},{28,0},{1,29},{... | collective-permute-start | bytes 98312 | tf_op jit(solution)/shard_map/ppermute | solution.py:361
  40.5 12.1 %collective-permute-start.7 = (bf16[256,128]{1,0:T(8,128)(2,1)S(1)}, bf16[256,128]{1,0:T(8,128)(2,1)S(1)}, u32[]{:S(2)}, u32[]{:S(2)}) collective-permute-start(bf16[256,128]{1,0:T(8,128)(2,1)S(1)} %get-tuple-element.37), channel_id=1, source_target_pairs={{0,1},{1,0},{2,3},{3,2},{4,5},{5,4},{6,7},{7,6},{8,9},{9,8},{10,11... | collective-permute-start | bytes 196616 | tf_op jit(solution)/shard_map/ppermute | solution.py:361
  42.2 10.5 %collective-permute-start.8 = (bf16[256,128]{1,0:T(8,128)(2,1)S(1)}, bf16[256,128]{1,0:T(8,128)(2,1)S(1)}, u32[]{:S(2)}, u32[]{:S(2)}) collective-permute-start(bf16[256,128]{1,0:T(8,128)(2,1)S(1)} %get-tuple-element.38), channel_id=1, source_target_pairs={{0,2},{1,3},{2,0},{3,1},{4,6},{5,7},{6,4},{7,5},{8,10},{9,11},{10,... | collective-permute-start | bytes 196616 | tf_op jit(solution)/shard_map/ppermute | solution.py:361
  44.7 7.9 %collective-permute-start.9 = (bf16[256,128]{1,0:T(8,128)(2,1)S(1)}, bf16[256,128]{1,0:T(8,128)(2,1)S(1)}, u32[]{:S(2)}, u32[]{:S(2)}) collective-permute-start(bf16[256,128]{1,0:T(8,128)(2,1)S(1)} %get-tuple-element.39), channel_id=1, source_target_pairs={{0,3},{1,2},{2,1},{3,0},{4,7},{5,6},{6,5},{7,4},{8,11},{9,10},{10,... | collective-permute-start | bytes 196616 | tf_op jit(solution)/shard_map/ppermute | solution.py:361
  53.7 11.5 %collective-permute-start.10 = (bf16[512,256]{1,0:T(8,128)(2,1)S(1)}, bf16[512,256]{1,0:T(8,128)(2,1)S(1)}, u32[]{:S(2)}, u32[]{:S(2)}) collective-permute-start(bf16[512,256]{1,0:T(8,128)(2,1)S(1)} %panel.1.refs_0_.refs_4_), channel_id=1, source_target_pairs={{0,24},{4,28},{8,16},{12,20},{16,8},{20,12},{24,0},{28,4},{1,25},{... | collective-permute-start | bytes 786440 | tf_op jit(solution)/shard_map/ppermute | solution.py:361
  54.8 12.9 %collective-permute-start.11 = (bf16[512,256]{1,0:T(8,128)(2,1)S(1)}, bf16[512,256]{1,0:T(8,128)(2,1)S(1)}, u32[]{:S(2)}, u32[]{:S(2)}) collective-permute-start(bf16[512,256]{1,0:T(8,128)(2,1)S(1)} %panel.1.refs_0_.refs_4_), channel_id=1, source_target_pairs={{0,16},{4,20},{8,24},{12,28},{16,0},{20,4},{24,8},{28,12},{1,17},{... | collective-permute-start | bytes 786440 | tf_op jit(solution)/shard_map/ppermute | solution.py:361
  55.7 12.0 %collective-permute-start.12 = (bf16[512,256]{1,0:T(8,128)(2,1)S(1)}, bf16[512,256]{1,0:T(8,128)(2,1)S(1)}, u32[]{:S(2)}, u32[]{:S(2)}) collective-permute-start(bf16[512,256]{1,0:T(8,128)(2,1)S(1)} %panel.1.refs_0_.refs_4_), channel_id=1, source_target_pairs={{0,8},{4,12},{8,0},{12,4},{16,24},{20,28},{24,16},{28,20},{1,9},{5... | collective-permute-start | bytes 786440 | tf_op jit(solution)/shard_map/ppermute | solution.py:361
  57.2 11.0 %collective-permute-start.13 = (bf16[512,256]{1,0:T(8,128)(2,1)S(1)}, bf16[512,256]{1,0:T(8,128)(2,1)S(1)}, u32[]{:S(2)}, u32[]{:S(2)}) collective-permute-start(bf16[512,256]{1,0:T(8,128)(2,1)S(1)} %panel.1.refs_0_.refs_4_), channel_id=1, source_target_pairs={{0,4},{4,0},{8,12},{12,8},{16,20},{20,16},{24,28},{28,24},{1,5},{5... | collective-permute-start | bytes 786440 | tf_op jit(solution)/shard_map/ppermute | solution.py:361
  67.7 2.6 %collective-permute-start.14 = (bf16[512,256]{1,0:T(8,128)(2,1)S(1)}, bf16[512,256]{1,0:T(8,128)(2,1)S(1)}, u32[]{:S(2)}, u32[]{:S(2)}) collective-permute-start(bf16[512,256]{1,0:T(8,128)(2,1)S(1)} %collective-permute-done.10.refs_2_), channel_id=1, source_target_pairs={{0,4},{4,0},{8,12},{12,8},{16,20},{20,16},{24,28},{28,24},{1,5},{5... | collective-permute-start | bytes 786440 | tf_op jit(solution)/shard_map/ppermute | solution.py:361
  67.7 2.6 %collective-permute-start.15 = (bf16[512,256]{1,0:T(8,128)(2,1)S(1)}, bf16[512,256]{1,0:T(8,128)(2,1)S(1)}, u32[]{:S(2)}, u32[]{:S(2)}) collective-permute-start(bf16[512,256]{1,0:T(8,128)(2,1)S(1)} %collective-permute-done.11.refs_3_), channel_id=1, source_target_pairs={{0,4},{4,0},{8,12},{12,8},{16,20},{20,16},{24,28},{28,24},{1,5},{5... | collective-permute-start | bytes 786440 | tf_op jit(solution)/shard_map/ppermute | solution.py:361
  68.2 2.1 %collective-permute-start.16 = (bf16[512,256]{1,0:T(8,128)(2,1)S(1)}, bf16[512,256]{1,0:T(8,128)(2,1)S(1)}, u32[]{:S(2)}, u32[]{:S(2)}) collective-permute-start(bf16[512,256]{1,0:T(8,128)(2,1)S(1)} %collective-permute-done.12.refs_4_), channel_id=1, source_target_pairs={{0,4},{4,0},{8,12},{12,8},{16,20},{20,16},{24,28},{28,24},{1,5},{5... | collective-permute-start | bytes 786440 | tf_op jit(solution)/shard_map/ppermute | solution.py:361
  71.8 11.4 %collective-permute-start.17 = (bf16[512,256]{1,0:T(8,128)(2,1)S(1)}, bf16[512,256]{1,0:T(8,128)(2,1)S(1)}, u32[]{:S(2)}, u32[]{:S(2)}) collective-permute-start(bf16[512,256]{1,0:T(8,128)(2,1)S(1)} %terms.17), channel_id=1, source_target_pairs={{0,1},{1,3},{3,2},{2,0},{4,5},{5,7},{7,6},{6,4},{8,9},{9,11},{11,1... | collective-permute-start | bytes 786440 | tf_op jit(solution)/shard_map/ppermute | solution.py:369
  75.4 18.3 %copy-start.1 = (f32[2]{0:T(128)S(1)}, f32[2]{0:T(128)}, u32[]{:S(2)}) copy-start(f32[2]{0:T(128)} %wave_ref.5) | copy-start | bytes 28
  75.4 12.9 %collective-permute-start.19 = (bf16[512,256]{1,0:T(8,128)(2,1)S(1)}, bf16[512,256]{1,0:T(8,128)(2,1)S(1)}, u32[]{:S(2)}, u32[]{:S(2)}) collective-permute-start(bf16[512,256]{1,0:T(8,128)(2,1)S(1)} %get-tuple-element.46), channel_id=1, source_target_pairs={{0,3},{3,0},{4,7},{7,4},{8,11},{11,8},{12,15},{15,12},{16,19},{19,... | collective-permute-start | bytes 786440 | tf_op jit(solution)/shard_map/ppermute | solution.py:372
  83.1 10.5 %collective-permute-start.18 = (bf16[512,256]{1,0:T(8,128)(2,1)S(1)}, bf16[512,256]{1,0:T(8,128)(2,1)S(1)}, u32[]{:S(2)}, u32[]{:S(2)}) collective-permute-start(bf16[512,256]{1,0:T(8,128)(2,1)S(1)} %terms.18), channel_id=1, source_target_pairs={{0,1},{1,0},{2,3},{3,2},{4,5},{5,4},{6,7},{7,6},{8,9},{9,8},{10,11... | collective-permute-start | bytes 786440 | tf_op jit(solution)/shard_map/ppermute | solution.py:361
  83.3 10.4 %collective-permute-start.20 = (bf16[512,256]{1,0:T(8,128)(2,1)S(1)}, bf16[512,256]{1,0:T(8,128)(2,1)S(1)}, u32[]{:S(2)}, u32[]{:S(2)}) collective-permute-start(bf16[512,256]{1,0:T(8,128)(2,1)S(1)} %sum.3), channel_id=1, source_target_pairs={{1,2},{2,1},{5,6},{6,5},{9,10},{10,9},{13,14},{14,13},{17,18},{18,... | collective-permute-start | bytes 786440 | tf_op jit(solution)/shard_map/ppermute | solution.py:373
  94.5 10.2 %collective-permute-start.24 = (bf16[512,256]{1,0:T(8,128)(2,1)S(1)}, bf16[512,256]{1,0:T(8,128)(2,1)S(1)}, u32[]{:S(2)}, u32[]{:S(2)}) collective-permute-start(bf16[512,256]{1,0:T(8,128)(2,1)S(1)} %update.3.refs_0_), channel_id=1, source_target_pairs={{0,24},{4,28},{8,16},{12,20},{16,8},{20,12},{24,0},{28,4},{1,25},{... | collective-permute-start | bytes 786440 | tf_op jit(solution)/shard_map/ppermute | solution.py:361
  95.7 13.6 %collective-permute-start.23 = (bf16[512,256]{1,0:T(8,128)(2,1)S(1)}, bf16[512,256]{1,0:T(8,128)(2,1)S(1)}, u32[]{:S(2)}, u32[]{:S(2)}) collective-permute-start(bf16[512,256]{1,0:T(8,128)(2,1)S(1)} %update.3.refs_0_), channel_id=1, source_target_pairs={{0,16},{4,20},{8,24},{12,28},{16,0},{20,4},{24,8},{28,12},{1,17},{... | collective-permute-start | bytes 786440 | tf_op jit(solution)/shard_map/ppermute | solution.py:361
  96.7 12.6 %collective-permute-start.22 = (bf16[512,256]{1,0:T(8,128)(2,1)S(1)}, bf16[512,256]{1,0:T(8,128)(2,1)S(1)}, u32[]{:S(2)}, u32[]{:S(2)}) collective-permute-start(bf16[512,256]{1,0:T(8,128)(2,1)S(1)} %update.3.refs_0_), channel_id=1, source_target_pairs={{0,8},{4,12},{8,0},{12,4},{16,24},{20,28},{24,16},{28,20},{1,9},{5... | collective-permute-start | bytes 786440 | tf_op jit(solution)/shard_map/ppermute | solution.py:361
  98.0 11.8 %collective-permute-start.21 = (bf16[512,256]{1,0:T(8,128)(2,1)S(1)}, bf16[512,256]{1,0:T(8,128)(2,1)S(1)}, u32[]{:S(2)}, u32[]{:S(2)}) collective-permute-start(bf16[512,256]{1,0:T(8,128)(2,1)S(1)} %update.3.refs_0_), channel_id=1, source_target_pairs={{0,4},{4,0},{8,12},{12,8},{16,20},{20,16},{24,28},{28,24},{1,5},{5... | collective-permute-start | bytes 786440 | tf_op jit(solution)/shard_map/ppermute | solution.py:361
  104.7 7.3 %collective-permute-start.25 = (bf16[512,256]{1,0:T(8,128)(2,1)S(1)}, bf16[512,256]{1,0:T(8,128)(2,1)S(1)}, u32[]{:S(2)}, u32[]{:S(2)}) collective-permute-start(bf16[512,256]{1,0:T(8,128)(2,1)S(1)} %collective-permute-done.24.refs_4_), channel_id=1, source_target_pairs={{0,4},{4,0},{8,12},{12,8},{16,20},{20,16},{24,28},{28,24},{1,5},{5... | collective-permute-start | bytes 786440 | tf_op jit(solution)/shard_map/ppermute | solution.py:361
  109.3 2.6 %collective-permute-start.26 = (bf16[512,256]{1,0:T(8,128)(2,1)S(1)}, bf16[512,256]{1,0:T(8,128)(2,1)S(1)}, u32[]{:S(2)}, u32[]{:S(2)}) collective-permute-start(bf16[512,256]{1,0:T(8,128)(2,1)S(1)} %collective-permute-done.23.refs_3_), channel_id=1, source_target_pairs={{0,4},{4,0},{8,12},{12,8},{16,20},{20,16},{24,28},{28,24},{1,5},{5... | collective-permute-start | bytes 786440 | tf_op jit(solution)/shard_map/ppermute | solution.py:361
  109.3 2.6 %collective-permute-start.27 = (bf16[512,256]{1,0:T(8,128)(2,1)S(1)}, bf16[512,256]{1,0:T(8,128)(2,1)S(1)}, u32[]{:S(2)}, u32[]{:S(2)}) collective-permute-start(bf16[512,256]{1,0:T(8,128)(2,1)S(1)} %collective-permute-done.22.refs_2_), channel_id=1, source_target_pairs={{0,4},{4,0},{8,12},{12,8},{16,20},{20,16},{24,28},{28,24},{1,5},{5... | collective-permute-start | bytes 786440 | tf_op jit(solution)/shard_map/ppermute | solution.py:361
  113.5 10.9 %collective-permute-start.28 = (bf16[512,256]{1,0:T(8,128)(2,1)S(1)}, bf16[512,256]{1,0:T(8,128)(2,1)S(1)}, u32[]{:S(2)}, u32[]{:S(2)}) collective-permute-start(bf16[512,256]{1,0:T(8,128)(2,1)S(1)} %terms.22), channel_id=1, source_target_pairs={{0,1},{1,3},{3,2},{2,0},{4,5},{5,7},{7,6},{6,4},{8,9},{9,11},{11,1... | collective-permute-start | bytes 786440 | tf_op jit(solution)/shard_map/ppermute | solution.py:369
  117.1 12.9 %collective-permute-start.30 = (bf16[512,256]{1,0:T(8,128)(2,1)S(1)}, bf16[512,256]{1,0:T(8,128)(2,1)S(1)}, u32[]{:S(2)}, u32[]{:S(2)}) collective-permute-start(bf16[512,256]{1,0:T(8,128)(2,1)S(1)} %get-tuple-element.48), channel_id=1, source_target_pairs={{0,3},{3,0},{4,7},{7,4},{8,11},{11,8},{12,15},{15,12},{16,19},{19,... | collective-permute-start | bytes 786440 | tf_op jit(solution)/shard_map/ppermute | solution.py:372
  124.3 10.1 %collective-permute-start.29 = (bf16[512,256]{1,0:T(8,128)(2,1)S(1)}, bf16[512,256]{1,0:T(8,128)(2,1)S(1)}, u32[]{:S(2)}, u32[]{:S(2)}) collective-permute-start(bf16[512,256]{1,0:T(8,128)(2,1)S(1)} %terms.23), channel_id=1, source_target_pairs={{0,1},{1,0},{2,3},{3,2},{4,5},{5,4},{6,7},{7,6},{8,9},{9,8},{10,11... | collective-permute-start | bytes 786440 | tf_op jit(solution)/shard_map/ppermute | solution.py:361
  124.4 10.0 %collective-permute-start.31 = (bf16[512,256]{1,0:T(8,128)(2,1)S(1)}, bf16[512,256]{1,0:T(8,128)(2,1)S(1)}, u32[]{:S(2)}, u32[]{:S(2)}) collective-permute-start(bf16[512,256]{1,0:T(8,128)(2,1)S(1)} %sum.4), channel_id=1, source_target_pairs={{1,2},{2,1},{5,6},{6,5},{9,10},{10,9},{13,14},{14,13},{17,18},{18,... | collective-permute-start | bytes 786440 | tf_op jit(solution)/shard_map/ppermute | solution.py:373
  135.2 10.2 %collective-permute-start.35 = (bf16[512,256]{1,0:T(8,128)(2,1)S(1)}, bf16[512,256]{1,0:T(8,128)(2,1)S(1)}, u32[]{:S(2)}, u32[]{:S(2)}) collective-permute-start(bf16[512,256]{1,0:T(8,128)(2,1)S(1)} %update.4.refs_0_), channel_id=1, source_target_pairs={{0,24},{4,28},{8,16},{12,20},{16,8},{20,12},{24,0},{28,4},{1,25},{... | collective-permute-start | bytes 786440 | tf_op jit(solution)/shard_map/ppermute | solution.py:361
  136.5 13.5 %collective-permute-start.34 = (bf16[512,256]{1,0:T(8,128)(2,1)S(1)}, bf16[512,256]{1,0:T(8,128)(2,1)S(1)}, u32[]{:S(2)}, u32[]{:S(2)}) collective-permute-start(bf16[512,256]{1,0:T(8,128)(2,1)S(1)} %update.4.refs_0_), channel_id=1, source_target_pairs={{0,16},{4,20},{8,24},{12,28},{16,0},{20,4},{24,8},{28,12},{1,17},{... | collective-permute-start | bytes 786440 | tf_op jit(solution)/shard_map/ppermute | solution.py:361
  137.4 12.5 %collective-permute-start.33 = (bf16[512,256]{1,0:T(8,128)(2,1)S(1)}, bf16[512,256]{1,0:T(8,128)(2,1)S(1)}, u32[]{:S(2)}, u32[]{:S(2)}) collective-permute-start(bf16[512,256]{1,0:T(8,128)(2,1)S(1)} %update.4.refs_0_), channel_id=1, source_target_pairs={{0,8},{4,12},{8,0},{12,4},{16,24},{20,28},{24,16},{28,20},{1,9},{5... | collective-permute-start | bytes 786440 | tf_op jit(solution)/shard_map/ppermute | solution.py:361
  138.8 11.7 %collective-permute-start.32 = (bf16[512,256]{1,0:T(8,128)(2,1)S(1)}, bf16[512,256]{1,0:T(8,128)(2,1)S(1)}, u32[]{:S(2)}, u32[]{:S(2)}) collective-permute-start(bf16[512,256]{1,0:T(8,128)(2,1)S(1)} %update.4.refs_0_), channel_id=1, source_target_pairs={{0,4},{4,0},{8,12},{12,8},{16,20},{20,16},{24,28},{28,24},{1,5},{5... | collective-permute-start | bytes 786440 | tf_op jit(solution)/shard_map/ppermute | solution.py:361
  145.4 7.1 %collective-permute-start.36 = (bf16[512,256]{1,0:T(8,128)(2,1)S(1)}, bf16[512,256]{1,0:T(8,128)(2,1)S(1)}, u32[]{:S(2)}, u32[]{:S(2)}) collective-permute-start(bf16[512,256]{1,0:T(8,128)(2,1)S(1)} %collective-permute-done.35.refs_4_), channel_id=1, source_target_pairs={{0,4},{4,0},{8,12},{12,8},{16,20},{20,16},{24,28},{28,24},{1,5},{5... | collective-permute-start | bytes 786440 | tf_op jit(solution)/shard_map/ppermute | solution.py:361
  149.9 2.6 %collective-permute-start.37 = (bf16[512,256]{1,0:T(8,128)(2,1)S(1)}, bf16[512,256]{1,0:T(8,128)(2,1)S(1)}, u32[]{:S(2)}, u32[]{:S(2)}) collective-permute-start(bf16[512,256]{1,0:T(8,128)(2,1)S(1)} %collective-permute-done.34.refs_3_), channel_id=1, source_target_pairs={{0,4},{4,0},{8,12},{12,8},{16,20},{20,16},{24,28},{28,24},{1,5},{5... | collective-permute-start | bytes 786440 | tf_op jit(solution)/shard_map/ppermute | solution.py:361
  149.9 2.6 %collective-permute-start.38 = (bf16[512,256]{1,0:T(8,128)(2,1)S(1)}, bf16[512,256]{1,0:T(8,128)(2,1)S(1)}, u32[]{:S(2)}, u32[]{:S(2)}) collective-permute-start(bf16[512,256]{1,0:T(8,128)(2,1)S(1)} %collective-permute-done.33.refs_2_), channel_id=1, source_target_pairs={{0,4},{4,0},{8,12},{12,8},{16,20},{20,16},{24,28},{28,24},{1,5},{5... | collective-permute-start | bytes 786440 | tf_op jit(solution)/shard_map/ppermute | solution.py:361
  154.1 10.5 %collective-permute-start.39 = (bf16[512,256]{1,0:T(8,128)(2,1)S(1)}, bf16[512,256]{1,0:T(8,128)(2,1)S(1)}, u32[]{:S(2)}, u32[]{:S(2)}) collective-permute-start(bf16[512,256]{1,0:T(8,128)(2,1)S(1)} %terms.27), channel_id=1, source_target_pairs={{0,1},{1,3},{3,2},{2,0},{4,5},{5,7},{7,6},{6,4},{8,9},{9,11},{11,1... | collective-permute-start | bytes 786440 | tf_op jit(solution)/shard_map/ppermute | solution.py:369
  157.2 12.9 %collective-permute-start.41 = (bf16[512,256]{1,0:T(8,128)(2,1)S(1)}, bf16[512,256]{1,0:T(8,128)(2,1)S(1)}, u32[]{:S(2)}, u32[]{:S(2)}) collective-permute-start(bf16[512,256]{1,0:T(8,128)(2,1)S(1)} %get-tuple-element.50), channel_id=1, source_target_pairs={{0,3},{3,0},{4,7},{7,4},{8,11},{11,8},{12,15},{15,12},{16,19},{19,... | collective-permute-start | bytes 786440 | tf_op jit(solution)/shard_map/ppermute | solution.py:372
  164.5 10.1 %collective-permute-start.40 = (bf16[512,256]{1,0:T(8,128)(2,1)S(1)}, bf16[512,256]{1,0:T(8,128)(2,1)S(1)}, u32[]{:S(2)}, u32[]{:S(2)}) collective-permute-start(bf16[512,256]{1,0:T(8,128)(2,1)S(1)} %terms.28), channel_id=1, source_target_pairs={{0,1},{1,0},{2,3},{3,2},{4,5},{5,4},{6,7},{7,6},{8,9},{9,8},{10,11... | collective-permute-start | bytes 786440 | tf_op jit(solution)/shard_map/ppermute | solution.py:361
  164.7 9.9 %collective-permute-start.42 = (bf16[512,256]{1,0:T(8,128)(2,1)S(1)}, bf16[512,256]{1,0:T(8,128)(2,1)S(1)}, u32[]{:S(2)}, u32[]{:S(2)}) collective-permute-start(bf16[512,256]{1,0:T(8,128)(2,1)S(1)} %sum.5), channel_id=1, source_target_pairs={{1,2},{2,1},{5,6},{6,5},{9,10},{10,9},{13,14},{14,13},{17,18},{18,... | collective-permute-start | bytes 786440 | tf_op jit(solution)/shard_map/ppermute | solution.py:373

commit v5 on v4

--- a/solution.py
+++ b/solution.py
@@ -68,7 +68,7 @@
 
 def spectra_kernel(packs, n_row, place_ref, traces_ref, table_ref, *refs):
     out_refs = refs[:n_row]
-    held, sems, table, table_sem = refs[n_row:]
+    held, sems, wide, table, table_sem = refs[n_row:]
     block = held.shape[1]
     steps = traces_ref.shape[0] // n_row // block
 
@@ -85,9 +85,10 @@
                 out_ref[step % steps] = packed
 
     def ready():
-        copy = pltpu.make_async_copy(table_ref, table, table_sem)
+        copy = pltpu.make_async_copy(table_ref, wide, table_sem)
         copy.start()
         copy.wait()
+        table[...] = wide[...].astype(table.dtype)
 
     streamed(n_row * steps, source, held, sems, work, ready)
 
@@ -95,14 +96,12 @@
 def spectra_of(packs, traces_ref, table_ref):
     block, shots, samples = traces_ref.shape
     width = 2 * shots
-    half = block // 2
-    shot = lax.broadcasted_iota(jnp.int32, (1, shots, 2 * LANES), 1)
-    lane = lax.broadcasted_iota(jnp.int32, (1, shots, 2 * LANES), 2)
+    shot = lax.broadcasted_iota(jnp.int32, (1, shots, LANES), 1)
+    lane = lax.broadcasted_iota(jnp.int32, (1, shots, LANES), 2)
     own = lane % shots == shot
-    sides = [traces_ref[side * half : (side + 1) * half].reshape(half * shots, samples) for side in range(2)]
-    terms = jnp.dot(jnp.concatenate(sides, axis=1), table_ref[...], preferred_element_type=jnp.float32)
-    rows = jnp.sum(jnp.where(own, terms.reshape(half, shots, 2 * LANES), 0.0), axis=1)
-    spectra = jnp.concatenate([rows[:, :LANES], rows[:, LANES:]], axis=0)
+    traces = traces_ref[...].reshape(block * shots, samples)
+    terms = jnp.dot(traces, table_ref[...], preferred_element_type=jnp.float32)
+    spectra = jnp.sum(jnp.where(own, terms.reshape(block, shots, LANES), 0.0), axis=1)
     short = block // packs
     column = lax.broadcasted_iota(jnp.int32, (short, LANES), 1)
     packed = spectra[:short]
@@ -116,7 +115,7 @@
     steps = block_rows // n_row // block
     short = block // packs
     columns = np.tile(np.repeat(dft_table(samples), shots, axis=1), (1, packs))
-    table = jnp.asarray(np.block([[columns, 0 * columns], [0 * columns, columns]]))
+    table = jnp.asarray(columns.astype(np.float32))
 
     outs = pl.pallas_call(
         functools.partial(spectra_kernel, packs, n_row),
@@ -126,7 +125,8 @@
         scratch_shapes=[
             pltpu.VMEM((BUFFERS, block, shots, samples), jnp.bfloat16),
             pltpu.SemaphoreType.DMA((BUFFERS,)),
-            pltpu.VMEM(table.shape, table.dtype),
+            pltpu.VMEM(table.shape, jnp.float32),
+            pltpu.VMEM(table.shape, jnp.bfloat16),
             pltpu.SemaphoreType.DMA,
         ],
         compiler_params=params(48),
@@ -136,7 +136,32 @@
     return [out.reshape(steps * short, LANES) for out in outs]
 
 
-def order_kernel(packs, n_src, place_ref, code_ref, *refs):
+def hits_kernel(packs, code_ref, after_ref, out_ref):
+    rows, depth = out_ref.shape
+    step = min(rows, 256)
+    column = lax.broadcasted_iota(jnp.int32, (step, LANES), 1)
+    for first in range(0, rows, step):
+        position = code_ref[first : first + step, :] // packs
+        for start in range(0, depth, LANES):
+            size = min(LANES, depth - start)
+            hit = jnp.where(position == column + start, 1.0, 0.0).astype(out_ref.dtype)
+            out_ref[first : first + step, start : start + size] = hit[:, :size]
+
+
+def make_hits(code, depth, packs, after):
+    rows = code.shape[0]
+    return pl.pallas_call(
+        functools.partial(hits_kernel, packs),
+        in_specs=[VMEM, ANY],
+        out_specs=VMEM,
+        out_shape=jax.ShapeDtypeStruct((rows, depth), jnp.bfloat16),
+        compiler_params=params(12),
+        cost_estimate=cost(rows * depth, 2 * rows * depth),
+        name="hits",
+    )(code, after)
+
+
+def order_kernel(packs, n_src, place_ref, code_ref, hits_ref, *refs):
     pieces, out_refs = refs[:-n_src], refs[-n_src:]
     width = LANES // packs
     held = jnp.concatenate([ref[...] for ref in pieces], axis=0)
@@ -144,7 +169,6 @@
         pltpu.roll(held.astype(jnp.float32), turn * width, 1).astype(jnp.bfloat16) for turn in range(1, packs)
     ]
     table = jnp.concatenate(rolled, axis=1)
-    depth = table.shape[0]
     slice_rows = code_ref.shape[0] // n_src
     short = slice_rows // packs
     column = lax.broadcasted_iota(jnp.int32, (short, LANES), 1)
@@ -152,13 +176,9 @@
         first = pl.multiple_of((place_ref[1] ^ turn) * slice_rows, slice_rows)
         packed = None
         for part in range(packs):
-            code = code_ref[pl.ds(pl.multiple_of(first + part * short, short), short), :]
-            position, side = code // packs, code % packs
-            hits = []
-            for start in range(0, depth, LANES):
-                hits.append(jnp.where(position == column + start, 1.0, 0.0).astype(jnp.bfloat16))
-            chosen = jnp.concatenate(hits, axis=1)[:, :depth]
-            rows = jnp.dot(chosen, table, preferred_element_type=jnp.float32)
+            chosen = pl.ds(pl.multiple_of(first + part * short, short), short)
+            side = code_ref[chosen, :] % packs
+            rows = jnp.dot(hits_ref[chosen, :], table, preferred_element_type=jnp.float32)
             moved = rows[:, :LANES]
             for turned in range(1, packs):
                 moved = jnp.where(
@@ -168,17 +188,17 @@
         out_ref[...] = packed.astype(jnp.bfloat16)
 
 
-def make_order(code, pieces, place, n_src, packs):
+def make_order(code, hits, pieces, place, n_src, packs):
     slice_rows = code.shape[0] // n_src
     return pl.pallas_call(
         functools.partial(order_kernel, packs, n_src),
-        in_specs=[SMEM] + [VMEM] * (1 + len(pieces)),
+        in_specs=[SMEM] + [VMEM] * (2 + len(pieces)),
         out_specs=[VMEM] * n_src,
         out_shape=[jax.ShapeDtypeStruct((slice_rows // packs, LANES), jnp.bfloat16)] * n_src,
-        compiler_params=params(8),
-        cost_estimate=cost(2 * code.shape[0] * len(pieces) * pieces[0].size * packs, 4 * code.size),
+        compiler_params=params(12),
+        cost_estimate=cost(2 * hits.size * LANES * packs, 4 * code.size),
         name="order",
-    )(place, code, *pieces)
+    )(place, code, hits, *pieces)
 
 
 def panel_kernel(packs, place_ref, *refs):
@@ -412,7 +432,8 @@
     code = position * packs + inside % block // short
     code = jnp.broadcast_to(code[:, None], (block_rows, LANES))
     real_data, _ = relay(slice_data, 0, spectra[0])
-    ordered = make_order(code, arrived, place, n_src, packs)
+    hits = make_hits(code, block_rows // packs, packs, spectra[0])
+    ordered = make_order(code, hits, arrived, place, n_src, packs)
     located = [ordered[0]] + [swap(ordered[turn], "src", turn) for turn in range(1, n_src)]
     imag_data, token = relay(slice_data, 1, ordered[0])
     panel = make_panel(located, place, packs, token)

time: 177 us -> 176 us (level)
  waiting for transfers between devices: 48.4 us -> 46.5 us
    ppermute x34, waiting for transfers between devices: 43.2 us -> 41.2 us  [swap(): lax.ppermute(array, axis, [(index, index ^ bits) for index in range(size)])]
  transfers between devices with their start and end apart: 43 -> 43, of which waited for: 14 -> 12; matrix products, arithmetic and copies ran while one was open for 0% -> 0% of each run, Pallas kernels for 27% -> 28%
where the time goes in v5:
time: 176 us
  Pallas kernels  85 us (48%)
  waiting for transfers between devices  46.5 us (26%)
  starting transfers between devices  41.9 us (24%)
    ppermute x34, waiting for transfers between devices, swap(): lax.ppermute(array, axis, [(index, index ^ bits) for index in range(size)])  41.2 us
    pallas_call x15, Pallas kernels, make_terms(): pl.pallas_call(functools.partial(terms_kernel, turns, numbers, len(partia...  36.6 us
    ppermute x34, starting transfers between devices, swap(): lax.ppermute(array, axis, [(index, index ^ bits) for index in range(size)])  24.5 us
    pallas_call x1, Pallas kernels, make_spectra(): pl.pallas_call(functools.partial(spectra_kernel, packs, n_row), in_specs=...  23.8 us
    pallas_call x2, Pallas kernels, relay(): pl.pallas_call(functools.partial(relay_kernel, part), in_specs=[ANY, ANY]...  15.7 us
    ppermute x3, starting transfers between devices, exchange(): outer = lax.ppermute(sent, 'src', [(0, 3), (3, 0)])  13.5 us
    ppermute x3, waiting for transfers between devices, exchange(): outer = lax.ppermute(sent, 'src', [(0, 3), (3, 0)])  5.22 us
    pallas_call x3, Pallas kernels, make_update(): pl.pallas_call(functools.partial(last_kernel if last else estimate_kernel...  3.77 us
  transfers between devices with their start and end apart: 43, of which 12 were waited for; matrix products, arithmetic and copies ran while one was open for 0% of the time, Pallas kernels for 28%

profile of v5, /device:TPU:0, one launch (start us, length us, event | category | flops | bytes accessed | tf_op | source)
XLA Modules:
  0.0 175.8 jit_solution(15271844181310203449)
XLA Ops:
  1.7 23.8 %spectra.1 = (bf16[2,64,128]{2,1,0:T(8,128)(2,1)S(1)}, bf16[2,64,128]{2,1,0:T(8,128)(2,1)S(1)}, bf16[2,64,128]{2,1,0:T(8,128)(2,1)S(1)}, bf16[2,64,128]{2,1,0:T(...) custom-call(s32[2]{0:T(128)S(1)} %pad_add_fusion.place_ref, ...), custom_call_target="tpu_custom_call" | custom-call | flops 8589934592 | bytes 67108864 | tf_op jit(solution)/shard_map/spectra/pallas_call | solution.py:120
  26.0 2.6 %collective-permute-start.1 = (bf16[128,128]{1,0:T(8,128)(2,1)S(1)}, bf16[128,128]{1,0:T(8,128)(2,1)S(1)}, u32[]{:S(2)}, u32[]{:S(2)}) collective-permute-start(bf16[128,128]{1,0:T(8,128)(2,1)S(1)} %bitcast.18), channel_id=1, source_target_pairs={{0,8},{4,12},{8,0},{12,4},{16,24},{20,28},{24,16},{28,20},{1,9},{5... | collective-permute-start | bytes 98312 | tf_op jit(solution)/shard_map/ppermute | solution.py:381
  28.6 1.8 %collective-permute-start.3 = (bf16[128,128]{1,0:T(8,128)(2,1)S(1)}, bf16[128,128]{1,0:T(8,128)(2,1)S(1)}, u32[]{:S(2)}, u32[]{:S(2)}) collective-permute-start(bf16[128,128]{1,0:T(8,128)(2,1)S(1)} %bitcast.16), channel_id=1, source_target_pairs={{0,16},{4,20},{8,24},{12,28},{16,0},{20,4},{24,8},{28,12},{1,17},{... | collective-permute-start | bytes 98312 | tf_op jit(solution)/shard_map/ppermute | solution.py:381
  30.4 2.6 %collective-permute-start.5 = (bf16[128,128]{1,0:T(8,128)(2,1)S(1)}, bf16[128,128]{1,0:T(8,128)(2,1)S(1)}, u32[]{:S(2)}, u32[]{:S(2)}) collective-permute-start(bf16[128,128]{1,0:T(8,128)(2,1)S(1)} %bitcast.14), channel_id=1, source_target_pairs={{0,24},{4,28},{8,16},{12,20},{16,8},{20,12},{24,0},{28,4},{1,25},{... | collective-permute-start | bytes 98312 | tf_op jit(solution)/shard_map/ppermute | solution.py:381
  33.5 1.7 hits.1.hits_ref
  35.2 2.0 %collective-permute-done.6.refs_7_ = bf16[128,128]{1,0:T(8,128)(2,1)S(1)} collective-permute-done((bf16[128,128]{1,0:T(8,128)(2,1)S(1)}, bf16[128,128]{1,0:T(8,128)(2,1)S(1)}, u32[]{:S(2)}, u32[]{:S(2)}) %collective-permute-start.6) | collective-permute-done | bytes 32800 | tf_op jit(solution)/shard_map/ppermute | solution.py:381
  37.2 2.3 %order.1 = (bf16[256,128]{1,0:T(8,128)(2,1)S(1)}, bf16[256,128]{1,0:T(8,128)(2,1)S(1)}, bf16[256,128]{1,0:T(8,128)(2,1)S(1)}, bf16[256,128]{1,0:T(8,128)(2,1)S(1)}) custom-call(s32[2]{0:T(128)S(1)} %pad_add_fusion.place_ref, s32[2048,128]{1,0:T(8,128)S(1)} %broadcast_in_dim.2.code_ref, bf16[2048,1024]{1,0:T(8,128)(2,1)S(1)} %hits.1.hits_ref, ...), custom_call_target="tpu_custom_call" | custom-call | flops 1073741824 | bytes 1048576 | tf_op jit(solution)/shard_map/order/pallas_call | solution.py:193
  39.6 1.6 collective-permute-start.7
  41.2 2.6 %collective-permute-start.8 = (bf16[256,128]{1,0:T(8,128)(2,1)S(1)}, bf16[256,128]{1,0:T(8,128)(2,1)S(1)}, u32[]{:S(2)}, u32[]{:S(2)}) collective-permute-start(bf16[256,128]{1,0:T(8,128)(2,1)S(1)} %get-tuple-element.38), channel_id=1, source_target_pairs={{0,2},{1,3},{2,0},{3,1},{4,6},{5,7},{6,4},{7,5},{8,10},{9,11},{10,... | collective-permute-start | bytes 196616 | tf_op jit(solution)/shard_map/ppermute | solution.py:381
  44.0 7.7 %relay.3 = (bf16[8,2048,512]{2,1,0:T(8,128)(2,1)S(1)}, f32[8,128]{1,0:T(8,128)S(1)}) custom-call(bf16[2,2048,8,512]{3,2,1,0:T(8,128)(2,1)} %data_ref.3, bf16[256,128]{1,0:T(8,128)(2,1)S(1)} %get-tuple-element.36.after_ref.refs_0_), custom_call_target="tpu_custom_call" | custom-call | bytes 33554432 | tf_op jit(solution)/shard_map/relay/pallas_call | solution.py:256
  52.7 1.1 collective-permute-start.10
  54.8 1.5 collective-permute-start.12
  56.3 8.0 %relay.2 = (bf16[8,2048,512]{2,1,0:T(8,128)(2,1)S(1)}, f32[8,128]{1,0:T(8,128)}) custom-call(bf16[2,2048,8,512]{3,2,1,0:T(8,128)(2,1)} %data_ref.3, bf16[128,128]{1,0:T(8,128)(2,1)S(1)} %bitcast.12), custom_call_target="tpu_custom_call" | custom-call | bytes 33554432 | tf_op jit(solution)/shard_map/relay/pallas_call | solution.py:256
  64.3 2.5 %collective-permute-done.11.refs_3_ = bf16[512,256]{1,0:T(8,128)(2,1)S(1)} collective-permute-done((bf16[512,256]{1,0:T(8,128)(2,1)S(1)}, bf16[512,256]{1,0:T(8,128)(2,1)S(1)}, u32[]{:S(2)}, u32[]{:S(2)}) %collective-permute-start.11) | collective-permute-done | bytes 262176 | tf_op jit(solution)/shard_map/ppermute | solution.py:381
  67.3 2.1 %terms.16.refs_3_ = f32[512,256]{1,0:T(8,128)S(1)} custom-call(s32[2]{0:T(128)S(1)} %pad_add_fusion.place_ref, bf16[8,2048,512]{2,1,0:T(8,128)(2,1)S(1)} %get-tuple-element.41.real_ref, bf16[8,2048,512]{2,1,0:T(8,128)(2,1)S(1)} %get-tuple-element.42.imag_ref, bf16[512,256]{1,0:T(8,128)(2,1)S(1)} %panel.1.refs_0_.refs_4_, ...), custom_call_target="tpu_custom_call" | custom-call | flops 1342177280 | bytes 5242880 | tf_op jit(solution)/shard_map/terms/pallas_call | solution.py:305
  69.4 1.5 terms.17
  71.6 2.9 %terms.19 = (bf16[512,256]{1,0:T(8,128)(2,1)S(1)}, f32[512,256]{1,0:T(8,128)S(1)}) custom-call(s32[2]{0:T(128)S(1)} %pad_add_fusion.place_ref, bf16[8,2048,512]{2,1,0:T(8,128)(2,1)S(1)} %get-tuple-element.41.real_ref, bf16[8,2048,512]{2,1,0:T(8,128)(2,1)S(1)} %get-tuple-element.42.imag_ref, bf16[512,256]{1,0:T(8,128)(2,1)S(1)} %panel.1.refs_0_.refs_4_, ...), custom_call_target="tpu_custom_call" | custom-call | flops 2147483648 | bytes 8388608 | tf_op jit(solution)/shard_map/terms/pallas_call | solution.py:305
  74.5 4.8 %collective-permute-start.19 = (bf16[512,256]{1,0:T(8,128)(2,1)S(1)}, bf16[512,256]{1,0:T(8,128)(2,1)S(1)}, u32[]{:S(2)}, u32[]{:S(2)}) collective-permute-start(bf16[512,256]{1,0:T(8,128)(2,1)S(1)} %get-tuple-element.46), channel_id=1, source_target_pairs={{0,3},{3,0},{4,7},{7,4},{8,11},{11,8},{12,15},{15,12},{16,19},{19,... | collective-permute-start | bytes 786440 | tf_op jit(solution)/shard_map/ppermute | solution.py:392
  79.3 2.9 %terms.18 = bf16[512,256]{1,0:T(8,128)(2,1)S(1)} custom-call(s32[2]{0:T(128)S(1)} %pad_add_fusion.place_ref, bf16[8,2048,512]{2,1,0:T(8,128)(2,1)S(1)} %get-tuple-element.41.real_ref, bf16[8,2048,512]{2,1,0:T(8,128)(2,1)S(1)} %get-tuple-element.42.imag_ref, bf16[512,256]{1,0:T(8,128)(2,1)S(1)} %panel.1.refs_0_.refs_4_, ...), custom_call_target="tpu_custom_call" | custom-call | flops 2147483648 | bytes 8388608 | tf_op jit(solution)/shard_map/terms/pallas_call | solution.py:305
  83.2 2.9 %terms.15.own_ref = f32[512,256]{1,0:T(8,128)S(1)} custom-call(s32[2]{0:T(128)S(1)} %pad_add_fusion.place_ref, bf16[8,2048,512]{2,1,0:T(8,128)(2,1)S(1)} %get-tuple-element.41.real_ref, bf16[8,2048,512]{2,1,0:T(8,128)(2,1)S(1)} %get-tuple-element.42.imag_ref, bf16[512,256]{1,0:T(8,128)(2,1)S(1)} %panel.1.refs_0_.refs_4_, ...), custom_call_target="tpu_custom_call" | custom-call | flops 2147483648 | bytes 8388608 | tf_op jit(solution)/shard_map/terms/pallas_call | solution.py:305
  86.1 1.3 collective-permute-done.19.refs_2_
  87.4 5.3 %collective-permute-done.18.refs_1_ = bf16[512,256]{1,0:T(8,128)(2,1)S(1)} collective-permute-done((bf16[512,256]{1,0:T(8,128)(2,1)S(1)}, bf16[512,256]{1,0:T(8,128)(2,1)S(1)}, u32[]{:S(2)}, u32[]{:S(2)}) %collective-permute-start.18) | collective-permute-done | bytes 262176 | tf_op jit(solution)/shard_map/ppermute | solution.py:381
  93.6 1.2 collective-permute-start.24
  95.8 1.3 collective-permute-start.22
  97.1 6.6 %collective-permute-done.24.refs_4_ = bf16[512,256]{1,0:T(8,128)(2,1)S(1)} collective-permute-done((bf16[512,256]{1,0:T(8,128)(2,1)S(1)}, bf16[512,256]{1,0:T(8,128)(2,1)S(1)}, u32[]{:S(2)}, u32[]{:S(2)}) %collective-permute-start.24) | collective-permute-done | bytes 262176 | tf_op jit(solution)/shard_map/ppermute | solution.py:381
  103.7 4.7 %collective-permute-done.23.refs_3_ = bf16[512,256]{1,0:T(8,128)(2,1)S(1)} collective-permute-done((bf16[512,256]{1,0:T(8,128)(2,1)S(1)}, bf16[512,256]{1,0:T(8,128)(2,1)S(1)}, u32[]{:S(2)}, u32[]{:S(2)}) %collective-permute-start.23) | collective-permute-done | bytes 262176 | tf_op jit(solution)/shard_map/ppermute | solution.py:381
  108.9 2.1 %terms.21.refs_3_ = f32[512,256]{1,0:T(8,128)S(1)} custom-call(s32[2]{0:T(128)S(1)} %pad_add_fusion.place_ref, bf16[8,2048,512]{2,1,0:T(8,128)(2,1)S(1)} %get-tuple-element.41.real_ref, bf16[8,2048,512]{2,1,0:T(8,128)(2,1)S(1)} %get-tuple-element.42.imag_ref, bf16[512,256]{1,0:T(8,128)(2,1)S(1)} %update.3.refs_0_, ...), custom_call_target="tpu_custom_call" | custom-call | flops 1342177280 | bytes 5242880 | tf_op jit(solution)/shard_map/terms/pallas_call | solution.py:305
  111.0 1.5 terms.22
  113.3 2.9 %terms.24 = (bf16[512,256]{1,0:T(8,128)(2,1)S(1)}, f32[512,256]{1,0:T(8,128)S(1)}) custom-call(s32[2]{0:T(128)S(1)} %pad_add_fusion.place_ref, bf16[8,2048,512]{2,1,0:T(8,128)(2,1)S(1)} %get-tuple-element.41.real_ref, bf16[8,2048,512]{2,1,0:T(8,128)(2,1)S(1)} %get-tuple-element.42.imag_ref, bf16[512,256]{1,0:T(8,128)(2,1)S(1)} %update.3.refs_0_, ...), custom_call_target="tpu_custom_call" | custom-call | flops 2147483648 | bytes 8388608 | tf_op jit(solution)/shard_map/terms/pallas_call | solution.py:305
  116.2 4.2 %collective-permute-start.30 = (bf16[512,256]{1,0:T(8,128)(2,1)S(1)}, bf16[512,256]{1,0:T(8,128)(2,1)S(1)}, u32[]{:S(2)}, u32[]{:S(2)}) collective-permute-start(bf16[512,256]{1,0:T(8,128)(2,1)S(1)} %get-tuple-element.48), channel_id=1, source_target_pairs={{0,3},{3,0},{4,7},{7,4},{8,11},{11,8},{12,15},{15,12},{16,19},{19,... | collective-permute-start | bytes 786440 | tf_op jit(solution)/shard_map/ppermute | solution.py:392
  120.4 2.9 %terms.23 = bf16[512,256]{1,0:T(8,128)(2,1)S(1)} custom-call(s32[2]{0:T(128)S(1)} %pad_add_fusion.place_ref, bf16[8,2048,512]{2,1,0:T(8,128)(2,1)S(1)} %get-tuple-element.41.real_ref, bf16[8,2048,512]{2,1,0:T(8,128)(2,1)S(1)} %get-tuple-element.42.imag_ref, bf16[512,256]{1,0:T(8,128)(2,1)S(1)} %update.3.refs_0_, ...), custom_call_target="tpu_custom_call" | custom-call | flops 2147483648 | bytes 8388608 | tf_op jit(solution)/shard_map/terms/pallas_call | solution.py:305
  124.2 2.9 %terms.20.own_ref = f32[512,256]{1,0:T(8,128)S(1)} custom-call(s32[2]{0:T(128)S(1)} %pad_add_fusion.place_ref, bf16[8,2048,512]{2,1,0:T(8,128)(2,1)S(1)} %get-tuple-element.41.real_ref, bf16[8,2048,512]{2,1,0:T(8,128)(2,1)S(1)} %get-tuple-element.42.imag_ref, bf16[512,256]{1,0:T(8,128)(2,1)S(1)} %update.3.refs_0_, ...), custom_call_target="tpu_custom_call" | custom-call | flops 2147483648 | bytes 8388608 | tf_op jit(solution)/shard_map/terms/pallas_call | solution.py:305
  127.0 2.1 %collective-permute-done.30.refs_2_ = bf16[512,256]{1,0:T(8,128)(2,1)S(1)} collective-permute-done((bf16[512,256]{1,0:T(8,128)(2,1)S(1)}, bf16[512,256]{1,0:T(8,128)(2,1)S(1)}, u32[]{:S(2)}, u32[]{:S(2)}) %collective-permute-start.30) | collective-permute-done | bytes 262176 | tf_op jit(solution)/shard_map/ppermute | solution.py:392
  129.1 4.3 %collective-permute-done.29.refs_1_ = bf16[512,256]{1,0:T(8,128)(2,1)S(1)} collective-permute-done((bf16[512,256]{1,0:T(8,128)(2,1)S(1)}, bf16[512,256]{1,0:T(8,128)(2,1)S(1)}, u32[]{:S(2)}, u32[]{:S(2)}) %collective-permute-start.29) | collective-permute-done | bytes 262176 | tf_op jit(solution)/shard_map/ppermute | solution.py:381
  134.3 1.2 collective-permute-start.35
  135.5 1.0 collective-permute-start.34
  136.5 1.3 collective-permute-start.33
  137.8 6.6 %collective-permute-done.35.refs_4_ = bf16[512,256]{1,0:T(8,128)(2,1)S(1)} collective-permute-done((bf16[512,256]{1,0:T(8,128)(2,1)S(1)}, bf16[512,256]{1,0:T(8,128)(2,1)S(1)}, u32[]{:S(2)}, u32[]{:S(2)}) %collective-permute-start.35) | collective-permute-done | bytes 262176 | tf_op jit(solution)/shard_map/ppermute | solution.py:381
  144.5 4.5 %collective-permute-done.34.refs_3_ = bf16[512,256]{1,0:T(8,128)(2,1)S(1)} collective-permute-done((bf16[512,256]{1,0:T(8,128)(2,1)S(1)}, bf16[512,256]{1,0:T(8,128)(2,1)S(1)}, u32[]{:S(2)}, u32[]{:S(2)}) %collective-permute-start.34) | collective-permute-done | bytes 262176 | tf_op jit(solution)/shard_map/ppermute | solution.py:381
  149.5 2.1 %terms.26.refs_3_ = f32[512,256]{1,0:T(8,128)S(1)} custom-call(s32[2]{0:T(128)S(1)} %pad_add_fusion.place_ref, bf16[8,2048,512]{2,1,0:T(8,128)(2,1)S(1)} %get-tuple-element.41.real_ref, bf16[8,2048,512]{2,1,0:T(8,128)(2,1)S(1)} %get-tuple-element.42.imag_ref, bf16[512,256]{1,0:T(8,128)(2,1)S(1)} %update.4.refs_0_, ...), custom_call_target="tpu_custom_call" | custom-call | flops 1342177280 | bytes 5242880 | tf_op jit(solution)/shard_map/terms/pallas_call | solution.py:305
  151.6 1.5 terms.27
  153.4 2.9 %terms.29 = (bf16[512,256]{1,0:T(8,128)(2,1)S(1)}, f32[512,256]{1,0:T(8,128)S(1)}) custom-call(s32[2]{0:T(128)S(1)} %pad_add_fusion.place_ref, bf16[8,2048,512]{2,1,0:T(8,128)(2,1)S(1)} %get-tuple-element.41.real_ref, bf16[8,2048,512]{2,1,0:T(8,128)(2,1)S(1)} %get-tuple-element.42.imag_ref, bf16[512,256]{1,0:T(8,128)(2,1)S(1)} %update.4.refs_0_, ...), custom_call_target="tpu_custom_call" | custom-call | flops 2147483648 | bytes 8388608 | tf_op jit(solution)/shard_map/terms/pallas_call | solution.py:305
  156.3 4.4 %collective-permute-start.41 = (bf16[512,256]{1,0:T(8,128)(2,1)S(1)}, bf16[512,256]{1,0:T(8,128)(2,1)S(1)}, u32[]{:S(2)}, u32[]{:S(2)}) collective-permute-start(bf16[512,256]{1,0:T(8,128)(2,1)S(1)} %get-tuple-element.50), channel_id=1, source_target_pairs={{0,3},{3,0},{4,7},{7,4},{8,11},{11,8},{12,15},{15,12},{16,19},{19,... | collective-permute-start | bytes 786440 | tf_op jit(solution)/shard_map/ppermute | solution.py:392
  160.7 2.9 %terms.28 = bf16[512,256]{1,0:T(8,128)(2,1)S(1)} custom-call(s32[2]{0:T(128)S(1)} %pad_add_fusion.place_ref, bf16[8,2048,512]{2,1,0:T(8,128)(2,1)S(1)} %get-tuple-element.41.real_ref, bf16[8,2048,512]{2,1,0:T(8,128)(2,1)S(1)} %get-tuple-element.42.imag_ref, bf16[512,256]{1,0:T(8,128)(2,1)S(1)} %update.4.refs_0_, ...), custom_call_target="tpu_custom_call" | custom-call | flops 2147483648 | bytes 8388608 | tf_op jit(solution)/shard_map/terms/pallas_call | solution.py:305
  164.4 2.9 %terms.25.own_ref = f32[512,256]{1,0:T(8,128)S(1)} custom-call(s32[2]{0:T(128)S(1)} %pad_add_fusion.place_ref, bf16[8,2048,512]{2,1,0:T(8,128)(2,1)S(1)} %get-tuple-element.41.real_ref, bf16[8,2048,512]{2,1,0:T(8,128)(2,1)S(1)} %get-tuple-element.42.imag_ref, bf16[512,256]{1,0:T(8,128)(2,1)S(1)} %update.4.refs_0_, ...), custom_call_target="tpu_custom_call" | custom-call | flops 2147483648 | bytes 8388608 | tf_op jit(solution)/shard_map/terms/pallas_call | solution.py:305
  167.3 1.8 %collective-permute-done.41.refs_2_ = bf16[512,256]{1,0:T(8,128)(2,1)S(1)} collective-permute-done((bf16[512,256]{1,0:T(8,128)(2,1)S(1)}, bf16[512,256]{1,0:T(8,128)(2,1)S(1)}, u32[]{:S(2)}, u32[]{:S(2)}) %collective-permute-start.41) | collective-permute-done | bytes 262176 | tf_op jit(solution)/shard_map/ppermute | solution.py:392
  169.1 4.5 %collective-permute-done.40.refs_1_ = bf16[512,256]{1,0:T(8,128)(2,1)S(1)} collective-permute-done((bf16[512,256]{1,0:T(8,128)(2,1)S(1)}, bf16[512,256]{1,0:T(8,128)(2,1)S(1)}, u32[]{:S(2)}, u32[]{:S(2)}) %collective-permute-start.40) | collective-permute-done | bytes 262176 | tf_op jit(solution)/shard_map/ppermute | solution.py:381
  173.7 2.1 %update.5 = (f32[512,2,128]{2,1,0:T(2,128)}, f32[512,2,128]{2,1,0:T(2,128)}) custom-call(s32[2]{0:T(128)S(1)} %pad_add_fusion.place_ref, f32[2]{0:T(128)S(1)} %copy-done.1, f32[512,256]{1,0:T(8,128)S(1)} %terms.25.own_ref, bf16[512,256]{1,0:T(8,128)(2,1)S(1)} %collective-permute-done.39.other_ref.refs_0_, ...), custom_call_target="tpu_custom_call" | custom-call | flops 2097152 | bytes 2097152 | tf_op jit(solution)/shard_map/update/pallas_call | solution.py:368
  (74 shorter events, 12.8 us)
Async XLA Ops:
  0.7 1.0 copy-start
  1.7 31.4 %copy-start.2 = (s32[2048]{0:T(1024)S(1)}, s32[2048]{0:T(1024)}, u32[]{:S(2)}) copy-start(s32[2048]{0:T(1024)} %param.6) | copy-start | bytes 24580
  25.5 4.9 %collective-permute-start = (bf16[128,128]{1,0:T(8,128)(2,1)S(1)}, bf16[128,128]{1,0:T(8,128)(2,1)S(1)}, u32[]{:S(2)}, u32[]{:S(2)}) collective-permute-start(bf16[128,128]{1,0:T(8,128)(2,1)S(1)} %bitcast.19), channel_id=1, source_target_pairs={{0,4},{4,0},{8,12},{12,8},{16,20},{20,16},{24,28},{28,24},{1,5},{5... | collective-permute-start | bytes 98312 | tf_op jit(solution)/shard_map/ppermute | solution.py:381
  26.0 7.0 %collective-permute-start.1 = (bf16[128,128]{1,0:T(8,128)(2,1)S(1)}, bf16[128,128]{1,0:T(8,128)(2,1)S(1)}, u32[]{:S(2)}, u32[]{:S(2)}) collective-permute-start(bf16[128,128]{1,0:T(8,128)(2,1)S(1)} %bitcast.18), channel_id=1, source_target_pairs={{0,8},{4,12},{8,0},{12,4},{16,24},{20,28},{24,16},{28,20},{1,9},{5... | collective-permute-start | bytes 98312 | tf_op jit(solution)/shard_map/ppermute | solution.py:381
  28.5 6.6 %collective-permute-start.2 = (bf16[128,128]{1,0:T(8,128)(2,1)S(1)}, bf16[128,128]{1,0:T(8,128)(2,1)S(1)}, u32[]{:S(2)}, u32[]{:S(2)}) collective-permute-start(bf16[128,128]{1,0:T(8,128)(2,1)S(1)} %bitcast.17), channel_id=1, source_target_pairs={{0,12},{4,8},{8,4},{12,0},{16,28},{20,24},{24,20},{28,16},{1,13},{... | collective-permute-start | bytes 98312 | tf_op jit(solution)/shard_map/ppermute | solution.py:381
  28.6 6.6 %collective-permute-start.3 = (bf16[128,128]{1,0:T(8,128)(2,1)S(1)}, bf16[128,128]{1,0:T(8,128)(2,1)S(1)}, u32[]{:S(2)}, u32[]{:S(2)}) collective-permute-start(bf16[128,128]{1,0:T(8,128)(2,1)S(1)} %bitcast.16), channel_id=1, source_target_pairs={{0,16},{4,20},{8,24},{12,28},{16,0},{20,4},{24,8},{28,12},{1,17},{... | collective-permute-start | bytes 98312 | tf_op jit(solution)/shard_map/ppermute | solution.py:381
  30.4 4.8 %collective-permute-start.4 = (bf16[128,128]{1,0:T(8,128)(2,1)S(1)}, bf16[128,128]{1,0:T(8,128)(2,1)S(1)}, u32[]{:S(2)}, u32[]{:S(2)}) collective-permute-start(bf16[128,128]{1,0:T(8,128)(2,1)S(1)} %bitcast.15), channel_id=1, source_target_pairs={{0,20},{4,16},{8,28},{12,24},{16,4},{20,0},{24,12},{28,8},{1,21},{... | collective-permute-start | bytes 98312 | tf_op jit(solution)/shard_map/ppermute | solution.py:381
  30.4 4.8 %collective-permute-start.5 = (bf16[128,128]{1,0:T(8,128)(2,1)S(1)}, bf16[128,128]{1,0:T(8,128)(2,1)S(1)}, u32[]{:S(2)}, u32[]{:S(2)}) collective-permute-start(bf16[128,128]{1,0:T(8,128)(2,1)S(1)} %bitcast.14), channel_id=1, source_target_pairs={{0,24},{4,28},{8,16},{12,20},{16,8},{20,12},{24,0},{28,4},{1,25},{... | collective-permute-start | bytes 98312 | tf_op jit(solution)/shard_map/ppermute | solution.py:381
  33.0 4.2 %collective-permute-start.6 = (bf16[128,128]{1,0:T(8,128)(2,1)S(1)}, bf16[128,128]{1,0:T(8,128)(2,1)S(1)}, u32[]{:S(2)}, u32[]{:S(2)}) collective-permute-start(bf16[128,128]{1,0:T(8,128)(2,1)S(1)} %bitcast.13), channel_id=1, source_target_pairs={{0,28},{4,24},{8,20},{12,16},{16,12},{20,8},{24,4},{28,0},{1,29},{... | collective-permute-start | bytes 98312 | tf_op jit(solution)/shard_map/ppermute | solution.py:381
  39.6 12.1 %collective-permute-start.7 = (bf16[256,128]{1,0:T(8,128)(2,1)S(1)}, bf16[256,128]{1,0:T(8,128)(2,1)S(1)}, u32[]{:S(2)}, u32[]{:S(2)}) collective-permute-start(bf16[256,128]{1,0:T(8,128)(2,1)S(1)} %get-tuple-element.37), channel_id=1, source_target_pairs={{0,1},{1,0},{2,3},{3,2},{4,5},{5,4},{6,7},{7,6},{8,9},{9,8},{10,11... | collective-permute-start | bytes 196616 | tf_op jit(solution)/shard_map/ppermute | solution.py:381
  41.2 10.5 %collective-permute-start.8 = (bf16[256,128]{1,0:T(8,128)(2,1)S(1)}, bf16[256,128]{1,0:T(8,128)(2,1)S(1)}, u32[]{:S(2)}, u32[]{:S(2)}) collective-permute-start(bf16[256,128]{1,0:T(8,128)(2,1)S(1)} %get-tuple-element.38), channel_id=1, source_target_pairs={{0,2},{1,3},{2,0},{3,1},{4,6},{5,7},{6,4},{7,5},{8,10},{9,11},{10,... | collective-permute-start | bytes 196616 | tf_op jit(solution)/shard_map/ppermute | solution.py:381
  43.8 7.9 %collective-permute-start.9 = (bf16[256,128]{1,0:T(8,128)(2,1)S(1)}, bf16[256,128]{1,0:T(8,128)(2,1)S(1)}, u32[]{:S(2)}, u32[]{:S(2)}) collective-permute-start(bf16[256,128]{1,0:T(8,128)(2,1)S(1)} %get-tuple-element.39), channel_id=1, source_target_pairs={{0,3},{1,2},{2,1},{3,0},{4,7},{5,6},{6,5},{7,4},{8,11},{9,10},{10,... | collective-permute-start | bytes 196616 | tf_op jit(solution)/shard_map/ppermute | solution.py:381
  52.7 11.5 %collective-permute-start.10 = (bf16[512,256]{1,0:T(8,128)(2,1)S(1)}, bf16[512,256]{1,0:T(8,128)(2,1)S(1)}, u32[]{:S(2)}, u32[]{:S(2)}) collective-permute-start(bf16[512,256]{1,0:T(8,128)(2,1)S(1)} %panel.1.refs_0_.refs_4_), channel_id=1, source_target_pairs={{0,24},{4,28},{8,16},{12,20},{16,8},{20,12},{24,0},{28,4},{1,25},{... | collective-permute-start | bytes 786440 | tf_op jit(solution)/shard_map/ppermute | solution.py:381
  53.9 12.9 %collective-permute-start.11 = (bf16[512,256]{1,0:T(8,128)(2,1)S(1)}, bf16[512,256]{1,0:T(8,128)(2,1)S(1)}, u32[]{:S(2)}, u32[]{:S(2)}) collective-permute-start(bf16[512,256]{1,0:T(8,128)(2,1)S(1)} %panel.1.refs_0_.refs_4_), channel_id=1, source_target_pairs={{0,16},{4,20},{8,24},{12,28},{16,0},{20,4},{24,8},{28,12},{1,17},{... | collective-permute-start | bytes 786440 | tf_op jit(solution)/shard_map/ppermute | solution.py:381
  54.8 12.0 %collective-permute-start.12 = (bf16[512,256]{1,0:T(8,128)(2,1)S(1)}, bf16[512,256]{1,0:T(8,128)(2,1)S(1)}, u32[]{:S(2)}, u32[]{:S(2)}) collective-permute-start(bf16[512,256]{1,0:T(8,128)(2,1)S(1)} %panel.1.refs_0_.refs_4_), channel_id=1, source_target_pairs={{0,8},{4,12},{8,0},{12,4},{16,24},{20,28},{24,16},{28,20},{1,9},{5... | collective-permute-start | bytes 786440 | tf_op jit(solution)/shard_map/ppermute | solution.py:381
  56.3 11.0 %collective-permute-start.13 = (bf16[512,256]{1,0:T(8,128)(2,1)S(1)}, bf16[512,256]{1,0:T(8,128)(2,1)S(1)}, u32[]{:S(2)}, u32[]{:S(2)}) collective-permute-start(bf16[512,256]{1,0:T(8,128)(2,1)S(1)} %panel.1.refs_0_.refs_4_), channel_id=1, source_target_pairs={{0,4},{4,0},{8,12},{12,8},{16,20},{20,16},{24,28},{28,24},{1,5},{5... | collective-permute-start | bytes 786440 | tf_op jit(solution)/shard_map/ppermute | solution.py:381
  66.8 2.6 %collective-permute-start.14 = (bf16[512,256]{1,0:T(8,128)(2,1)S(1)}, bf16[512,256]{1,0:T(8,128)(2,1)S(1)}, u32[]{:S(2)}, u32[]{:S(2)}) collective-permute-start(bf16[512,256]{1,0:T(8,128)(2,1)S(1)} %collective-permute-done.10.refs_2_), channel_id=1, source_target_pairs={{0,4},{4,0},{8,12},{12,8},{16,20},{20,16},{24,28},{28,24},{1,5},{5... | collective-permute-start | bytes 786440 | tf_op jit(solution)/shard_map/ppermute | solution.py:381
  66.8 2.6 %collective-permute-start.15 = (bf16[512,256]{1,0:T(8,128)(2,1)S(1)}, bf16[512,256]{1,0:T(8,128)(2,1)S(1)}, u32[]{:S(2)}, u32[]{:S(2)}) collective-permute-start(bf16[512,256]{1,0:T(8,128)(2,1)S(1)} %collective-permute-done.11.refs_3_), channel_id=1, source_target_pairs={{0,4},{4,0},{8,12},{12,8},{16,20},{20,16},{24,28},{28,24},{1,5},{5... | collective-permute-start | bytes 786440 | tf_op jit(solution)/shard_map/ppermute | solution.py:381
  67.3 2.1 %collective-permute-start.16 = (bf16[512,256]{1,0:T(8,128)(2,1)S(1)}, bf16[512,256]{1,0:T(8,128)(2,1)S(1)}, u32[]{:S(2)}, u32[]{:S(2)}) collective-permute-start(bf16[512,256]{1,0:T(8,128)(2,1)S(1)} %collective-permute-done.12.refs_4_), channel_id=1, source_target_pairs={{0,4},{4,0},{8,12},{12,8},{16,20},{20,16},{24,28},{28,24},{1,5},{5... | collective-permute-start | bytes 786440 | tf_op jit(solution)/shard_map/ppermute | solution.py:381
  70.9 11.4 %collective-permute-start.17 = (bf16[512,256]{1,0:T(8,128)(2,1)S(1)}, bf16[512,256]{1,0:T(8,128)(2,1)S(1)}, u32[]{:S(2)}, u32[]{:S(2)}) collective-permute-start(bf16[512,256]{1,0:T(8,128)(2,1)S(1)} %terms.17), channel_id=1, source_target_pairs={{0,1},{1,3},{3,2},{2,0},{4,5},{5,7},{7,6},{6,4},{8,9},{9,11},{11,1... | collective-permute-start | bytes 786440 | tf_op jit(solution)/shard_map/ppermute | solution.py:389
  74.5 12.9 %collective-permute-start.19 = (bf16[512,256]{1,0:T(8,128)(2,1)S(1)}, bf16[512,256]{1,0:T(8,128)(2,1)S(1)}, u32[]{:S(2)}, u32[]{:S(2)}) collective-permute-start(bf16[512,256]{1,0:T(8,128)(2,1)S(1)} %get-tuple-element.46), channel_id=1, source_target_pairs={{0,3},{3,0},{4,7},{7,4},{8,11},{11,8},{12,15},{15,12},{16,19},{19,... | collective-permute-start | bytes 786440 | tf_op jit(solution)/shard_map/ppermute | solution.py:392
  82.2 10.5 %collective-permute-start.18 = (bf16[512,256]{1,0:T(8,128)(2,1)S(1)}, bf16[512,256]{1,0:T(8,128)(2,1)S(1)}, u32[]{:S(2)}, u32[]{:S(2)}) collective-permute-start(bf16[512,256]{1,0:T(8,128)(2,1)S(1)} %terms.18), channel_id=1, source_target_pairs={{0,1},{1,0},{2,3},{3,2},{4,5},{5,4},{6,7},{7,6},{8,9},{9,8},{10,11... | collective-permute-start | bytes 786440 | tf_op jit(solution)/shard_map/ppermute | solution.py:381
  82.4 10.4 %copy-start.1 = (f32[2]{0:T(128)S(1)}, f32[2]{0:T(128)}, u32[]{:S(2)}) copy-start(f32[2]{0:T(128)} %wave_ref.5) | copy-start | bytes 28
  82.4 10.4 %collective-permute-start.20 = (bf16[512,256]{1,0:T(8,128)(2,1)S(1)}, bf16[512,256]{1,0:T(8,128)(2,1)S(1)}, u32[]{:S(2)}, u32[]{:S(2)}) collective-permute-start(bf16[512,256]{1,0:T(8,128)(2,1)S(1)} %sum.3), channel_id=1, source_target_pairs={{1,2},{2,1},{5,6},{6,5},{9,10},{10,9},{13,14},{14,13},{17,18},{18,... | collective-permute-start | bytes 786440 | tf_op jit(solution)/shard_map/ppermute | solution.py:393
  93.6 10.2 %collective-permute-start.24 = (bf16[512,256]{1,0:T(8,128)(2,1)S(1)}, bf16[512,256]{1,0:T(8,128)(2,1)S(1)}, u32[]{:S(2)}, u32[]{:S(2)}) collective-permute-start(bf16[512,256]{1,0:T(8,128)(2,1)S(1)} %update.3.refs_0_), channel_id=1, source_target_pairs={{0,24},{4,28},{8,16},{12,20},{16,8},{20,12},{24,0},{28,4},{1,25},{... | collective-permute-start | bytes 786440 | tf_op jit(solution)/shard_map/ppermute | solution.py:381
  94.8 13.6 %collective-permute-start.23 = (bf16[512,256]{1,0:T(8,128)(2,1)S(1)}, bf16[512,256]{1,0:T(8,128)(2,1)S(1)}, u32[]{:S(2)}, u32[]{:S(2)}) collective-permute-start(bf16[512,256]{1,0:T(8,128)(2,1)S(1)} %update.3.refs_0_), channel_id=1, source_target_pairs={{0,16},{4,20},{8,24},{12,28},{16,0},{20,4},{24,8},{28,12},{1,17},{... | collective-permute-start | bytes 786440 | tf_op jit(solution)/shard_map/ppermute | solution.py:381
  95.8 12.6 %collective-permute-start.22 = (bf16[512,256]{1,0:T(8,128)(2,1)S(1)}, bf16[512,256]{1,0:T(8,128)(2,1)S(1)}, u32[]{:S(2)}, u32[]{:S(2)}) collective-permute-start(bf16[512,256]{1,0:T(8,128)(2,1)S(1)} %update.3.refs_0_), channel_id=1, source_target_pairs={{0,8},{4,12},{8,0},{12,4},{16,24},{20,28},{24,16},{28,20},{1,9},{5... | collective-permute-start | bytes 786440 | tf_op jit(solution)/shard_map/ppermute | solution.py:381
  97.1 11.8 %collective-permute-start.21 = (bf16[512,256]{1,0:T(8,128)(2,1)S(1)}, bf16[512,256]{1,0:T(8,128)(2,1)S(1)}, u32[]{:S(2)}, u32[]{:S(2)}) collective-permute-start(bf16[512,256]{1,0:T(8,128)(2,1)S(1)} %update.3.refs_0_), channel_id=1, source_target_pairs={{0,4},{4,0},{8,12},{12,8},{16,20},{20,16},{24,28},{28,24},{1,5},{5... | collective-permute-start | bytes 786440 | tf_op jit(solution)/shard_map/ppermute | solution.py:381
  103.7 7.2 %collective-permute-start.25 = (bf16[512,256]{1,0:T(8,128)(2,1)S(1)}, bf16[512,256]{1,0:T(8,128)(2,1)S(1)}, u32[]{:S(2)}, u32[]{:S(2)}) collective-permute-start(bf16[512,256]{1,0:T(8,128)(2,1)S(1)} %collective-permute-done.24.refs_4_), channel_id=1, source_target_pairs={{0,4},{4,0},{8,12},{12,8},{16,20},{20,16},{24,28},{28,24},{1,5},{5... | collective-permute-start | bytes 786440 | tf_op jit(solution)/shard_map/ppermute | solution.py:381
  108.4 2.6 %collective-permute-start.26 = (bf16[512,256]{1,0:T(8,128)(2,1)S(1)}, bf16[512,256]{1,0:T(8,128)(2,1)S(1)}, u32[]{:S(2)}, u32[]{:S(2)}) collective-permute-start(bf16[512,256]{1,0:T(8,128)(2,1)S(1)} %collective-permute-done.23.refs_3_), channel_id=1, source_target_pairs={{0,4},{4,0},{8,12},{12,8},{16,20},{20,16},{24,28},{28,24},{1,5},{5... | collective-permute-start | bytes 786440 | tf_op jit(solution)/shard_map/ppermute | solution.py:381
  108.4 2.6 %collective-permute-start.27 = (bf16[512,256]{1,0:T(8,128)(2,1)S(1)}, bf16[512,256]{1,0:T(8,128)(2,1)S(1)}, u32[]{:S(2)}, u32[]{:S(2)}) collective-permute-start(bf16[512,256]{1,0:T(8,128)(2,1)S(1)} %collective-permute-done.22.refs_2_), channel_id=1, source_target_pairs={{0,4},{4,0},{8,12},{12,8},{16,20},{20,16},{24,28},{28,24},{1,5},{5... | collective-permute-start | bytes 786440 | tf_op jit(solution)/shard_map/ppermute | solution.py:381
  112.6 10.8 %collective-permute-start.28 = (bf16[512,256]{1,0:T(8,128)(2,1)S(1)}, bf16[512,256]{1,0:T(8,128)(2,1)S(1)}, u32[]{:S(2)}, u32[]{:S(2)}) collective-permute-start(bf16[512,256]{1,0:T(8,128)(2,1)S(1)} %terms.22), channel_id=1, source_target_pairs={{0,1},{1,3},{3,2},{2,0},{4,5},{5,7},{7,6},{6,4},{8,9},{9,11},{11,1... | collective-permute-start | bytes 786440 | tf_op jit(solution)/shard_map/ppermute | solution.py:389
  116.2 12.9 %collective-permute-start.30 = (bf16[512,256]{1,0:T(8,128)(2,1)S(1)}, bf16[512,256]{1,0:T(8,128)(2,1)S(1)}, u32[]{:S(2)}, u32[]{:S(2)}) collective-permute-start(bf16[512,256]{1,0:T(8,128)(2,1)S(1)} %get-tuple-element.48), channel_id=1, source_target_pairs={{0,3},{3,0},{4,7},{7,4},{8,11},{11,8},{12,15},{15,12},{16,19},{19,... | collective-permute-start | bytes 786440 | tf_op jit(solution)/shard_map/ppermute | solution.py:392
  123.3 10.2 %collective-permute-start.29 = (bf16[512,256]{1,0:T(8,128)(2,1)S(1)}, bf16[512,256]{1,0:T(8,128)(2,1)S(1)}, u32[]{:S(2)}, u32[]{:S(2)}) collective-permute-start(bf16[512,256]{1,0:T(8,128)(2,1)S(1)} %terms.23), channel_id=1, source_target_pairs={{0,1},{1,0},{2,3},{3,2},{4,5},{5,4},{6,7},{7,6},{8,9},{9,8},{10,11... | collective-permute-start | bytes 786440 | tf_op jit(solution)/shard_map/ppermute | solution.py:381
  123.5 10.0 %collective-permute-start.31 = (bf16[512,256]{1,0:T(8,128)(2,1)S(1)}, bf16[512,256]{1,0:T(8,128)(2,1)S(1)}, u32[]{:S(2)}, u32[]{:S(2)}) collective-permute-start(bf16[512,256]{1,0:T(8,128)(2,1)S(1)} %sum.4), channel_id=1, source_target_pairs={{1,2},{2,1},{5,6},{6,5},{9,10},{10,9},{13,14},{14,13},{17,18},{18,... | collective-permute-start | bytes 786440 | tf_op jit(solution)/shard_map/ppermute | solution.py:393
  134.3 10.2 %collective-permute-start.35 = (bf16[512,256]{1,0:T(8,128)(2,1)S(1)}, bf16[512,256]{1,0:T(8,128)(2,1)S(1)}, u32[]{:S(2)}, u32[]{:S(2)}) collective-permute-start(bf16[512,256]{1,0:T(8,128)(2,1)S(1)} %update.4.refs_0_), channel_id=1, source_target_pairs={{0,24},{4,28},{8,16},{12,20},{16,8},{20,12},{24,0},{28,4},{1,25},{... | collective-permute-start | bytes 786440 | tf_op jit(solution)/shard_map/ppermute | solution.py:381
  135.5 13.5 %collective-permute-start.34 = (bf16[512,256]{1,0:T(8,128)(2,1)S(1)}, bf16[512,256]{1,0:T(8,128)(2,1)S(1)}, u32[]{:S(2)}, u32[]{:S(2)}) collective-permute-start(bf16[512,256]{1,0:T(8,128)(2,1)S(1)} %update.4.refs_0_), channel_id=1, source_target_pairs={{0,16},{4,20},{8,24},{12,28},{16,0},{20,4},{24,8},{28,12},{1,17},{... | collective-permute-start | bytes 786440 | tf_op jit(solution)/shard_map/ppermute | solution.py:381
  136.5 12.5 %collective-permute-start.33 = (bf16[512,256]{1,0:T(8,128)(2,1)S(1)}, bf16[512,256]{1,0:T(8,128)(2,1)S(1)}, u32[]{:S(2)}, u32[]{:S(2)}) collective-permute-start(bf16[512,256]{1,0:T(8,128)(2,1)S(1)} %update.4.refs_0_), channel_id=1, source_target_pairs={{0,8},{4,12},{8,0},{12,4},{16,24},{20,28},{24,16},{28,20},{1,9},{5... | collective-permute-start | bytes 786440 | tf_op jit(solution)/shard_map/ppermute | solution.py:381
  137.8 11.7 %collective-permute-start.32 = (bf16[512,256]{1,0:T(8,128)(2,1)S(1)}, bf16[512,256]{1,0:T(8,128)(2,1)S(1)}, u32[]{:S(2)}, u32[]{:S(2)}) collective-permute-start(bf16[512,256]{1,0:T(8,128)(2,1)S(1)} %update.4.refs_0_), channel_id=1, source_target_pairs={{0,4},{4,0},{8,12},{12,8},{16,20},{20,16},{24,28},{28,24},{1,5},{5... | collective-permute-start | bytes 786440 | tf_op jit(solution)/shard_map/ppermute | solution.py:381
  144.5 7.1 %collective-permute-start.36 = (bf16[512,256]{1,0:T(8,128)(2,1)S(1)}, bf16[512,256]{1,0:T(8,128)(2,1)S(1)}, u32[]{:S(2)}, u32[]{:S(2)}) collective-permute-start(bf16[512,256]{1,0:T(8,128)(2,1)S(1)} %collective-permute-done.35.refs_4_), channel_id=1, source_target_pairs={{0,4},{4,0},{8,12},{12,8},{16,20},{20,16},{24,28},{28,24},{1,5},{5... | collective-permute-start | bytes 786440 | tf_op jit(solution)/shard_map/ppermute | solution.py:381
  149.0 2.6 %collective-permute-start.37 = (bf16[512,256]{1,0:T(8,128)(2,1)S(1)}, bf16[512,256]{1,0:T(8,128)(2,1)S(1)}, u32[]{:S(2)}, u32[]{:S(2)}) collective-permute-start(bf16[512,256]{1,0:T(8,128)(2,1)S(1)} %collective-permute-done.34.refs_3_), channel_id=1, source_target_pairs={{0,4},{4,0},{8,12},{12,8},{16,20},{20,16},{24,28},{28,24},{1,5},{5... | collective-permute-start | bytes 786440 | tf_op jit(solution)/shard_map/ppermute | solution.py:381
  149.0 2.6 %collective-permute-start.38 = (bf16[512,256]{1,0:T(8,128)(2,1)S(1)}, bf16[512,256]{1,0:T(8,128)(2,1)S(1)}, u32[]{:S(2)}, u32[]{:S(2)}) collective-permute-start(bf16[512,256]{1,0:T(8,128)(2,1)S(1)} %collective-permute-done.33.refs_2_), channel_id=1, source_target_pairs={{0,4},{4,0},{8,12},{12,8},{16,20},{20,16},{24,28},{28,24},{1,5},{5... | collective-permute-start | bytes 786440 | tf_op jit(solution)/shard_map/ppermute | solution.py:381
  153.2 10.5 %collective-permute-start.39 = (bf16[512,256]{1,0:T(8,128)(2,1)S(1)}, bf16[512,256]{1,0:T(8,128)(2,1)S(1)}, u32[]{:S(2)}, u32[]{:S(2)}) collective-permute-start(bf16[512,256]{1,0:T(8,128)(2,1)S(1)} %terms.27), channel_id=1, source_target_pairs={{0,1},{1,3},{3,2},{2,0},{4,5},{5,7},{7,6},{6,4},{8,9},{9,11},{11,1... | collective-permute-start | bytes 786440 | tf_op jit(solution)/shard_map/ppermute | solution.py:389
  156.3 12.9 %collective-permute-start.41 = (bf16[512,256]{1,0:T(8,128)(2,1)S(1)}, bf16[512,256]{1,0:T(8,128)(2,1)S(1)}, u32[]{:S(2)}, u32[]{:S(2)}) collective-permute-start(bf16[512,256]{1,0:T(8,128)(2,1)S(1)} %get-tuple-element.50), channel_id=1, source_target_pairs={{0,3},{3,0},{4,7},{7,4},{8,11},{11,8},{12,15},{15,12},{16,19},{19,... | collective-permute-start | bytes 786440 | tf_op jit(solution)/shard_map/ppermute | solution.py:392
  163.6 10.1 %collective-permute-start.40 = (bf16[512,256]{1,0:T(8,128)(2,1)S(1)}, bf16[512,256]{1,0:T(8,128)(2,1)S(1)}, u32[]{:S(2)}, u32[]{:S(2)}) collective-permute-start(bf16[512,256]{1,0:T(8,128)(2,1)S(1)} %terms.28), channel_id=1, source_target_pairs={{0,1},{1,0},{2,3},{3,2},{4,5},{5,4},{6,7},{7,6},{8,9},{9,8},{10,11... | collective-permute-start | bytes 786440 | tf_op jit(solution)/shard_map/ppermute | solution.py:381
  163.7 9.9 %collective-permute-start.42 = (bf16[512,256]{1,0:T(8,128)(2,1)S(1)}, bf16[512,256]{1,0:T(8,128)(2,1)S(1)}, u32[]{:S(2)}, u32[]{:S(2)}) collective-permute-start(bf16[512,256]{1,0:T(8,128)(2,1)S(1)} %sum.5), channel_id=1, source_target_pairs={{1,2},{2,1},{5,6},{6,5},{9,10},{10,9},{13,14},{14,13},{17,18},{18,... | collective-permute-start | bytes 786440 | tf_op jit(solution)/shard_map/ppermute | solution.py:393

commit v6 on v5

--- a/solution.py
+++ b/solution.py
@@ -162,13 +162,14 @@
 
 
 def order_kernel(packs, n_src, place_ref, code_ref, hits_ref, *refs):
-    pieces, out_refs = refs[:-n_src], refs[-n_src:]
+    pieces, out_refs, found = refs[: -n_src - 1], refs[-n_src - 1 : -1], refs[-1]
     width = LANES // packs
     held = jnp.concatenate([ref[...] for ref in pieces], axis=0)
     rolled = [held] + [
         pltpu.roll(held.astype(jnp.float32), turn * width, 1).astype(jnp.bfloat16) for turn in range(1, packs)
     ]
     table = jnp.concatenate(rolled, axis=1)
+    found[...] = jnp.dot(hits_ref[...], table, preferred_element_type=jnp.float32)
     slice_rows = code_ref.shape[0] // n_src
     short = slice_rows // packs
     column = lax.broadcasted_iota(jnp.int32, (short, LANES), 1)
@@ -178,7 +179,7 @@
         for part in range(packs):
             chosen = pl.ds(pl.multiple_of(first + part * short, short), short)
             side = code_ref[chosen, :] % packs
-            rows = jnp.dot(hits_ref[chosen, :], table, preferred_element_type=jnp.float32)
+            rows = found[chosen, :]
             moved = rows[:, :LANES]
             for turned in range(1, packs):
                 moved = jnp.where(
@@ -195,6 +196,7 @@
         in_specs=[SMEM] + [VMEM] * (2 + len(pieces)),
         out_specs=[VMEM] * n_src,
         out_shape=[jax.ShapeDtypeStruct((slice_rows // packs, LANES), jnp.bfloat16)] * n_src,
+        scratch_shapes=[pltpu.VMEM((code.shape[0], LANES * packs), jnp.float32)],
         compiler_params=params(12),
         cost_estimate=cost(2 * hits.size * LANES * packs, 4 * code.size),
         name="order",
@@ -329,29 +331,24 @@
     )(own, other)
 
 
-def update(place_ref, wave_ref, own_ref, others, panel_ref, folded):
+def update(wave_ref, own_ref, others, panel_ref):
     predicted = own_ref[...]
-    for number, other in enumerate(others):
-        term = other[...].astype(jnp.float32)
-        if folded and number == 0:
-            inner = place_ref[1] % 2 != place_ref[1] // 2 % 2
-            term = jnp.where(inner, 0.0, term)
-        predicted += term
+    for other in others:
+        predicted += other[...].astype(jnp.float32)
     kept = predicted.shape[1] // 2
     turned = jnp.concatenate([-predicted[:, kept:], predicted[:, :kept]], axis=1)
     scaled = wave_ref[0] * predicted + wave_ref[1] * turned
     return predicted, panel_ref[...].astype(jnp.float32) - scaled
 
 
-def estimate_kernel(folded, place_ref, wave_ref, own_ref, *refs):
+def estimate_kernel(wave_ref, own_ref, *refs):
     *others, panel_ref, out_ref = refs
-    primaries = update(place_ref, wave_ref, own_ref, others, panel_ref, folded)[1]
-    out_ref[...] = primaries.astype(jnp.bfloat16)
-
-
-def last_kernel(folded, place_ref, wave_ref, own_ref, *refs):
+    out_ref[...] = update(wave_ref, own_ref, others, panel_ref)[1].astype(jnp.bfloat16)
+
+
+def last_kernel(wave_ref, own_ref, *refs):
     *others, panel_ref, multiples_ref, primaries_ref = refs
-    predicted, primaries = update(place_ref, wave_ref, own_ref, others, panel_ref, folded)
+    predicted, primaries = update(wave_ref, own_ref, others, panel_ref)
     kept = predicted.shape[1] // 2
     multiples_ref[:, 0, :] = predicted[:, :kept]
     multiples_ref[:, 1, :] = predicted[:, kept:]
@@ -359,21 +356,21 @@
     primaries_ref[:, 1, :] = primaries[:, kept:]
 
 
-def make_update(place, wavelet, own, others, panel, folded, last):
+def make_update(wavelet, own, others, panel, last):
     rows, columns = panel.shape
     if last:
         shape = [jax.ShapeDtypeStruct((rows, 2, columns // 2), jnp.float32)] * 2
     else:
         shape = jax.ShapeDtypeStruct((rows, columns), jnp.bfloat16)
     return pl.pallas_call(
-        functools.partial(last_kernel if last else estimate_kernel, folded),
-        in_specs=[SMEM] * 2 + [VMEM] * (2 + len(others)),
+        last_kernel if last else estimate_kernel,
+        in_specs=[SMEM] + [VMEM] * (2 + len(others)),
         out_specs=[VMEM] * 2 if last else VMEM,
         out_shape=shape,
         compiler_params=params(8),
         cost_estimate=cost(16 * rows * columns, 16 * rows * columns),
         name="update",
-    )(place, wavelet, own, *others, panel)
+    )(wavelet, own, *others, panel)
 
 
 def swap(array, axis, bits):
@@ -385,13 +382,15 @@
     bf16, f32 = jnp.bfloat16, jnp.float32
     if n_src != 4:
         arriving = [swap(make(turn, [bf16])[0], "src", turn) for turn in range(n_src - 1, 0, -1)]
-        return make(0, [f32])[0], arriving, False
-    first = lax.ppermute(make(2, [bf16])[0], "src", [(0, 1), (1, 3), (3, 2), (2, 0)])
-    sent, kept = make(3, [bf16, f32])
+        return make(0, [f32])[0], arriving
+    farthest = make(3, [bf16])[0]
+    passed = lax.ppermute(farthest, "src", [(0, 1), (3, 2)])
+    middle = lax.ppermute(farthest, "src", [(1, 2), (2, 1)])
+    sent, kept = make(2, [bf16, f32])
     beside = swap(make(1, [bf16])[0], "src", 1)
-    outer = lax.ppermute(sent, "src", [(0, 3), (3, 0)])
-    inner = lax.ppermute(make_sum(kept, first), "src", [(1, 2), (2, 1)])
-    return make(0, [f32])[0], [first, beside, outer, inner], True
+    inward = lax.ppermute(sent, "src", [(0, 2), (3, 1)])
+    outward = lax.ppermute(make_sum(kept, passed), "src", [(1, 3), (2, 0)])
+    return make(0, [f32])[0], [middle, beside, inward, outward]
 
 
 def iterate(estimate, data, place, n_row, n_src, slice_rows, fresh):
@@ -403,10 +402,10 @@
     passed = {turn + 1: swap(piece, "row", 1) for turn, piece in {0: estimate, **direct}.items()}
     early = {0: estimate, 1: passed[1], **direct}
     late = {turn: passed[turn] for turn in range(n_row - 1, 1, -2)}
-    begun = make_terms(data, place, early, (n_src // 2,), [], slice_rows, [jnp.float32])
+    begun = make_terms(data, place, early, (n_src - 1,), [], slice_rows, [jnp.float32])
 
     def make(turn, types):
-        if turn == n_src // 2:
+        if turn == n_src - 1:
             return make_terms(data, place, late, (turn,), begun, slice_rows, types)
         return make_terms(data, place, {**early, **late}, (turn,), [], slice_rows, types)
 
@@ -441,8 +440,8 @@
     estimate = panel
     data = real_data, imag_data
     for iteration in range(ITERS):
-        own, arriving, folded, data = iterate(estimate, data, place, n_row, n_src, slice_rows, iteration == 0)
-        estimate = make_update(place, wavelet_inverse, own, arriving, panel, folded, iteration == ITERS - 1)
+        own, arriving, data = iterate(estimate, data, place, n_row, n_src, slice_rows, iteration == 0)
+        estimate = make_update(wavelet_inverse, own, arriving, panel, iteration == ITERS - 1)
     return tuple(estimate)
 
 

time: 176 us -> 188 us (1.068)
  waiting for transfers between devices: 46.5 us -> 52.5 us
  starting transfers between devices: 41.9 us -> 47.7 us
    ppermute x34, waiting for transfers between devices: 41.2 us -> 52.4 us  [swap(): lax.ppermute(array, axis, [(index, index ^ bits) for index in range(size)])]
    ppermute x9 -> x12, starting transfers between devices: 17.3 us -> 23.1 us  [the longest x3 11.7 us: exchange(): inward = lax.ppermute(sent, 'src', [(0, 2), (3, 1)])]
    ppermute x9 -> x12, waiting for transfers between devices: 5.24 us -> 0.03 us  [the longest x3 0.01 us: exchange(): passed = lax.ppermute(farthest, 'src', [(0, 1), (3, 2)])]
  transfers between devices with their start and end apart: 43 -> 46, of which waited for: 12 -> 9; matrix products, arithmetic and copies ran while one was open for 0% -> 0% of each run, Pallas kernels for 28% -> 26%
where the time goes in v6:
time: 188 us
  Pallas kernels  85.4 us (45%)
  waiting for transfers between devices  52.5 us (28%)
  starting transfers between devices  47.7 us (25%)
    ppermute x34, waiting for transfers between devices, swap(): lax.ppermute(array, axis, [(index, index ^ bits) for index in range(size)])  52.4 us
    pallas_call x15, Pallas kernels, make_terms(): pl.pallas_call(functools.partial(terms_kernel, turns, numbers, len(partia...  36.6 us
    ppermute x34, starting transfers between devices, swap(): lax.ppermute(array, axis, [(index, index ^ bits) for index in range(size)])  24.5 us
    pallas_call x1, Pallas kernels, make_spectra(): pl.pallas_call(functools.partial(spectra_kernel, packs, n_row), in_specs=...  23.8 us
    pallas_call x2, Pallas kernels, relay(): pl.pallas_call(functools.partial(relay_kernel, part), in_specs=[ANY, ANY]...  15.7 us
    ppermute x3, starting transfers between devices, exchange(): inward = lax.ppermute(sent, 'src', [(0, 2), (3, 1)])  11.7 us
    ppermute x3, starting transfers between devices, exchange(): passed = lax.ppermute(farthest, 'src', [(0, 1), (3, 2)])  5.31 us
    ppermute x3, starting transfers between devices, exchange(): outward = lax.ppermute(make_sum(kept, passed), 'src', [(1, 3), (2, 0)])  3.88 us
  transfers between devices with their start and end apart: 46, of which 9 were waited for; matrix products, arithmetic and copies ran while one was open for 0% of the time, Pallas kernels for 26%

profile of v6, /device:TPU:0, one launch (start us, length us, event | category | flops | bytes accessed | tf_op | source)
XLA Modules:
  0.0 188.0 jit_solution(3361056189059397678)
XLA Ops:
  1.7 23.8 %spectra.1 = (bf16[2,64,128]{2,1,0:T(8,128)(2,1)S(1)}, bf16[2,64,128]{2,1,0:T(8,128)(2,1)S(1)}, bf16[2,64,128]{2,1,0:T(8,128)(2,1)S(1)}, bf16[2,64,128]{2,1,0:T(...) custom-call(s32[2]{0:T(128)S(1)} %pad_add_fusion.place_ref, ...), custom_call_target="tpu_custom_call" | custom-call | flops 8589934592 | bytes 67108864 | tf_op jit(solution)/shard_map/spectra/pallas_call | solution.py:120
  26.0 2.6 %collective-permute-start.1 = (bf16[128,128]{1,0:T(8,128)(2,1)S(1)}, bf16[128,128]{1,0:T(8,128)(2,1)S(1)}, u32[]{:S(2)}, u32[]{:S(2)}) collective-permute-start(bf16[128,128]{1,0:T(8,128)(2,1)S(1)} %bitcast.18), channel_id=1, source_target_pairs={{0,8},{4,12},{8,0},{12,4},{16,24},{20,28},{24,16},{28,20},{1,9},{5... | collective-permute-start | bytes 98312 | tf_op jit(solution)/shard_map/ppermute | solution.py:378
  28.6 1.8 collective-permute-start.3
  30.4 2.6 %collective-permute-start.5 = (bf16[128,128]{1,0:T(8,128)(2,1)S(1)}, bf16[128,128]{1,0:T(8,128)(2,1)S(1)}, u32[]{:S(2)}, u32[]{:S(2)}) collective-permute-start(bf16[128,128]{1,0:T(8,128)(2,1)S(1)} %bitcast.14), channel_id=1, source_target_pairs={{0,24},{4,28},{8,16},{12,20},{16,8},{20,12},{24,0},{28,4},{1,25},{... | collective-permute-start | bytes 98312 | tf_op jit(solution)/shard_map/ppermute | solution.py:378
  33.5 1.7 hits.1.hits_ref
  35.2 2.0 %collective-permute-done.6.refs_7_ = bf16[128,128]{1,0:T(8,128)(2,1)S(1)} collective-permute-done((bf16[128,128]{1,0:T(8,128)(2,1)S(1)}, bf16[128,128]{1,0:T(8,128)(2,1)S(1)}, u32[]{:S(2)}, u32[]{:S(2)}) %collective-permute-start.6) | collective-permute-done | bytes 32800 | tf_op jit(solution)/shard_map/ppermute | solution.py:378
  37.2 2.8 %order.1 = (bf16[256,128]{1,0:T(8,128)(2,1)S(1)}, bf16[256,128]{1,0:T(8,128)(2,1)S(1)}, bf16[256,128]{1,0:T(8,128)(2,1)S(1)}, bf16[256,128]{1,0:T(8,128)(2,1)S(1)}) custom-call(s32[2]{0:T(128)S(1)} %pad_add_fusion.place_ref, s32[2048,128]{1,0:T(8,128)S(1)} %broadcast_in_dim.2.code_ref, bf16[2048,1024]{1,0:T(8,128)(2,1)S(1)} %hits.1.hits_ref, ...), custom_call_target="tpu_custom_call" | custom-call | flops 1073741824 | bytes 1048576 | tf_op jit(solution)/shard_map/order/pallas_call | solution.py:194
  40.1 1.6 collective-permute-start.7
  41.7 2.6 %collective-permute-start.8 = (bf16[256,128]{1,0:T(8,128)(2,1)S(1)}, bf16[256,128]{1,0:T(8,128)(2,1)S(1)}, u32[]{:S(2)}, u32[]{:S(2)}) collective-permute-start(bf16[256,128]{1,0:T(8,128)(2,1)S(1)} %get-tuple-element.38), channel_id=1, source_target_pairs={{0,2},{1,3},{2,0},{3,1},{4,6},{5,7},{6,4},{7,5},{8,10},{9,11},{10,... | collective-permute-start | bytes 196616 | tf_op jit(solution)/shard_map/ppermute | solution.py:378
  44.5 7.7 %relay.3 = (bf16[8,2048,512]{2,1,0:T(8,128)(2,1)S(1)}, f32[8,128]{1,0:T(8,128)S(1)}) custom-call(bf16[2,2048,8,512]{3,2,1,0:T(8,128)(2,1)} %data_ref.3, bf16[256,128]{1,0:T(8,128)(2,1)S(1)} %get-tuple-element.36.after_ref.refs_0_), custom_call_target="tpu_custom_call" | custom-call | bytes 33554432 | tf_op jit(solution)/shard_map/relay/pallas_call | solution.py:258
  55.3 1.5 collective-permute-start.12
  56.8 8.0 %relay.2 = (bf16[8,2048,512]{2,1,0:T(8,128)(2,1)S(1)}, f32[8,128]{1,0:T(8,128)}) custom-call(bf16[2,2048,8,512]{3,2,1,0:T(8,128)(2,1)} %data_ref.3, bf16[128,128]{1,0:T(8,128)(2,1)S(1)} %bitcast.12), custom_call_target="tpu_custom_call" | custom-call | bytes 33554432 | tf_op jit(solution)/shard_map/relay/pallas_call | solution.py:258
  64.8 2.5 %collective-permute-done.11.refs_3_ = bf16[512,256]{1,0:T(8,128)(2,1)S(1)} collective-permute-done((bf16[512,256]{1,0:T(8,128)(2,1)S(1)}, bf16[512,256]{1,0:T(8,128)(2,1)S(1)}, u32[]{:S(2)}, u32[]{:S(2)}) %collective-permute-start.11) | collective-permute-done | bytes 262176 | tf_op jit(solution)/shard_map/ppermute | solution.py:378
  67.8 2.1 %terms.16.refs_3_ = f32[512,256]{1,0:T(8,128)S(1)} custom-call(s32[2]{0:T(128)S(1)} %pad_add_fusion.place_ref, bf16[8,2048,512]{2,1,0:T(8,128)(2,1)S(1)} %get-tuple-element.41.real_ref, bf16[8,2048,512]{2,1,0:T(8,128)(2,1)S(1)} %get-tuple-element.42.imag_ref, bf16[512,256]{1,0:T(8,128)(2,1)S(1)} %panel.1.refs_0_.refs_4_, ...), custom_call_target="tpu_custom_call" | custom-call | flops 1342177280 | bytes 5242880 | tf_op jit(solution)/shard_map/terms/pallas_call | solution.py:307
  69.9 1.5 terms.17
  71.4 2.5 %collective-permute-start.20 = (bf16[512,256]{1,0:T(8,128)(2,1)S(1)}, bf16[512,256]{1,0:T(8,128)(2,1)S(1)}, u32[]{:S(2)}, u32[]{:S(2)}) collective-permute-start(bf16[512,256]{1,0:T(8,128)(2,1)S(1)} %terms.17), channel_id=1, source_target_pairs={{0,1},{3,2},{4,5},{7,6},{8,9},{11,10},{12,13},{15,14},{16,17},{19,... | collective-permute-start | bytes 786440 | tf_op jit(solution)/shard_map/ppermute | solution.py:387
  74.6 2.9 %terms.19 = (bf16[512,256]{1,0:T(8,128)(2,1)S(1)}, f32[512,256]{1,0:T(8,128)S(1)}) custom-call(s32[2]{0:T(128)S(1)} %pad_add_fusion.place_ref, bf16[8,2048,512]{2,1,0:T(8,128)(2,1)S(1)} %get-tuple-element.41.real_ref, bf16[8,2048,512]{2,1,0:T(8,128)(2,1)S(1)} %get-tuple-element.42.imag_ref, bf16[512,256]{1,0:T(8,128)(2,1)S(1)} %panel.1.refs_0_.refs_4_, ...), custom_call_target="tpu_custom_call" | custom-call | flops 2147483648 | bytes 8388608 | tf_op jit(solution)/shard_map/terms/pallas_call | solution.py:307
  77.5 4.2 %collective-permute-start.19 = (bf16[512,256]{1,0:T(8,128)(2,1)S(1)}, bf16[512,256]{1,0:T(8,128)(2,1)S(1)}, u32[]{:S(2)}, u32[]{:S(2)}) collective-permute-start(bf16[512,256]{1,0:T(8,128)(2,1)S(1)} %get-tuple-element.46), channel_id=1, source_target_pairs={{0,2},{3,1},{4,6},{7,5},{8,10},{11,9},{12,14},{15,13},{16,18},{19,... | collective-permute-start | bytes 786440 | tf_op jit(solution)/shard_map/ppermute | solution.py:391
  81.7 2.9 %terms.18 = bf16[512,256]{1,0:T(8,128)(2,1)S(1)} custom-call(s32[2]{0:T(128)S(1)} %pad_add_fusion.place_ref, bf16[8,2048,512]{2,1,0:T(8,128)(2,1)S(1)} %get-tuple-element.41.real_ref, bf16[8,2048,512]{2,1,0:T(8,128)(2,1)S(1)} %get-tuple-element.42.imag_ref, bf16[512,256]{1,0:T(8,128)(2,1)S(1)} %panel.1.refs_0_.refs_4_, ...), custom_call_target="tpu_custom_call" | custom-call | flops 2147483648 | bytes 8388608 | tf_op jit(solution)/shard_map/terms/pallas_call | solution.py:307
  84.7 1.3 collective-permute-start.21
  86.0 2.9 %terms.15.own_ref = f32[512,256]{1,0:T(8,128)S(1)} custom-call(s32[2]{0:T(128)S(1)} %pad_add_fusion.place_ref, bf16[8,2048,512]{2,1,0:T(8,128)(2,1)S(1)} %get-tuple-element.41.real_ref, bf16[8,2048,512]{2,1,0:T(8,128)(2,1)S(1)} %get-tuple-element.42.imag_ref, bf16[512,256]{1,0:T(8,128)(2,1)S(1)} %panel.1.refs_0_.refs_4_, ...), custom_call_target="tpu_custom_call" | custom-call | flops 2147483648 | bytes 8388608 | tf_op jit(solution)/shard_map/terms/pallas_call | solution.py:307
  88.9 9.5 %collective-permute-done.18.refs_1_ = bf16[512,256]{1,0:T(8,128)(2,1)S(1)} collective-permute-done((bf16[512,256]{1,0:T(8,128)(2,1)S(1)}, bf16[512,256]{1,0:T(8,128)(2,1)S(1)}, u32[]{:S(2)}, u32[]{:S(2)}) %collective-permute-start.18) | collective-permute-done | bytes 262176 | tf_op jit(solution)/shard_map/ppermute | solution.py:378
  101.4 1.3 collective-permute-start.23
  102.8 6.7 %collective-permute-done.25.refs_4_ = bf16[512,256]{1,0:T(8,128)(2,1)S(1)} collective-permute-done((bf16[512,256]{1,0:T(8,128)(2,1)S(1)}, bf16[512,256]{1,0:T(8,128)(2,1)S(1)}, u32[]{:S(2)}, u32[]{:S(2)}) %collective-permute-start.25) | collective-permute-done | bytes 262176 | tf_op jit(solution)/shard_map/ppermute | solution.py:378
  109.4 3.7 %collective-permute-done.24.refs_3_ = bf16[512,256]{1,0:T(8,128)(2,1)S(1)} collective-permute-done((bf16[512,256]{1,0:T(8,128)(2,1)S(1)}, bf16[512,256]{1,0:T(8,128)(2,1)S(1)}, u32[]{:S(2)}, u32[]{:S(2)}) %collective-permute-start.24) | collective-permute-done | bytes 262176 | tf_op jit(solution)/shard_map/ppermute | solution.py:378
  113.6 2.1 %terms.21.refs_3_ = f32[512,256]{1,0:T(8,128)S(1)} custom-call(s32[2]{0:T(128)S(1)} %pad_add_fusion.place_ref, bf16[8,2048,512]{2,1,0:T(8,128)(2,1)S(1)} %get-tuple-element.41.real_ref, bf16[8,2048,512]{2,1,0:T(8,128)(2,1)S(1)} %get-tuple-element.42.imag_ref, bf16[512,256]{1,0:T(8,128)(2,1)S(1)} %update.3.refs_0_, ...), custom_call_target="tpu_custom_call" | custom-call | flops 1342177280 | bytes 5242880 | tf_op jit(solution)/shard_map/terms/pallas_call | solution.py:307
  115.7 1.5 terms.22
  117.2 1.5 collective-permute-start.32
  119.4 2.9 %terms.24 = (bf16[512,256]{1,0:T(8,128)(2,1)S(1)}, f32[512,256]{1,0:T(8,128)S(1)}) custom-call(s32[2]{0:T(128)S(1)} %pad_add_fusion.place_ref, bf16[8,2048,512]{2,1,0:T(8,128)(2,1)S(1)} %get-tuple-element.41.real_ref, bf16[8,2048,512]{2,1,0:T(8,128)(2,1)S(1)} %get-tuple-element.42.imag_ref, bf16[512,256]{1,0:T(8,128)(2,1)S(1)} %update.3.refs_0_, ...), custom_call_target="tpu_custom_call" | custom-call | flops 2147483648 | bytes 8388608 | tf_op jit(solution)/shard_map/terms/pallas_call | solution.py:307
  122.3 4.0 %collective-permute-start.31 = (bf16[512,256]{1,0:T(8,128)(2,1)S(1)}, bf16[512,256]{1,0:T(8,128)(2,1)S(1)}, u32[]{:S(2)}, u32[]{:S(2)}) collective-permute-start(bf16[512,256]{1,0:T(8,128)(2,1)S(1)} %get-tuple-element.48), channel_id=1, source_target_pairs={{0,2},{3,1},{4,6},{7,5},{8,10},{11,9},{12,14},{15,13},{16,18},{19,... | collective-permute-start | bytes 786440 | tf_op jit(solution)/shard_map/ppermute | solution.py:391
  126.3 2.9 %terms.23 = bf16[512,256]{1,0:T(8,128)(2,1)S(1)} custom-call(s32[2]{0:T(128)S(1)} %pad_add_fusion.place_ref, bf16[8,2048,512]{2,1,0:T(8,128)(2,1)S(1)} %get-tuple-element.41.real_ref, bf16[8,2048,512]{2,1,0:T(8,128)(2,1)S(1)} %get-tuple-element.42.imag_ref, bf16[512,256]{1,0:T(8,128)(2,1)S(1)} %update.3.refs_0_, ...), custom_call_target="tpu_custom_call" | custom-call | flops 2147483648 | bytes 8388608 | tf_op jit(solution)/shard_map/terms/pallas_call | solution.py:307
  129.3 1.3 collective-permute-start.33
  130.6 2.9 %terms.20.own_ref = f32[512,256]{1,0:T(8,128)S(1)} custom-call(s32[2]{0:T(128)S(1)} %pad_add_fusion.place_ref, bf16[8,2048,512]{2,1,0:T(8,128)(2,1)S(1)} %get-tuple-element.41.real_ref, bf16[8,2048,512]{2,1,0:T(8,128)(2,1)S(1)} %get-tuple-element.42.imag_ref, bf16[512,256]{1,0:T(8,128)(2,1)S(1)} %update.3.refs_0_, ...), custom_call_target="tpu_custom_call" | custom-call | flops 2147483648 | bytes 8388608 | tf_op jit(solution)/shard_map/terms/pallas_call | solution.py:307
  133.5 9.0 %collective-permute-done.30.refs_1_ = bf16[512,256]{1,0:T(8,128)(2,1)S(1)} collective-permute-done((bf16[512,256]{1,0:T(8,128)(2,1)S(1)}, bf16[512,256]{1,0:T(8,128)(2,1)S(1)}, u32[]{:S(2)}, u32[]{:S(2)}) %collective-permute-start.30) | collective-permute-done | bytes 262176 | tf_op jit(solution)/shard_map/ppermute | solution.py:378
  143.3 1.3 collective-permute-start.37
  145.5 1.3 collective-permute-start.35
  146.8 6.6 %collective-permute-done.37.refs_4_ = bf16[512,256]{1,0:T(8,128)(2,1)S(1)} collective-permute-done((bf16[512,256]{1,0:T(8,128)(2,1)S(1)}, bf16[512,256]{1,0:T(8,128)(2,1)S(1)}, u32[]{:S(2)}, u32[]{:S(2)}) %collective-permute-start.37) | collective-permute-done | bytes 262176 | tf_op jit(solution)/shard_map/ppermute | solution.py:378
  153.5 3.1 %collective-permute-done.36.refs_3_ = bf16[512,256]{1,0:T(8,128)(2,1)S(1)} collective-permute-done((bf16[512,256]{1,0:T(8,128)(2,1)S(1)}, bf16[512,256]{1,0:T(8,128)(2,1)S(1)}, u32[]{:S(2)}, u32[]{:S(2)}) %collective-permute-start.36) | collective-permute-done | bytes 262176 | tf_op jit(solution)/shard_map/ppermute | solution.py:378
  157.1 2.1 %terms.26.refs_3_ = f32[512,256]{1,0:T(8,128)S(1)} custom-call(s32[2]{0:T(128)S(1)} %pad_add_fusion.place_ref, bf16[8,2048,512]{2,1,0:T(8,128)(2,1)S(1)} %get-tuple-element.41.real_ref, bf16[8,2048,512]{2,1,0:T(8,128)(2,1)S(1)} %get-tuple-element.42.imag_ref, bf16[512,256]{1,0:T(8,128)(2,1)S(1)} %update.4.refs_0_, ...), custom_call_target="tpu_custom_call" | custom-call | flops 1342177280 | bytes 5242880 | tf_op jit(solution)/shard_map/terms/pallas_call | solution.py:307
  159.2 1.5 terms.27
  160.8 1.3 collective-permute-start.44
  163.0 2.9 %terms.29 = (bf16[512,256]{1,0:T(8,128)(2,1)S(1)}, f32[512,256]{1,0:T(8,128)S(1)}) custom-call(s32[2]{0:T(128)S(1)} %pad_add_fusion.place_ref, bf16[8,2048,512]{2,1,0:T(8,128)(2,1)S(1)} %get-tuple-element.41.real_ref, bf16[8,2048,512]{2,1,0:T(8,128)(2,1)S(1)} %get-tuple-element.42.imag_ref, bf16[512,256]{1,0:T(8,128)(2,1)S(1)} %update.4.refs_0_, ...), custom_call_target="tpu_custom_call" | custom-call | flops 2147483648 | bytes 8388608 | tf_op jit(solution)/shard_map/terms/pallas_call | solution.py:307
  165.9 3.6 %collective-permute-start.43 = (bf16[512,256]{1,0:T(8,128)(2,1)S(1)}, bf16[512,256]{1,0:T(8,128)(2,1)S(1)}, u32[]{:S(2)}, u32[]{:S(2)}) collective-permute-start(bf16[512,256]{1,0:T(8,128)(2,1)S(1)} %get-tuple-element.50), channel_id=1, source_target_pairs={{0,2},{3,1},{4,6},{7,5},{8,10},{11,9},{12,14},{15,13},{16,18},{19,... | collective-permute-start | bytes 786440 | tf_op jit(solution)/shard_map/ppermute | solution.py:391
  169.4 2.9 %terms.28 = bf16[512,256]{1,0:T(8,128)(2,1)S(1)} custom-call(s32[2]{0:T(128)S(1)} %pad_add_fusion.place_ref, bf16[8,2048,512]{2,1,0:T(8,128)(2,1)S(1)} %get-tuple-element.41.real_ref, bf16[8,2048,512]{2,1,0:T(8,128)(2,1)S(1)} %get-tuple-element.42.imag_ref, bf16[512,256]{1,0:T(8,128)(2,1)S(1)} %update.4.refs_0_, ...), custom_call_target="tpu_custom_call" | custom-call | flops 2147483648 | bytes 8388608 | tf_op jit(solution)/shard_map/terms/pallas_call | solution.py:307
  172.5 1.3 collective-permute-start.45
  173.8 2.9 %terms.25.own_ref = f32[512,256]{1,0:T(8,128)S(1)} custom-call(s32[2]{0:T(128)S(1)} %pad_add_fusion.place_ref, bf16[8,2048,512]{2,1,0:T(8,128)(2,1)S(1)} %get-tuple-element.41.real_ref, bf16[8,2048,512]{2,1,0:T(8,128)(2,1)S(1)} %get-tuple-element.42.imag_ref, bf16[512,256]{1,0:T(8,128)(2,1)S(1)} %update.4.refs_0_, ...), custom_call_target="tpu_custom_call" | custom-call | flops 2147483648 | bytes 8388608 | tf_op jit(solution)/shard_map/terms/pallas_call | solution.py:307
  176.7 9.3 %collective-permute-done.42.refs_1_ = bf16[512,256]{1,0:T(8,128)(2,1)S(1)} collective-permute-done((bf16[512,256]{1,0:T(8,128)(2,1)S(1)}, bf16[512,256]{1,0:T(8,128)(2,1)S(1)}, u32[]{:S(2)}, u32[]{:S(2)}) %collective-permute-start.42) | collective-permute-done | bytes 262176 | tf_op jit(solution)/shard_map/ppermute | solution.py:378
  186.0 2.1 %update.5 = (f32[512,2,128]{2,1,0:T(2,128)}, f32[512,2,128]{2,1,0:T(2,128)}) custom-call(f32[2]{0:T(128)S(1)} %copy-done.1, f32[512,256]{1,0:T(8,128)S(1)} %terms.25.own_ref, bf16[512,256]{1,0:T(8,128)(2,1)S(1)} %collective-permute-done.41.refs_0_, bf16[512,256]{1,0:T(8,128)(2,1)S(1)} %collective-permute-done.42.refs_1_, ...), custom_call_target="tpu_custom_call" | custom-call | flops 2097152 | bytes 2097152 | tf_op jit(solution)/shard_map/update/pallas_call | solution.py:365
  (80 shorter events, 14.4 us)
Async XLA Ops:
  1.7 31.4 %copy-start.2 = (s32[2048]{0:T(1024)S(1)}, s32[2048]{0:T(1024)}, u32[]{:S(2)}) copy-start(s32[2048]{0:T(1024)} %param.6) | copy-start | bytes 24580
  25.5 4.9 %collective-permute-start = (bf16[128,128]{1,0:T(8,128)(2,1)S(1)}, bf16[128,128]{1,0:T(8,128)(2,1)S(1)}, u32[]{:S(2)}, u32[]{:S(2)}) collective-permute-start(bf16[128,128]{1,0:T(8,128)(2,1)S(1)} %bitcast.19), channel_id=1, source_target_pairs={{0,4},{4,0},{8,12},{12,8},{16,20},{20,16},{24,28},{28,24},{1,5},{5... | collective-permute-start | bytes 98312 | tf_op jit(solution)/shard_map/ppermute | solution.py:378
  26.0 7.0 %collective-permute-start.1 = (bf16[128,128]{1,0:T(8,128)(2,1)S(1)}, bf16[128,128]{1,0:T(8,128)(2,1)S(1)}, u32[]{:S(2)}, u32[]{:S(2)}) collective-permute-start(bf16[128,128]{1,0:T(8,128)(2,1)S(1)} %bitcast.18), channel_id=1, source_target_pairs={{0,8},{4,12},{8,0},{12,4},{16,24},{20,28},{24,16},{28,20},{1,9},{5... | collective-permute-start | bytes 98312 | tf_op jit(solution)/shard_map/ppermute | solution.py:378
  28.5 6.6 %collective-permute-start.2 = (bf16[128,128]{1,0:T(8,128)(2,1)S(1)}, bf16[128,128]{1,0:T(8,128)(2,1)S(1)}, u32[]{:S(2)}, u32[]{:S(2)}) collective-permute-start(bf16[128,128]{1,0:T(8,128)(2,1)S(1)} %bitcast.17), channel_id=1, source_target_pairs={{0,12},{4,8},{8,4},{12,0},{16,28},{20,24},{24,20},{28,16},{1,13},{... | collective-permute-start | bytes 98312 | tf_op jit(solution)/shard_map/ppermute | solution.py:378
  28.6 6.6 %collective-permute-start.3 = (bf16[128,128]{1,0:T(8,128)(2,1)S(1)}, bf16[128,128]{1,0:T(8,128)(2,1)S(1)}, u32[]{:S(2)}, u32[]{:S(2)}) collective-permute-start(bf16[128,128]{1,0:T(8,128)(2,1)S(1)} %bitcast.16), channel_id=1, source_target_pairs={{0,16},{4,20},{8,24},{12,28},{16,0},{20,4},{24,8},{28,12},{1,17},{... | collective-permute-start | bytes 98312 | tf_op jit(solution)/shard_map/ppermute | solution.py:378
  30.4 4.8 %collective-permute-start.4 = (bf16[128,128]{1,0:T(8,128)(2,1)S(1)}, bf16[128,128]{1,0:T(8,128)(2,1)S(1)}, u32[]{:S(2)}, u32[]{:S(2)}) collective-permute-start(bf16[128,128]{1,0:T(8,128)(2,1)S(1)} %bitcast.15), channel_id=1, source_target_pairs={{0,20},{4,16},{8,28},{12,24},{16,4},{20,0},{24,12},{28,8},{1,21},{... | collective-permute-start | bytes 98312 | tf_op jit(solution)/shard_map/ppermute | solution.py:378
  30.4 4.8 %collective-permute-start.5 = (bf16[128,128]{1,0:T(8,128)(2,1)S(1)}, bf16[128,128]{1,0:T(8,128)(2,1)S(1)}, u32[]{:S(2)}, u32[]{:S(2)}) collective-permute-start(bf16[128,128]{1,0:T(8,128)(2,1)S(1)} %bitcast.14), channel_id=1, source_target_pairs={{0,24},{4,28},{8,16},{12,20},{16,8},{20,12},{24,0},{28,4},{1,25},{... | collective-permute-start | bytes 98312 | tf_op jit(solution)/shard_map/ppermute | solution.py:378
  33.0 4.2 %collective-permute-start.6 = (bf16[128,128]{1,0:T(8,128)(2,1)S(1)}, bf16[128,128]{1,0:T(8,128)(2,1)S(1)}, u32[]{:S(2)}, u32[]{:S(2)}) collective-permute-start(bf16[128,128]{1,0:T(8,128)(2,1)S(1)} %bitcast.13), channel_id=1, source_target_pairs={{0,28},{4,24},{8,20},{12,16},{16,12},{20,8},{24,4},{28,0},{1,29},{... | collective-permute-start | bytes 98312 | tf_op jit(solution)/shard_map/ppermute | solution.py:378
  40.1 12.1 %collective-permute-start.7 = (bf16[256,128]{1,0:T(8,128)(2,1)S(1)}, bf16[256,128]{1,0:T(8,128)(2,1)S(1)}, u32[]{:S(2)}, u32[]{:S(2)}) collective-permute-start(bf16[256,128]{1,0:T(8,128)(2,1)S(1)} %get-tuple-element.37), channel_id=1, source_target_pairs={{0,1},{1,0},{2,3},{3,2},{4,5},{5,4},{6,7},{7,6},{8,9},{9,8},{10,11... | collective-permute-start | bytes 196616 | tf_op jit(solution)/shard_map/ppermute | solution.py:378
  41.7 10.5 %collective-permute-start.8 = (bf16[256,128]{1,0:T(8,128)(2,1)S(1)}, bf16[256,128]{1,0:T(8,128)(2,1)S(1)}, u32[]{:S(2)}, u32[]{:S(2)}) collective-permute-start(bf16[256,128]{1,0:T(8,128)(2,1)S(1)} %get-tuple-element.38), channel_id=1, source_target_pairs={{0,2},{1,3},{2,0},{3,1},{4,6},{5,7},{6,4},{7,5},{8,10},{9,11},{10,... | collective-permute-start | bytes 196616 | tf_op jit(solution)/shard_map/ppermute | solution.py:378
  44.3 7.9 %collective-permute-start.9 = (bf16[256,128]{1,0:T(8,128)(2,1)S(1)}, bf16[256,128]{1,0:T(8,128)(2,1)S(1)}, u32[]{:S(2)}, u32[]{:S(2)}) collective-permute-start(bf16[256,128]{1,0:T(8,128)(2,1)S(1)} %get-tuple-element.39), channel_id=1, source_target_pairs={{0,3},{1,2},{2,1},{3,0},{4,7},{5,6},{6,5},{7,4},{8,11},{9,10},{10,... | collective-permute-start | bytes 196616 | tf_op jit(solution)/shard_map/ppermute | solution.py:378
  53.2 11.5 %collective-permute-start.10 = (bf16[512,256]{1,0:T(8,128)(2,1)S(1)}, bf16[512,256]{1,0:T(8,128)(2,1)S(1)}, u32[]{:S(2)}, u32[]{:S(2)}) collective-permute-start(bf16[512,256]{1,0:T(8,128)(2,1)S(1)} %panel.1.refs_0_.refs_4_), channel_id=1, source_target_pairs={{0,24},{4,28},{8,16},{12,20},{16,8},{20,12},{24,0},{28,4},{1,25},{... | collective-permute-start | bytes 786440 | tf_op jit(solution)/shard_map/ppermute | solution.py:378
  54.4 12.9 %collective-permute-start.11 = (bf16[512,256]{1,0:T(8,128)(2,1)S(1)}, bf16[512,256]{1,0:T(8,128)(2,1)S(1)}, u32[]{:S(2)}, u32[]{:S(2)}) collective-permute-start(bf16[512,256]{1,0:T(8,128)(2,1)S(1)} %panel.1.refs_0_.refs_4_), channel_id=1, source_target_pairs={{0,16},{4,20},{8,24},{12,28},{16,0},{20,4},{24,8},{28,12},{1,17},{... | collective-permute-start | bytes 786440 | tf_op jit(solution)/shard_map/ppermute | solution.py:378
  55.3 12.0 %collective-permute-start.12 = (bf16[512,256]{1,0:T(8,128)(2,1)S(1)}, bf16[512,256]{1,0:T(8,128)(2,1)S(1)}, u32[]{:S(2)}, u32[]{:S(2)}) collective-permute-start(bf16[512,256]{1,0:T(8,128)(2,1)S(1)} %panel.1.refs_0_.refs_4_), channel_id=1, source_target_pairs={{0,8},{4,12},{8,0},{12,4},{16,24},{20,28},{24,16},{28,20},{1,9},{5... | collective-permute-start | bytes 786440 | tf_op jit(solution)/shard_map/ppermute | solution.py:378
  56.8 11.0 %collective-permute-start.13 = (bf16[512,256]{1,0:T(8,128)(2,1)S(1)}, bf16[512,256]{1,0:T(8,128)(2,1)S(1)}, u32[]{:S(2)}, u32[]{:S(2)}) collective-permute-start(bf16[512,256]{1,0:T(8,128)(2,1)S(1)} %panel.1.refs_0_.refs_4_), channel_id=1, source_target_pairs={{0,4},{4,0},{8,12},{12,8},{16,20},{20,16},{24,28},{28,24},{1,5},{5... | collective-permute-start | bytes 786440 | tf_op jit(solution)/shard_map/ppermute | solution.py:378
  67.2 2.6 %collective-permute-start.14 = (bf16[512,256]{1,0:T(8,128)(2,1)S(1)}, bf16[512,256]{1,0:T(8,128)(2,1)S(1)}, u32[]{:S(2)}, u32[]{:S(2)}) collective-permute-start(bf16[512,256]{1,0:T(8,128)(2,1)S(1)} %collective-permute-done.10.refs_2_), channel_id=1, source_target_pairs={{0,4},{4,0},{8,12},{12,8},{16,20},{20,16},{24,28},{28,24},{1,5},{5... | collective-permute-start | bytes 786440 | tf_op jit(solution)/shard_map/ppermute | solution.py:378
  67.2 2.6 %collective-permute-start.15 = (bf16[512,256]{1,0:T(8,128)(2,1)S(1)}, bf16[512,256]{1,0:T(8,128)(2,1)S(1)}, u32[]{:S(2)}, u32[]{:S(2)}) collective-permute-start(bf16[512,256]{1,0:T(8,128)(2,1)S(1)} %collective-permute-done.11.refs_3_), channel_id=1, source_target_pairs={{0,4},{4,0},{8,12},{12,8},{16,20},{20,16},{24,28},{28,24},{1,5},{5... | collective-permute-start | bytes 786440 | tf_op jit(solution)/shard_map/ppermute | solution.py:378
  67.8 2.1 %collective-permute-start.16 = (bf16[512,256]{1,0:T(8,128)(2,1)S(1)}, bf16[512,256]{1,0:T(8,128)(2,1)S(1)}, u32[]{:S(2)}, u32[]{:S(2)}) collective-permute-start(bf16[512,256]{1,0:T(8,128)(2,1)S(1)} %collective-permute-done.12.refs_4_), channel_id=1, source_target_pairs={{0,4},{4,0},{8,12},{12,8},{16,20},{20,16},{24,28},{28,24},{1,5},{5... | collective-permute-start | bytes 786440 | tf_op jit(solution)/shard_map/ppermute | solution.py:378
  71.4 13.2 %collective-permute-start.20 = (bf16[512,256]{1,0:T(8,128)(2,1)S(1)}, bf16[512,256]{1,0:T(8,128)(2,1)S(1)}, u32[]{:S(2)}, u32[]{:S(2)}) collective-permute-start(bf16[512,256]{1,0:T(8,128)(2,1)S(1)} %terms.17), channel_id=1, source_target_pairs={{0,1},{3,2},{4,5},{7,6},{8,9},{11,10},{12,13},{15,14},{16,17},{19,... | collective-permute-start | bytes 786440 | tf_op jit(solution)/shard_map/ppermute | solution.py:387
  73.9 24.5 %collective-permute-start.17 = (bf16[512,256]{1,0:T(8,128)(2,1)S(1)}, bf16[512,256]{1,0:T(8,128)(2,1)S(1)}, u32[]{:S(2)}, u32[]{:S(2)}) collective-permute-start(bf16[512,256]{1,0:T(8,128)(2,1)S(1)} %terms.17), channel_id=1, source_target_pairs={{1,2},{2,1},{5,6},{6,5},{9,10},{10,9},{13,14},{14,13},{17,18},{18,... | collective-permute-start | bytes 786440 | tf_op jit(solution)/shard_map/ppermute | solution.py:388
  77.5 11.4 %collective-permute-start.19 = (bf16[512,256]{1,0:T(8,128)(2,1)S(1)}, bf16[512,256]{1,0:T(8,128)(2,1)S(1)}, u32[]{:S(2)}, u32[]{:S(2)}) collective-permute-start(bf16[512,256]{1,0:T(8,128)(2,1)S(1)} %get-tuple-element.46), channel_id=1, source_target_pairs={{0,2},{3,1},{4,6},{7,5},{8,10},{11,9},{12,14},{15,13},{16,18},{19,... | collective-permute-start | bytes 786440 | tf_op jit(solution)/shard_map/ppermute | solution.py:391
  84.6 13.8 %collective-permute-start.18 = (bf16[512,256]{1,0:T(8,128)(2,1)S(1)}, bf16[512,256]{1,0:T(8,128)(2,1)S(1)}, u32[]{:S(2)}, u32[]{:S(2)}) collective-permute-start(bf16[512,256]{1,0:T(8,128)(2,1)S(1)} %terms.18), channel_id=1, source_target_pairs={{0,1},{1,0},{2,3},{3,2},{4,5},{5,4},{6,7},{7,6},{8,9},{9,8},{10,11... | collective-permute-start | bytes 786440 | tf_op jit(solution)/shard_map/ppermute | solution.py:378
  84.7 13.7 %copy-start.1 = (f32[2]{0:T(128)S(1)}, f32[2]{0:T(128)}, u32[]{:S(2)}) copy-start(f32[2]{0:T(128)} %wave_ref.5) | copy-start | bytes 28
  84.7 13.7 %collective-permute-start.21 = (bf16[512,256]{1,0:T(8,128)(2,1)S(1)}, bf16[512,256]{1,0:T(8,128)(2,1)S(1)}, u32[]{:S(2)}, u32[]{:S(2)}) collective-permute-start(bf16[512,256]{1,0:T(8,128)(2,1)S(1)} %sum.3), channel_id=1, source_target_pairs={{1,3},{2,0},{5,7},{6,4},{9,11},{10,8},{13,15},{14,12},{17,19},{18,... | collective-permute-start | bytes 786440 | tf_op jit(solution)/shard_map/ppermute | solution.py:392
  99.2 10.2 %collective-permute-start.25 = (bf16[512,256]{1,0:T(8,128)(2,1)S(1)}, bf16[512,256]{1,0:T(8,128)(2,1)S(1)}, u32[]{:S(2)}, u32[]{:S(2)}) collective-permute-start(bf16[512,256]{1,0:T(8,128)(2,1)S(1)} %update.3.refs_0_), channel_id=1, source_target_pairs={{0,24},{4,28},{8,16},{12,20},{16,8},{20,12},{24,0},{28,4},{1,25},{... | collective-permute-start | bytes 786440 | tf_op jit(solution)/shard_map/ppermute | solution.py:378
  100.4 12.6 %collective-permute-start.24 = (bf16[512,256]{1,0:T(8,128)(2,1)S(1)}, bf16[512,256]{1,0:T(8,128)(2,1)S(1)}, u32[]{:S(2)}, u32[]{:S(2)}) collective-permute-start(bf16[512,256]{1,0:T(8,128)(2,1)S(1)} %update.3.refs_0_), channel_id=1, source_target_pairs={{0,16},{4,20},{8,24},{12,28},{16,0},{20,4},{24,8},{28,12},{1,17},{... | collective-permute-start | bytes 786440 | tf_op jit(solution)/shard_map/ppermute | solution.py:378
  101.4 11.7 %collective-permute-start.23 = (bf16[512,256]{1,0:T(8,128)(2,1)S(1)}, bf16[512,256]{1,0:T(8,128)(2,1)S(1)}, u32[]{:S(2)}, u32[]{:S(2)}) collective-permute-start(bf16[512,256]{1,0:T(8,128)(2,1)S(1)} %update.3.refs_0_), channel_id=1, source_target_pairs={{0,8},{4,12},{8,0},{12,4},{16,24},{20,28},{24,16},{28,20},{1,9},{5... | collective-permute-start | bytes 786440 | tf_op jit(solution)/shard_map/ppermute | solution.py:378
  102.8 10.8 %collective-permute-start.22 = (bf16[512,256]{1,0:T(8,128)(2,1)S(1)}, bf16[512,256]{1,0:T(8,128)(2,1)S(1)}, u32[]{:S(2)}, u32[]{:S(2)}) collective-permute-start(bf16[512,256]{1,0:T(8,128)(2,1)S(1)} %update.3.refs_0_), channel_id=1, source_target_pairs={{0,4},{4,0},{8,12},{12,8},{16,20},{20,16},{24,28},{28,24},{1,5},{5... | collective-permute-start | bytes 786440 | tf_op jit(solution)/shard_map/ppermute | solution.py:378
  109.4 6.3 %collective-permute-start.26 = (bf16[512,256]{1,0:T(8,128)(2,1)S(1)}, bf16[512,256]{1,0:T(8,128)(2,1)S(1)}, u32[]{:S(2)}, u32[]{:S(2)}) collective-permute-start(bf16[512,256]{1,0:T(8,128)(2,1)S(1)} %collective-permute-done.25.refs_4_), channel_id=1, source_target_pairs={{0,4},{4,0},{8,12},{12,8},{16,20},{20,16},{24,28},{28,24},{1,5},{5... | collective-permute-start | bytes 786440 | tf_op jit(solution)/shard_map/ppermute | solution.py:378
  113.1 2.6 %collective-permute-start.27 = (bf16[512,256]{1,0:T(8,128)(2,1)S(1)}, bf16[512,256]{1,0:T(8,128)(2,1)S(1)}, u32[]{:S(2)}, u32[]{:S(2)}) collective-permute-start(bf16[512,256]{1,0:T(8,128)(2,1)S(1)} %collective-permute-done.24.refs_3_), channel_id=1, source_target_pairs={{0,4},{4,0},{8,12},{12,8},{16,20},{20,16},{24,28},{28,24},{1,5},{5... | collective-permute-start | bytes 786440 | tf_op jit(solution)/shard_map/ppermute | solution.py:378
  113.1 2.6 %collective-permute-start.28 = (bf16[512,256]{1,0:T(8,128)(2,1)S(1)}, bf16[512,256]{1,0:T(8,128)(2,1)S(1)}, u32[]{:S(2)}, u32[]{:S(2)}) collective-permute-start(bf16[512,256]{1,0:T(8,128)(2,1)S(1)} %collective-permute-done.23.refs_2_), channel_id=1, source_target_pairs={{0,4},{4,0},{8,12},{12,8},{16,20},{20,16},{24,28},{28,24},{1,5},{5... | collective-permute-start | bytes 786440 | tf_op jit(solution)/shard_map/ppermute | solution.py:378
  117.2 12.0 %collective-permute-start.32 = (bf16[512,256]{1,0:T(8,128)(2,1)S(1)}, bf16[512,256]{1,0:T(8,128)(2,1)S(1)}, u32[]{:S(2)}, u32[]{:S(2)}) collective-permute-start(bf16[512,256]{1,0:T(8,128)(2,1)S(1)} %terms.22), channel_id=1, source_target_pairs={{0,1},{3,2},{4,5},{7,6},{8,9},{11,10},{12,13},{15,14},{16,17},{19,... | collective-permute-start | bytes 786440 | tf_op jit(solution)/shard_map/ppermute | solution.py:387
  118.7 23.8 %collective-permute-start.29 = (bf16[512,256]{1,0:T(8,128)(2,1)S(1)}, bf16[512,256]{1,0:T(8,128)(2,1)S(1)}, u32[]{:S(2)}, u32[]{:S(2)}) collective-permute-start(bf16[512,256]{1,0:T(8,128)(2,1)S(1)} %terms.22), channel_id=1, source_target_pairs={{1,2},{2,1},{5,6},{6,5},{9,10},{10,9},{13,14},{14,13},{17,18},{18,... | collective-permute-start | bytes 786440 | tf_op jit(solution)/shard_map/ppermute | solution.py:388
  122.3 11.2 %collective-permute-start.31 = (bf16[512,256]{1,0:T(8,128)(2,1)S(1)}, bf16[512,256]{1,0:T(8,128)(2,1)S(1)}, u32[]{:S(2)}, u32[]{:S(2)}) collective-permute-start(bf16[512,256]{1,0:T(8,128)(2,1)S(1)} %get-tuple-element.48), channel_id=1, source_target_pairs={{0,2},{3,1},{4,6},{7,5},{8,10},{11,9},{12,14},{15,13},{16,18},{19,... | collective-permute-start | bytes 786440 | tf_op jit(solution)/shard_map/ppermute | solution.py:391
  129.1 13.3 %collective-permute-start.30 = (bf16[512,256]{1,0:T(8,128)(2,1)S(1)}, bf16[512,256]{1,0:T(8,128)(2,1)S(1)}, u32[]{:S(2)}, u32[]{:S(2)}) collective-permute-start(bf16[512,256]{1,0:T(8,128)(2,1)S(1)} %terms.23), channel_id=1, source_target_pairs={{0,1},{1,0},{2,3},{3,2},{4,5},{5,4},{6,7},{7,6},{8,9},{9,8},{10,11... | collective-permute-start | bytes 786440 | tf_op jit(solution)/shard_map/ppermute | solution.py:378
  129.3 13.2 %collective-permute-start.33 = (bf16[512,256]{1,0:T(8,128)(2,1)S(1)}, bf16[512,256]{1,0:T(8,128)(2,1)S(1)}, u32[]{:S(2)}, u32[]{:S(2)}) collective-permute-start(bf16[512,256]{1,0:T(8,128)(2,1)S(1)} %sum.4), channel_id=1, source_target_pairs={{1,3},{2,0},{5,7},{6,4},{9,11},{10,8},{13,15},{14,12},{17,19},{18,... | collective-permute-start | bytes 786440 | tf_op jit(solution)/shard_map/ppermute | solution.py:392
  143.3 10.2 %collective-permute-start.37 = (bf16[512,256]{1,0:T(8,128)(2,1)S(1)}, bf16[512,256]{1,0:T(8,128)(2,1)S(1)}, u32[]{:S(2)}, u32[]{:S(2)}) collective-permute-start(bf16[512,256]{1,0:T(8,128)(2,1)S(1)} %update.4.refs_0_), channel_id=1, source_target_pairs={{0,24},{4,28},{8,16},{12,20},{16,8},{20,12},{24,0},{28,4},{1,25},{... | collective-permute-start | bytes 786440 | tf_op jit(solution)/shard_map/ppermute | solution.py:378
  144.5 12.1 %collective-permute-start.36 = (bf16[512,256]{1,0:T(8,128)(2,1)S(1)}, bf16[512,256]{1,0:T(8,128)(2,1)S(1)}, u32[]{:S(2)}, u32[]{:S(2)}) collective-permute-start(bf16[512,256]{1,0:T(8,128)(2,1)S(1)} %update.4.refs_0_), channel_id=1, source_target_pairs={{0,16},{4,20},{8,24},{12,28},{16,0},{20,4},{24,8},{28,12},{1,17},{... | collective-permute-start | bytes 786440 | tf_op jit(solution)/shard_map/ppermute | solution.py:378
  145.5 11.1 %collective-permute-start.35 = (bf16[512,256]{1,0:T(8,128)(2,1)S(1)}, bf16[512,256]{1,0:T(8,128)(2,1)S(1)}, u32[]{:S(2)}, u32[]{:S(2)}) collective-permute-start(bf16[512,256]{1,0:T(8,128)(2,1)S(1)} %update.4.refs_0_), channel_id=1, source_target_pairs={{0,8},{4,12},{8,0},{12,4},{16,24},{20,28},{24,16},{28,20},{1,9},{5... | collective-permute-start | bytes 786440 | tf_op jit(solution)/shard_map/ppermute | solution.py:378
  146.8 10.3 %collective-permute-start.34 = (bf16[512,256]{1,0:T(8,128)(2,1)S(1)}, bf16[512,256]{1,0:T(8,128)(2,1)S(1)}, u32[]{:S(2)}, u32[]{:S(2)}) collective-permute-start(bf16[512,256]{1,0:T(8,128)(2,1)S(1)} %update.4.refs_0_), channel_id=1, source_target_pairs={{0,4},{4,0},{8,12},{12,8},{16,20},{20,16},{24,28},{28,24},{1,5},{5... | collective-permute-start | bytes 786440 | tf_op jit(solution)/shard_map/ppermute | solution.py:378
  153.5 5.7 %collective-permute-start.38 = (bf16[512,256]{1,0:T(8,128)(2,1)S(1)}, bf16[512,256]{1,0:T(8,128)(2,1)S(1)}, u32[]{:S(2)}, u32[]{:S(2)}) collective-permute-start(bf16[512,256]{1,0:T(8,128)(2,1)S(1)} %collective-permute-done.37.refs_4_), channel_id=1, source_target_pairs={{0,4},{4,0},{8,12},{12,8},{16,20},{20,16},{24,28},{28,24},{1,5},{5... | collective-permute-start | bytes 786440 | tf_op jit(solution)/shard_map/ppermute | solution.py:378
  156.6 2.6 %collective-permute-start.39 = (bf16[512,256]{1,0:T(8,128)(2,1)S(1)}, bf16[512,256]{1,0:T(8,128)(2,1)S(1)}, u32[]{:S(2)}, u32[]{:S(2)}) collective-permute-start(bf16[512,256]{1,0:T(8,128)(2,1)S(1)} %collective-permute-done.36.refs_3_), channel_id=1, source_target_pairs={{0,4},{4,0},{8,12},{12,8},{16,20},{20,16},{24,28},{28,24},{1,5},{5... | collective-permute-start | bytes 786440 | tf_op jit(solution)/shard_map/ppermute | solution.py:378
  156.6 2.6 %collective-permute-start.40 = (bf16[512,256]{1,0:T(8,128)(2,1)S(1)}, bf16[512,256]{1,0:T(8,128)(2,1)S(1)}, u32[]{:S(2)}, u32[]{:S(2)}) collective-permute-start(bf16[512,256]{1,0:T(8,128)(2,1)S(1)} %collective-permute-done.35.refs_2_), channel_id=1, source_target_pairs={{0,4},{4,0},{8,12},{12,8},{16,20},{20,16},{24,28},{28,24},{1,5},{5... | collective-permute-start | bytes 786440 | tf_op jit(solution)/shard_map/ppermute | solution.py:378
  160.8 11.6 %collective-permute-start.44 = (bf16[512,256]{1,0:T(8,128)(2,1)S(1)}, bf16[512,256]{1,0:T(8,128)(2,1)S(1)}, u32[]{:S(2)}, u32[]{:S(2)}) collective-permute-start(bf16[512,256]{1,0:T(8,128)(2,1)S(1)} %terms.27), channel_id=1, source_target_pairs={{0,1},{3,2},{4,5},{7,6},{8,9},{11,10},{12,13},{15,14},{16,17},{19,... | collective-permute-start | bytes 786440 | tf_op jit(solution)/shard_map/ppermute | solution.py:387
  162.1 23.9 %collective-permute-start.41 = (bf16[512,256]{1,0:T(8,128)(2,1)S(1)}, bf16[512,256]{1,0:T(8,128)(2,1)S(1)}, u32[]{:S(2)}, u32[]{:S(2)}) collective-permute-start(bf16[512,256]{1,0:T(8,128)(2,1)S(1)} %terms.27), channel_id=1, source_target_pairs={{1,2},{2,1},{5,6},{6,5},{9,10},{10,9},{13,14},{14,13},{17,18},{18,... | collective-permute-start | bytes 786440 | tf_op jit(solution)/shard_map/ppermute | solution.py:388
  165.9 10.8 %collective-permute-start.43 = (bf16[512,256]{1,0:T(8,128)(2,1)S(1)}, bf16[512,256]{1,0:T(8,128)(2,1)S(1)}, u32[]{:S(2)}, u32[]{:S(2)}) collective-permute-start(bf16[512,256]{1,0:T(8,128)(2,1)S(1)} %get-tuple-element.50), channel_id=1, source_target_pairs={{0,2},{3,1},{4,6},{7,5},{8,10},{11,9},{12,14},{15,13},{16,18},{19,... | collective-permute-start | bytes 786440 | tf_op jit(solution)/shard_map/ppermute | solution.py:391
  172.3 13.6 %collective-permute-start.42 = (bf16[512,256]{1,0:T(8,128)(2,1)S(1)}, bf16[512,256]{1,0:T(8,128)(2,1)S(1)}, u32[]{:S(2)}, u32[]{:S(2)}) collective-permute-start(bf16[512,256]{1,0:T(8,128)(2,1)S(1)} %terms.28), channel_id=1, source_target_pairs={{0,1},{1,0},{2,3},{3,2},{4,5},{5,4},{6,7},{7,6},{8,9},{9,8},{10,11... | collective-permute-start | bytes 786440 | tf_op jit(solution)/shard_map/ppermute | solution.py:378
  172.5 13.5 %collective-permute-start.45 = (bf16[512,256]{1,0:T(8,128)(2,1)S(1)}, bf16[512,256]{1,0:T(8,128)(2,1)S(1)}, u32[]{:S(2)}, u32[]{:S(2)}) collective-permute-start(bf16[512,256]{1,0:T(8,128)(2,1)S(1)} %sum.5), channel_id=1, source_target_pairs={{1,3},{2,0},{5,7},{6,4},{9,11},{10,8},{13,15},{14,12},{17,19},{18,... | collective-permute-start | bytes 786440 | tf_op jit(solution)/shard_map/ppermute | solution.py:392
  (1 other events, 1.0 us)

commit v7 on v5

--- a/solution.py
+++ b/solution.py
@@ -175,10 +175,10 @@
     for turn, out_ref in enumerate(out_refs):
         first = pl.multiple_of((place_ref[1] ^ turn) * slice_rows, slice_rows)
         packed = None
+        found = jnp.dot(hits_ref[pl.ds(first, slice_rows), :], table, preferred_element_type=jnp.float32)
         for part in range(packs):
-            chosen = pl.ds(pl.multiple_of(first + part * short, short), short)
-            side = code_ref[chosen, :] % packs
-            rows = jnp.dot(hits_ref[chosen, :], table, preferred_element_type=jnp.float32)
+            side = code_ref[pl.ds(pl.multiple_of(first + part * short, short), short), :] % packs
+            rows = found[part * short : (part + 1) * short]
             moved = rows[:, :LANES]
             for turned in range(1, packs):
                 moved = jnp.where(
@@ -388,15 +388,15 @@
         return make(0, [f32])[0], arriving, False
     first = lax.ppermute(make(2, [bf16])[0], "src", [(0, 1), (1, 3), (3, 2), (2, 0)])
     sent, kept = make(3, [bf16, f32])
-    beside = swap(make(1, [bf16])[0], "src", 1)
     outer = lax.ppermute(sent, "src", [(0, 3), (3, 0)])
     inner = lax.ppermute(make_sum(kept, first), "src", [(1, 2), (2, 1)])
-    return make(0, [f32])[0], [first, beside, outer, inner], True
+    beside = swap(make(1, [bf16])[0], "src", 1)
+    return make(0, [f32])[0], [first, outer, inner, beside], True
 
 
 def iterate(estimate, data, place, n_row, n_src, slice_rows, fresh):
     turns = range(2, n_row, 2)
-    direct = {turn: swap(estimate, "row", turn) for turn in (reversed(turns) if fresh else turns)}
+    direct = {turn: swap(estimate, "row", turn) for turn in turns}
     if fresh:
         real_data, *held = lax.optimization_barrier((data[0], *direct.values()))
         data, direct = (real_data, data[1]), dict(zip(direct, held))

time: 176 us -> 183 us (1.040); the launches traced: 176 us -> 180 us
  starting transfers between devices: 41.9 us -> 49.5 us
  waiting for transfers between devices: 46.5 us -> 43.4 us
    ppermute x34, waiting for transfers between devices: 41.2 us -> 25.2 us  [swap(): lax.ppermute(array, axis, [(index, index ^ bits) for index in range(size)])]
    ppermute x3, waiting for transfers between devices: 5.22 us -> 18.2 us  [exchange(): outer = lax.ppermute(sent, 'src', [(0, 3), (3, 0)])]
    ppermute x3, starting transfers between devices: 1.65 us -> 10.4 us  [exchange(): lax.ppermute(make(2, [bf16])[0], 'src', [(0, 1), (1, 3), (3, 2), (2, 0)])]
    ppermute x3, starting transfers between devices: 13.5 us -> 8.92 us  [exchange(): outer = lax.ppermute(sent, 'src', [(0, 3), (3, 0)])]
    ppermute x34, starting transfers between devices: 24.5 us -> 28 us  [swap(): lax.ppermute(array, axis, [(index, index ^ bits) for index in range(size)])]
  transfers between devices with their start and end apart: 43 -> 43, of which waited for: 12 -> 9; matrix products, arithmetic and copies ran while one was open for 0% -> 0% of each run, Pallas kernels for 28% -> 27%
where the time goes in v7:
time: 183 us; the launch traced here: 180 us
  Pallas kernels  85 us (46%)
  starting transfers between devices  49.5 us (27%)
  waiting for transfers between devices  43.4 us (24%)
    pallas_call x15, Pallas kernels, make_terms(): pl.pallas_call(functools.partial(terms_kernel, turns, numbers, len(partia...  36.6 us
    ppermute x34, starting transfers between devices, swap(): lax.ppermute(array, axis, [(index, index ^ bits) for index in range(size)])  28 us
    ppermute x34, waiting for transfers between devices, swap(): lax.ppermute(array, axis, [(index, index ^ bits) for index in range(size)])  25.2 us
    pallas_call x1, Pallas kernels, make_spectra(): pl.pallas_call(functools.partial(spectra_kernel, packs, n_row), in_specs=...  23.8 us
    ppermute x3, waiting for transfers between devices, exchange(): outer = lax.ppermute(sent, 'src', [(0, 3), (3, 0)])  18.2 us
    pallas_call x2, Pallas kernels, relay(): pl.pallas_call(functools.partial(relay_kernel, part), in_specs=[ANY, ANY]...  15.7 us
    ppermute x3, starting transfers between devices, exchange(): lax.ppermute(make(2, [bf16])[0], 'src', [(0, 1), (1, 3), (3, 2), (2, 0)])  10.4 us
    ppermute x3, starting transfers between devices, exchange(): outer = lax.ppermute(sent, 'src', [(0, 3), (3, 0)])  8.92 us
  transfers between devices with their start and end apart: 43, of which 9 were waited for; matrix products, arithmetic and copies ran while one was open for 0% of the time, Pallas kernels for 27%

profile of v7, /device:TPU:0, one launch (start us, length us, event | category | flops | bytes accessed | tf_op | source)
XLA Modules:
  0.0 180.5 jit_solution(9512859036274610194)
XLA Ops:
  1.7 23.8 %spectra.1 = (bf16[2,64,128]{2,1,0:T(8,128)(2,1)S(1)}, bf16[2,64,128]{2,1,0:T(8,128)(2,1)S(1)}, bf16[2,64,128]{2,1,0:T(8,128)(2,1)S(1)}, bf16[2,64,128]{2,1,0:T(...) custom-call(s32[2]{0:T(128)S(1)} %pad_add_fusion.place_ref, ...), custom_call_target="tpu_custom_call" | custom-call | flops 8589934592 | bytes 67108864 | tf_op jit(solution)/shard_map/spectra/pallas_call | solution.py:120
  26.0 2.6 %collective-permute-start.1 = (bf16[128,128]{1,0:T(8,128)(2,1)S(1)}, bf16[128,128]{1,0:T(8,128)(2,1)S(1)}, u32[]{:S(2)}, u32[]{:S(2)}) collective-permute-start(bf16[128,128]{1,0:T(8,128)(2,1)S(1)} %bitcast.18), channel_id=1, source_target_pairs={{0,8},{4,12},{8,0},{12,4},{16,24},{20,28},{24,16},{28,20},{1,9},{5... | collective-permute-start | bytes 98312 | tf_op jit(solution)/shard_map/ppermute | solution.py:381
  28.6 1.8 collective-permute-start.3
  30.4 2.6 %collective-permute-start.5 = (bf16[128,128]{1,0:T(8,128)(2,1)S(1)}, bf16[128,128]{1,0:T(8,128)(2,1)S(1)}, u32[]{:S(2)}, u32[]{:S(2)}) collective-permute-start(bf16[128,128]{1,0:T(8,128)(2,1)S(1)} %bitcast.14), channel_id=1, source_target_pairs={{0,24},{4,28},{8,16},{12,20},{16,8},{20,12},{24,0},{28,4},{1,25},{... | collective-permute-start | bytes 98312 | tf_op jit(solution)/shard_map/ppermute | solution.py:381
  33.5 1.7 hits.1.hits_ref
  35.2 2.0 %collective-permute-done.6.refs_7_ = bf16[128,128]{1,0:T(8,128)(2,1)S(1)} collective-permute-done((bf16[128,128]{1,0:T(8,128)(2,1)S(1)}, bf16[128,128]{1,0:T(8,128)(2,1)S(1)}, u32[]{:S(2)}, u32[]{:S(2)}) %collective-permute-start.6) | collective-permute-done | bytes 32800 | tf_op jit(solution)/shard_map/ppermute | solution.py:381
  37.2 2.4 %order.1 = (bf16[256,128]{1,0:T(8,128)(2,1)S(1)}, bf16[256,128]{1,0:T(8,128)(2,1)S(1)}, bf16[256,128]{1,0:T(8,128)(2,1)S(1)}, bf16[256,128]{1,0:T(8,128)(2,1)S(1)}) custom-call(s32[2]{0:T(128)S(1)} %pad_add_fusion.place_ref, s32[2048,128]{1,0:T(8,128)S(1)} %broadcast_in_dim.2.code_ref, bf16[2048,1024]{1,0:T(8,128)(2,1)S(1)} %hits.1.hits_ref, ...), custom_call_target="tpu_custom_call" | custom-call | flops 1073741824 | bytes 1048576 | tf_op jit(solution)/shard_map/order/pallas_call | solution.py:193
  39.6 1.6 collective-permute-start.7
  41.3 2.6 %collective-permute-start.8 = (bf16[256,128]{1,0:T(8,128)(2,1)S(1)}, bf16[256,128]{1,0:T(8,128)(2,1)S(1)}, u32[]{:S(2)}, u32[]{:S(2)}) collective-permute-start(bf16[256,128]{1,0:T(8,128)(2,1)S(1)} %get-tuple-element.38), channel_id=1, source_target_pairs={{0,2},{1,3},{2,0},{3,1},{4,6},{5,7},{6,4},{7,5},{8,10},{9,11},{10,... | collective-permute-start | bytes 196616 | tf_op jit(solution)/shard_map/ppermute | solution.py:381
  44.1 7.7 %relay.3 = (bf16[8,2048,512]{2,1,0:T(8,128)(2,1)S(1)}, f32[8,128]{1,0:T(8,128)S(1)}) custom-call(bf16[2,2048,8,512]{3,2,1,0:T(8,128)(2,1)} %data_ref.3, bf16[256,128]{1,0:T(8,128)(2,1)S(1)} %get-tuple-element.36.after_ref.refs_0_), custom_call_target="tpu_custom_call" | custom-call | bytes 33554432 | tf_op jit(solution)/shard_map/relay/pallas_call | solution.py:256
  51.8 1.0 panel.1.refs_0_.refs_4_
  52.8 1.1 collective-permute-start.12
  54.9 1.5 collective-permute-start.10
  56.3 8.0 %relay.2 = (bf16[8,2048,512]{2,1,0:T(8,128)(2,1)S(1)}, f32[8,128]{1,0:T(8,128)}) custom-call(bf16[2,2048,8,512]{3,2,1,0:T(8,128)(2,1)} %data_ref.3, bf16[128,128]{1,0:T(8,128)(2,1)S(1)} %bitcast.12), custom_call_target="tpu_custom_call" | custom-call | bytes 33554432 | tf_op jit(solution)/shard_map/relay/pallas_call | solution.py:256
  64.3 2.5 %collective-permute-done.11.refs_3_ = bf16[512,256]{1,0:T(8,128)(2,1)S(1)} collective-permute-done((bf16[512,256]{1,0:T(8,128)(2,1)S(1)}, bf16[512,256]{1,0:T(8,128)(2,1)S(1)}, u32[]{:S(2)}, u32[]{:S(2)}) %collective-permute-start.11) | collective-permute-done | bytes 262176 | tf_op jit(solution)/shard_map/ppermute | solution.py:381
  67.3 2.1 %terms.16.refs_3_ = f32[512,256]{1,0:T(8,128)S(1)} custom-call(s32[2]{0:T(128)S(1)} %pad_add_fusion.place_ref, bf16[8,2048,512]{2,1,0:T(8,128)(2,1)S(1)} %get-tuple-element.41.real_ref, bf16[8,2048,512]{2,1,0:T(8,128)(2,1)S(1)} %get-tuple-element.42.imag_ref, bf16[512,256]{1,0:T(8,128)(2,1)S(1)} %panel.1.refs_0_.refs_4_, ...), custom_call_target="tpu_custom_call" | custom-call | flops 1342177280 | bytes 5242880 | tf_op jit(solution)/shard_map/terms/pallas_call | solution.py:305
  69.4 1.5 terms.17
  71.7 2.9 %terms.19 = bf16[512,256]{1,0:T(8,128)(2,1)S(1)} custom-call(s32[2]{0:T(128)S(1)} %pad_add_fusion.place_ref, bf16[8,2048,512]{2,1,0:T(8,128)(2,1)S(1)} %get-tuple-element.41.real_ref, bf16[8,2048,512]{2,1,0:T(8,128)(2,1)S(1)} %get-tuple-element.42.imag_ref, bf16[512,256]{1,0:T(8,128)(2,1)S(1)} %panel.1.refs_0_.refs_4_, ...), custom_call_target="tpu_custom_call" | custom-call | flops 2147483648 | bytes 8388608 | tf_op jit(solution)/shard_map/terms/pallas_call | solution.py:305
  74.5 3.6 %collective-permute-start.20 = (bf16[512,256]{1,0:T(8,128)(2,1)S(1)}, bf16[512,256]{1,0:T(8,128)(2,1)S(1)}, u32[]{:S(2)}, u32[]{:S(2)}) collective-permute-start(bf16[512,256]{1,0:T(8,128)(2,1)S(1)} %terms.19), channel_id=1, source_target_pairs={{0,1},{1,0},{2,3},{3,2},{4,5},{5,4},{6,7},{7,6},{8,9},{9,8},{10,11... | collective-permute-start | bytes 786440 | tf_op jit(solution)/shard_map/ppermute | solution.py:381
  78.1 2.9 %terms.18 = (bf16[512,256]{1,0:T(8,128)(2,1)S(1)}, f32[512,256]{1,0:T(8,128)S(1)}) custom-call(s32[2]{0:T(128)S(1)} %pad_add_fusion.place_ref, bf16[8,2048,512]{2,1,0:T(8,128)(2,1)S(1)} %get-tuple-element.41.real_ref, bf16[8,2048,512]{2,1,0:T(8,128)(2,1)S(1)} %get-tuple-element.42.imag_ref, bf16[512,256]{1,0:T(8,128)(2,1)S(1)} %panel.1.refs_0_.refs_4_, ...), custom_call_target="tpu_custom_call" | custom-call | flops 2147483648 | bytes 8388608 | tf_op jit(solution)/shard_map/terms/pallas_call | solution.py:305
  81.0 2.2 %collective-permute-start.18 = (bf16[512,256]{1,0:T(8,128)(2,1)S(1)}, bf16[512,256]{1,0:T(8,128)(2,1)S(1)}, u32[]{:S(2)}, u32[]{:S(2)}) collective-permute-start(bf16[512,256]{1,0:T(8,128)(2,1)S(1)} %get-tuple-element.46), channel_id=1, source_target_pairs={{0,3},{3,0},{4,7},{7,4},{8,11},{11,8},{12,15},{15,12},{16,19},{19,... | collective-permute-start | bytes 786440 | tf_op jit(solution)/shard_map/ppermute | solution.py:391
  84.1 2.9 %terms.15.own_ref = f32[512,256]{1,0:T(8,128)S(1)} custom-call(s32[2]{0:T(128)S(1)} %pad_add_fusion.place_ref, bf16[8,2048,512]{2,1,0:T(8,128)(2,1)S(1)} %get-tuple-element.41.real_ref, bf16[8,2048,512]{2,1,0:T(8,128)(2,1)S(1)} %get-tuple-element.42.imag_ref, bf16[512,256]{1,0:T(8,128)(2,1)S(1)} %panel.1.refs_0_.refs_4_, ...), custom_call_target="tpu_custom_call" | custom-call | flops 2147483648 | bytes 8388608 | tf_op jit(solution)/shard_map/terms/pallas_call | solution.py:305
  87.0 5.9 %collective-permute-done.18.refs_1_ = bf16[512,256]{1,0:T(8,128)(2,1)S(1)} collective-permute-done((bf16[512,256]{1,0:T(8,128)(2,1)S(1)}, bf16[512,256]{1,0:T(8,128)(2,1)S(1)}, u32[]{:S(2)}, u32[]{:S(2)}) %collective-permute-start.18) | collective-permute-done | bytes 262176 | tf_op jit(solution)/shard_map/ppermute | solution.py:391
  93.7 1.2 collective-permute-start.24
  96.0 1.3 collective-permute-start.22
  97.3 6.7 %collective-permute-done.24.refs_4_ = bf16[512,256]{1,0:T(8,128)(2,1)S(1)} collective-permute-done((bf16[512,256]{1,0:T(8,128)(2,1)S(1)}, bf16[512,256]{1,0:T(8,128)(2,1)S(1)}, u32[]{:S(2)}, u32[]{:S(2)}) %collective-permute-start.24) | collective-permute-done | bytes 262176 | tf_op jit(solution)/shard_map/ppermute | solution.py:381
  103.9 3.6 %collective-permute-done.23.refs_3_ = bf16[512,256]{1,0:T(8,128)(2,1)S(1)} collective-permute-done((bf16[512,256]{1,0:T(8,128)(2,1)S(1)}, bf16[512,256]{1,0:T(8,128)(2,1)S(1)}, u32[]{:S(2)}, u32[]{:S(2)}) %collective-permute-start.23) | collective-permute-done | bytes 262176 | tf_op jit(solution)/shard_map/ppermute | solution.py:381
  108.1 2.1 %terms.21.refs_3_ = f32[512,256]{1,0:T(8,128)S(1)} custom-call(s32[2]{0:T(128)S(1)} %pad_add_fusion.place_ref, bf16[8,2048,512]{2,1,0:T(8,128)(2,1)S(1)} %get-tuple-element.41.real_ref, bf16[8,2048,512]{2,1,0:T(8,128)(2,1)S(1)} %get-tuple-element.42.imag_ref, bf16[512,256]{1,0:T(8,128)(2,1)S(1)} %update.3.refs_0_, ...), custom_call_target="tpu_custom_call" | custom-call | flops 1342177280 | bytes 5242880 | tf_op jit(solution)/shard_map/terms/pallas_call | solution.py:305
  110.2 1.5 terms.22
  111.8 5.2 %collective-permute-start.28 = (bf16[512,256]{1,0:T(8,128)(2,1)S(1)}, bf16[512,256]{1,0:T(8,128)(2,1)S(1)}, u32[]{:S(2)}, u32[]{:S(2)}) collective-permute-start(bf16[512,256]{1,0:T(8,128)(2,1)S(1)} %terms.22), channel_id=1, source_target_pairs={{0,1},{1,3},{3,2},{2,0},{4,5},{5,7},{7,6},{6,4},{8,9},{9,11},{11,1... | collective-permute-start | bytes 786440 | tf_op jit(solution)/shard_map/ppermute | solution.py:389
  116.9 2.9 %terms.24 = bf16[512,256]{1,0:T(8,128)(2,1)S(1)} custom-call(s32[2]{0:T(128)S(1)} %pad_add_fusion.place_ref, bf16[8,2048,512]{2,1,0:T(8,128)(2,1)S(1)} %get-tuple-element.41.real_ref, bf16[8,2048,512]{2,1,0:T(8,128)(2,1)S(1)} %get-tuple-element.42.imag_ref, bf16[512,256]{1,0:T(8,128)(2,1)S(1)} %update.3.refs_0_, ...), custom_call_target="tpu_custom_call" | custom-call | flops 2147483648 | bytes 8388608 | tf_op jit(solution)/shard_map/terms/pallas_call | solution.py:305
  119.9 2.9 %terms.23 = (bf16[512,256]{1,0:T(8,128)(2,1)S(1)}, f32[512,256]{1,0:T(8,128)S(1)}) custom-call(s32[2]{0:T(128)S(1)} %pad_add_fusion.place_ref, bf16[8,2048,512]{2,1,0:T(8,128)(2,1)S(1)} %get-tuple-element.41.real_ref, bf16[8,2048,512]{2,1,0:T(8,128)(2,1)S(1)} %get-tuple-element.42.imag_ref, bf16[512,256]{1,0:T(8,128)(2,1)S(1)} %update.3.refs_0_, ...), custom_call_target="tpu_custom_call" | custom-call | flops 2147483648 | bytes 8388608 | tf_op jit(solution)/shard_map/terms/pallas_call | solution.py:305
  122.7 3.5 %collective-permute-start.29 = (bf16[512,256]{1,0:T(8,128)(2,1)S(1)}, bf16[512,256]{1,0:T(8,128)(2,1)S(1)}, u32[]{:S(2)}, u32[]{:S(2)}) collective-permute-start(bf16[512,256]{1,0:T(8,128)(2,1)S(1)} %get-tuple-element.48), channel_id=1, source_target_pairs={{0,3},{3,0},{4,7},{7,4},{8,11},{11,8},{12,15},{15,12},{16,19},{19,... | collective-permute-start | bytes 786440 | tf_op jit(solution)/shard_map/ppermute | solution.py:391
  127.0 2.9 %terms.20.own_ref = f32[512,256]{1,0:T(8,128)S(1)} custom-call(s32[2]{0:T(128)S(1)} %pad_add_fusion.place_ref, bf16[8,2048,512]{2,1,0:T(8,128)(2,1)S(1)} %get-tuple-element.41.real_ref, bf16[8,2048,512]{2,1,0:T(8,128)(2,1)S(1)} %get-tuple-element.42.imag_ref, bf16[512,256]{1,0:T(8,128)(2,1)S(1)} %update.3.refs_0_, ...), custom_call_target="tpu_custom_call" | custom-call | flops 2147483648 | bytes 8388608 | tf_op jit(solution)/shard_map/terms/pallas_call | solution.py:305
  129.9 6.1 %collective-permute-done.29.refs_1_ = bf16[512,256]{1,0:T(8,128)(2,1)S(1)} collective-permute-done((bf16[512,256]{1,0:T(8,128)(2,1)S(1)}, bf16[512,256]{1,0:T(8,128)(2,1)S(1)}, u32[]{:S(2)}, u32[]{:S(2)}) %collective-permute-start.29) | collective-permute-done | bytes 262176 | tf_op jit(solution)/shard_map/ppermute | solution.py:391
  136.9 1.3 collective-permute-start.35
  139.1 1.3 collective-permute-start.33
  140.4 6.7 %collective-permute-done.35.refs_4_ = bf16[512,256]{1,0:T(8,128)(2,1)S(1)} collective-permute-done((bf16[512,256]{1,0:T(8,128)(2,1)S(1)}, bf16[512,256]{1,0:T(8,128)(2,1)S(1)}, u32[]{:S(2)}, u32[]{:S(2)}) %collective-permute-start.35) | collective-permute-done | bytes 262176 | tf_op jit(solution)/shard_map/ppermute | solution.py:381
  147.1 3.7 %collective-permute-done.34.refs_3_ = bf16[512,256]{1,0:T(8,128)(2,1)S(1)} collective-permute-done((bf16[512,256]{1,0:T(8,128)(2,1)S(1)}, bf16[512,256]{1,0:T(8,128)(2,1)S(1)}, u32[]{:S(2)}, u32[]{:S(2)}) %collective-permute-start.34) | collective-permute-done | bytes 262176 | tf_op jit(solution)/shard_map/ppermute | solution.py:381
  151.3 2.1 %terms.26.refs_3_ = f32[512,256]{1,0:T(8,128)S(1)} custom-call(s32[2]{0:T(128)S(1)} %pad_add_fusion.place_ref, bf16[8,2048,512]{2,1,0:T(8,128)(2,1)S(1)} %get-tuple-element.41.real_ref, bf16[8,2048,512]{2,1,0:T(8,128)(2,1)S(1)} %get-tuple-element.42.imag_ref, bf16[512,256]{1,0:T(8,128)(2,1)S(1)} %update.4.refs_0_, ...), custom_call_target="tpu_custom_call" | custom-call | flops 1342177280 | bytes 5242880 | tf_op jit(solution)/shard_map/terms/pallas_call | solution.py:305
  153.4 1.5 terms.27
  154.9 4.5 %collective-permute-start.39 = (bf16[512,256]{1,0:T(8,128)(2,1)S(1)}, bf16[512,256]{1,0:T(8,128)(2,1)S(1)}, u32[]{:S(2)}, u32[]{:S(2)}) collective-permute-start(bf16[512,256]{1,0:T(8,128)(2,1)S(1)} %terms.27), channel_id=1, source_target_pairs={{0,1},{1,3},{3,2},{2,0},{4,5},{5,7},{7,6},{6,4},{8,9},{9,11},{11,1... | collective-permute-start | bytes 786440 | tf_op jit(solution)/shard_map/ppermute | solution.py:389
  159.5 2.9 %terms.29 = bf16[512,256]{1,0:T(8,128)(2,1)S(1)} custom-call(s32[2]{0:T(128)S(1)} %pad_add_fusion.place_ref, bf16[8,2048,512]{2,1,0:T(8,128)(2,1)S(1)} %get-tuple-element.41.real_ref, bf16[8,2048,512]{2,1,0:T(8,128)(2,1)S(1)} %get-tuple-element.42.imag_ref, bf16[512,256]{1,0:T(8,128)(2,1)S(1)} %update.4.refs_0_, ...), custom_call_target="tpu_custom_call" | custom-call | flops 2147483648 | bytes 8388608 | tf_op jit(solution)/shard_map/terms/pallas_call | solution.py:305
  162.4 2.9 %terms.28 = (bf16[512,256]{1,0:T(8,128)(2,1)S(1)}, f32[512,256]{1,0:T(8,128)S(1)}) custom-call(s32[2]{0:T(128)S(1)} %pad_add_fusion.place_ref, bf16[8,2048,512]{2,1,0:T(8,128)(2,1)S(1)} %get-tuple-element.41.real_ref, bf16[8,2048,512]{2,1,0:T(8,128)(2,1)S(1)} %get-tuple-element.42.imag_ref, bf16[512,256]{1,0:T(8,128)(2,1)S(1)} %update.4.refs_0_, ...), custom_call_target="tpu_custom_call" | custom-call | flops 2147483648 | bytes 8388608 | tf_op jit(solution)/shard_map/terms/pallas_call | solution.py:305
  165.3 3.2 %collective-permute-start.40 = (bf16[512,256]{1,0:T(8,128)(2,1)S(1)}, bf16[512,256]{1,0:T(8,128)(2,1)S(1)}, u32[]{:S(2)}, u32[]{:S(2)}) collective-permute-start(bf16[512,256]{1,0:T(8,128)(2,1)S(1)} %get-tuple-element.50), channel_id=1, source_target_pairs={{0,3},{3,0},{4,7},{7,4},{8,11},{11,8},{12,15},{15,12},{16,19},{19,... | collective-permute-start | bytes 786440 | tf_op jit(solution)/shard_map/ppermute | solution.py:391
  169.3 2.9 %terms.25.own_ref = f32[512,256]{1,0:T(8,128)S(1)} custom-call(s32[2]{0:T(128)S(1)} %pad_add_fusion.place_ref, bf16[8,2048,512]{2,1,0:T(8,128)(2,1)S(1)} %get-tuple-element.41.real_ref, bf16[8,2048,512]{2,1,0:T(8,128)(2,1)S(1)} %get-tuple-element.42.imag_ref, bf16[512,256]{1,0:T(8,128)(2,1)S(1)} %update.4.refs_0_, ...), custom_call_target="tpu_custom_call" | custom-call | flops 2147483648 | bytes 8388608 | tf_op jit(solution)/shard_map/terms/pallas_call | solution.py:305
  172.2 6.1 %collective-permute-done.40.refs_1_ = bf16[512,256]{1,0:T(8,128)(2,1)S(1)} collective-permute-done((bf16[512,256]{1,0:T(8,128)(2,1)S(1)}, bf16[512,256]{1,0:T(8,128)(2,1)S(1)}, u32[]{:S(2)}, u32[]{:S(2)}) %collective-permute-start.40) | collective-permute-done | bytes 262176 | tf_op jit(solution)/shard_map/ppermute | solution.py:391
  178.3 2.1 %update.5 = (f32[512,2,128]{2,1,0:T(2,128)}, f32[512,2,128]{2,1,0:T(2,128)}) custom-call(s32[2]{0:T(128)S(1)} %pad_add_fusion.place_ref, f32[2]{0:T(128)S(1)} %copy-done.1, f32[512,256]{1,0:T(8,128)S(1)} %terms.25.own_ref, bf16[512,256]{1,0:T(8,128)(2,1)S(1)} %collective-permute-done.39.other_ref.refs_0_, ...), custom_call_target="tpu_custom_call" | custom-call | flops 2097152 | bytes 2097152 | tf_op jit(solution)/shard_map/update/pallas_call | solution.py:368
  (74 shorter events, 11.7 us)
Async XLA Ops:
  0.7 1.0 copy-start
  1.7 31.4 %copy-start.2 = (s32[2048]{0:T(1024)S(1)}, s32[2048]{0:T(1024)}, u32[]{:S(2)}) copy-start(s32[2048]{0:T(1024)} %param.6) | copy-start | bytes 24580
  25.5 4.9 %collective-permute-start = (bf16[128,128]{1,0:T(8,128)(2,1)S(1)}, bf16[128,128]{1,0:T(8,128)(2,1)S(1)}, u32[]{:S(2)}, u32[]{:S(2)}) collective-permute-start(bf16[128,128]{1,0:T(8,128)(2,1)S(1)} %bitcast.19), channel_id=1, source_target_pairs={{0,4},{4,0},{8,12},{12,8},{16,20},{20,16},{24,28},{28,24},{1,5},{5... | collective-permute-start | bytes 98312 | tf_op jit(solution)/shard_map/ppermute | solution.py:381
  26.0 7.0 %collective-permute-start.1 = (bf16[128,128]{1,0:T(8,128)(2,1)S(1)}, bf16[128,128]{1,0:T(8,128)(2,1)S(1)}, u32[]{:S(2)}, u32[]{:S(2)}) collective-permute-start(bf16[128,128]{1,0:T(8,128)(2,1)S(1)} %bitcast.18), channel_id=1, source_target_pairs={{0,8},{4,12},{8,0},{12,4},{16,24},{20,28},{24,16},{28,20},{1,9},{5... | collective-permute-start | bytes 98312 | tf_op jit(solution)/shard_map/ppermute | solution.py:381
  28.5 6.6 %collective-permute-start.2 = (bf16[128,128]{1,0:T(8,128)(2,1)S(1)}, bf16[128,128]{1,0:T(8,128)(2,1)S(1)}, u32[]{:S(2)}, u32[]{:S(2)}) collective-permute-start(bf16[128,128]{1,0:T(8,128)(2,1)S(1)} %bitcast.17), channel_id=1, source_target_pairs={{0,12},{4,8},{8,4},{12,0},{16,28},{20,24},{24,20},{28,16},{1,13},{... | collective-permute-start | bytes 98312 | tf_op jit(solution)/shard_map/ppermute | solution.py:381
  28.6 6.6 %collective-permute-start.3 = (bf16[128,128]{1,0:T(8,128)(2,1)S(1)}, bf16[128,128]{1,0:T(8,128)(2,1)S(1)}, u32[]{:S(2)}, u32[]{:S(2)}) collective-permute-start(bf16[128,128]{1,0:T(8,128)(2,1)S(1)} %bitcast.16), channel_id=1, source_target_pairs={{0,16},{4,20},{8,24},{12,28},{16,0},{20,4},{24,8},{28,12},{1,17},{... | collective-permute-start | bytes 98312 | tf_op jit(solution)/shard_map/ppermute | solution.py:381
  30.4 4.8 %collective-permute-start.4 = (bf16[128,128]{1,0:T(8,128)(2,1)S(1)}, bf16[128,128]{1,0:T(8,128)(2,1)S(1)}, u32[]{:S(2)}, u32[]{:S(2)}) collective-permute-start(bf16[128,128]{1,0:T(8,128)(2,1)S(1)} %bitcast.15), channel_id=1, source_target_pairs={{0,20},{4,16},{8,28},{12,24},{16,4},{20,0},{24,12},{28,8},{1,21},{... | collective-permute-start | bytes 98312 | tf_op jit(solution)/shard_map/ppermute | solution.py:381
  30.4 4.8 %collective-permute-start.5 = (bf16[128,128]{1,0:T(8,128)(2,1)S(1)}, bf16[128,128]{1,0:T(8,128)(2,1)S(1)}, u32[]{:S(2)}, u32[]{:S(2)}) collective-permute-start(bf16[128,128]{1,0:T(8,128)(2,1)S(1)} %bitcast.14), channel_id=1, source_target_pairs={{0,24},{4,28},{8,16},{12,20},{16,8},{20,12},{24,0},{28,4},{1,25},{... | collective-permute-start | bytes 98312 | tf_op jit(solution)/shard_map/ppermute | solution.py:381
  33.0 4.2 %collective-permute-start.6 = (bf16[128,128]{1,0:T(8,128)(2,1)S(1)}, bf16[128,128]{1,0:T(8,128)(2,1)S(1)}, u32[]{:S(2)}, u32[]{:S(2)}) collective-permute-start(bf16[128,128]{1,0:T(8,128)(2,1)S(1)} %bitcast.13), channel_id=1, source_target_pairs={{0,28},{4,24},{8,20},{12,16},{16,12},{20,8},{24,4},{28,0},{1,29},{... | collective-permute-start | bytes 98312 | tf_op jit(solution)/shard_map/ppermute | solution.py:381
  39.6 12.1 %collective-permute-start.7 = (bf16[256,128]{1,0:T(8,128)(2,1)S(1)}, bf16[256,128]{1,0:T(8,128)(2,1)S(1)}, u32[]{:S(2)}, u32[]{:S(2)}) collective-permute-start(bf16[256,128]{1,0:T(8,128)(2,1)S(1)} %get-tuple-element.37), channel_id=1, source_target_pairs={{0,1},{1,0},{2,3},{3,2},{4,5},{5,4},{6,7},{7,6},{8,9},{9,8},{10,11... | collective-permute-start | bytes 196616 | tf_op jit(solution)/shard_map/ppermute | solution.py:381
  41.3 10.5 %collective-permute-start.8 = (bf16[256,128]{1,0:T(8,128)(2,1)S(1)}, bf16[256,128]{1,0:T(8,128)(2,1)S(1)}, u32[]{:S(2)}, u32[]{:S(2)}) collective-permute-start(bf16[256,128]{1,0:T(8,128)(2,1)S(1)} %get-tuple-element.38), channel_id=1, source_target_pairs={{0,2},{1,3},{2,0},{3,1},{4,6},{5,7},{6,4},{7,5},{8,10},{9,11},{10,... | collective-permute-start | bytes 196616 | tf_op jit(solution)/shard_map/ppermute | solution.py:381
  43.9 7.9 %collective-permute-start.9 = (bf16[256,128]{1,0:T(8,128)(2,1)S(1)}, bf16[256,128]{1,0:T(8,128)(2,1)S(1)}, u32[]{:S(2)}, u32[]{:S(2)}) collective-permute-start(bf16[256,128]{1,0:T(8,128)(2,1)S(1)} %get-tuple-element.39), channel_id=1, source_target_pairs={{0,3},{1,2},{2,1},{3,0},{4,7},{5,6},{6,5},{7,4},{8,11},{9,10},{10,... | collective-permute-start | bytes 196616 | tf_op jit(solution)/shard_map/ppermute | solution.py:381
  52.8 11.5 %collective-permute-start.12 = (bf16[512,256]{1,0:T(8,128)(2,1)S(1)}, bf16[512,256]{1,0:T(8,128)(2,1)S(1)}, u32[]{:S(2)}, u32[]{:S(2)}) collective-permute-start(bf16[512,256]{1,0:T(8,128)(2,1)S(1)} %panel.1.refs_0_.refs_4_), channel_id=1, source_target_pairs={{0,24},{4,28},{8,16},{12,20},{16,8},{20,12},{24,0},{28,4},{1,25},{... | collective-permute-start | bytes 786440 | tf_op jit(solution)/shard_map/ppermute | solution.py:381
  53.9 12.9 %collective-permute-start.11 = (bf16[512,256]{1,0:T(8,128)(2,1)S(1)}, bf16[512,256]{1,0:T(8,128)(2,1)S(1)}, u32[]{:S(2)}, u32[]{:S(2)}) collective-permute-start(bf16[512,256]{1,0:T(8,128)(2,1)S(1)} %panel.1.refs_0_.refs_4_), channel_id=1, source_target_pairs={{0,16},{4,20},{8,24},{12,28},{16,0},{20,4},{24,8},{28,12},{1,17},{... | collective-permute-start | bytes 786440 | tf_op jit(solution)/shard_map/ppermute | solution.py:381
  54.9 12.0 %collective-permute-start.10 = (bf16[512,256]{1,0:T(8,128)(2,1)S(1)}, bf16[512,256]{1,0:T(8,128)(2,1)S(1)}, u32[]{:S(2)}, u32[]{:S(2)}) collective-permute-start(bf16[512,256]{1,0:T(8,128)(2,1)S(1)} %panel.1.refs_0_.refs_4_), channel_id=1, source_target_pairs={{0,8},{4,12},{8,0},{12,4},{16,24},{20,28},{24,16},{28,20},{1,9},{5... | collective-permute-start | bytes 786440 | tf_op jit(solution)/shard_map/ppermute | solution.py:381
  56.3 11.0 %collective-permute-start.13 = (bf16[512,256]{1,0:T(8,128)(2,1)S(1)}, bf16[512,256]{1,0:T(8,128)(2,1)S(1)}, u32[]{:S(2)}, u32[]{:S(2)}) collective-permute-start(bf16[512,256]{1,0:T(8,128)(2,1)S(1)} %panel.1.refs_0_.refs_4_), channel_id=1, source_target_pairs={{0,4},{4,0},{8,12},{12,8},{16,20},{20,16},{24,28},{28,24},{1,5},{5... | collective-permute-start | bytes 786440 | tf_op jit(solution)/shard_map/ppermute | solution.py:381
  66.8 2.6 %collective-permute-start.16 = (bf16[512,256]{1,0:T(8,128)(2,1)S(1)}, bf16[512,256]{1,0:T(8,128)(2,1)S(1)}, u32[]{:S(2)}, u32[]{:S(2)}) collective-permute-start(bf16[512,256]{1,0:T(8,128)(2,1)S(1)} %collective-permute-done.10.refs_2_), channel_id=1, source_target_pairs={{0,4},{4,0},{8,12},{12,8},{16,20},{20,16},{24,28},{28,24},{1,5},{5... | collective-permute-start | bytes 786440 | tf_op jit(solution)/shard_map/ppermute | solution.py:381
  66.8 2.6 %collective-permute-start.15 = (bf16[512,256]{1,0:T(8,128)(2,1)S(1)}, bf16[512,256]{1,0:T(8,128)(2,1)S(1)}, u32[]{:S(2)}, u32[]{:S(2)}) collective-permute-start(bf16[512,256]{1,0:T(8,128)(2,1)S(1)} %collective-permute-done.11.refs_3_), channel_id=1, source_target_pairs={{0,4},{4,0},{8,12},{12,8},{16,20},{20,16},{24,28},{28,24},{1,5},{5... | collective-permute-start | bytes 786440 | tf_op jit(solution)/shard_map/ppermute | solution.py:381
  67.3 2.1 %collective-permute-start.14 = (bf16[512,256]{1,0:T(8,128)(2,1)S(1)}, bf16[512,256]{1,0:T(8,128)(2,1)S(1)}, u32[]{:S(2)}, u32[]{:S(2)}) collective-permute-start(bf16[512,256]{1,0:T(8,128)(2,1)S(1)} %collective-permute-done.12.refs_4_), channel_id=1, source_target_pairs={{0,4},{4,0},{8,12},{12,8},{16,20},{20,16},{24,28},{28,24},{1,5},{5... | collective-permute-start | bytes 786440 | tf_op jit(solution)/shard_map/ppermute | solution.py:381
  71.0 12.2 %collective-permute-start.17 = (bf16[512,256]{1,0:T(8,128)(2,1)S(1)}, bf16[512,256]{1,0:T(8,128)(2,1)S(1)}, u32[]{:S(2)}, u32[]{:S(2)}) collective-permute-start(bf16[512,256]{1,0:T(8,128)(2,1)S(1)} %terms.17), channel_id=1, source_target_pairs={{0,1},{1,3},{3,2},{2,0},{4,5},{5,7},{7,6},{6,4},{8,9},{9,11},{11,1... | collective-permute-start | bytes 786440 | tf_op jit(solution)/shard_map/ppermute | solution.py:389
  74.5 12.4 %collective-permute-start.20 = (bf16[512,256]{1,0:T(8,128)(2,1)S(1)}, bf16[512,256]{1,0:T(8,128)(2,1)S(1)}, u32[]{:S(2)}, u32[]{:S(2)}) collective-permute-start(bf16[512,256]{1,0:T(8,128)(2,1)S(1)} %terms.19), channel_id=1, source_target_pairs={{0,1},{1,0},{2,3},{3,2},{4,5},{5,4},{6,7},{7,6},{8,9},{9,8},{10,11... | collective-permute-start | bytes 786440 | tf_op jit(solution)/shard_map/ppermute | solution.py:381
  81.0 12.0 %collective-permute-start.18 = (bf16[512,256]{1,0:T(8,128)(2,1)S(1)}, bf16[512,256]{1,0:T(8,128)(2,1)S(1)}, u32[]{:S(2)}, u32[]{:S(2)}) collective-permute-start(bf16[512,256]{1,0:T(8,128)(2,1)S(1)} %get-tuple-element.46), channel_id=1, source_target_pairs={{0,3},{3,0},{4,7},{7,4},{8,11},{11,8},{12,15},{15,12},{16,19},{19,... | collective-permute-start | bytes 786440 | tf_op jit(solution)/shard_map/ppermute | solution.py:391
  83.2 9.7 %copy-start.1 = (f32[2]{0:T(128)S(1)}, f32[2]{0:T(128)}, u32[]{:S(2)}) copy-start(f32[2]{0:T(128)} %wave_ref.5) | copy-start | bytes 28
  83.2 9.7 %collective-permute-start.19 = (bf16[512,256]{1,0:T(8,128)(2,1)S(1)}, bf16[512,256]{1,0:T(8,128)(2,1)S(1)}, u32[]{:S(2)}, u32[]{:S(2)}) collective-permute-start(bf16[512,256]{1,0:T(8,128)(2,1)S(1)} %sum.3), channel_id=1, source_target_pairs={{1,2},{2,1},{5,6},{6,5},{9,10},{10,9},{13,14},{14,13},{17,18},{18,... | collective-permute-start | bytes 786440 | tf_op jit(solution)/shard_map/ppermute | solution.py:392
  93.7 10.2 %collective-permute-start.24 = (bf16[512,256]{1,0:T(8,128)(2,1)S(1)}, bf16[512,256]{1,0:T(8,128)(2,1)S(1)}, u32[]{:S(2)}, u32[]{:S(2)}) collective-permute-start(bf16[512,256]{1,0:T(8,128)(2,1)S(1)} %update.3.refs_0_), channel_id=1, source_target_pairs={{0,24},{4,28},{8,16},{12,20},{16,8},{20,12},{24,0},{28,4},{1,25},{... | collective-permute-start | bytes 786440 | tf_op jit(solution)/shard_map/ppermute | solution.py:381
  95.0 12.6 %collective-permute-start.23 = (bf16[512,256]{1,0:T(8,128)(2,1)S(1)}, bf16[512,256]{1,0:T(8,128)(2,1)S(1)}, u32[]{:S(2)}, u32[]{:S(2)}) collective-permute-start(bf16[512,256]{1,0:T(8,128)(2,1)S(1)} %update.3.refs_0_), channel_id=1, source_target_pairs={{0,16},{4,20},{8,24},{12,28},{16,0},{20,4},{24,8},{28,12},{1,17},{... | collective-permute-start | bytes 786440 | tf_op jit(solution)/shard_map/ppermute | solution.py:381
  96.0 11.7 %collective-permute-start.22 = (bf16[512,256]{1,0:T(8,128)(2,1)S(1)}, bf16[512,256]{1,0:T(8,128)(2,1)S(1)}, u32[]{:S(2)}, u32[]{:S(2)}) collective-permute-start(bf16[512,256]{1,0:T(8,128)(2,1)S(1)} %update.3.refs_0_), channel_id=1, source_target_pairs={{0,8},{4,12},{8,0},{12,4},{16,24},{20,28},{24,16},{28,20},{1,9},{5... | collective-permute-start | bytes 786440 | tf_op jit(solution)/shard_map/ppermute | solution.py:381
  97.3 10.8 %collective-permute-start.21 = (bf16[512,256]{1,0:T(8,128)(2,1)S(1)}, bf16[512,256]{1,0:T(8,128)(2,1)S(1)}, u32[]{:S(2)}, u32[]{:S(2)}) collective-permute-start(bf16[512,256]{1,0:T(8,128)(2,1)S(1)} %update.3.refs_0_), channel_id=1, source_target_pairs={{0,4},{4,0},{8,12},{12,8},{16,20},{20,16},{24,28},{28,24},{1,5},{5... | collective-permute-start | bytes 786440 | tf_op jit(solution)/shard_map/ppermute | solution.py:381
  103.9 6.2 %collective-permute-start.25 = (bf16[512,256]{1,0:T(8,128)(2,1)S(1)}, bf16[512,256]{1,0:T(8,128)(2,1)S(1)}, u32[]{:S(2)}, u32[]{:S(2)}) collective-permute-start(bf16[512,256]{1,0:T(8,128)(2,1)S(1)} %collective-permute-done.24.refs_4_), channel_id=1, source_target_pairs={{0,4},{4,0},{8,12},{12,8},{16,20},{20,16},{24,28},{28,24},{1,5},{5... | collective-permute-start | bytes 786440 | tf_op jit(solution)/shard_map/ppermute | solution.py:381
  107.6 2.6 %collective-permute-start.26 = (bf16[512,256]{1,0:T(8,128)(2,1)S(1)}, bf16[512,256]{1,0:T(8,128)(2,1)S(1)}, u32[]{:S(2)}, u32[]{:S(2)}) collective-permute-start(bf16[512,256]{1,0:T(8,128)(2,1)S(1)} %collective-permute-done.23.refs_3_), channel_id=1, source_target_pairs={{0,4},{4,0},{8,12},{12,8},{16,20},{20,16},{24,28},{28,24},{1,5},{5... | collective-permute-start | bytes 786440 | tf_op jit(solution)/shard_map/ppermute | solution.py:381
  107.6 2.6 %collective-permute-start.27 = (bf16[512,256]{1,0:T(8,128)(2,1)S(1)}, bf16[512,256]{1,0:T(8,128)(2,1)S(1)}, u32[]{:S(2)}, u32[]{:S(2)}) collective-permute-start(bf16[512,256]{1,0:T(8,128)(2,1)S(1)} %collective-permute-done.22.refs_2_), channel_id=1, source_target_pairs={{0,4},{4,0},{8,12},{12,8},{16,20},{20,16},{24,28},{28,24},{1,5},{5... | collective-permute-start | bytes 786440 | tf_op jit(solution)/shard_map/ppermute | solution.py:381
  111.8 14.5 %collective-permute-start.28 = (bf16[512,256]{1,0:T(8,128)(2,1)S(1)}, bf16[512,256]{1,0:T(8,128)(2,1)S(1)}, u32[]{:S(2)}, u32[]{:S(2)}) collective-permute-start(bf16[512,256]{1,0:T(8,128)(2,1)S(1)} %terms.22), channel_id=1, source_target_pairs={{0,1},{1,3},{3,2},{2,0},{4,5},{5,7},{7,6},{6,4},{8,9},{9,11},{11,1... | collective-permute-start | bytes 786440 | tf_op jit(solution)/shard_map/ppermute | solution.py:389
  119.8 10.1 %collective-permute-start.31 = (bf16[512,256]{1,0:T(8,128)(2,1)S(1)}, bf16[512,256]{1,0:T(8,128)(2,1)S(1)}, u32[]{:S(2)}, u32[]{:S(2)}) collective-permute-start(bf16[512,256]{1,0:T(8,128)(2,1)S(1)} %terms.24), channel_id=1, source_target_pairs={{0,1},{1,0},{2,3},{3,2},{4,5},{5,4},{6,7},{7,6},{8,9},{9,8},{10,11... | collective-permute-start | bytes 786440 | tf_op jit(solution)/shard_map/ppermute | solution.py:381
  122.7 13.3 %collective-permute-start.29 = (bf16[512,256]{1,0:T(8,128)(2,1)S(1)}, bf16[512,256]{1,0:T(8,128)(2,1)S(1)}, u32[]{:S(2)}, u32[]{:S(2)}) collective-permute-start(bf16[512,256]{1,0:T(8,128)(2,1)S(1)} %get-tuple-element.48), channel_id=1, source_target_pairs={{0,3},{3,0},{4,7},{7,4},{8,11},{11,8},{12,15},{15,12},{16,19},{19,... | collective-permute-start | bytes 786440 | tf_op jit(solution)/shard_map/ppermute | solution.py:391
  126.4 9.7 %collective-permute-start.30 = (bf16[512,256]{1,0:T(8,128)(2,1)S(1)}, bf16[512,256]{1,0:T(8,128)(2,1)S(1)}, u32[]{:S(2)}, u32[]{:S(2)}) collective-permute-start(bf16[512,256]{1,0:T(8,128)(2,1)S(1)} %sum.4), channel_id=1, source_target_pairs={{1,2},{2,1},{5,6},{6,5},{9,10},{10,9},{13,14},{14,13},{17,18},{18,... | collective-permute-start | bytes 786440 | tf_op jit(solution)/shard_map/ppermute | solution.py:392
  136.9 10.2 %collective-permute-start.35 = (bf16[512,256]{1,0:T(8,128)(2,1)S(1)}, bf16[512,256]{1,0:T(8,128)(2,1)S(1)}, u32[]{:S(2)}, u32[]{:S(2)}) collective-permute-start(bf16[512,256]{1,0:T(8,128)(2,1)S(1)} %update.4.refs_0_), channel_id=1, source_target_pairs={{0,24},{4,28},{8,16},{12,20},{16,8},{20,12},{24,0},{28,4},{1,25},{... | collective-permute-start | bytes 786440 | tf_op jit(solution)/shard_map/ppermute | solution.py:381
  138.1 12.6 %collective-permute-start.34 = (bf16[512,256]{1,0:T(8,128)(2,1)S(1)}, bf16[512,256]{1,0:T(8,128)(2,1)S(1)}, u32[]{:S(2)}, u32[]{:S(2)}) collective-permute-start(bf16[512,256]{1,0:T(8,128)(2,1)S(1)} %update.4.refs_0_), channel_id=1, source_target_pairs={{0,16},{4,20},{8,24},{12,28},{16,0},{20,4},{24,8},{28,12},{1,17},{... | collective-permute-start | bytes 786440 | tf_op jit(solution)/shard_map/ppermute | solution.py:381
  139.1 11.7 %collective-permute-start.33 = (bf16[512,256]{1,0:T(8,128)(2,1)S(1)}, bf16[512,256]{1,0:T(8,128)(2,1)S(1)}, u32[]{:S(2)}, u32[]{:S(2)}) collective-permute-start(bf16[512,256]{1,0:T(8,128)(2,1)S(1)} %update.4.refs_0_), channel_id=1, source_target_pairs={{0,8},{4,12},{8,0},{12,4},{16,24},{20,28},{24,16},{28,20},{1,9},{5... | collective-permute-start | bytes 786440 | tf_op jit(solution)/shard_map/ppermute | solution.py:381
  140.4 10.8 %collective-permute-start.32 = (bf16[512,256]{1,0:T(8,128)(2,1)S(1)}, bf16[512,256]{1,0:T(8,128)(2,1)S(1)}, u32[]{:S(2)}, u32[]{:S(2)}) collective-permute-start(bf16[512,256]{1,0:T(8,128)(2,1)S(1)} %update.4.refs_0_), channel_id=1, source_target_pairs={{0,4},{4,0},{8,12},{12,8},{16,20},{20,16},{24,28},{28,24},{1,5},{5... | collective-permute-start | bytes 786440 | tf_op jit(solution)/shard_map/ppermute | solution.py:381
  147.1 6.3 %collective-permute-start.36 = (bf16[512,256]{1,0:T(8,128)(2,1)S(1)}, bf16[512,256]{1,0:T(8,128)(2,1)S(1)}, u32[]{:S(2)}, u32[]{:S(2)}) collective-permute-start(bf16[512,256]{1,0:T(8,128)(2,1)S(1)} %collective-permute-done.35.refs_4_), channel_id=1, source_target_pairs={{0,4},{4,0},{8,12},{12,8},{16,20},{20,16},{24,28},{28,24},{1,5},{5... | collective-permute-start | bytes 786440 | tf_op jit(solution)/shard_map/ppermute | solution.py:381
  150.8 2.6 %collective-permute-start.37 = (bf16[512,256]{1,0:T(8,128)(2,1)S(1)}, bf16[512,256]{1,0:T(8,128)(2,1)S(1)}, u32[]{:S(2)}, u32[]{:S(2)}) collective-permute-start(bf16[512,256]{1,0:T(8,128)(2,1)S(1)} %collective-permute-done.34.refs_3_), channel_id=1, source_target_pairs={{0,4},{4,0},{8,12},{12,8},{16,20},{20,16},{24,28},{28,24},{1,5},{5... | collective-permute-start | bytes 786440 | tf_op jit(solution)/shard_map/ppermute | solution.py:381
  150.8 2.6 %collective-permute-start.38 = (bf16[512,256]{1,0:T(8,128)(2,1)S(1)}, bf16[512,256]{1,0:T(8,128)(2,1)S(1)}, u32[]{:S(2)}, u32[]{:S(2)}) collective-permute-start(bf16[512,256]{1,0:T(8,128)(2,1)S(1)} %collective-permute-done.33.refs_2_), channel_id=1, source_target_pairs={{0,4},{4,0},{8,12},{12,8},{16,20},{20,16},{24,28},{28,24},{1,5},{5... | collective-permute-start | bytes 786440 | tf_op jit(solution)/shard_map/ppermute | solution.py:381
  154.9 13.6 %collective-permute-start.39 = (bf16[512,256]{1,0:T(8,128)(2,1)S(1)}, bf16[512,256]{1,0:T(8,128)(2,1)S(1)}, u32[]{:S(2)}, u32[]{:S(2)}) collective-permute-start(bf16[512,256]{1,0:T(8,128)(2,1)S(1)} %terms.27), channel_id=1, source_target_pairs={{0,1},{1,3},{3,2},{2,0},{4,5},{5,7},{7,6},{6,4},{8,9},{9,11},{11,1... | collective-permute-start | bytes 786440 | tf_op jit(solution)/shard_map/ppermute | solution.py:389
  162.3 9.8 %collective-permute-start.42 = (bf16[512,256]{1,0:T(8,128)(2,1)S(1)}, bf16[512,256]{1,0:T(8,128)(2,1)S(1)}, u32[]{:S(2)}, u32[]{:S(2)}) collective-permute-start(bf16[512,256]{1,0:T(8,128)(2,1)S(1)} %terms.29), channel_id=1, source_target_pairs={{0,1},{1,0},{2,3},{3,2},{4,5},{5,4},{6,7},{7,6},{8,9},{9,8},{10,11... | collective-permute-start | bytes 786440 | tf_op jit(solution)/shard_map/ppermute | solution.py:381
  165.3 13.0 %collective-permute-start.40 = (bf16[512,256]{1,0:T(8,128)(2,1)S(1)}, bf16[512,256]{1,0:T(8,128)(2,1)S(1)}, u32[]{:S(2)}, u32[]{:S(2)}) collective-permute-start(bf16[512,256]{1,0:T(8,128)(2,1)S(1)} %get-tuple-element.50), channel_id=1, source_target_pairs={{0,3},{3,0},{4,7},{7,4},{8,11},{11,8},{12,15},{15,12},{16,19},{19,... | collective-permute-start | bytes 786440 | tf_op jit(solution)/shard_map/ppermute | solution.py:391
  168.6 9.7 %collective-permute-start.41 = (bf16[512,256]{1,0:T(8,128)(2,1)S(1)}, bf16[512,256]{1,0:T(8,128)(2,1)S(1)}, u32[]{:S(2)}, u32[]{:S(2)}) collective-permute-start(bf16[512,256]{1,0:T(8,128)(2,1)S(1)} %sum.5), channel_id=1, source_target_pairs={{1,2},{2,1},{5,6},{6,5},{9,10},{10,9},{13,14},{14,13},{17,18},{18,... | collective-permute-start | bytes 786440 | tf_op jit(solution)/shard_map/ppermute | solution.py:392

commit v8 on v5

--- a/solution.py
+++ b/solution.py
@@ -123,8 +123,8 @@
         out_specs=[VMEM] * n_row,
         out_shape=[jax.ShapeDtypeStruct((steps, short, LANES), jnp.bfloat16)] * n_row,
         scratch_shapes=[
-            pltpu.VMEM((BUFFERS, block, shots, samples), jnp.bfloat16),
-            pltpu.SemaphoreType.DMA((BUFFERS,)),
+            pltpu.VMEM((BUFFERS + 2, block, shots, samples), jnp.bfloat16),
+            pltpu.SemaphoreType.DMA((BUFFERS + 2,)),
             pltpu.VMEM(table.shape, jnp.float32),
             pltpu.VMEM(table.shape, jnp.bfloat16),
             pltpu.SemaphoreType.DMA,
@@ -164,7 +164,7 @@
 def order_kernel(packs, n_src, place_ref, code_ref, hits_ref, *refs):
     pieces, out_refs = refs[:-n_src], refs[-n_src:]
     width = LANES // packs
-    held = jnp.concatenate([ref[...] for ref in pieces], axis=0)
+    held = jnp.concatenate([ref[...] for ref in reversed(pieces)], axis=0)
     rolled = [held] + [
         pltpu.roll(held.astype(jnp.float32), turn * width, 1).astype(jnp.bfloat16) for turn in range(1, packs)
     ]
@@ -425,7 +425,7 @@
     short = block // packs
 
     spectra = make_spectra(traces, place, n_row, packs, block)
-    arrived = [spectra[0]] + [swap(spectra[turn], "row", turn) for turn in range(1, n_row)]
+    arrived = [swap(spectra[turn], "row", turn) for turn in range(n_row - 1, 0, -1)] + [spectra[0]]
 
     inside = row_source % group_rows
     position = (row_source // block_rows ^ row) * (group_rows // packs) + inside // block * short + inside % short

time: 176 us -> 175 us (level)
  transfers between devices with their start and end apart: 43 -> 43, of which waited for: 12 -> 13; matrix products, arithmetic and copies ran while one was open for 0% -> 0% of each run, Pallas kernels for 28% -> 28%
where the time goes in v8:
time: 175 us
  Pallas kernels  85 us (49%)
  waiting for transfers between devices  45.7 us (26%)
  starting transfers between devices  41.8 us (24%)
    ppermute x34, waiting for transfers between devices, swap(): lax.ppermute(array, axis, [(index, index ^ bits) for index in range(size)])  40.5 us
    pallas_call x15, Pallas kernels, make_terms(): pl.pallas_call(functools.partial(terms_kernel, turns, numbers, len(partia...  36.6 us
    ppermute x34, starting transfers between devices, swap(): lax.ppermute(array, axis, [(index, index ^ bits) for index in range(size)])  24.5 us
    pallas_call x1, Pallas kernels, make_spectra(): pl.pallas_call(functools.partial(spectra_kernel, packs, n_row), in_specs=...  23.8 us
    pallas_call x2, Pallas kernels, relay(): pl.pallas_call(functools.partial(relay_kernel, part), in_specs=[ANY, ANY]...  15.7 us
    ppermute x3, starting transfers between devices, exchange(): outer = lax.ppermute(sent, 'src', [(0, 3), (3, 0)])  13.5 us
    ppermute x3, waiting for transfers between devices, exchange(): outer = lax.ppermute(sent, 'src', [(0, 3), (3, 0)])  5.23 us
    pallas_call x3, Pallas kernels, make_update(): pl.pallas_call(functools.partial(last_kernel if last else estimate_kernel...  3.77 us
  transfers between devices with their start and end apart: 43, of which 13 were waited for; matrix products, arithmetic and copies ran while one was open for 0% of the time, Pallas kernels for 28%

profile of v8, /device:TPU:0, one launch (start us, length us, event | category | flops | bytes accessed | tf_op | source)
XLA Modules:
  0.0 175.0 jit_solution(7262155940033109479)
XLA Ops:
  0.7 0.9 copy-done
  1.7 23.8 %spectra.1 = (bf16[2,64,128]{2,1,0:T(8,128)(2,1)S(1)}, bf16[2,64,128]{2,1,0:T(8,128)(2,1)S(1)}, bf16[2,64,128]{2,1,0:T(8,128)(2,1)S(1)}, bf16[2,64,128]{2,1,0:T(...) custom-call(s32[2]{0:T(128)S(1)} %pad_add_fusion.place_ref, ...), custom_call_target="tpu_custom_call" | custom-call | flops 8589934592 | bytes 67108864 | tf_op jit(solution)/shard_map/spectra/pallas_call | solution.py:120
  25.5 3.4 %collective-permute-start = (bf16[128,128]{1,0:T(8,128)(2,1)S(1)}, bf16[128,128]{1,0:T(8,128)(2,1)S(1)}, u32[]{:S(2)}, u32[]{:S(2)}) collective-permute-start(bf16[128,128]{1,0:T(8,128)(2,1)S(1)} %bitcast.19), channel_id=1, source_target_pairs={{0,28},{4,24},{8,20},{12,16},{16,12},{20,8},{24,4},{28,0},{1,29},{... | collective-permute-start | bytes 98312 | tf_op jit(solution)/shard_map/ppermute | solution.py:381
  29.5 1.4 collective-permute-start.2
  31.2 1.2 collective-permute-start.4
  34.2 1.7 hits.1.hits_ref
  36.3 2.4 %order.1 = (bf16[256,128]{1,0:T(8,128)(2,1)S(1)}, bf16[256,128]{1,0:T(8,128)(2,1)S(1)}, bf16[256,128]{1,0:T(8,128)(2,1)S(1)}, bf16[256,128]{1,0:T(8,128)(2,1)S(1)}) custom-call(s32[2]{0:T(128)S(1)} %pad_add_fusion.place_ref, s32[2048,128]{1,0:T(8,128)S(1)} %broadcast_in_dim.2.code_ref, bf16[2048,1024]{1,0:T(8,128)(2,1)S(1)} %hits.1.hits_ref, ...), custom_call_target="tpu_custom_call" | custom-call | flops 1073741824 | bytes 1048576 | tf_op jit(solution)/shard_map/order/pallas_call | solution.py:193
  38.6 1.6 collective-permute-start.7
  40.3 2.6 %collective-permute-start.8 = (bf16[256,128]{1,0:T(8,128)(2,1)S(1)}, bf16[256,128]{1,0:T(8,128)(2,1)S(1)}, u32[]{:S(2)}, u32[]{:S(2)}) collective-permute-start(bf16[256,128]{1,0:T(8,128)(2,1)S(1)} %get-tuple-element.38), channel_id=1, source_target_pairs={{0,2},{1,3},{2,0},{3,1},{4,6},{5,7},{6,4},{7,5},{8,10},{9,11},{10,... | collective-permute-start | bytes 196616 | tf_op jit(solution)/shard_map/ppermute | solution.py:381
  43.1 7.7 %relay.3 = (bf16[8,2048,512]{2,1,0:T(8,128)(2,1)S(1)}, f32[8,128]{1,0:T(8,128)S(1)}) custom-call(bf16[2,2048,8,512]{3,2,1,0:T(8,128)(2,1)} %data_ref.3, bf16[256,128]{1,0:T(8,128)(2,1)S(1)} %get-tuple-element.36.after_ref.refs_0_), custom_call_target="tpu_custom_call" | custom-call | bytes 33554432 | tf_op jit(solution)/shard_map/relay/pallas_call | solution.py:256
  50.8 1.0 panel.1.refs_0_.refs_4_
  51.8 2.0 %collective-permute-start.10 = (bf16[512,256]{1,0:T(8,128)(2,1)S(1)}, bf16[512,256]{1,0:T(8,128)(2,1)S(1)}, u32[]{:S(2)}, u32[]{:S(2)}) collective-permute-start(bf16[512,256]{1,0:T(8,128)(2,1)S(1)} %panel.1.refs_0_.refs_4_), channel_id=1, source_target_pairs={{0,24},{4,28},{8,16},{12,20},{16,8},{20,12},{24,0},{28,4},{1,25},{... | collective-permute-start | bytes 786440 | tf_op jit(solution)/shard_map/ppermute | solution.py:381
  54.3 1.1 collective-permute-start.12
  55.4 8.0 %relay.2 = (bf16[8,2048,512]{2,1,0:T(8,128)(2,1)S(1)}, f32[8,128]{1,0:T(8,128)}) custom-call(bf16[2,2048,8,512]{3,2,1,0:T(8,128)(2,1)} %data_ref.3, bf16[128,128]{1,0:T(8,128)(2,1)S(1)} %bitcast.12), custom_call_target="tpu_custom_call" | custom-call | bytes 33554432 | tf_op jit(solution)/shard_map/relay/pallas_call | solution.py:256
  63.4 2.6 %collective-permute-done.11.refs_3_ = bf16[512,256]{1,0:T(8,128)(2,1)S(1)} collective-permute-done((bf16[512,256]{1,0:T(8,128)(2,1)S(1)}, bf16[512,256]{1,0:T(8,128)(2,1)S(1)}, u32[]{:S(2)}, u32[]{:S(2)}) %collective-permute-start.11) | collective-permute-done | bytes 262176 | tf_op jit(solution)/shard_map/ppermute | solution.py:381
  66.5 2.1 %terms.16.refs_3_ = f32[512,256]{1,0:T(8,128)S(1)} custom-call(s32[2]{0:T(128)S(1)} %pad_add_fusion.place_ref, bf16[8,2048,512]{2,1,0:T(8,128)(2,1)S(1)} %get-tuple-element.41.real_ref, bf16[8,2048,512]{2,1,0:T(8,128)(2,1)S(1)} %get-tuple-element.42.imag_ref, bf16[512,256]{1,0:T(8,128)(2,1)S(1)} %panel.1.refs_0_.refs_4_, ...), custom_call_target="tpu_custom_call" | custom-call | flops 1342177280 | bytes 5242880 | tf_op jit(solution)/shard_map/terms/pallas_call | solution.py:305
  68.6 1.5 terms.17
  70.8 2.9 %terms.19 = (bf16[512,256]{1,0:T(8,128)(2,1)S(1)}, f32[512,256]{1,0:T(8,128)S(1)}) custom-call(s32[2]{0:T(128)S(1)} %pad_add_fusion.place_ref, bf16[8,2048,512]{2,1,0:T(8,128)(2,1)S(1)} %get-tuple-element.41.real_ref, bf16[8,2048,512]{2,1,0:T(8,128)(2,1)S(1)} %get-tuple-element.42.imag_ref, bf16[512,256]{1,0:T(8,128)(2,1)S(1)} %panel.1.refs_0_.refs_4_, ...), custom_call_target="tpu_custom_call" | custom-call | flops 2147483648 | bytes 8388608 | tf_op jit(solution)/shard_map/terms/pallas_call | solution.py:305
  73.7 4.9 %collective-permute-start.19 = (bf16[512,256]{1,0:T(8,128)(2,1)S(1)}, bf16[512,256]{1,0:T(8,128)(2,1)S(1)}, u32[]{:S(2)}, u32[]{:S(2)}) collective-permute-start(bf16[512,256]{1,0:T(8,128)(2,1)S(1)} %get-tuple-element.46), channel_id=1, source_target_pairs={{0,3},{3,0},{4,7},{7,4},{8,11},{11,8},{12,15},{15,12},{16,19},{19,... | collective-permute-start | bytes 786440 | tf_op jit(solution)/shard_map/ppermute | solution.py:392
  78.6 2.9 %terms.18 = bf16[512,256]{1,0:T(8,128)(2,1)S(1)} custom-call(s32[2]{0:T(128)S(1)} %pad_add_fusion.place_ref, bf16[8,2048,512]{2,1,0:T(8,128)(2,1)S(1)} %get-tuple-element.41.real_ref, bf16[8,2048,512]{2,1,0:T(8,128)(2,1)S(1)} %get-tuple-element.42.imag_ref, bf16[512,256]{1,0:T(8,128)(2,1)S(1)} %panel.1.refs_0_.refs_4_, ...), custom_call_target="tpu_custom_call" | custom-call | flops 2147483648 | bytes 8388608 | tf_op jit(solution)/shard_map/terms/pallas_call | solution.py:305
  82.5 2.9 %terms.15.own_ref = f32[512,256]{1,0:T(8,128)S(1)} custom-call(s32[2]{0:T(128)S(1)} %pad_add_fusion.place_ref, bf16[8,2048,512]{2,1,0:T(8,128)(2,1)S(1)} %get-tuple-element.41.real_ref, bf16[8,2048,512]{2,1,0:T(8,128)(2,1)S(1)} %get-tuple-element.42.imag_ref, bf16[512,256]{1,0:T(8,128)(2,1)S(1)} %panel.1.refs_0_.refs_4_, ...), custom_call_target="tpu_custom_call" | custom-call | flops 2147483648 | bytes 8388608 | tf_op jit(solution)/shard_map/terms/pallas_call | solution.py:305
  85.3 1.3 collective-permute-done.19.refs_2_
  86.6 5.3 %collective-permute-done.18.refs_1_ = bf16[512,256]{1,0:T(8,128)(2,1)S(1)} collective-permute-done((bf16[512,256]{1,0:T(8,128)(2,1)S(1)}, bf16[512,256]{1,0:T(8,128)(2,1)S(1)}, u32[]{:S(2)}, u32[]{:S(2)}) %collective-permute-start.18) | collective-permute-done | bytes 262176 | tf_op jit(solution)/shard_map/ppermute | solution.py:381
  92.8 1.8 %collective-permute-start.24 = (bf16[512,256]{1,0:T(8,128)(2,1)S(1)}, bf16[512,256]{1,0:T(8,128)(2,1)S(1)}, u32[]{:S(2)}, u32[]{:S(2)}) collective-permute-start(bf16[512,256]{1,0:T(8,128)(2,1)S(1)} %update.3.refs_0_), channel_id=1, source_target_pairs={{0,24},{4,28},{8,16},{12,20},{16,8},{20,12},{24,0},{28,4},{1,25},{... | collective-permute-start | bytes 786440 | tf_op jit(solution)/shard_map/ppermute | solution.py:381
  95.3 1.0 collective-permute-start.22
  96.3 6.6 %collective-permute-done.24.refs_4_ = bf16[512,256]{1,0:T(8,128)(2,1)S(1)} collective-permute-done((bf16[512,256]{1,0:T(8,128)(2,1)S(1)}, bf16[512,256]{1,0:T(8,128)(2,1)S(1)}, u32[]{:S(2)}, u32[]{:S(2)}) %collective-permute-start.24) | collective-permute-done | bytes 262176 | tf_op jit(solution)/shard_map/ppermute | solution.py:381
  103.0 4.7 %collective-permute-done.23.refs_3_ = bf16[512,256]{1,0:T(8,128)(2,1)S(1)} collective-permute-done((bf16[512,256]{1,0:T(8,128)(2,1)S(1)}, bf16[512,256]{1,0:T(8,128)(2,1)S(1)}, u32[]{:S(2)}, u32[]{:S(2)}) %collective-permute-start.23) | collective-permute-done | bytes 262176 | tf_op jit(solution)/shard_map/ppermute | solution.py:381
  108.1 2.1 %terms.21.refs_3_ = f32[512,256]{1,0:T(8,128)S(1)} custom-call(s32[2]{0:T(128)S(1)} %pad_add_fusion.place_ref, bf16[8,2048,512]{2,1,0:T(8,128)(2,1)S(1)} %get-tuple-element.41.real_ref, bf16[8,2048,512]{2,1,0:T(8,128)(2,1)S(1)} %get-tuple-element.42.imag_ref, bf16[512,256]{1,0:T(8,128)(2,1)S(1)} %update.3.refs_0_, ...), custom_call_target="tpu_custom_call" | custom-call | flops 1342177280 | bytes 5242880 | tf_op jit(solution)/shard_map/terms/pallas_call | solution.py:305
  110.2 1.5 terms.22
  112.6 2.9 %terms.24 = (bf16[512,256]{1,0:T(8,128)(2,1)S(1)}, f32[512,256]{1,0:T(8,128)S(1)}) custom-call(s32[2]{0:T(128)S(1)} %pad_add_fusion.place_ref, bf16[8,2048,512]{2,1,0:T(8,128)(2,1)S(1)} %get-tuple-element.41.real_ref, bf16[8,2048,512]{2,1,0:T(8,128)(2,1)S(1)} %get-tuple-element.42.imag_ref, bf16[512,256]{1,0:T(8,128)(2,1)S(1)} %update.3.refs_0_, ...), custom_call_target="tpu_custom_call" | custom-call | flops 2147483648 | bytes 8388608 | tf_op jit(solution)/shard_map/terms/pallas_call | solution.py:305
  115.4 4.2 %collective-permute-start.30 = (bf16[512,256]{1,0:T(8,128)(2,1)S(1)}, bf16[512,256]{1,0:T(8,128)(2,1)S(1)}, u32[]{:S(2)}, u32[]{:S(2)}) collective-permute-start(bf16[512,256]{1,0:T(8,128)(2,1)S(1)} %get-tuple-element.48), channel_id=1, source_target_pairs={{0,3},{3,0},{4,7},{7,4},{8,11},{11,8},{12,15},{15,12},{16,19},{19,... | collective-permute-start | bytes 786440 | tf_op jit(solution)/shard_map/ppermute | solution.py:392
  119.7 2.9 %terms.23 = bf16[512,256]{1,0:T(8,128)(2,1)S(1)} custom-call(s32[2]{0:T(128)S(1)} %pad_add_fusion.place_ref, bf16[8,2048,512]{2,1,0:T(8,128)(2,1)S(1)} %get-tuple-element.41.real_ref, bf16[8,2048,512]{2,1,0:T(8,128)(2,1)S(1)} %get-tuple-element.42.imag_ref, bf16[512,256]{1,0:T(8,128)(2,1)S(1)} %update.3.refs_0_, ...), custom_call_target="tpu_custom_call" | custom-call | flops 2147483648 | bytes 8388608 | tf_op jit(solution)/shard_map/terms/pallas_call | solution.py:305
  123.4 2.9 %terms.20.own_ref = f32[512,256]{1,0:T(8,128)S(1)} custom-call(s32[2]{0:T(128)S(1)} %pad_add_fusion.place_ref, bf16[8,2048,512]{2,1,0:T(8,128)(2,1)S(1)} %get-tuple-element.41.real_ref, bf16[8,2048,512]{2,1,0:T(8,128)(2,1)S(1)} %get-tuple-element.42.imag_ref, bf16[512,256]{1,0:T(8,128)(2,1)S(1)} %update.3.refs_0_, ...), custom_call_target="tpu_custom_call" | custom-call | flops 2147483648 | bytes 8388608 | tf_op jit(solution)/shard_map/terms/pallas_call | solution.py:305
  126.3 2.1 %collective-permute-done.30.refs_2_ = bf16[512,256]{1,0:T(8,128)(2,1)S(1)} collective-permute-done((bf16[512,256]{1,0:T(8,128)(2,1)S(1)}, bf16[512,256]{1,0:T(8,128)(2,1)S(1)}, u32[]{:S(2)}, u32[]{:S(2)}) %collective-permute-start.30) | collective-permute-done | bytes 262176 | tf_op jit(solution)/shard_map/ppermute | solution.py:392
  128.3 4.3 %collective-permute-done.29.refs_1_ = bf16[512,256]{1,0:T(8,128)(2,1)S(1)} collective-permute-done((bf16[512,256]{1,0:T(8,128)(2,1)S(1)}, bf16[512,256]{1,0:T(8,128)(2,1)S(1)}, u32[]{:S(2)}, u32[]{:S(2)}) %collective-permute-start.29) | collective-permute-done | bytes 262176 | tf_op jit(solution)/shard_map/ppermute | solution.py:381
  133.5 1.8 %collective-permute-start.35 = (bf16[512,256]{1,0:T(8,128)(2,1)S(1)}, bf16[512,256]{1,0:T(8,128)(2,1)S(1)}, u32[]{:S(2)}, u32[]{:S(2)}) collective-permute-start(bf16[512,256]{1,0:T(8,128)(2,1)S(1)} %update.4.refs_0_), channel_id=1, source_target_pairs={{0,24},{4,28},{8,16},{12,20},{16,8},{20,12},{24,0},{28,4},{1,25},{... | collective-permute-start | bytes 786440 | tf_op jit(solution)/shard_map/ppermute | solution.py:381
  136.1 1.0 collective-permute-start.33
  137.1 6.6 %collective-permute-done.35.refs_4_ = bf16[512,256]{1,0:T(8,128)(2,1)S(1)} collective-permute-done((bf16[512,256]{1,0:T(8,128)(2,1)S(1)}, bf16[512,256]{1,0:T(8,128)(2,1)S(1)}, u32[]{:S(2)}, u32[]{:S(2)}) %collective-permute-start.35) | collective-permute-done | bytes 262176 | tf_op jit(solution)/shard_map/ppermute | solution.py:381
  143.7 4.5 %collective-permute-done.34.refs_3_ = bf16[512,256]{1,0:T(8,128)(2,1)S(1)} collective-permute-done((bf16[512,256]{1,0:T(8,128)(2,1)S(1)}, bf16[512,256]{1,0:T(8,128)(2,1)S(1)}, u32[]{:S(2)}, u32[]{:S(2)}) %collective-permute-start.34) | collective-permute-done | bytes 262176 | tf_op jit(solution)/shard_map/ppermute | solution.py:381
  148.8 2.1 %terms.26.refs_3_ = f32[512,256]{1,0:T(8,128)S(1)} custom-call(s32[2]{0:T(128)S(1)} %pad_add_fusion.place_ref, bf16[8,2048,512]{2,1,0:T(8,128)(2,1)S(1)} %get-tuple-element.41.real_ref, bf16[8,2048,512]{2,1,0:T(8,128)(2,1)S(1)} %get-tuple-element.42.imag_ref, bf16[512,256]{1,0:T(8,128)(2,1)S(1)} %update.4.refs_0_, ...), custom_call_target="tpu_custom_call" | custom-call | flops 1342177280 | bytes 5242880 | tf_op jit(solution)/shard_map/terms/pallas_call | solution.py:305
  150.9 1.5 terms.27
  152.6 2.9 %terms.29 = (bf16[512,256]{1,0:T(8,128)(2,1)S(1)}, f32[512,256]{1,0:T(8,128)S(1)}) custom-call(s32[2]{0:T(128)S(1)} %pad_add_fusion.place_ref, bf16[8,2048,512]{2,1,0:T(8,128)(2,1)S(1)} %get-tuple-element.41.real_ref, bf16[8,2048,512]{2,1,0:T(8,128)(2,1)S(1)} %get-tuple-element.42.imag_ref, bf16[512,256]{1,0:T(8,128)(2,1)S(1)} %update.4.refs_0_, ...), custom_call_target="tpu_custom_call" | custom-call | flops 2147483648 | bytes 8388608 | tf_op jit(solution)/shard_map/terms/pallas_call | solution.py:305
  155.5 4.4 %collective-permute-start.41 = (bf16[512,256]{1,0:T(8,128)(2,1)S(1)}, bf16[512,256]{1,0:T(8,128)(2,1)S(1)}, u32[]{:S(2)}, u32[]{:S(2)}) collective-permute-start(bf16[512,256]{1,0:T(8,128)(2,1)S(1)} %get-tuple-element.50), channel_id=1, source_target_pairs={{0,3},{3,0},{4,7},{7,4},{8,11},{11,8},{12,15},{15,12},{16,19},{19,... | collective-permute-start | bytes 786440 | tf_op jit(solution)/shard_map/ppermute | solution.py:392
  159.9 2.9 %terms.28 = bf16[512,256]{1,0:T(8,128)(2,1)S(1)} custom-call(s32[2]{0:T(128)S(1)} %pad_add_fusion.place_ref, bf16[8,2048,512]{2,1,0:T(8,128)(2,1)S(1)} %get-tuple-element.41.real_ref, bf16[8,2048,512]{2,1,0:T(8,128)(2,1)S(1)} %get-tuple-element.42.imag_ref, bf16[512,256]{1,0:T(8,128)(2,1)S(1)} %update.4.refs_0_, ...), custom_call_target="tpu_custom_call" | custom-call | flops 2147483648 | bytes 8388608 | tf_op jit(solution)/shard_map/terms/pallas_call | solution.py:305
  163.6 2.9 %terms.25.own_ref = f32[512,256]{1,0:T(8,128)S(1)} custom-call(s32[2]{0:T(128)S(1)} %pad_add_fusion.place_ref, bf16[8,2048,512]{2,1,0:T(8,128)(2,1)S(1)} %get-tuple-element.41.real_ref, bf16[8,2048,512]{2,1,0:T(8,128)(2,1)S(1)} %get-tuple-element.42.imag_ref, bf16[512,256]{1,0:T(8,128)(2,1)S(1)} %update.4.refs_0_, ...), custom_call_target="tpu_custom_call" | custom-call | flops 2147483648 | bytes 8388608 | tf_op jit(solution)/shard_map/terms/pallas_call | solution.py:305
  166.5 1.9 %collective-permute-done.41.refs_2_ = bf16[512,256]{1,0:T(8,128)(2,1)S(1)} collective-permute-done((bf16[512,256]{1,0:T(8,128)(2,1)S(1)}, bf16[512,256]{1,0:T(8,128)(2,1)S(1)}, u32[]{:S(2)}, u32[]{:S(2)}) %collective-permute-start.41) | collective-permute-done | bytes 262176 | tf_op jit(solution)/shard_map/ppermute | solution.py:392
  168.4 4.5 %collective-permute-done.40.refs_1_ = bf16[512,256]{1,0:T(8,128)(2,1)S(1)} collective-permute-done((bf16[512,256]{1,0:T(8,128)(2,1)S(1)}, bf16[512,256]{1,0:T(8,128)(2,1)S(1)}, u32[]{:S(2)}, u32[]{:S(2)}) %collective-permute-start.40) | collective-permute-done | bytes 262176 | tf_op jit(solution)/shard_map/ppermute | solution.py:381
  172.9 2.1 %update.5 = (f32[512,2,128]{2,1,0:T(2,128)}, f32[512,2,128]{2,1,0:T(2,128)}) custom-call(s32[2]{0:T(128)S(1)} %pad_add_fusion.place_ref, f32[2]{0:T(128)S(1)} %copy-done.1, f32[512,256]{1,0:T(8,128)S(1)} %terms.25.own_ref, bf16[512,256]{1,0:T(8,128)(2,1)S(1)} %collective-permute-done.39.other_ref.refs_0_, ...), custom_call_target="tpu_custom_call" | custom-call | flops 2097152 | bytes 2097152 | tf_op jit(solution)/shard_map/update/pallas_call | solution.py:368
  (74 shorter events, 13.0 us)
Async XLA Ops:
  0.7 1.0 copy-start
  1.7 32.2 %copy-start.2 = (s32[2048]{0:T(1024)S(1)}, s32[2048]{0:T(1024)}, u32[]{:S(2)}) copy-start(s32[2048]{0:T(1024)} %param.6) | copy-start | bytes 24580
  25.5 6.9 %collective-permute-start = (bf16[128,128]{1,0:T(8,128)(2,1)S(1)}, bf16[128,128]{1,0:T(8,128)(2,1)S(1)}, u32[]{:S(2)}, u32[]{:S(2)}) collective-permute-start(bf16[128,128]{1,0:T(8,128)(2,1)S(1)} %bitcast.19), channel_id=1, source_target_pairs={{0,28},{4,24},{8,20},{12,16},{16,12},{20,8},{24,4},{28,0},{1,29},{... | collective-permute-start | bytes 98312 | tf_op jit(solution)/shard_map/ppermute | solution.py:381
  28.9 5.0 %collective-permute-start.1 = (bf16[128,128]{1,0:T(8,128)(2,1)S(1)}, bf16[128,128]{1,0:T(8,128)(2,1)S(1)}, u32[]{:S(2)}, u32[]{:S(2)}) collective-permute-start(bf16[128,128]{1,0:T(8,128)(2,1)S(1)} %bitcast.18), channel_id=1, source_target_pairs={{0,24},{4,28},{8,16},{12,20},{16,8},{20,12},{24,0},{28,4},{1,25},{... | collective-permute-start | bytes 98312 | tf_op jit(solution)/shard_map/ppermute | solution.py:381
  29.5 6.4 %collective-permute-start.2 = (bf16[128,128]{1,0:T(8,128)(2,1)S(1)}, bf16[128,128]{1,0:T(8,128)(2,1)S(1)}, u32[]{:S(2)}, u32[]{:S(2)}) collective-permute-start(bf16[128,128]{1,0:T(8,128)(2,1)S(1)} %bitcast.17), channel_id=1, source_target_pairs={{0,20},{4,16},{8,28},{12,24},{16,4},{20,0},{24,12},{28,8},{1,21},{... | collective-permute-start | bytes 98312 | tf_op jit(solution)/shard_map/ppermute | solution.py:381
  30.9 5.0 %collective-permute-start.3 = (bf16[128,128]{1,0:T(8,128)(2,1)S(1)}, bf16[128,128]{1,0:T(8,128)(2,1)S(1)}, u32[]{:S(2)}, u32[]{:S(2)}) collective-permute-start(bf16[128,128]{1,0:T(8,128)(2,1)S(1)} %bitcast.16), channel_id=1, source_target_pairs={{0,16},{4,20},{8,24},{12,28},{16,0},{20,4},{24,8},{28,12},{1,17},{... | collective-permute-start | bytes 98312 | tf_op jit(solution)/shard_map/ppermute | solution.py:381
  31.2 4.7 %collective-permute-start.4 = (bf16[128,128]{1,0:T(8,128)(2,1)S(1)}, bf16[128,128]{1,0:T(8,128)(2,1)S(1)}, u32[]{:S(2)}, u32[]{:S(2)}) collective-permute-start(bf16[128,128]{1,0:T(8,128)(2,1)S(1)} %bitcast.15), channel_id=1, source_target_pairs={{0,12},{4,8},{8,4},{12,0},{16,28},{20,24},{24,20},{28,16},{1,13},{... | collective-permute-start | bytes 98312 | tf_op jit(solution)/shard_map/ppermute | solution.py:381
  32.3 3.9 %collective-permute-start.5 = (bf16[128,128]{1,0:T(8,128)(2,1)S(1)}, bf16[128,128]{1,0:T(8,128)(2,1)S(1)}, u32[]{:S(2)}, u32[]{:S(2)}) collective-permute-start(bf16[128,128]{1,0:T(8,128)(2,1)S(1)} %bitcast.14), channel_id=1, source_target_pairs={{0,8},{4,12},{8,0},{12,4},{16,24},{20,28},{24,16},{28,20},{1,9},{5... | collective-permute-start | bytes 98312 | tf_op jit(solution)/shard_map/ppermute | solution.py:381
  33.8 2.4 %collective-permute-start.6 = (bf16[128,128]{1,0:T(8,128)(2,1)S(1)}, bf16[128,128]{1,0:T(8,128)(2,1)S(1)}, u32[]{:S(2)}, u32[]{:S(2)}) collective-permute-start(bf16[128,128]{1,0:T(8,128)(2,1)S(1)} %bitcast.13), channel_id=1, source_target_pairs={{0,4},{4,0},{8,12},{12,8},{16,20},{20,16},{24,28},{28,24},{1,5},{5... | collective-permute-start | bytes 98312 | tf_op jit(solution)/shard_map/ppermute | solution.py:381
  38.6 12.1 %collective-permute-start.7 = (bf16[256,128]{1,0:T(8,128)(2,1)S(1)}, bf16[256,128]{1,0:T(8,128)(2,1)S(1)}, u32[]{:S(2)}, u32[]{:S(2)}) collective-permute-start(bf16[256,128]{1,0:T(8,128)(2,1)S(1)} %get-tuple-element.37), channel_id=1, source_target_pairs={{0,1},{1,0},{2,3},{3,2},{4,5},{5,4},{6,7},{7,6},{8,9},{9,8},{10,11... | collective-permute-start | bytes 196616 | tf_op jit(solution)/shard_map/ppermute | solution.py:381
  40.3 10.5 %collective-permute-start.8 = (bf16[256,128]{1,0:T(8,128)(2,1)S(1)}, bf16[256,128]{1,0:T(8,128)(2,1)S(1)}, u32[]{:S(2)}, u32[]{:S(2)}) collective-permute-start(bf16[256,128]{1,0:T(8,128)(2,1)S(1)} %get-tuple-element.38), channel_id=1, source_target_pairs={{0,2},{1,3},{2,0},{3,1},{4,6},{5,7},{6,4},{7,5},{8,10},{9,11},{10,... | collective-permute-start | bytes 196616 | tf_op jit(solution)/shard_map/ppermute | solution.py:381
  42.9 7.9 %collective-permute-start.9 = (bf16[256,128]{1,0:T(8,128)(2,1)S(1)}, bf16[256,128]{1,0:T(8,128)(2,1)S(1)}, u32[]{:S(2)}, u32[]{:S(2)}) collective-permute-start(bf16[256,128]{1,0:T(8,128)(2,1)S(1)} %get-tuple-element.39), channel_id=1, source_target_pairs={{0,3},{1,2},{2,1},{3,0},{4,7},{5,6},{6,5},{7,4},{8,11},{9,10},{10,... | collective-permute-start | bytes 196616 | tf_op jit(solution)/shard_map/ppermute | solution.py:381
  51.8 11.5 %collective-permute-start.10 = (bf16[512,256]{1,0:T(8,128)(2,1)S(1)}, bf16[512,256]{1,0:T(8,128)(2,1)S(1)}, u32[]{:S(2)}, u32[]{:S(2)}) collective-permute-start(bf16[512,256]{1,0:T(8,128)(2,1)S(1)} %panel.1.refs_0_.refs_4_), channel_id=1, source_target_pairs={{0,24},{4,28},{8,16},{12,20},{16,8},{20,12},{24,0},{28,4},{1,25},{... | collective-permute-start | bytes 786440 | tf_op jit(solution)/shard_map/ppermute | solution.py:381
  53.8 12.2 %collective-permute-start.11 = (bf16[512,256]{1,0:T(8,128)(2,1)S(1)}, bf16[512,256]{1,0:T(8,128)(2,1)S(1)}, u32[]{:S(2)}, u32[]{:S(2)}) collective-permute-start(bf16[512,256]{1,0:T(8,128)(2,1)S(1)} %panel.1.refs_0_.refs_4_), channel_id=1, source_target_pairs={{0,16},{4,20},{8,24},{12,28},{16,0},{20,4},{24,8},{28,12},{1,17},{... | collective-permute-start | bytes 786440 | tf_op jit(solution)/shard_map/ppermute | solution.py:381
  54.3 11.7 %collective-permute-start.12 = (bf16[512,256]{1,0:T(8,128)(2,1)S(1)}, bf16[512,256]{1,0:T(8,128)(2,1)S(1)}, u32[]{:S(2)}, u32[]{:S(2)}) collective-permute-start(bf16[512,256]{1,0:T(8,128)(2,1)S(1)} %panel.1.refs_0_.refs_4_), channel_id=1, source_target_pairs={{0,8},{4,12},{8,0},{12,4},{16,24},{20,28},{24,16},{28,20},{1,9},{5... | collective-permute-start | bytes 786440 | tf_op jit(solution)/shard_map/ppermute | solution.py:381
  55.4 11.2 %collective-permute-start.13 = (bf16[512,256]{1,0:T(8,128)(2,1)S(1)}, bf16[512,256]{1,0:T(8,128)(2,1)S(1)}, u32[]{:S(2)}, u32[]{:S(2)}) collective-permute-start(bf16[512,256]{1,0:T(8,128)(2,1)S(1)} %panel.1.refs_0_.refs_4_), channel_id=1, source_target_pairs={{0,4},{4,0},{8,12},{12,8},{16,20},{20,16},{24,28},{28,24},{1,5},{5... | collective-permute-start | bytes 786440 | tf_op jit(solution)/shard_map/ppermute | solution.py:381
  66.0 2.6 %collective-permute-start.14 = (bf16[512,256]{1,0:T(8,128)(2,1)S(1)}, bf16[512,256]{1,0:T(8,128)(2,1)S(1)}, u32[]{:S(2)}, u32[]{:S(2)}) collective-permute-start(bf16[512,256]{1,0:T(8,128)(2,1)S(1)} %collective-permute-done.10.refs_2_), channel_id=1, source_target_pairs={{0,4},{4,0},{8,12},{12,8},{16,20},{20,16},{24,28},{28,24},{1,5},{5... | collective-permute-start | bytes 786440 | tf_op jit(solution)/shard_map/ppermute | solution.py:381
  66.0 2.6 %collective-permute-start.15 = (bf16[512,256]{1,0:T(8,128)(2,1)S(1)}, bf16[512,256]{1,0:T(8,128)(2,1)S(1)}, u32[]{:S(2)}, u32[]{:S(2)}) collective-permute-start(bf16[512,256]{1,0:T(8,128)(2,1)S(1)} %collective-permute-done.11.refs_3_), channel_id=1, source_target_pairs={{0,4},{4,0},{8,12},{12,8},{16,20},{20,16},{24,28},{28,24},{1,5},{5... | collective-permute-start | bytes 786440 | tf_op jit(solution)/shard_map/ppermute | solution.py:381
  66.5 2.1 %collective-permute-start.16 = (bf16[512,256]{1,0:T(8,128)(2,1)S(1)}, bf16[512,256]{1,0:T(8,128)(2,1)S(1)}, u32[]{:S(2)}, u32[]{:S(2)}) collective-permute-start(bf16[512,256]{1,0:T(8,128)(2,1)S(1)} %collective-permute-done.12.refs_4_), channel_id=1, source_target_pairs={{0,4},{4,0},{8,12},{12,8},{16,20},{20,16},{24,28},{28,24},{1,5},{5... | collective-permute-start | bytes 786440 | tf_op jit(solution)/shard_map/ppermute | solution.py:381
  70.2 11.4 %collective-permute-start.17 = (bf16[512,256]{1,0:T(8,128)(2,1)S(1)}, bf16[512,256]{1,0:T(8,128)(2,1)S(1)}, u32[]{:S(2)}, u32[]{:S(2)}) collective-permute-start(bf16[512,256]{1,0:T(8,128)(2,1)S(1)} %terms.17), channel_id=1, source_target_pairs={{0,1},{1,3},{3,2},{2,0},{4,5},{5,7},{7,6},{6,4},{8,9},{9,11},{11,1... | collective-permute-start | bytes 786440 | tf_op jit(solution)/shard_map/ppermute | solution.py:389
  73.7 12.9 %collective-permute-start.19 = (bf16[512,256]{1,0:T(8,128)(2,1)S(1)}, bf16[512,256]{1,0:T(8,128)(2,1)S(1)}, u32[]{:S(2)}, u32[]{:S(2)}) collective-permute-start(bf16[512,256]{1,0:T(8,128)(2,1)S(1)} %get-tuple-element.46), channel_id=1, source_target_pairs={{0,3},{3,0},{4,7},{7,4},{8,11},{11,8},{12,15},{15,12},{16,19},{19,... | collective-permute-start | bytes 786440 | tf_op jit(solution)/shard_map/ppermute | solution.py:392
  81.4 10.5 %collective-permute-start.18 = (bf16[512,256]{1,0:T(8,128)(2,1)S(1)}, bf16[512,256]{1,0:T(8,128)(2,1)S(1)}, u32[]{:S(2)}, u32[]{:S(2)}) collective-permute-start(bf16[512,256]{1,0:T(8,128)(2,1)S(1)} %terms.18), channel_id=1, source_target_pairs={{0,1},{1,0},{2,3},{3,2},{4,5},{5,4},{6,7},{7,6},{8,9},{9,8},{10,11... | collective-permute-start | bytes 786440 | tf_op jit(solution)/shard_map/ppermute | solution.py:381
  81.6 10.4 %copy-start.1 = (f32[2]{0:T(128)S(1)}, f32[2]{0:T(128)}, u32[]{:S(2)}) copy-start(f32[2]{0:T(128)} %wave_ref.5) | copy-start | bytes 28
  81.6 10.3 %collective-permute-start.20 = (bf16[512,256]{1,0:T(8,128)(2,1)S(1)}, bf16[512,256]{1,0:T(8,128)(2,1)S(1)}, u32[]{:S(2)}, u32[]{:S(2)}) collective-permute-start(bf16[512,256]{1,0:T(8,128)(2,1)S(1)} %sum.3), channel_id=1, source_target_pairs={{1,2},{2,1},{5,6},{6,5},{9,10},{10,9},{13,14},{14,13},{17,18},{18,... | collective-permute-start | bytes 786440 | tf_op jit(solution)/shard_map/ppermute | solution.py:393
  92.8 10.2 %collective-permute-start.24 = (bf16[512,256]{1,0:T(8,128)(2,1)S(1)}, bf16[512,256]{1,0:T(8,128)(2,1)S(1)}, u32[]{:S(2)}, u32[]{:S(2)}) collective-permute-start(bf16[512,256]{1,0:T(8,128)(2,1)S(1)} %update.3.refs_0_), channel_id=1, source_target_pairs={{0,24},{4,28},{8,16},{12,20},{16,8},{20,12},{24,0},{28,4},{1,25},{... | collective-permute-start | bytes 786440 | tf_op jit(solution)/shard_map/ppermute | solution.py:381
  94.6 13.0 %collective-permute-start.23 = (bf16[512,256]{1,0:T(8,128)(2,1)S(1)}, bf16[512,256]{1,0:T(8,128)(2,1)S(1)}, u32[]{:S(2)}, u32[]{:S(2)}) collective-permute-start(bf16[512,256]{1,0:T(8,128)(2,1)S(1)} %update.3.refs_0_), channel_id=1, source_target_pairs={{0,16},{4,20},{8,24},{12,28},{16,0},{20,4},{24,8},{28,12},{1,17},{... | collective-permute-start | bytes 786440 | tf_op jit(solution)/shard_map/ppermute | solution.py:381
  95.3 12.3 %collective-permute-start.22 = (bf16[512,256]{1,0:T(8,128)(2,1)S(1)}, bf16[512,256]{1,0:T(8,128)(2,1)S(1)}, u32[]{:S(2)}, u32[]{:S(2)}) collective-permute-start(bf16[512,256]{1,0:T(8,128)(2,1)S(1)} %update.3.refs_0_), channel_id=1, source_target_pairs={{0,8},{4,12},{8,0},{12,4},{16,24},{20,28},{24,16},{28,20},{1,9},{5... | collective-permute-start | bytes 786440 | tf_op jit(solution)/shard_map/ppermute | solution.py:381
  96.3 11.8 %collective-permute-start.21 = (bf16[512,256]{1,0:T(8,128)(2,1)S(1)}, bf16[512,256]{1,0:T(8,128)(2,1)S(1)}, u32[]{:S(2)}, u32[]{:S(2)}) collective-permute-start(bf16[512,256]{1,0:T(8,128)(2,1)S(1)} %update.3.refs_0_), channel_id=1, source_target_pairs={{0,4},{4,0},{8,12},{12,8},{16,20},{20,16},{24,28},{28,24},{1,5},{5... | collective-permute-start | bytes 786440 | tf_op jit(solution)/shard_map/ppermute | solution.py:381
  103.0 7.3 %collective-permute-start.25 = (bf16[512,256]{1,0:T(8,128)(2,1)S(1)}, bf16[512,256]{1,0:T(8,128)(2,1)S(1)}, u32[]{:S(2)}, u32[]{:S(2)}) collective-permute-start(bf16[512,256]{1,0:T(8,128)(2,1)S(1)} %collective-permute-done.24.refs_4_), channel_id=1, source_target_pairs={{0,4},{4,0},{8,12},{12,8},{16,20},{20,16},{24,28},{28,24},{1,5},{5... | collective-permute-start | bytes 786440 | tf_op jit(solution)/shard_map/ppermute | solution.py:381
  107.6 2.6 %collective-permute-start.26 = (bf16[512,256]{1,0:T(8,128)(2,1)S(1)}, bf16[512,256]{1,0:T(8,128)(2,1)S(1)}, u32[]{:S(2)}, u32[]{:S(2)}) collective-permute-start(bf16[512,256]{1,0:T(8,128)(2,1)S(1)} %collective-permute-done.23.refs_3_), channel_id=1, source_target_pairs={{0,4},{4,0},{8,12},{12,8},{16,20},{20,16},{24,28},{28,24},{1,5},{5... | collective-permute-start | bytes 786440 | tf_op jit(solution)/shard_map/ppermute | solution.py:381
  107.6 2.6 %collective-permute-start.27 = (bf16[512,256]{1,0:T(8,128)(2,1)S(1)}, bf16[512,256]{1,0:T(8,128)(2,1)S(1)}, u32[]{:S(2)}, u32[]{:S(2)}) collective-permute-start(bf16[512,256]{1,0:T(8,128)(2,1)S(1)} %collective-permute-done.22.refs_2_), channel_id=1, source_target_pairs={{0,4},{4,0},{8,12},{12,8},{16,20},{20,16},{24,28},{28,24},{1,5},{5... | collective-permute-start | bytes 786440 | tf_op jit(solution)/shard_map/ppermute | solution.py:381
  111.8 10.8 %collective-permute-start.28 = (bf16[512,256]{1,0:T(8,128)(2,1)S(1)}, bf16[512,256]{1,0:T(8,128)(2,1)S(1)}, u32[]{:S(2)}, u32[]{:S(2)}) collective-permute-start(bf16[512,256]{1,0:T(8,128)(2,1)S(1)} %terms.22), channel_id=1, source_target_pairs={{0,1},{1,3},{3,2},{2,0},{4,5},{5,7},{7,6},{6,4},{8,9},{9,11},{11,1... | collective-permute-start | bytes 786440 | tf_op jit(solution)/shard_map/ppermute | solution.py:389
  115.4 12.9 %collective-permute-start.30 = (bf16[512,256]{1,0:T(8,128)(2,1)S(1)}, bf16[512,256]{1,0:T(8,128)(2,1)S(1)}, u32[]{:S(2)}, u32[]{:S(2)}) collective-permute-start(bf16[512,256]{1,0:T(8,128)(2,1)S(1)} %get-tuple-element.48), channel_id=1, source_target_pairs={{0,3},{3,0},{4,7},{7,4},{8,11},{11,8},{12,15},{15,12},{16,19},{19,... | collective-permute-start | bytes 786440 | tf_op jit(solution)/shard_map/ppermute | solution.py:392
  122.5 10.2 %collective-permute-start.29 = (bf16[512,256]{1,0:T(8,128)(2,1)S(1)}, bf16[512,256]{1,0:T(8,128)(2,1)S(1)}, u32[]{:S(2)}, u32[]{:S(2)}) collective-permute-start(bf16[512,256]{1,0:T(8,128)(2,1)S(1)} %terms.23), channel_id=1, source_target_pairs={{0,1},{1,0},{2,3},{3,2},{4,5},{5,4},{6,7},{7,6},{8,9},{9,8},{10,11... | collective-permute-start | bytes 786440 | tf_op jit(solution)/shard_map/ppermute | solution.py:381
  122.7 10.0 %collective-permute-start.31 = (bf16[512,256]{1,0:T(8,128)(2,1)S(1)}, bf16[512,256]{1,0:T(8,128)(2,1)S(1)}, u32[]{:S(2)}, u32[]{:S(2)}) collective-permute-start(bf16[512,256]{1,0:T(8,128)(2,1)S(1)} %sum.4), channel_id=1, source_target_pairs={{1,2},{2,1},{5,6},{6,5},{9,10},{10,9},{13,14},{14,13},{17,18},{18,... | collective-permute-start | bytes 786440 | tf_op jit(solution)/shard_map/ppermute | solution.py:393
  133.5 10.2 %collective-permute-start.35 = (bf16[512,256]{1,0:T(8,128)(2,1)S(1)}, bf16[512,256]{1,0:T(8,128)(2,1)S(1)}, u32[]{:S(2)}, u32[]{:S(2)}) collective-permute-start(bf16[512,256]{1,0:T(8,128)(2,1)S(1)} %update.4.refs_0_), channel_id=1, source_target_pairs={{0,24},{4,28},{8,16},{12,20},{16,8},{20,12},{24,0},{28,4},{1,25},{... | collective-permute-start | bytes 786440 | tf_op jit(solution)/shard_map/ppermute | solution.py:381
  135.3 12.9 %collective-permute-start.34 = (bf16[512,256]{1,0:T(8,128)(2,1)S(1)}, bf16[512,256]{1,0:T(8,128)(2,1)S(1)}, u32[]{:S(2)}, u32[]{:S(2)}) collective-permute-start(bf16[512,256]{1,0:T(8,128)(2,1)S(1)} %update.4.refs_0_), channel_id=1, source_target_pairs={{0,16},{4,20},{8,24},{12,28},{16,0},{20,4},{24,8},{28,12},{1,17},{... | collective-permute-start | bytes 786440 | tf_op jit(solution)/shard_map/ppermute | solution.py:381
  136.1 12.2 %collective-permute-start.33 = (bf16[512,256]{1,0:T(8,128)(2,1)S(1)}, bf16[512,256]{1,0:T(8,128)(2,1)S(1)}, u32[]{:S(2)}, u32[]{:S(2)}) collective-permute-start(bf16[512,256]{1,0:T(8,128)(2,1)S(1)} %update.4.refs_0_), channel_id=1, source_target_pairs={{0,8},{4,12},{8,0},{12,4},{16,24},{20,28},{24,16},{28,20},{1,9},{5... | collective-permute-start | bytes 786440 | tf_op jit(solution)/shard_map/ppermute | solution.py:381
  137.1 11.7 %collective-permute-start.32 = (bf16[512,256]{1,0:T(8,128)(2,1)S(1)}, bf16[512,256]{1,0:T(8,128)(2,1)S(1)}, u32[]{:S(2)}, u32[]{:S(2)}) collective-permute-start(bf16[512,256]{1,0:T(8,128)(2,1)S(1)} %update.4.refs_0_), channel_id=1, source_target_pairs={{0,4},{4,0},{8,12},{12,8},{16,20},{20,16},{24,28},{28,24},{1,5},{5... | collective-permute-start | bytes 786440 | tf_op jit(solution)/shard_map/ppermute | solution.py:381
  143.7 7.1 %collective-permute-start.36 = (bf16[512,256]{1,0:T(8,128)(2,1)S(1)}, bf16[512,256]{1,0:T(8,128)(2,1)S(1)}, u32[]{:S(2)}, u32[]{:S(2)}) collective-permute-start(bf16[512,256]{1,0:T(8,128)(2,1)S(1)} %collective-permute-done.35.refs_4_), channel_id=1, source_target_pairs={{0,4},{4,0},{8,12},{12,8},{16,20},{20,16},{24,28},{28,24},{1,5},{5... | collective-permute-start | bytes 786440 | tf_op jit(solution)/shard_map/ppermute | solution.py:381
  148.2 2.6 %collective-permute-start.37 = (bf16[512,256]{1,0:T(8,128)(2,1)S(1)}, bf16[512,256]{1,0:T(8,128)(2,1)S(1)}, u32[]{:S(2)}, u32[]{:S(2)}) collective-permute-start(bf16[512,256]{1,0:T(8,128)(2,1)S(1)} %collective-permute-done.34.refs_3_), channel_id=1, source_target_pairs={{0,4},{4,0},{8,12},{12,8},{16,20},{20,16},{24,28},{28,24},{1,5},{5... | collective-permute-start | bytes 786440 | tf_op jit(solution)/shard_map/ppermute | solution.py:381
  148.3 2.6 %collective-permute-start.38 = (bf16[512,256]{1,0:T(8,128)(2,1)S(1)}, bf16[512,256]{1,0:T(8,128)(2,1)S(1)}, u32[]{:S(2)}, u32[]{:S(2)}) collective-permute-start(bf16[512,256]{1,0:T(8,128)(2,1)S(1)} %collective-permute-done.33.refs_2_), channel_id=1, source_target_pairs={{0,4},{4,0},{8,12},{12,8},{16,20},{20,16},{24,28},{28,24},{1,5},{5... | collective-permute-start | bytes 786440 | tf_op jit(solution)/shard_map/ppermute | solution.py:381
  152.4 10.5 %collective-permute-start.39 = (bf16[512,256]{1,0:T(8,128)(2,1)S(1)}, bf16[512,256]{1,0:T(8,128)(2,1)S(1)}, u32[]{:S(2)}, u32[]{:S(2)}) collective-permute-start(bf16[512,256]{1,0:T(8,128)(2,1)S(1)} %terms.27), channel_id=1, source_target_pairs={{0,1},{1,3},{3,2},{2,0},{4,5},{5,7},{7,6},{6,4},{8,9},{9,11},{11,1... | collective-permute-start | bytes 786440 | tf_op jit(solution)/shard_map/ppermute | solution.py:389
  155.5 12.9 %collective-permute-start.41 = (bf16[512,256]{1,0:T(8,128)(2,1)S(1)}, bf16[512,256]{1,0:T(8,128)(2,1)S(1)}, u32[]{:S(2)}, u32[]{:S(2)}) collective-permute-start(bf16[512,256]{1,0:T(8,128)(2,1)S(1)} %get-tuple-element.50), channel_id=1, source_target_pairs={{0,3},{3,0},{4,7},{7,4},{8,11},{11,8},{12,15},{15,12},{16,19},{19,... | collective-permute-start | bytes 786440 | tf_op jit(solution)/shard_map/ppermute | solution.py:392
  162.8 10.1 %collective-permute-start.40 = (bf16[512,256]{1,0:T(8,128)(2,1)S(1)}, bf16[512,256]{1,0:T(8,128)(2,1)S(1)}, u32[]{:S(2)}, u32[]{:S(2)}) collective-permute-start(bf16[512,256]{1,0:T(8,128)(2,1)S(1)} %terms.28), channel_id=1, source_target_pairs={{0,1},{1,0},{2,3},{3,2},{4,5},{5,4},{6,7},{7,6},{8,9},{9,8},{10,11... | collective-permute-start | bytes 786440 | tf_op jit(solution)/shard_map/ppermute | solution.py:381
  163.0 9.9 %collective-permute-start.42 = (bf16[512,256]{1,0:T(8,128)(2,1)S(1)}, bf16[512,256]{1,0:T(8,128)(2,1)S(1)}, u32[]{:S(2)}, u32[]{:S(2)}) collective-permute-start(bf16[512,256]{1,0:T(8,128)(2,1)S(1)} %sum.5), channel_id=1, source_target_pairs={{1,2},{2,1},{5,6},{6,5},{9,10},{10,9},{13,14},{14,13},{17,18},{18,... | collective-permute-start | bytes 786440 | tf_op jit(solution)/shard_map/ppermute | solution.py:393

commit v9 on v8

--- a/solution.py
+++ b/solution.py
@@ -13,6 +13,7 @@
 ITERS = 3
 LANES = 128
 BUFFERS = 4
+SPARE_ROWS = 2**14
 VMEM = pl.BlockSpec(memory_space=pltpu.VMEM)
 ANY = pl.BlockSpec(memory_space=pl.ANY)
 SMEM = pl.BlockSpec(memory_space=pltpu.SMEM)
@@ -85,7 +86,7 @@
                 out_ref[step % steps] = packed
 
     def ready():
-        copy = pltpu.make_async_copy(table_ref, wide, table_sem)
+        copy = pltpu.make_async_copy(table_ref.at[pl.ds(0, wide.shape[0])], wide, table_sem)
         copy.start()
         copy.wait()
         table[...] = wide[...].astype(table.dtype)
@@ -115,7 +116,7 @@
     steps = block_rows // n_row // block
     short = block // packs
     columns = np.tile(np.repeat(dft_table(samples), shots, axis=1), (1, packs))
-    table = jnp.asarray(columns.astype(np.float32))
+    table = jnp.asarray(np.pad(columns.astype(np.float32), ((0, SPARE_ROWS), (0, 0))))
 
     outs = pl.pallas_call(
         functools.partial(spectra_kernel, packs, n_row),
@@ -125,11 +126,11 @@
         scratch_shapes=[
             pltpu.VMEM((BUFFERS + 2, block, shots, samples), jnp.bfloat16),
             pltpu.SemaphoreType.DMA((BUFFERS + 2,)),
-            pltpu.VMEM(table.shape, jnp.float32),
-            pltpu.VMEM(table.shape, jnp.bfloat16),
+            pltpu.VMEM(columns.shape, jnp.float32),
+            pltpu.VMEM(columns.shape, jnp.bfloat16),
             pltpu.SemaphoreType.DMA,
         ],
-        compiler_params=params(48),
+        compiler_params=params(50),
         cost_estimate=cost(2 * traces.size * LANES, 2 * traces.size),
         name="spectra",
     )(place, traces, table)
@@ -210,7 +211,7 @@
     lane = lax.broadcasted_iota(jnp.int32, (LANES, packs * columns), 0)
     target = lax.broadcasted_iota(jnp.int32, (LANES, packs * columns), 1)
     total = None
-    for turn, piece in enumerate(pieces):
+    for turn, piece in enumerate(reversed(pieces)):
         shot = (place_ref[1] ^ turn) * shots + lane % shots
         goes = lane // width * columns + lane % width // shots * (columns // 2) + shot
         chosen = jnp.where(target == goes, 1.0, 0.0).astype(jnp.bfloat16)
@@ -434,7 +435,7 @@
     real_data, _ = relay(slice_data, 0, spectra[0])
     hits = make_hits(code, block_rows // packs, packs, spectra[0])
     ordered = make_order(code, hits, arrived, place, n_src, packs)
-    located = [ordered[0]] + [swap(ordered[turn], "src", turn) for turn in range(1, n_src)]
+    located = [swap(ordered[turn], "src", turn) for turn in range(n_src - 1, 0, -1)] + [ordered[0]]
     imag_data, token = relay(slice_data, 1, ordered[0])
     panel = make_panel(located, place, packs, token)
 

time: 175 us -> 179 us (1.023)
  Pallas kernels: 85 us -> 89.9 us
    pallas_call x1, Pallas kernels: 23.8 us -> 28.6 us  [make_spectra(): pl.pallas_call(functools.partial(spectra_kernel, packs, n_row), in_specs=...]
where the time goes in v9:
time: 179 us
  Pallas kernels  89.9 us (50%)
  waiting for transfers between devices  46.1 us (26%)
  starting transfers between devices  41.3 us (23%)
    ppermute x34, waiting for transfers between devices, swap(): lax.ppermute(array, axis, [(index, index ^ bits) for index in range(size)])  40.4 us
    pallas_call x15, Pallas kernels, make_terms(): pl.pallas_call(functools.partial(terms_kernel, turns, numbers, len(partia...  36.6 us
    pallas_call x1, Pallas kernels, make_spectra(): pl.pallas_call(functools.partial(spectra_kernel, packs, n_row), in_specs=...  28.6 us
    ppermute x34, starting transfers between devices, swap(): lax.ppermute(array, axis, [(index, index ^ bits) for index in range(size)])  24.5 us
    pallas_call x2, Pallas kernels, relay(): pl.pallas_call(functools.partial(relay_kernel, part), in_specs=[ANY, ANY]...  15.7 us
    ppermute x3, starting transfers between devices, exchange(): outer = lax.ppermute(sent, 'src', [(0, 3), (3, 0)])  12.8 us
    ppermute x3, waiting for transfers between devices, exchange(): outer = lax.ppermute(sent, 'src', [(0, 3), (3, 0)])  5.73 us
    pallas_call x3, Pallas kernels, make_update(): pl.pallas_call(functools.partial(last_kernel if last else estimate_kernel...  3.77 us
  transfers between devices with their start and end apart: 43, of which 13 were waited for; matrix products, arithmetic and copies ran while one was open for 0% of the time, Pallas kernels for 28%

profile of v9, /device:TPU:0, one launch (start us, length us, event | category | flops | bytes accessed | tf_op | source)
XLA Modules:
  0.0 178.8 jit_solution(16422999910089695988)
XLA Ops:
  0.7 28.6 %spectra.1 = (bf16[2,64,128]{2,1,0:T(8,128)(2,1)S(1)}, bf16[2,64,128]{2,1,0:T(8,128)(2,1)S(1)}, bf16[2,64,128]{2,1,0:T(8,128)(2,1)S(1)}, bf16[2,64,128]{2,1,0:T(...) custom-call(s32[2]{0:T(128)S(1)} %pad_add_fusion.place_ref, ...), custom_call_target="tpu_custom_call" | custom-call | flops 8589934592 | bytes 67108864 | tf_op jit(solution)/shard_map/spectra/pallas_call | solution.py:121
  29.4 3.4 %collective-permute-start = (bf16[128,128]{1,0:T(8,128)(2,1)S(1)}, bf16[128,128]{1,0:T(8,128)(2,1)S(1)}, u32[]{:S(2)}, u32[]{:S(2)}) collective-permute-start(bf16[128,128]{1,0:T(8,128)(2,1)S(1)} %bitcast.19), channel_id=1, source_target_pairs={{0,28},{4,24},{8,20},{12,16},{16,12},{20,8},{24,4},{28,0},{1,29},{... | collective-permute-start | bytes 98312 | tf_op jit(solution)/shard_map/ppermute | solution.py:382
  33.4 1.4 collective-permute-start.2
  35.1 1.1 collective-permute-start.4
  38.1 1.7 hits.1.hits_ref
  40.2 2.4 %order.1 = (bf16[256,128]{1,0:T(8,128)(2,1)S(1)}, bf16[256,128]{1,0:T(8,128)(2,1)S(1)}, bf16[256,128]{1,0:T(8,128)(2,1)S(1)}, bf16[256,128]{1,0:T(8,128)(2,1)S(1)}) custom-call(s32[2]{0:T(128)S(1)} %pad_add_fusion.place_ref, s32[2048,128]{1,0:T(8,128)S(1)} %broadcast_in_dim.2.code_ref, bf16[2048,1024]{1,0:T(8,128)(2,1)S(1)} %hits.1.hits_ref, ...), custom_call_target="tpu_custom_call" | custom-call | flops 1073741824 | bytes 1048576 | tf_op jit(solution)/shard_map/order/pallas_call | solution.py:194
  42.6 3.7 %collective-permute-start.7 = (bf16[256,128]{1,0:T(8,128)(2,1)S(1)}, bf16[256,128]{1,0:T(8,128)(2,1)S(1)}, u32[]{:S(2)}, u32[]{:S(2)}) collective-permute-start(bf16[256,128]{1,0:T(8,128)(2,1)S(1)} %get-tuple-element.36), channel_id=1, source_target_pairs={{0,3},{1,2},{2,1},{3,0},{4,7},{5,6},{6,5},{7,4},{8,11},{9,10},{10,... | collective-permute-start | bytes 196616 | tf_op jit(solution)/shard_map/ppermute | solution.py:382
  47.0 7.7 %relay.3 = (bf16[8,2048,512]{2,1,0:T(8,128)(2,1)S(1)}, f32[8,128]{1,0:T(8,128)S(1)}) custom-call(bf16[2,2048,8,512]{3,2,1,0:T(8,128)(2,1)} %data_ref.3, bf16[256,128]{1,0:T(8,128)(2,1)S(1)} %get-tuple-element.39.after_ref.refs_3_), custom_call_target="tpu_custom_call" | custom-call | bytes 33554432 | tf_op jit(solution)/shard_map/relay/pallas_call | solution.py:257
  54.7 1.0 panel.1.refs_0_.refs_4_
  55.7 2.0 %collective-permute-start.10 = (bf16[512,256]{1,0:T(8,128)(2,1)S(1)}, bf16[512,256]{1,0:T(8,128)(2,1)S(1)}, u32[]{:S(2)}, u32[]{:S(2)}) collective-permute-start(bf16[512,256]{1,0:T(8,128)(2,1)S(1)} %panel.1.refs_0_.refs_4_), channel_id=1, source_target_pairs={{0,24},{4,28},{8,16},{12,20},{16,8},{20,12},{24,0},{28,4},{1,25},{... | collective-permute-start | bytes 786440 | tf_op jit(solution)/shard_map/ppermute | solution.py:382
  58.2 1.1 collective-permute-start.12
  59.3 8.0 %relay.2 = (bf16[8,2048,512]{2,1,0:T(8,128)(2,1)S(1)}, f32[8,128]{1,0:T(8,128)}) custom-call(bf16[2,2048,8,512]{3,2,1,0:T(8,128)(2,1)} %data_ref.3, bf16[128,128]{1,0:T(8,128)(2,1)S(1)} %bitcast.12), custom_call_target="tpu_custom_call" | custom-call | bytes 33554432 | tf_op jit(solution)/shard_map/relay/pallas_call | solution.py:257
  67.3 2.7 %collective-permute-done.11.refs_3_ = bf16[512,256]{1,0:T(8,128)(2,1)S(1)} collective-permute-done((bf16[512,256]{1,0:T(8,128)(2,1)S(1)}, bf16[512,256]{1,0:T(8,128)(2,1)S(1)}, u32[]{:S(2)}, u32[]{:S(2)}) %collective-permute-start.11) | collective-permute-done | bytes 262176 | tf_op jit(solution)/shard_map/ppermute | solution.py:382
  70.5 2.1 %terms.16.refs_3_ = f32[512,256]{1,0:T(8,128)S(1)} custom-call(s32[2]{0:T(128)S(1)} %pad_add_fusion.place_ref, bf16[8,2048,512]{2,1,0:T(8,128)(2,1)S(1)} %get-tuple-element.41.real_ref, bf16[8,2048,512]{2,1,0:T(8,128)(2,1)S(1)} %get-tuple-element.42.imag_ref, bf16[512,256]{1,0:T(8,128)(2,1)S(1)} %panel.1.refs_0_.refs_4_, ...), custom_call_target="tpu_custom_call" | custom-call | flops 1342177280 | bytes 5242880 | tf_op jit(solution)/shard_map/terms/pallas_call | solution.py:306
  72.6 1.5 terms.17
  74.1 1.4 collective-permute-start.17
  75.5 2.9 %terms.19 = (bf16[512,256]{1,0:T(8,128)(2,1)S(1)}, f32[512,256]{1,0:T(8,128)S(1)}) custom-call(s32[2]{0:T(128)S(1)} %pad_add_fusion.place_ref, bf16[8,2048,512]{2,1,0:T(8,128)(2,1)S(1)} %get-tuple-element.41.real_ref, bf16[8,2048,512]{2,1,0:T(8,128)(2,1)S(1)} %get-tuple-element.42.imag_ref, bf16[512,256]{1,0:T(8,128)(2,1)S(1)} %panel.1.refs_0_.refs_4_, ...), custom_call_target="tpu_custom_call" | custom-call | flops 2147483648 | bytes 8388608 | tf_op jit(solution)/shard_map/terms/pallas_call | solution.py:306
  78.4 4.3 %collective-permute-start.19 = (bf16[512,256]{1,0:T(8,128)(2,1)S(1)}, bf16[512,256]{1,0:T(8,128)(2,1)S(1)}, u32[]{:S(2)}, u32[]{:S(2)}) collective-permute-start(bf16[512,256]{1,0:T(8,128)(2,1)S(1)} %get-tuple-element.46), channel_id=1, source_target_pairs={{0,3},{3,0},{4,7},{7,4},{8,11},{11,8},{12,15},{15,12},{16,19},{19,... | collective-permute-start | bytes 786440 | tf_op jit(solution)/shard_map/ppermute | solution.py:393
  82.7 2.9 %terms.18 = bf16[512,256]{1,0:T(8,128)(2,1)S(1)} custom-call(s32[2]{0:T(128)S(1)} %pad_add_fusion.place_ref, bf16[8,2048,512]{2,1,0:T(8,128)(2,1)S(1)} %get-tuple-element.41.real_ref, bf16[8,2048,512]{2,1,0:T(8,128)(2,1)S(1)} %get-tuple-element.42.imag_ref, bf16[512,256]{1,0:T(8,128)(2,1)S(1)} %panel.1.refs_0_.refs_4_, ...), custom_call_target="tpu_custom_call" | custom-call | flops 2147483648 | bytes 8388608 | tf_op jit(solution)/shard_map/terms/pallas_call | solution.py:306
  85.7 0.9 collective-permute-start.20
  86.6 2.9 %terms.15.own_ref = f32[512,256]{1,0:T(8,128)S(1)} custom-call(s32[2]{0:T(128)S(1)} %pad_add_fusion.place_ref, bf16[8,2048,512]{2,1,0:T(8,128)(2,1)S(1)} %get-tuple-element.41.real_ref, bf16[8,2048,512]{2,1,0:T(8,128)(2,1)S(1)} %get-tuple-element.42.imag_ref, bf16[512,256]{1,0:T(8,128)(2,1)S(1)} %panel.1.refs_0_.refs_4_, ...), custom_call_target="tpu_custom_call" | custom-call | flops 2147483648 | bytes 8388608 | tf_op jit(solution)/shard_map/terms/pallas_call | solution.py:306
  89.5 1.8 collective-permute-done.19.refs_2_
  91.2 4.9 %collective-permute-done.18.refs_1_ = bf16[512,256]{1,0:T(8,128)(2,1)S(1)} collective-permute-done((bf16[512,256]{1,0:T(8,128)(2,1)S(1)}, bf16[512,256]{1,0:T(8,128)(2,1)S(1)}, u32[]{:S(2)}, u32[]{:S(2)}) %collective-permute-start.18) | collective-permute-done | bytes 262176 | tf_op jit(solution)/shard_map/ppermute | solution.py:382
  97.0 1.8 %collective-permute-start.24 = (bf16[512,256]{1,0:T(8,128)(2,1)S(1)}, bf16[512,256]{1,0:T(8,128)(2,1)S(1)}, u32[]{:S(2)}, u32[]{:S(2)}) collective-permute-start(bf16[512,256]{1,0:T(8,128)(2,1)S(1)} %update.3.refs_0_), channel_id=1, source_target_pairs={{0,24},{4,28},{8,16},{12,20},{16,8},{20,12},{24,0},{28,4},{1,25},{... | collective-permute-start | bytes 786440 | tf_op jit(solution)/shard_map/ppermute | solution.py:382
  99.5 1.1 collective-permute-start.22
  100.5 6.6 %collective-permute-done.24.refs_4_ = bf16[512,256]{1,0:T(8,128)(2,1)S(1)} collective-permute-done((bf16[512,256]{1,0:T(8,128)(2,1)S(1)}, bf16[512,256]{1,0:T(8,128)(2,1)S(1)}, u32[]{:S(2)}, u32[]{:S(2)}) %collective-permute-start.24) | collective-permute-done | bytes 262176 | tf_op jit(solution)/shard_map/ppermute | solution.py:382
  107.1 4.6 %collective-permute-done.23.refs_3_ = bf16[512,256]{1,0:T(8,128)(2,1)S(1)} collective-permute-done((bf16[512,256]{1,0:T(8,128)(2,1)S(1)}, bf16[512,256]{1,0:T(8,128)(2,1)S(1)}, u32[]{:S(2)}, u32[]{:S(2)}) %collective-permute-start.23) | collective-permute-done | bytes 262176 | tf_op jit(solution)/shard_map/ppermute | solution.py:382
  112.3 2.1 %terms.21.refs_3_ = f32[512,256]{1,0:T(8,128)S(1)} custom-call(s32[2]{0:T(128)S(1)} %pad_add_fusion.place_ref, bf16[8,2048,512]{2,1,0:T(8,128)(2,1)S(1)} %get-tuple-element.41.real_ref, bf16[8,2048,512]{2,1,0:T(8,128)(2,1)S(1)} %get-tuple-element.42.imag_ref, bf16[512,256]{1,0:T(8,128)(2,1)S(1)} %update.3.refs_0_, ...), custom_call_target="tpu_custom_call" | custom-call | flops 1342177280 | bytes 5242880 | tf_op jit(solution)/shard_map/terms/pallas_call | solution.py:306
  114.4 1.5 terms.22
  116.1 2.9 %terms.24 = (bf16[512,256]{1,0:T(8,128)(2,1)S(1)}, f32[512,256]{1,0:T(8,128)S(1)}) custom-call(s32[2]{0:T(128)S(1)} %pad_add_fusion.place_ref, bf16[8,2048,512]{2,1,0:T(8,128)(2,1)S(1)} %get-tuple-element.41.real_ref, bf16[8,2048,512]{2,1,0:T(8,128)(2,1)S(1)} %get-tuple-element.42.imag_ref, bf16[512,256]{1,0:T(8,128)(2,1)S(1)} %update.3.refs_0_, ...), custom_call_target="tpu_custom_call" | custom-call | flops 2147483648 | bytes 8388608 | tf_op jit(solution)/shard_map/terms/pallas_call | solution.py:306
  119.0 4.2 %collective-permute-start.30 = (bf16[512,256]{1,0:T(8,128)(2,1)S(1)}, bf16[512,256]{1,0:T(8,128)(2,1)S(1)}, u32[]{:S(2)}, u32[]{:S(2)}) collective-permute-start(bf16[512,256]{1,0:T(8,128)(2,1)S(1)} %get-tuple-element.48), channel_id=1, source_target_pairs={{0,3},{3,0},{4,7},{7,4},{8,11},{11,8},{12,15},{15,12},{16,19},{19,... | collective-permute-start | bytes 786440 | tf_op jit(solution)/shard_map/ppermute | solution.py:393
  123.2 2.9 %terms.23 = bf16[512,256]{1,0:T(8,128)(2,1)S(1)} custom-call(s32[2]{0:T(128)S(1)} %pad_add_fusion.place_ref, bf16[8,2048,512]{2,1,0:T(8,128)(2,1)S(1)} %get-tuple-element.41.real_ref, bf16[8,2048,512]{2,1,0:T(8,128)(2,1)S(1)} %get-tuple-element.42.imag_ref, bf16[512,256]{1,0:T(8,128)(2,1)S(1)} %update.3.refs_0_, ...), custom_call_target="tpu_custom_call" | custom-call | flops 2147483648 | bytes 8388608 | tf_op jit(solution)/shard_map/terms/pallas_call | solution.py:306
  126.9 2.9 %terms.20.own_ref = f32[512,256]{1,0:T(8,128)S(1)} custom-call(s32[2]{0:T(128)S(1)} %pad_add_fusion.place_ref, bf16[8,2048,512]{2,1,0:T(8,128)(2,1)S(1)} %get-tuple-element.41.real_ref, bf16[8,2048,512]{2,1,0:T(8,128)(2,1)S(1)} %get-tuple-element.42.imag_ref, bf16[512,256]{1,0:T(8,128)(2,1)S(1)} %update.3.refs_0_, ...), custom_call_target="tpu_custom_call" | custom-call | flops 2147483648 | bytes 8388608 | tf_op jit(solution)/shard_map/terms/pallas_call | solution.py:306
  129.8 2.1 %collective-permute-done.30.refs_2_ = bf16[512,256]{1,0:T(8,128)(2,1)S(1)} collective-permute-done((bf16[512,256]{1,0:T(8,128)(2,1)S(1)}, bf16[512,256]{1,0:T(8,128)(2,1)S(1)}, u32[]{:S(2)}, u32[]{:S(2)}) %collective-permute-start.30) | collective-permute-done | bytes 262176 | tf_op jit(solution)/shard_map/ppermute | solution.py:393
  131.9 4.6 %collective-permute-done.29.refs_1_ = bf16[512,256]{1,0:T(8,128)(2,1)S(1)} collective-permute-done((bf16[512,256]{1,0:T(8,128)(2,1)S(1)}, bf16[512,256]{1,0:T(8,128)(2,1)S(1)}, u32[]{:S(2)}, u32[]{:S(2)}) %collective-permute-start.29) | collective-permute-done | bytes 262176 | tf_op jit(solution)/shard_map/ppermute | solution.py:382
  137.3 1.8 %collective-permute-start.35 = (bf16[512,256]{1,0:T(8,128)(2,1)S(1)}, bf16[512,256]{1,0:T(8,128)(2,1)S(1)}, u32[]{:S(2)}, u32[]{:S(2)}) collective-permute-start(bf16[512,256]{1,0:T(8,128)(2,1)S(1)} %update.4.refs_0_), channel_id=1, source_target_pairs={{0,24},{4,28},{8,16},{12,20},{16,8},{20,12},{24,0},{28,4},{1,25},{... | collective-permute-start | bytes 786440 | tf_op jit(solution)/shard_map/ppermute | solution.py:382
  139.8 1.1 collective-permute-start.33
  140.8 6.6 %collective-permute-done.35.refs_4_ = bf16[512,256]{1,0:T(8,128)(2,1)S(1)} collective-permute-done((bf16[512,256]{1,0:T(8,128)(2,1)S(1)}, bf16[512,256]{1,0:T(8,128)(2,1)S(1)}, u32[]{:S(2)}, u32[]{:S(2)}) %collective-permute-start.35) | collective-permute-done | bytes 262176 | tf_op jit(solution)/shard_map/ppermute | solution.py:382
  147.4 4.6 %collective-permute-done.34.refs_3_ = bf16[512,256]{1,0:T(8,128)(2,1)S(1)} collective-permute-done((bf16[512,256]{1,0:T(8,128)(2,1)S(1)}, bf16[512,256]{1,0:T(8,128)(2,1)S(1)}, u32[]{:S(2)}, u32[]{:S(2)}) %collective-permute-start.34) | collective-permute-done | bytes 262176 | tf_op jit(solution)/shard_map/ppermute | solution.py:382
  152.6 2.1 %terms.26.refs_3_ = f32[512,256]{1,0:T(8,128)S(1)} custom-call(s32[2]{0:T(128)S(1)} %pad_add_fusion.place_ref, bf16[8,2048,512]{2,1,0:T(8,128)(2,1)S(1)} %get-tuple-element.41.real_ref, bf16[8,2048,512]{2,1,0:T(8,128)(2,1)S(1)} %get-tuple-element.42.imag_ref, bf16[512,256]{1,0:T(8,128)(2,1)S(1)} %update.4.refs_0_, ...), custom_call_target="tpu_custom_call" | custom-call | flops 1342177280 | bytes 5242880 | tf_op jit(solution)/shard_map/terms/pallas_call | solution.py:306
  154.7 1.5 terms.27
  156.4 2.9 %terms.29 = (bf16[512,256]{1,0:T(8,128)(2,1)S(1)}, f32[512,256]{1,0:T(8,128)S(1)}) custom-call(s32[2]{0:T(128)S(1)} %pad_add_fusion.place_ref, bf16[8,2048,512]{2,1,0:T(8,128)(2,1)S(1)} %get-tuple-element.41.real_ref, bf16[8,2048,512]{2,1,0:T(8,128)(2,1)S(1)} %get-tuple-element.42.imag_ref, bf16[512,256]{1,0:T(8,128)(2,1)S(1)} %update.4.refs_0_, ...), custom_call_target="tpu_custom_call" | custom-call | flops 2147483648 | bytes 8388608 | tf_op jit(solution)/shard_map/terms/pallas_call | solution.py:306
  159.3 4.4 %collective-permute-start.41 = (bf16[512,256]{1,0:T(8,128)(2,1)S(1)}, bf16[512,256]{1,0:T(8,128)(2,1)S(1)}, u32[]{:S(2)}, u32[]{:S(2)}) collective-permute-start(bf16[512,256]{1,0:T(8,128)(2,1)S(1)} %get-tuple-element.50), channel_id=1, source_target_pairs={{0,3},{3,0},{4,7},{7,4},{8,11},{11,8},{12,15},{15,12},{16,19},{19,... | collective-permute-start | bytes 786440 | tf_op jit(solution)/shard_map/ppermute | solution.py:393
  163.7 2.9 %terms.28 = bf16[512,256]{1,0:T(8,128)(2,1)S(1)} custom-call(s32[2]{0:T(128)S(1)} %pad_add_fusion.place_ref, bf16[8,2048,512]{2,1,0:T(8,128)(2,1)S(1)} %get-tuple-element.41.real_ref, bf16[8,2048,512]{2,1,0:T(8,128)(2,1)S(1)} %get-tuple-element.42.imag_ref, bf16[512,256]{1,0:T(8,128)(2,1)S(1)} %update.4.refs_0_, ...), custom_call_target="tpu_custom_call" | custom-call | flops 2147483648 | bytes 8388608 | tf_op jit(solution)/shard_map/terms/pallas_call | solution.py:306
  167.4 2.9 %terms.25.own_ref = f32[512,256]{1,0:T(8,128)S(1)} custom-call(s32[2]{0:T(128)S(1)} %pad_add_fusion.place_ref, bf16[8,2048,512]{2,1,0:T(8,128)(2,1)S(1)} %get-tuple-element.41.real_ref, bf16[8,2048,512]{2,1,0:T(8,128)(2,1)S(1)} %get-tuple-element.42.imag_ref, bf16[512,256]{1,0:T(8,128)(2,1)S(1)} %update.4.refs_0_, ...), custom_call_target="tpu_custom_call" | custom-call | flops 2147483648 | bytes 8388608 | tf_op jit(solution)/shard_map/terms/pallas_call | solution.py:306
  170.3 1.9 %collective-permute-done.41.refs_2_ = bf16[512,256]{1,0:T(8,128)(2,1)S(1)} collective-permute-done((bf16[512,256]{1,0:T(8,128)(2,1)S(1)}, bf16[512,256]{1,0:T(8,128)(2,1)S(1)}, u32[]{:S(2)}, u32[]{:S(2)}) %collective-permute-start.41) | collective-permute-done | bytes 262176 | tf_op jit(solution)/shard_map/ppermute | solution.py:393
  172.2 4.5 %collective-permute-done.40.refs_1_ = bf16[512,256]{1,0:T(8,128)(2,1)S(1)} collective-permute-done((bf16[512,256]{1,0:T(8,128)(2,1)S(1)}, bf16[512,256]{1,0:T(8,128)(2,1)S(1)}, u32[]{:S(2)}, u32[]{:S(2)}) %collective-permute-start.40) | collective-permute-done | bytes 262176 | tf_op jit(solution)/shard_map/ppermute | solution.py:382
  176.7 2.1 %update.5 = (f32[512,2,128]{2,1,0:T(2,128)}, f32[512,2,128]{2,1,0:T(2,128)}) custom-call(s32[2]{0:T(128)S(1)} %pad_add_fusion.place_ref, f32[2]{0:T(128)S(1)} %copy-done, f32[512,256]{1,0:T(8,128)S(1)} %terms.25.own_ref, bf16[512,256]{1,0:T(8,128)(2,1)S(1)} %collective-permute-done.39.other_ref.refs_0_, ...), custom_call_target="tpu_custom_call" | custom-call | flops 2097152 | bytes 2097152 | tf_op jit(solution)/shard_map/update/pallas_call | solution.py:369
  (72 shorter events, 11.4 us)
Async XLA Ops:
  0.7 37.0 %copy-start.1 = (s32[2048]{0:T(1024)S(1)}, s32[2048]{0:T(1024)}, u32[]{:S(2)}) copy-start(s32[2048]{0:T(1024)} %param.6) | copy-start | bytes 24580
  29.4 6.8 %collective-permute-start = (bf16[128,128]{1,0:T(8,128)(2,1)S(1)}, bf16[128,128]{1,0:T(8,128)(2,1)S(1)}, u32[]{:S(2)}, u32[]{:S(2)}) collective-permute-start(bf16[128,128]{1,0:T(8,128)(2,1)S(1)} %bitcast.19), channel_id=1, source_target_pairs={{0,28},{4,24},{8,20},{12,16},{16,12},{20,8},{24,4},{28,0},{1,29},{... | collective-permute-start | bytes 98312 | tf_op jit(solution)/shard_map/ppermute | solution.py:382
  32.7 5.0 %collective-permute-start.1 = (bf16[128,128]{1,0:T(8,128)(2,1)S(1)}, bf16[128,128]{1,0:T(8,128)(2,1)S(1)}, u32[]{:S(2)}, u32[]{:S(2)}) collective-permute-start(bf16[128,128]{1,0:T(8,128)(2,1)S(1)} %bitcast.18), channel_id=1, source_target_pairs={{0,24},{4,28},{8,16},{12,20},{16,8},{20,12},{24,0},{28,4},{1,25},{... | collective-permute-start | bytes 98312 | tf_op jit(solution)/shard_map/ppermute | solution.py:382
  33.4 6.4 %collective-permute-start.2 = (bf16[128,128]{1,0:T(8,128)(2,1)S(1)}, bf16[128,128]{1,0:T(8,128)(2,1)S(1)}, u32[]{:S(2)}, u32[]{:S(2)}) collective-permute-start(bf16[128,128]{1,0:T(8,128)(2,1)S(1)} %bitcast.17), channel_id=1, source_target_pairs={{0,20},{4,16},{8,28},{12,24},{16,4},{20,0},{24,12},{28,8},{1,21},{... | collective-permute-start | bytes 98312 | tf_op jit(solution)/shard_map/ppermute | solution.py:382
  34.7 5.0 %collective-permute-start.3 = (bf16[128,128]{1,0:T(8,128)(2,1)S(1)}, bf16[128,128]{1,0:T(8,128)(2,1)S(1)}, u32[]{:S(2)}, u32[]{:S(2)}) collective-permute-start(bf16[128,128]{1,0:T(8,128)(2,1)S(1)} %bitcast.16), channel_id=1, source_target_pairs={{0,16},{4,20},{8,24},{12,28},{16,0},{20,4},{24,8},{28,12},{1,17},{... | collective-permute-start | bytes 98312 | tf_op jit(solution)/shard_map/ppermute | solution.py:382
  35.1 4.7 %collective-permute-start.4 = (bf16[128,128]{1,0:T(8,128)(2,1)S(1)}, bf16[128,128]{1,0:T(8,128)(2,1)S(1)}, u32[]{:S(2)}, u32[]{:S(2)}) collective-permute-start(bf16[128,128]{1,0:T(8,128)(2,1)S(1)} %bitcast.15), channel_id=1, source_target_pairs={{0,12},{4,8},{8,4},{12,0},{16,28},{20,24},{24,20},{28,16},{1,13},{... | collective-permute-start | bytes 98312 | tf_op jit(solution)/shard_map/ppermute | solution.py:382
  36.2 4.0 %collective-permute-start.5 = (bf16[128,128]{1,0:T(8,128)(2,1)S(1)}, bf16[128,128]{1,0:T(8,128)(2,1)S(1)}, u32[]{:S(2)}, u32[]{:S(2)}) collective-permute-start(bf16[128,128]{1,0:T(8,128)(2,1)S(1)} %bitcast.14), channel_id=1, source_target_pairs={{0,8},{4,12},{8,0},{12,4},{16,24},{20,28},{24,16},{28,20},{1,9},{5... | collective-permute-start | bytes 98312 | tf_op jit(solution)/shard_map/ppermute | solution.py:382
  37.7 2.5 %collective-permute-start.6 = (bf16[128,128]{1,0:T(8,128)(2,1)S(1)}, bf16[128,128]{1,0:T(8,128)(2,1)S(1)}, u32[]{:S(2)}, u32[]{:S(2)}) collective-permute-start(bf16[128,128]{1,0:T(8,128)(2,1)S(1)} %bitcast.13), channel_id=1, source_target_pairs={{0,4},{4,0},{8,12},{12,8},{16,20},{20,16},{24,28},{28,24},{1,5},{5... | collective-permute-start | bytes 98312 | tf_op jit(solution)/shard_map/ppermute | solution.py:382
  42.6 12.1 %collective-permute-start.7 = (bf16[256,128]{1,0:T(8,128)(2,1)S(1)}, bf16[256,128]{1,0:T(8,128)(2,1)S(1)}, u32[]{:S(2)}, u32[]{:S(2)}) collective-permute-start(bf16[256,128]{1,0:T(8,128)(2,1)S(1)} %get-tuple-element.36), channel_id=1, source_target_pairs={{0,3},{1,2},{2,1},{3,0},{4,7},{5,6},{6,5},{7,4},{8,11},{9,10},{10,... | collective-permute-start | bytes 196616 | tf_op jit(solution)/shard_map/ppermute | solution.py:382
  46.2 8.5 %collective-permute-start.8 = (bf16[256,128]{1,0:T(8,128)(2,1)S(1)}, bf16[256,128]{1,0:T(8,128)(2,1)S(1)}, u32[]{:S(2)}, u32[]{:S(2)}) collective-permute-start(bf16[256,128]{1,0:T(8,128)(2,1)S(1)} %get-tuple-element.37), channel_id=1, source_target_pairs={{0,2},{1,3},{2,0},{3,1},{4,6},{5,7},{6,4},{7,5},{8,10},{9,11},{10,... | collective-permute-start | bytes 196616 | tf_op jit(solution)/shard_map/ppermute | solution.py:382
  46.2 8.5 %collective-permute-start.9 = (bf16[256,128]{1,0:T(8,128)(2,1)S(1)}, bf16[256,128]{1,0:T(8,128)(2,1)S(1)}, u32[]{:S(2)}, u32[]{:S(2)}) collective-permute-start(bf16[256,128]{1,0:T(8,128)(2,1)S(1)} %get-tuple-element.38), channel_id=1, source_target_pairs={{0,1},{1,0},{2,3},{3,2},{4,5},{5,4},{6,7},{7,6},{8,9},{9,8},{10,11... | collective-permute-start | bytes 196616 | tf_op jit(solution)/shard_map/ppermute | solution.py:382
  55.7 11.5 %collective-permute-start.10 = (bf16[512,256]{1,0:T(8,128)(2,1)S(1)}, bf16[512,256]{1,0:T(8,128)(2,1)S(1)}, u32[]{:S(2)}, u32[]{:S(2)}) collective-permute-start(bf16[512,256]{1,0:T(8,128)(2,1)S(1)} %panel.1.refs_0_.refs_4_), channel_id=1, source_target_pairs={{0,24},{4,28},{8,16},{12,20},{16,8},{20,12},{24,0},{28,4},{1,25},{... | collective-permute-start | bytes 786440 | tf_op jit(solution)/shard_map/ppermute | solution.py:382
  57.7 12.3 %collective-permute-start.11 = (bf16[512,256]{1,0:T(8,128)(2,1)S(1)}, bf16[512,256]{1,0:T(8,128)(2,1)S(1)}, u32[]{:S(2)}, u32[]{:S(2)}) collective-permute-start(bf16[512,256]{1,0:T(8,128)(2,1)S(1)} %panel.1.refs_0_.refs_4_), channel_id=1, source_target_pairs={{0,16},{4,20},{8,24},{12,28},{16,0},{20,4},{24,8},{28,12},{1,17},{... | collective-permute-start | bytes 786440 | tf_op jit(solution)/shard_map/ppermute | solution.py:382
  58.2 11.7 %collective-permute-start.12 = (bf16[512,256]{1,0:T(8,128)(2,1)S(1)}, bf16[512,256]{1,0:T(8,128)(2,1)S(1)}, u32[]{:S(2)}, u32[]{:S(2)}) collective-permute-start(bf16[512,256]{1,0:T(8,128)(2,1)S(1)} %panel.1.refs_0_.refs_4_), channel_id=1, source_target_pairs={{0,8},{4,12},{8,0},{12,4},{16,24},{20,28},{24,16},{28,20},{1,9},{5... | collective-permute-start | bytes 786440 | tf_op jit(solution)/shard_map/ppermute | solution.py:382
  59.3 11.2 %collective-permute-start.13 = (bf16[512,256]{1,0:T(8,128)(2,1)S(1)}, bf16[512,256]{1,0:T(8,128)(2,1)S(1)}, u32[]{:S(2)}, u32[]{:S(2)}) collective-permute-start(bf16[512,256]{1,0:T(8,128)(2,1)S(1)} %panel.1.refs_0_.refs_4_), channel_id=1, source_target_pairs={{0,4},{4,0},{8,12},{12,8},{16,20},{20,16},{24,28},{28,24},{1,5},{5... | collective-permute-start | bytes 786440 | tf_op jit(solution)/shard_map/ppermute | solution.py:382
  69.9 2.6 %collective-permute-start.14 = (bf16[512,256]{1,0:T(8,128)(2,1)S(1)}, bf16[512,256]{1,0:T(8,128)(2,1)S(1)}, u32[]{:S(2)}, u32[]{:S(2)}) collective-permute-start(bf16[512,256]{1,0:T(8,128)(2,1)S(1)} %collective-permute-done.10.refs_2_), channel_id=1, source_target_pairs={{0,4},{4,0},{8,12},{12,8},{16,20},{20,16},{24,28},{28,24},{1,5},{5... | collective-permute-start | bytes 786440 | tf_op jit(solution)/shard_map/ppermute | solution.py:382
  69.9 2.6 %collective-permute-start.15 = (bf16[512,256]{1,0:T(8,128)(2,1)S(1)}, bf16[512,256]{1,0:T(8,128)(2,1)S(1)}, u32[]{:S(2)}, u32[]{:S(2)}) collective-permute-start(bf16[512,256]{1,0:T(8,128)(2,1)S(1)} %collective-permute-done.11.refs_3_), channel_id=1, source_target_pairs={{0,4},{4,0},{8,12},{12,8},{16,20},{20,16},{24,28},{28,24},{1,5},{5... | collective-permute-start | bytes 786440 | tf_op jit(solution)/shard_map/ppermute | solution.py:382
  70.4 2.1 %collective-permute-start.16 = (bf16[512,256]{1,0:T(8,128)(2,1)S(1)}, bf16[512,256]{1,0:T(8,128)(2,1)S(1)}, u32[]{:S(2)}, u32[]{:S(2)}) collective-permute-start(bf16[512,256]{1,0:T(8,128)(2,1)S(1)} %collective-permute-done.12.refs_4_), channel_id=1, source_target_pairs={{0,4},{4,0},{8,12},{12,8},{16,20},{20,16},{24,28},{28,24},{1,5},{5... | collective-permute-start | bytes 786440 | tf_op jit(solution)/shard_map/ppermute | solution.py:382
  74.1 11.5 %collective-permute-start.17 = (bf16[512,256]{1,0:T(8,128)(2,1)S(1)}, bf16[512,256]{1,0:T(8,128)(2,1)S(1)}, u32[]{:S(2)}, u32[]{:S(2)}) collective-permute-start(bf16[512,256]{1,0:T(8,128)(2,1)S(1)} %terms.17), channel_id=1, source_target_pairs={{0,1},{1,3},{3,2},{2,0},{4,5},{5,7},{7,6},{6,4},{8,9},{9,11},{11,1... | collective-permute-start | bytes 786440 | tf_op jit(solution)/shard_map/ppermute | solution.py:390
  78.4 12.8 %collective-permute-start.19 = (bf16[512,256]{1,0:T(8,128)(2,1)S(1)}, bf16[512,256]{1,0:T(8,128)(2,1)S(1)}, u32[]{:S(2)}, u32[]{:S(2)}) collective-permute-start(bf16[512,256]{1,0:T(8,128)(2,1)S(1)} %get-tuple-element.46), channel_id=1, source_target_pairs={{0,3},{3,0},{4,7},{7,4},{8,11},{11,8},{12,15},{15,12},{16,19},{19,... | collective-permute-start | bytes 786440 | tf_op jit(solution)/shard_map/ppermute | solution.py:393
  85.6 10.6 %collective-permute-start.18 = (bf16[512,256]{1,0:T(8,128)(2,1)S(1)}, bf16[512,256]{1,0:T(8,128)(2,1)S(1)}, u32[]{:S(2)}, u32[]{:S(2)}) collective-permute-start(bf16[512,256]{1,0:T(8,128)(2,1)S(1)} %terms.18), channel_id=1, source_target_pairs={{0,1},{1,0},{2,3},{3,2},{4,5},{5,4},{6,7},{7,6},{8,9},{9,8},{10,11... | collective-permute-start | bytes 786440 | tf_op jit(solution)/shard_map/ppermute | solution.py:382
  85.7 10.4 %copy-start = (f32[2]{0:T(128)S(1)}, f32[2]{0:T(128)}, u32[]{:S(2)}) copy-start(f32[2]{0:T(128)} %wave_ref.5) | copy-start | bytes 28
  85.7 10.4 %collective-permute-start.20 = (bf16[512,256]{1,0:T(8,128)(2,1)S(1)}, bf16[512,256]{1,0:T(8,128)(2,1)S(1)}, u32[]{:S(2)}, u32[]{:S(2)}) collective-permute-start(bf16[512,256]{1,0:T(8,128)(2,1)S(1)} %sum.3), channel_id=1, source_target_pairs={{1,2},{2,1},{5,6},{6,5},{9,10},{10,9},{13,14},{14,13},{17,18},{18,... | collective-permute-start | bytes 786440 | tf_op jit(solution)/shard_map/ppermute | solution.py:394
  97.0 10.2 %collective-permute-start.24 = (bf16[512,256]{1,0:T(8,128)(2,1)S(1)}, bf16[512,256]{1,0:T(8,128)(2,1)S(1)}, u32[]{:S(2)}, u32[]{:S(2)}) collective-permute-start(bf16[512,256]{1,0:T(8,128)(2,1)S(1)} %update.3.refs_0_), channel_id=1, source_target_pairs={{0,24},{4,28},{8,16},{12,20},{16,8},{20,12},{24,0},{28,4},{1,25},{... | collective-permute-start | bytes 786440 | tf_op jit(solution)/shard_map/ppermute | solution.py:382
  98.8 13.0 %collective-permute-start.23 = (bf16[512,256]{1,0:T(8,128)(2,1)S(1)}, bf16[512,256]{1,0:T(8,128)(2,1)S(1)}, u32[]{:S(2)}, u32[]{:S(2)}) collective-permute-start(bf16[512,256]{1,0:T(8,128)(2,1)S(1)} %update.3.refs_0_), channel_id=1, source_target_pairs={{0,16},{4,20},{8,24},{12,28},{16,0},{20,4},{24,8},{28,12},{1,17},{... | collective-permute-start | bytes 786440 | tf_op jit(solution)/shard_map/ppermute | solution.py:382
  99.5 12.3 %collective-permute-start.22 = (bf16[512,256]{1,0:T(8,128)(2,1)S(1)}, bf16[512,256]{1,0:T(8,128)(2,1)S(1)}, u32[]{:S(2)}, u32[]{:S(2)}) collective-permute-start(bf16[512,256]{1,0:T(8,128)(2,1)S(1)} %update.3.refs_0_), channel_id=1, source_target_pairs={{0,8},{4,12},{8,0},{12,4},{16,24},{20,28},{24,16},{28,20},{1,9},{5... | collective-permute-start | bytes 786440 | tf_op jit(solution)/shard_map/ppermute | solution.py:382
  100.5 11.8 %collective-permute-start.21 = (bf16[512,256]{1,0:T(8,128)(2,1)S(1)}, bf16[512,256]{1,0:T(8,128)(2,1)S(1)}, u32[]{:S(2)}, u32[]{:S(2)}) collective-permute-start(bf16[512,256]{1,0:T(8,128)(2,1)S(1)} %update.3.refs_0_), channel_id=1, source_target_pairs={{0,4},{4,0},{8,12},{12,8},{16,20},{20,16},{24,28},{28,24},{1,5},{5... | collective-permute-start | bytes 786440 | tf_op jit(solution)/shard_map/ppermute | solution.py:382
  107.1 7.2 %collective-permute-start.25 = (bf16[512,256]{1,0:T(8,128)(2,1)S(1)}, bf16[512,256]{1,0:T(8,128)(2,1)S(1)}, u32[]{:S(2)}, u32[]{:S(2)}) collective-permute-start(bf16[512,256]{1,0:T(8,128)(2,1)S(1)} %collective-permute-done.24.refs_4_), channel_id=1, source_target_pairs={{0,4},{4,0},{8,12},{12,8},{16,20},{20,16},{24,28},{28,24},{1,5},{5... | collective-permute-start | bytes 786440 | tf_op jit(solution)/shard_map/ppermute | solution.py:382
  111.8 2.6 %collective-permute-start.26 = (bf16[512,256]{1,0:T(8,128)(2,1)S(1)}, bf16[512,256]{1,0:T(8,128)(2,1)S(1)}, u32[]{:S(2)}, u32[]{:S(2)}) collective-permute-start(bf16[512,256]{1,0:T(8,128)(2,1)S(1)} %collective-permute-done.23.refs_3_), channel_id=1, source_target_pairs={{0,4},{4,0},{8,12},{12,8},{16,20},{20,16},{24,28},{28,24},{1,5},{5... | collective-permute-start | bytes 786440 | tf_op jit(solution)/shard_map/ppermute | solution.py:382
  111.8 2.6 %collective-permute-start.27 = (bf16[512,256]{1,0:T(8,128)(2,1)S(1)}, bf16[512,256]{1,0:T(8,128)(2,1)S(1)}, u32[]{:S(2)}, u32[]{:S(2)}) collective-permute-start(bf16[512,256]{1,0:T(8,128)(2,1)S(1)} %collective-permute-done.22.refs_2_), channel_id=1, source_target_pairs={{0,4},{4,0},{8,12},{12,8},{16,20},{20,16},{24,28},{28,24},{1,5},{5... | collective-permute-start | bytes 786440 | tf_op jit(solution)/shard_map/ppermute | solution.py:382
  115.9 10.2 %collective-permute-start.28 = (bf16[512,256]{1,0:T(8,128)(2,1)S(1)}, bf16[512,256]{1,0:T(8,128)(2,1)S(1)}, u32[]{:S(2)}, u32[]{:S(2)}) collective-permute-start(bf16[512,256]{1,0:T(8,128)(2,1)S(1)} %terms.22), channel_id=1, source_target_pairs={{0,1},{1,3},{3,2},{2,0},{4,5},{5,7},{7,6},{6,4},{8,9},{9,11},{11,1... | collective-permute-start | bytes 786440 | tf_op jit(solution)/shard_map/ppermute | solution.py:390
  119.0 12.9 %collective-permute-start.30 = (bf16[512,256]{1,0:T(8,128)(2,1)S(1)}, bf16[512,256]{1,0:T(8,128)(2,1)S(1)}, u32[]{:S(2)}, u32[]{:S(2)}) collective-permute-start(bf16[512,256]{1,0:T(8,128)(2,1)S(1)} %get-tuple-element.48), channel_id=1, source_target_pairs={{0,3},{3,0},{4,7},{7,4},{8,11},{11,8},{12,15},{15,12},{16,19},{19,... | collective-permute-start | bytes 786440 | tf_op jit(solution)/shard_map/ppermute | solution.py:393
  126.1 10.4 %collective-permute-start.29 = (bf16[512,256]{1,0:T(8,128)(2,1)S(1)}, bf16[512,256]{1,0:T(8,128)(2,1)S(1)}, u32[]{:S(2)}, u32[]{:S(2)}) collective-permute-start(bf16[512,256]{1,0:T(8,128)(2,1)S(1)} %terms.23), channel_id=1, source_target_pairs={{0,1},{1,0},{2,3},{3,2},{4,5},{5,4},{6,7},{7,6},{8,9},{9,8},{10,11... | collective-permute-start | bytes 786440 | tf_op jit(solution)/shard_map/ppermute | solution.py:382
  126.2 10.2 %collective-permute-start.31 = (bf16[512,256]{1,0:T(8,128)(2,1)S(1)}, bf16[512,256]{1,0:T(8,128)(2,1)S(1)}, u32[]{:S(2)}, u32[]{:S(2)}) collective-permute-start(bf16[512,256]{1,0:T(8,128)(2,1)S(1)} %sum.4), channel_id=1, source_target_pairs={{1,2},{2,1},{5,6},{6,5},{9,10},{10,9},{13,14},{14,13},{17,18},{18,... | collective-permute-start | bytes 786440 | tf_op jit(solution)/shard_map/ppermute | solution.py:394
  137.3 10.2 %collective-permute-start.35 = (bf16[512,256]{1,0:T(8,128)(2,1)S(1)}, bf16[512,256]{1,0:T(8,128)(2,1)S(1)}, u32[]{:S(2)}, u32[]{:S(2)}) collective-permute-start(bf16[512,256]{1,0:T(8,128)(2,1)S(1)} %update.4.refs_0_), channel_id=1, source_target_pairs={{0,24},{4,28},{8,16},{12,20},{16,8},{20,12},{24,0},{28,4},{1,25},{... | collective-permute-start | bytes 786440 | tf_op jit(solution)/shard_map/ppermute | solution.py:382
  139.1 13.0 %collective-permute-start.34 = (bf16[512,256]{1,0:T(8,128)(2,1)S(1)}, bf16[512,256]{1,0:T(8,128)(2,1)S(1)}, u32[]{:S(2)}, u32[]{:S(2)}) collective-permute-start(bf16[512,256]{1,0:T(8,128)(2,1)S(1)} %update.4.refs_0_), channel_id=1, source_target_pairs={{0,16},{4,20},{8,24},{12,28},{16,0},{20,4},{24,8},{28,12},{1,17},{... | collective-permute-start | bytes 786440 | tf_op jit(solution)/shard_map/ppermute | solution.py:382
  139.8 12.3 %collective-permute-start.33 = (bf16[512,256]{1,0:T(8,128)(2,1)S(1)}, bf16[512,256]{1,0:T(8,128)(2,1)S(1)}, u32[]{:S(2)}, u32[]{:S(2)}) collective-permute-start(bf16[512,256]{1,0:T(8,128)(2,1)S(1)} %update.4.refs_0_), channel_id=1, source_target_pairs={{0,8},{4,12},{8,0},{12,4},{16,24},{20,28},{24,16},{28,20},{1,9},{5... | collective-permute-start | bytes 786440 | tf_op jit(solution)/shard_map/ppermute | solution.py:382
  140.8 11.8 %collective-permute-start.32 = (bf16[512,256]{1,0:T(8,128)(2,1)S(1)}, bf16[512,256]{1,0:T(8,128)(2,1)S(1)}, u32[]{:S(2)}, u32[]{:S(2)}) collective-permute-start(bf16[512,256]{1,0:T(8,128)(2,1)S(1)} %update.4.refs_0_), channel_id=1, source_target_pairs={{0,4},{4,0},{8,12},{12,8},{16,20},{20,16},{24,28},{28,24},{1,5},{5... | collective-permute-start | bytes 786440 | tf_op jit(solution)/shard_map/ppermute | solution.py:382
  147.4 7.2 %collective-permute-start.36 = (bf16[512,256]{1,0:T(8,128)(2,1)S(1)}, bf16[512,256]{1,0:T(8,128)(2,1)S(1)}, u32[]{:S(2)}, u32[]{:S(2)}) collective-permute-start(bf16[512,256]{1,0:T(8,128)(2,1)S(1)} %collective-permute-done.35.refs_4_), channel_id=1, source_target_pairs={{0,4},{4,0},{8,12},{12,8},{16,20},{20,16},{24,28},{28,24},{1,5},{5... | collective-permute-start | bytes 786440 | tf_op jit(solution)/shard_map/ppermute | solution.py:382
  152.1 2.6 %collective-permute-start.37 = (bf16[512,256]{1,0:T(8,128)(2,1)S(1)}, bf16[512,256]{1,0:T(8,128)(2,1)S(1)}, u32[]{:S(2)}, u32[]{:S(2)}) collective-permute-start(bf16[512,256]{1,0:T(8,128)(2,1)S(1)} %collective-permute-done.34.refs_3_), channel_id=1, source_target_pairs={{0,4},{4,0},{8,12},{12,8},{16,20},{20,16},{24,28},{28,24},{1,5},{5... | collective-permute-start | bytes 786440 | tf_op jit(solution)/shard_map/ppermute | solution.py:382
  152.1 2.6 %collective-permute-start.38 = (bf16[512,256]{1,0:T(8,128)(2,1)S(1)}, bf16[512,256]{1,0:T(8,128)(2,1)S(1)}, u32[]{:S(2)}, u32[]{:S(2)}) collective-permute-start(bf16[512,256]{1,0:T(8,128)(2,1)S(1)} %collective-permute-done.33.refs_2_), channel_id=1, source_target_pairs={{0,4},{4,0},{8,12},{12,8},{16,20},{20,16},{24,28},{28,24},{1,5},{5... | collective-permute-start | bytes 786440 | tf_op jit(solution)/shard_map/ppermute | solution.py:382
  156.2 10.4 %collective-permute-start.39 = (bf16[512,256]{1,0:T(8,128)(2,1)S(1)}, bf16[512,256]{1,0:T(8,128)(2,1)S(1)}, u32[]{:S(2)}, u32[]{:S(2)}) collective-permute-start(bf16[512,256]{1,0:T(8,128)(2,1)S(1)} %terms.27), channel_id=1, source_target_pairs={{0,1},{1,3},{3,2},{2,0},{4,5},{5,7},{7,6},{6,4},{8,9},{9,11},{11,1... | collective-permute-start | bytes 786440 | tf_op jit(solution)/shard_map/ppermute | solution.py:390
  159.3 12.9 %collective-permute-start.41 = (bf16[512,256]{1,0:T(8,128)(2,1)S(1)}, bf16[512,256]{1,0:T(8,128)(2,1)S(1)}, u32[]{:S(2)}, u32[]{:S(2)}) collective-permute-start(bf16[512,256]{1,0:T(8,128)(2,1)S(1)} %get-tuple-element.50), channel_id=1, source_target_pairs={{0,3},{3,0},{4,7},{7,4},{8,11},{11,8},{12,15},{15,12},{16,19},{19,... | collective-permute-start | bytes 786440 | tf_op jit(solution)/shard_map/ppermute | solution.py:393
  166.6 10.1 %collective-permute-start.40 = (bf16[512,256]{1,0:T(8,128)(2,1)S(1)}, bf16[512,256]{1,0:T(8,128)(2,1)S(1)}, u32[]{:S(2)}, u32[]{:S(2)}) collective-permute-start(bf16[512,256]{1,0:T(8,128)(2,1)S(1)} %terms.28), channel_id=1, source_target_pairs={{0,1},{1,0},{2,3},{3,2},{4,5},{5,4},{6,7},{7,6},{8,9},{9,8},{10,11... | collective-permute-start | bytes 786440 | tf_op jit(solution)/shard_map/ppermute | solution.py:382
  166.7 10.0 %collective-permute-start.42 = (bf16[512,256]{1,0:T(8,128)(2,1)S(1)}, bf16[512,256]{1,0:T(8,128)(2,1)S(1)}, u32[]{:S(2)}, u32[]{:S(2)}) collective-permute-start(bf16[512,256]{1,0:T(8,128)(2,1)S(1)} %sum.5), channel_id=1, source_target_pairs={{1,2},{2,1},{5,6},{6,5},{9,10},{10,9},{13,14},{14,13},{17,18},{18,... | collective-permute-start | bytes 786440 | tf_op jit(solution)/shard_map/ppermute | solution.py:394
